TPU v7x, 32 devices: a whole 2x2x4 slice. The times are simulated.
32 devices in a mesh: seq: 8 (over y, x, core), chan: 4 (over z).
Axes of the slice: x: 2, y: 2, z: 4, core: 2. Of those that a mesh axis runs over, the one named last changes fastest.
Arguments:
- outer_gate: bfloat16 [1024, 8192], P('chan', 'seq'), may hold values from -6 to 6
- inner_gate: bfloat16 [1024, 8192], P('chan', 'seq'), may hold values from -6 to 6
- signal: bfloat16 [1024, 8192], P('chan', 'seq'), may hold values from -6 to 6
- long_filter: bfloat16 [1024, 8192], P('chan', 'seq'), may hold values from -2 to 2
- grad_output: bfloat16 [8192, 8192], P('chan', 'seq'), may hold values from -6 to 6
- out_proj: bfloat16 [1024, 8192], P(None, 'chan'), may hold values from -0.0625 to 0.0625
Outputs:
- grad_outer: bfloat16 [1024, 8192], P('chan', 'seq')
- grad_inner: bfloat16 [1024, 8192], P('chan', 'seq')
- grad_signal: bfloat16 [1024, 8192], P('chan', 'seq')
- grad_filter: float32 [1024, 8192], P('chan', 'seq')
- grad_proj: float32 [1024, 8192], P('seq', 'chan')
All inputs are finite; a program needn't handle non-finite values.
Results may differ from a plain program's by a relative error of at most 0.025.
Values may be sent and summed in bfloat16 or wider, within the bound.
No kernel may reach another device: no remote copies, remote signals or barrier semaphores. Data moves between devices by JAX's collectives and lax.ppermute only.
A program may use at most 128 MiB of HBM per device.

v0:
```python
import math

import jax
import jax.numpy as jnp
from jax import lax
from jax.sharding import PartitionSpec as P


def as_sent(x):

    def short(part):
        return part.astype(jnp.bfloat16) if part.dtype == jnp.float32 else part

    return jax.tree.map(short, x)


def twiddles(rows, cols, modulus, sign, row_shift, col_shift):
    row_index = lax.broadcasted_iota(jnp.int32, (rows, cols), 0) + row_shift
    col_index = lax.broadcasted_iota(jnp.int32, (rows, cols), 1) + col_shift
    angle = 2.0 * math.pi / modulus * (row_index * col_index % modulus).astype(jnp.float32)
    return (jnp.cos(angle), sign * jnp.sin(angle))


def contract(form, table, data):
    return jnp.einsum(form, table, data, precision=lax.Precision.HIGHEST)


def rotate(real_in, imag_in, cosine, sine):
    return (real_in * cosine - imag_in * sine, real_in * sine + imag_in * cosine)


def apply_table(form, cosine, sine, real_in, imag_in):
    if imag_in is None:
        return (contract(form, cosine, real_in), contract(form, sine, real_in))
    return (
        contract(form, cosine, real_in) - contract(form, sine, imag_in),
        contract(form, sine, real_in) + contract(form, cosine, imag_in),
    )


def local_dft(real_in, imag_in, sign, real_only=False):
    length = real_in.shape[-1]
    outer_len = 1
    while outer_len * outer_len < length and length % (outer_len * 2) == 0:
        outer_len = outer_len * 2
    inner_len = length // outer_len
    leading = real_in.shape[:-1]
    shaped = leading + (outer_len, inner_len)
    real_in = real_in.reshape(shaped)
    imag_in = imag_in.reshape(shaped)
    cos_left, sin_left = twiddles(outer_len, outer_len, outer_len, sign, 0, 0)
    part_re, part_im = apply_table("kt,...tj->...kj", cos_left, sin_left, real_in, imag_in)
    cos_mid, sin_mid = twiddles(outer_len, inner_len, length, sign, 0, 0)
    part_re, part_im = rotate(part_re, part_im, cos_mid, sin_mid)
    cos_right, sin_right = twiddles(inner_len, inner_len, inner_len, sign, 0, 0)
    out_re, out_im = apply_table("tm,...kt->...km", cos_right, sin_right, part_re, part_im)
    out_re = jnp.swapaxes(out_re, -1, -2).reshape(leading + (length,))
    out_im = jnp.swapaxes(out_im, -1, -2).reshape(leading + (length,))
    return (out_re, out_im)


def spectra_products(spec_re, spec_im):
    signal_re, kernel_re, grad_re = (spec_re[0], spec_re[1], spec_re[2])
    signal_im, kernel_im, grad_im = (spec_im[0], spec_im[1], spec_im[2])
    prod_re = jnp.stack(
        [
            kernel_re * signal_re - kernel_im * signal_im,
            kernel_re * grad_re + kernel_im * grad_im,
            signal_re * grad_re + signal_im * grad_im,
        ]
    )
    prod_im = jnp.stack(
        [
            kernel_re * signal_im + kernel_im * signal_re,
            kernel_re * grad_im - kernel_im * grad_re,
            signal_re * grad_im - signal_im * grad_re,
        ]
    )
    return (prod_re, prod_im)


def split_transform(stacked, chan_rows, block_len):
    seq_count = lax.axis_size("seq")
    seq_place = lax.axis_index("seq")
    col_count = block_len // seq_count
    freq_span = 2 * seq_count
    full_len = freq_span * block_len
    moved = lax.all_to_all(
        stacked.reshape(3, chan_rows, 1, block_len), "seq", split_axis=3, concat_axis=2, tiled=True
    )
    moved = moved.astype(jnp.float32)
    cos_first, sin_first = twiddles(freq_span, seq_count, freq_span, -1.0, 0, 0)
    part_re, part_im = apply_table("ca,...aj->...cj", cos_first, sin_first, moved, None)
    cos_second, sin_second = twiddles(
        freq_span, col_count, full_len, -1.0, 0, seq_place * col_count
    )
    part_re, part_im = rotate(part_re, part_im, cos_second, sin_second)
    turned = lax.all_to_all(
        jnp.stack([part_re, part_im]).astype(jnp.bfloat16),
        "seq",
        split_axis=3,
        concat_axis=4,
        tiled=True,
    ).astype(jnp.float32)
    spec_re, spec_im = local_dft(turned[0], turned[1], -1.0)
    prod_re, prod_im = spectra_products(spec_re, spec_im)
    back_re, back_im = local_dft(prod_re, prod_im, 1.0)
    cos_third, sin_third = twiddles(2, block_len, full_len, 1.0, 2 * seq_place, 0)
    back_re, back_im = rotate(back_re, back_im, cos_third, sin_third)
    returned = lax.all_to_all(
        as_sent(jnp.stack([back_re, back_im])), "seq", split_axis=4, concat_axis=3, tiled=True
    )
    cos_last, sin_last = twiddles(seq_count, freq_span, freq_span, 1.0, 0, 0)
    real_out = (
        contract("ac,...cj->...aj", cos_last, returned[0])
        - contract("ac,...cj->...aj", sin_last, returned[1])
    ) / full_len
    timed = lax.all_to_all(
        as_sent(real_out), "seq", split_axis=2, concat_axis=3, tiled=True
    ).astype(real_out.dtype)
    return timed.reshape(3, chan_rows, block_len)


def body(outer_gate, inner_gate, signal, long_filter, grad_output, out_proj):
    chan_rows = outer_gate.shape[0]
    block_len = outer_gate.shape[1]
    mixed_in = (inner_gate.astype(jnp.float32) * signal.astype(jnp.float32)).astype(jnp.bfloat16)
    rows = out_proj
    grad_mix = lax.psum_scatter(
        jnp.dot(rows, grad_output, preferred_element_type=jnp.float32).astype(jnp.bfloat16),
        "chan",
        scatter_dimension=0,
        tiled=True,
    ).astype(jnp.float32)
    grad_conv = (grad_mix * outer_gate.astype(jnp.float32)).astype(jnp.bfloat16)
    stacked = jnp.stack([mixed_in, long_filter, grad_conv])
    timed = split_transform(stacked, chan_rows, block_len)
    conv_out = timed[0]
    grad_prod = timed[1]
    grad_filter = timed[2]
    mixed = (outer_gate.astype(jnp.float32) * conv_out).astype(jnp.bfloat16)
    grad_outer = (grad_mix * conv_out).astype(jnp.bfloat16)
    grad_inner = (grad_prod * signal.astype(jnp.float32)).astype(jnp.bfloat16)
    grad_signal = (grad_prod * inner_gate.astype(jnp.float32)).astype(jnp.bfloat16)
    mixed_all = lax.all_gather(mixed, "chan", axis=0, tiled=True)
    rows = mixed_all
    grad_proj = lax.psum_scatter(
        lax.dot_general(
            rows, grad_output, (((1,), (1,)), ((), ())), preferred_element_type=jnp.float32
        ).astype(jnp.bfloat16),
        "seq",
        scatter_dimension=0,
        tiled=True,
    ).astype(jnp.float32)
    return (grad_outer, grad_inner, grad_signal, grad_filter, grad_proj)


def solution(mesh):
    in_specs = (
        P("chan", "seq"),
        P("chan", "seq"),
        P("chan", "seq"),
        P("chan", "seq"),
        P("chan", "seq"),
        P(None, "chan"),
    )
    out_specs = (
        P("chan", "seq"),
        P("chan", "seq"),
        P("chan", "seq"),
        P("chan", "seq"),
        P("seq", "chan"),
    )
    return jax.shard_map(body, mesh=mesh, in_specs=in_specs, out_specs=out_specs, check_vma=False)
```

profile of v0, /device:TPU:0, one launch (start us, length us, event | category | flops | bytes accessed | tf_op | source)
XLA Modules:
  0.0 647.2 jit_solution(3037993390639347505)
XLA Ops:
  7.3 9.4 %convolution_convert_fusion.1 = bf16[1024,1024]{1,0:T(8,128)(2,1)} fusion(bf16[1024,2048]{1,0:T(8,128)(2,1)} %param.11, bf16[2048,1024]{1,0:T(8,128)(2,1)} %param.10), kind=kOutput, calls=%fused_computation.74 | convolution fusion | flops 4296015872 | bytes 10485760 | tf_op jit(solution)/shard_map/dot_general | solution.py:130
  16.9 46.5 %reduce-scatter.3.cloned.1.call-done = bf16[256,1024]{1,0:T(8,128)(2,1)} async-done(((bf16[1024,1024]{1,0:T(8,128)(2,1)}), bf16[256,1024]{1,0:T(8,128)(2,1)}) %reduce-scatter.3.cloned.1.call-update) | async-done | bytes 524304 | tf_op jit(solution)/shard_map/reduce_scatter | solution.py:129
  71.5 26.5 %all-to-all-done = bf16[3,256,1,1024]{1,0,2,3:T(4,128)(2,1)S(1)} async-done(((bf16[3,256,1,1024]{1,0,2,3:T(4,128)(2,1)}), bf16[3,256,1,1024]{1,0,2,3:T(4,128)(2,1)S(1)}, u32[]{:S(2)}, u32[]{:S(2)}) %all-to-all-start) | async-done | bytes 1572896 | tf_op jit(solution)/shard_map/all_to_all | solution.py:88
  104.7 4.6 fusion.33
  114.2 4.8 all-to-all-start.1
  119.4 71.1 %all-to-all-done.1 = bf16[2,3,256,16,128]{4,2,1,0,3:T(8,128)(2,1)} async-done(((bf16[2,3,256,16,128]{4,2,1,0,3:T(8,128)(2,1)}), bf16[2,3,256,16,128]{4,2,1,0,3:T(8,128)(2,1)}, u32[]{:S(2)}, u32[]{:S(2)}) %all-to-all-start.1) | async-done | bytes 6291488 | tf_op jit(solution)/shard_map/all_to_all | solution.py:98
  200.6 5.5 fusion.34
  206.1 5.5 fusion.36
  214.8 5.5 fusion.40
  220.3 14.6 %fusion.6 = (f32[3,256,2,32,32]{1,3,4,2,0:T(8,128)S(1)}, f32[3,256,2,32,32]{1,3,4,2,0:T(8,128)S(1)}) fusion(f32[32,32]{0,1:T(8,128)S(1)} %get-tuple-element.39, f32[32,32]{0,1:T(8,128)S(1)} %get-tuple-element.40, f32[3,256,2,32,32]{1,4,3,2,0:T(8,128)} %fusion.34, f32[3,256,2,32,32]{1,4,3,2,0:T(8,128)} %fusion.40, f32[3,256,2,32,32]{1,4,3,2,0:T(8,128)} %fusion.36, ...), kind=kOutput, calls=%fused_computation.20 | convolution fusion | flops 616578048 | bytes 34611200 | tf_op jit(solution)/shard_map/kt,...tj->...kj/dot_general | solution.py:25
  235.0 10.0 %fusion.22 = f32[3,256,2,32,32]{1,4,3,2,0:T(8,128)S(1)} fusion(f32[3,256,2,32,32]{1,3,4,2,0:T(8,128)S(1)} %get-tuple-element.13), kind=kOutput, calls=%fused_computation.46 | convolution fusion | flops 603995136 | bytes 12582912 | tf_op jit(solution)/shard_map/tm,...kt->...km/dot_general | solution.py:25
  245.0 10.0 %fusion.20 = f32[3,256,2,32,32]{1,4,3,2,0:T(8,128)S(1)} fusion(f32[3,256,2,32,32]{1,3,4,2,0:T(8,128)S(1)} %get-tuple-element.13), kind=kOutput, calls=%fused_computation.44 | convolution fusion | flops 603994112 | bytes 12582912 | tf_op jit(solution)/shard_map/tm,...kt->...km/dot_general | solution.py:25
  255.0 11.0 %subtract_bitcast_fusion.1 = f32[3,256,2,32,32]{1,3,4,2,0:T(8,128)S(1)} fusion(f32[3,256,2,32,32]{1,4,3,2,0:T(8,128)S(1)} %fusion.22, f32[3,256,2,32,32]{1,3,4,2,0:T(8,128)S(1)} %get-tuple-element.12), kind=kOutput, calls=%fused_computation.35 | convolution fusion | flops 605566976 | bytes 18874368 | tf_op jit(solution)/shard_map/tm,...kt->...km/dot_general | solution.py:25
  266.0 10.3 %add_bitcast_fusion.1 = f32[3,256,2,32,32]{1,3,4,2,0:T(8,128)} fusion(f32[3,256,2,32,32]{1,4,3,2,0:T(8,128)S(1)} %fusion.20, f32[3,256,2,32,32]{1,3,4,2,0:T(8,128)S(1)} %get-tuple-element.12), kind=kOutput, calls=%fused_computation.34 | convolution fusion | flops 605568000 | bytes 18874368 | tf_op jit(solution)/shard_map/tm,...kt->...km/dot_general | solution.py:25
  276.3 5.7 multiply_add_fusion
  282.0 4.4 multiply_subtract_fusion.2
  286.4 7.6 %fusion.29 = f32[3,256,2,32,32]{1,4,3,2,0:T(8,128)} fusion(f32[1,256,2,32,32]{1,3,4,2,0:T(8,128)S(1)} %get-tuple-element.21, f32[1,256,2,32,32]{1,3,4,2,0:T(8,128)S(1)} %get-tuple-element.20, f32[1,256,2,32,32]{1,3,4,2,0:T(8,128)S(1)} %get-tuple-element.18), kind=kOutput, calls=%fused_computation.53 | convolution fusion | flops 607139840 | bytes 12582912 | tf_op jit(solution)/shard_map/kt,...tj->...kj/dot_general | solution.py:25
  294.1 7.4 %fusion.28 = f32[3,256,2,32,32]{1,4,3,2,0:T(8,128)} fusion(f32[1,256,2,32,32]{1,3,4,2,0:T(8,128)S(1)} %get-tuple-element.21, f32[1,256,2,32,32]{1,3,4,2,0:T(8,128)S(1)} %get-tuple-element.20, f32[1,256,2,32,32]{1,3,4,2,0:T(8,128)S(1)} %get-tuple-element.18), kind=kOutput, calls=%fused_computation.52 | convolution fusion | flops 607139840 | bytes 12582912 | tf_op jit(solution)/shard_map/kt,...tj->...kj/dot_general | solution.py:25
  301.5 7.5 %fusion.31 = f32[3,256,2,32,32]{1,4,3,2,0:T(8,128)} fusion(f32[1,256,2,32,32]{1,3,4,2,0:T(8,128)S(1)} %copy-done, f32[1,256,2,32,32]{1,3,4,2,0:T(8,128)S(1)} %get-tuple-element.23, f32[1,256,2,32,32]{1,3,4,2,0:T(8,128)S(1)} %get-tuple-element.22), kind=kOutput, calls=%fused_computation.55 | convolution fusion | flops 607139840 | bytes 12582912 | tf_op jit(solution)/shard_map/kt,...tj->...kj/dot_general | solution.py:25
  309.0 12.7 %fusion.4 = (f32[3,256,2,32,32]{1,3,4,2,0:T(8,128)S(1)}, f32[3,256,2,32,32]{1,3,4,2,0:T(8,128)S(1)}) fusion(f32[32,32]{0,1:T(8,128)S(1)} %fusion.100, f32[32,32]{0,1:T(8,128)S(1)} %get-tuple-element.40, f32[3,256,2,32,32]{1,4,3,2,0:T(8,128)} %fusion.28, f32[3,256,2,32,32]{1,4,3,2,0:T(8,128)} %fusion.31, f32[3,256,2,32,32]{1,4,3,2,0:T(8,128)} %fusion.29, ...), kind=kOutput, calls=%fused_computation.14 | convolution fusion | flops 619722752 | bytes 37756928 | tf_op jit(solution)/shard_map/kt,...tj->...kj/dot_general | solution.py:25
  321.7 9.9 %fusion.14 = f32[3,256,2,32,32]{1,4,3,2,0:T(8,128)S(1)} fusion(f32[3,256,2,32,32]{1,3,4,2,0:T(8,128)S(1)} %get-tuple-element.11), kind=kOutput, calls=%fused_computation.38 | convolution fusion | flops 603994112 | bytes 12582912 | tf_op jit(solution)/shard_map/tm,...kt->...km/dot_general | solution.py:25
  331.7 10.4 %fusion.12 = f32[3,256,2,32,32]{1,4,3,2,0:T(8,128)S(1)} fusion(f32[3,256,2,32,32]{1,3,4,2,0:T(8,128)S(1)} %get-tuple-element.11), kind=kOutput, calls=%fused_computation.36 | convolution fusion | flops 603994112 | bytes 12582912 | tf_op jit(solution)/shard_map/tm,...kt->...km/dot_general | solution.py:25
  342.0 9.9 %subtract_bitcast_fusion = f32[3,256,2,32,32]{1,3,4,2,0:T(8,128)S(1)} fusion(f32[3,256,2,32,32]{1,4,3,2,0:T(8,128)S(1)} %fusion.14, f32[3,256,2,32,32]{1,3,4,2,0:T(8,128)S(1)} %get-tuple-element.10), kind=kOutput, calls=%fused_computation.33 | convolution fusion | flops 605566976 | bytes 18874368 | tf_op jit(solution)/shard_map/tm,...kt->...km/dot_general | solution.py:25
  355.5 10.5 %add_bitcast_fusion = f32[3,256,2,32,32]{1,3,4,2,0:T(8,128)S(1)} fusion(f32[3,256,2,32,32]{1,4,3,2,0:T(8,128)S(1)} %fusion.12, f32[3,256,2,32,32]{1,3,4,2,0:T(8,128)S(1)} %get-tuple-element.10), kind=kOutput, calls=%fused_computation.32 | convolution fusion | flops 605566976 | bytes 18874368 | tf_op jit(solution)/shard_map/tm,...kt->...km/dot_general | solution.py:25
  372.8 26.1 %copy.109 = bf16[2,3,256,2,1024]{2,3,1,0,4:T(2,128)(2,1)S(1)} copy(bf16[2,3,256,2,1024]{2,4,3,1,0:T(8,128)(2,1)S(1)} %pad_maximum_fusion.3) | data formatting | bytes 12582912 | tf_op jit(solution)/shard_map/stack | solution.py:111
  398.9 75.1 %all_to_all.51 = bf16[2,3,256,2,1024]{2,3,1,0,4:T(2,128)(2,1)} all-to-all(bf16[2,3,256,2,1024]{2,3,1,0,4:T(2,128)(2,1)S(1)} %copy.109), channel_id=1, replica_groups=mesh['seq'=8,'chan'=4] {'seq'}, dimensions={4} | all-to-all | bytes 12582912 | tf_op jit(solution)/shard_map/all_to_all | solution.py:110
  474.0 21.4 %copy.110 = bf16[2,3,256,2,8,128]{5,3,4,2,1,0:T(2,128)(2,1)} copy(bf16[2,3,256,2,8,128]{2,3,1,0,5,4:T(2,128)(2,1)} %bitcast.195) | data formatting | bytes 12582912 | tf_op jit(solution)/shard_map/all_to_all | solution.py:110
  495.5 6.7 %fusion.244 = (bf16[1,3,256,8,2,128]{5,4,3,2,1,0:T(2,128)(2,1)S(1)}, bf16[1,3,256,8,2,128]{5,4,3,2,1,0:T(2,128)(2,1)S(1)}) fusion(bf16[2,3,256,8,2,128]{5,4,3,2,1,0:T(2,128)(2,1)} %bitcast.194), kind=kLoop, calls=%fused_computation.278 | loop fusion | bytes 12582912 | tf_op jit(solution)/shard_map/slice | solution.py:116
  505.5 23.4 %all_to_all.52 = bf16[3,256,8,128]{3,1,0,2:T(8,128)(2,1)S(1)} all-to-all(bf16[3,256,8,128]{3,1,0,2:T(8,128)(2,1)S(1)} %copy.111), channel_id=1, replica_groups=mesh['seq'=8,'chan'=4] {'seq'}, dimensions={2} | all-to-all | bytes 3145728 | tf_op jit(solution)/shard_map/all_to_all | solution.py:118
  535.3 43.6 %all-gather.2.cloned.1.call-done = bf16[1024,1024]{1,0:T(8,128)(2,1)} async-done(((bf16[256,1024]{1,0:T(8,128)(2,1)}), bf16[1024,1024]{1,0:T(8,128)(2,1)}) %all-gather.2.cloned.1.call-update) | async-done | bytes 2097168 | tf_op jit(solution)/shard_map/all_gather | solution.py:145
  578.9 9.3 %convolution_convert_fusion = bf16[1024,2048]{1,0:T(8,128)(2,1)} fusion(bf16[1024,1024]{1,0:T(8,128)(2,1)} %all-gather.2.cloned.1.call-done, bf16[2048,1024]{1,0:T(8,128)(2,1)} %param.10), kind=kOutput, calls=%fused_computation.56 | convolution fusion | flops 4297064448 | bytes 10485760 | tf_op jit(solution)/shard_map/dot_general | solution.py:148
  592.4 46.0 %reduce-scatter.5.cloned.1.call-done = bf16[128,2048]{1,0:T(8,128)(2,1)} async-done(((bf16[1024,2048]{1,0:T(8,128)(2,1)}), bf16[128,2048]{1,0:T(8,128)(2,1)}) %reduce-scatter.5.cloned.1.call-update) | async-done | bytes 524304 | tf_op jit(solution)/shard_map/reduce_scatter | solution.py:147
  (62 shorter events, 59.8 us)
Async XLA Ops:
  7.2 9.5 %copy-start.8 = (bf16[256,1024]{1,0:T(8,128)(2,1)S(1)}, bf16[256,1024]{1,0:T(8,128)(2,1)}, u32[]{:S(2)}) copy-start(bf16[256,1024]{1,0:T(8,128)(2,1)} %param.7) | copy-start | bytes 1572868
  7.2 9.5 %copy-start.6 = (bf16[256,1024]{1,0:T(8,128)(2,1)S(1)}, bf16[256,1024]{1,0:T(8,128)(2,1)}, u32[]{:S(2)}) copy-start(bf16[256,1024]{1,0:T(8,128)(2,1)} %param.8) | copy-start | bytes 1572868
  7.2 56.2 %copy-start.4 = (bf16[256,1024]{1,0:T(8,128)(2,1)S(1)}, bf16[256,1024]{1,0:T(8,128)(2,1)}, u32[]{:S(2)}) copy-start(bf16[256,1024]{1,0:T(8,128)(2,1)} %param.6) | copy-start | bytes 1572868
  7.2 57.5 %copy-start.10 = (bf16[256,1024]{1,0:T(8,128)(2,1)S(1)}, bf16[256,1024]{1,0:T(8,128)(2,1)}, u32[]{:S(2)}) copy-start(bf16[256,1024]{1,0:T(8,128)(2,1)} %param.9) | copy-start | bytes 1572868
  7.2 56.2 %reduce-scatter.3.cloned.1.call-start = ((), (), s32[]{:S(2)}) async-start(), calls=%async_computation.6 | async-start | bytes 2621440 | tf_op jit(solution)/shard_map/reduce_scatter | solution.py:129
  67.4 30.6 %all-to-all-start = ((bf16[3,256,1,1024]{1,0,2,3:T(4,128)(2,1)}), bf16[3,256,1,1024]{1,0,2,3:T(4,128)(2,1)S(1)}, u32[]{:S(2)}, u32[]{:S(2)}) async-start(bf16[3,256,1,1024]{1,0,2,3:T(4,128)(2,1)} %copy.81), calls=%async_computation.1 | async-start | bytes 4194304 | tf_op jit(solution)/shard_map/all_to_all | solution.py:88
  98.0 1.4 copy-start.3
  114.2 76.4 %all-to-all-start.1 = ((bf16[2,3,256,16,128]{4,2,1,0,3:T(8,128)(2,1)}), bf16[2,3,256,16,128]{4,2,1,0,3:T(8,128)(2,1)}, u32[]{:S(2)}, u32[]{:S(2)}) async-start(bf16[2,3,256,16,128]{4,2,1,0,3:T(8,128)(2,1)} %copy.83), calls=%async_computation.2 | async-start | bytes 12582912 | tf_op jit(solution)/shard_map/all_to_all | solution.py:98
  119.0 459.9 %all-gather.2.cloned.1.call-start = ((), (), s32[]{:S(2)}) async-start(), calls=%async_computation.7 | async-start | bytes 2621440 | tf_op jit(solution)/shard_map/all_gather | solution.py:145
  286.4 15.1 %copy-start.1 = (f32[1,256,2,32,32]{1,3,4,2,0:T(8,128)}, f32[1,256,2,32,32]{1,3,4,2,0:T(8,128)S(1)}, u32[]{:S(2)}) copy-start(f32[1,256,2,32,32]{1,3,4,2,0:T(8,128)S(1)} %get-tuple-element.22) | copy-start | bytes 6291460
  286.4 15.1 %copy-start.2 = (f32[1,256,2,32,32]{1,3,4,2,0:T(8,128)}, f32[1,256,2,32,32]{1,3,4,2,0:T(8,128)S(1)}, u32[]{:S(2)}) copy-start(f32[1,256,2,32,32]{1,3,4,2,0:T(8,128)S(1)} %get-tuple-element.23) | copy-start | bytes 6291460
  294.1 7.5 %copy-start = (f32[1,256,2,32,32]{1,3,4,2,0:T(8,128)S(1)}, f32[1,256,2,32,32]{1,3,4,2,0:T(8,128)}, u32[]{:S(2)}) copy-start(f32[1,256,2,32,32]{1,3,4,2,0:T(8,128)} %get-tuple-element.19) | copy-start | bytes 6291460
  529.6 3.3 copy-start.5
  535.3 103.1 %reduce-scatter.5.cloned.1.call-start = ((), (), s32[]{:S(2)}) async-start(), calls=%async_computation.8 | async-start | bytes 4718592 | tf_op jit(solution)/shard_map/reduce_scatter | solution.py:147
  588.2 3.0 copy-start.7
  588.2 3.0 copy-start.9
Sparse Core Ops, SparseCore 0:
  16.8 46.5 reduce-scatter.2
  535.4 43.4 all-gather.1
  588.3 50.0 reduce-scatter.4
where the time goes:
time: 652 us; the launch traced here: 647 us
  waiting for transfers between devices  234 us (36%)
  matrix products  178 us (27%)
  blocking collectives  98.5 us (15%)
  local copies, waits for them, and re-layouts  92.6 us (14%)
  other arithmetic  21.5 us (3%)
  between operations  14.3 us (2%)
  starting transfers between devices  8.84 us (1%)
    dot_general x20, matrix products, contract(): return jnp.einsum(form, table, data, precision=lax.Precision.HIGHEST)  159 us
    all_to_all x1, blocking collectives, split_transform(): lax.all_to_all(as_sent(jnp.stack([back_re, back_im])), 'seq', split_axis=...  75.1 us
    all_to_all x1, waiting for transfers between devices, split_transform(): lax.all_to_all(jnp.stack([part_re, part_im]).astype(jnp.bfloat16), 'seq',...  71.1 us
    reduce_scatter x1, waiting for transfers between devices, body(): lax.psum_scatter(jnp.dot(rows, grad_output, preferred_element_type=jnp.fl...  46.5 us
    reduce_scatter x1, waiting for transfers between devices, body(): lax.psum_scatter(lax.dot_general(rows, grad_output, (((1,), (1,)), ((), (...  46 us
    all_gather x1, waiting for transfers between devices, body(): mixed_all = lax.all_gather(mixed, 'chan', axis=0, tiled=True)  43.6 us
    all_to_all x1, waiting for transfers between devices, split_transform(): lax.all_to_all(stacked.reshape(3, chan_rows, 1, block_len), 'seq', split_...  26.5 us
    another operation x1, local copies, waits for them, and re-layouts, split_transform(): jnp.stack([back_re, back_im])  26.1 us
  transfers between devices with their start and end apart: 5, of which 5 were waited for; matrix products, arithmetic and copies ran while one was open for 1% of the time, Pallas kernels for 0%

commit v1 on v0

v1 whole, which is shorter than its diff:
```python
import functools
import math

import jax
import jax.numpy as jnp
import numpy as np
from jax import lax
from jax.experimental import pallas as pl
from jax.experimental.pallas import tpu as pltpu
from jax.sharding import PartitionSpec as P

LANES = 128
VMEM_BYTES = 48 * 1024 * 1024


def high_low(table, axis):
    high = table.astype(jnp.bfloat16)
    low = (table - high.astype(np.float64)).astype(jnp.bfloat16)
    return np.concatenate([high, low], axis=axis)


def dft_tables(tokens, blocks):
    outer = tokens // LANES
    per = outer // blocks
    freq = np.arange(outer) + 0.25
    angle = 2.0 * math.pi / outer * np.outer(freq, np.arange(outer))
    first = np.zeros((2, 2, outer, blocks, 2, per))
    last = np.zeros((blocks, 2, per, 2, 2, outer))
    for pair in range(2):
        first[pair, 0, :, :, pair, :] = np.cos(angle).reshape(outer, blocks, per)
        first[pair, 1, :, :, pair, :] = -np.sin(angle).reshape(outer, blocks, per)
        last[:, pair, :, pair, 0, :] = np.cos(angle.T).reshape(blocks, per, outer) / tokens
        last[:, pair, :, pair, 1, :] = -np.sin(angle.T).reshape(blocks, per, outer) / tokens
    first = high_low(first.reshape(4 * outer, 2 * outer), 1)
    last = high_low(last.reshape(2 * outer, 4 * outer), 1)
    turn = 2.0 * math.pi / tokens * np.outer(freq, np.arange(LANES))
    twiddle = np.stack([np.cos(turn), np.sin(turn)]).astype(np.float32)
    lane = 2.0 * math.pi / LANES * np.outer(np.arange(LANES), np.arange(LANES))
    cos, sin = np.cos(lane), np.sin(lane)
    forward = high_low(np.block([[cos, -sin], [sin, cos]]), 0)
    inverse = high_low(np.block([[cos, sin], [-sin, cos]]), 0)
    return first, forward, inverse, last, twiddle


def mxu(left, right):
    return jnp.dot(left, right, preferred_element_type=jnp.float32)


def forward_pair(pair_block, first, twiddle):
    outer = twiddle.shape[1]
    rows = pair_block.reshape(2 * outer, LANES)
    part = mxu(first, jnp.concatenate([rows, rows], axis=0))
    cos, sin = twiddle[0], twiddle[1]
    turned = []
    for pair in range(2):
        real = part[2 * pair * outer : (2 * pair + 1) * outer]
        imag = part[(2 * pair + 1) * outer : (2 * pair + 2) * outer]
        turned.append(
            jnp.concatenate([real * cos + imag * sin, imag * cos - real * sin], axis=1).astype(
                jnp.bfloat16
            )
        )
    return turned


def inverse_pair(spread, last, twiddle):
    cos, sin = twiddle[0], twiddle[1]
    parts = []
    for item in spread:
        real, imag = item[:, :LANES], item[:, LANES:]
        parts.append((real * cos - imag * sin).astype(jnp.bfloat16))
        parts.append((real * sin + imag * cos).astype(jnp.bfloat16))
    return mxu(last, jnp.concatenate(parts + parts, axis=0))


def lanes_dft(rows, table):
    return mxu(jnp.concatenate([rows, rows], axis=1), table)


def convolve_kernel(pairs_ref, first_ref, forward_ref, inverse_ref, last_ref, twiddle_ref,
                    conv_ref, signal_ref, filter_ref, turned, spread):
    outer = twiddle_ref.shape[1]
    step = pairs_ref.shape[1]
    twiddle = twiddle_ref[...]
    for chan in range(step):
        pieces = forward_pair(pairs_ref[:, chan], first_ref[...], twiddle)
        for pair in range(2):
            turned[pl.ds((pair * step + chan) * outer, outer), :] = pieces[pair]
    half = step * outer
    signal = lanes_dft(turned[pl.ds(0, half), :], forward_ref[...])
    kernel = lanes_dft(turned[pl.ds(half, half), :], forward_ref[...])
    signal_ref[...] = signal.reshape(signal_ref.shape)
    filter_ref[...] = kernel.reshape(filter_ref.shape)
    sr, si = signal[:, :LANES], signal[:, LANES:]
    kr, ki = kernel[:, :LANES], kernel[:, LANES:]
    product = jnp.concatenate([kr * sr - ki * si, kr * si + ki * sr], axis=1).astype(jnp.bfloat16)
    spread[...] = lanes_dft(product, inverse_ref[...])
    for pair in range(step // 2):
        items = [spread[pl.ds((2 * pair + one) * outer, outer), :] for one in range(2)]
        out = inverse_pair(items, last_ref[...], twiddle)
        conv_ref[:, pair] = out.reshape(conv_ref.shape[0], -1, LANES).astype(jnp.bfloat16)


def correlate_kernel(pairs_ref, signal_ref, filter_ref, first_ref, forward_ref, inverse_ref,
                     last_ref, twiddle_ref, out_ref, turned, spread):
    outer = twiddle_ref.shape[1]
    step = signal_ref.shape[0]
    twiddle = twiddle_ref[...]
    for pair in range(step // 2):
        pieces = forward_pair(pairs_ref[:, pair], first_ref[...], twiddle)
        for one in range(2):
            turned[pl.ds((2 * pair + one) * outer, outer), :] = pieces[one]
    half = step * outer
    grad = lanes_dft(turned[...], forward_ref[...])
    gr, gi = grad[:, :LANES], grad[:, LANES:]
    for place, ref in enumerate((filter_ref, signal_ref)):
        other = ref[...].reshape(half, 2 * LANES)
        kr, ki = other[:, :LANES], other[:, LANES:]
        product = jnp.concatenate([kr * gr + ki * gi, kr * gi - ki * gr], axis=1)
        spread[place] = lanes_dft(product.astype(jnp.bfloat16), inverse_ref[...])
    for chan in range(step):
        items = [spread[place, pl.ds(chan * outer, outer), :] for place in range(2)]
        out = inverse_pair(items, last_ref[...], twiddle)
        out_ref[:, chan] = out.reshape(out_ref.shape[0], -1, LANES).astype(jnp.bfloat16)


def whole(table):
    zeros = (0,) * table.ndim
    return pl.BlockSpec(table.shape, lambda i: zeros)


def convolve(pairs, tables, step=8):
    blocks, chans, rows, _ = pairs.shape
    outer = blocks * rows // 2
    spec = jax.ShapeDtypeStruct((chans, outer, 2 * LANES), jnp.float32)
    spec_block = pl.BlockSpec((step, outer, 2 * LANES), lambda i: (i, 0, 0))
    return pl.pallas_call(
        convolve_kernel,
        grid=(chans // step,),
        in_specs=[pl.BlockSpec((blocks, step, rows, LANES), lambda i: (0, i, 0, 0))]
        + [whole(table) for table in tables],
        out_specs=[
            pl.BlockSpec((blocks, step // 2, rows, LANES), lambda i: (0, i, 0, 0)),
            spec_block,
            spec_block,
        ],
        out_shape=[jax.ShapeDtypeStruct((blocks, chans // 2, rows, LANES), jnp.bfloat16), spec, spec],
        scratch_shapes=[
            pltpu.VMEM((2 * step * outer, 2 * LANES), jnp.bfloat16),
            pltpu.VMEM((step * outer, 2 * LANES), jnp.float32),
        ],
        compiler_params=pltpu.CompilerParams(vmem_limit_bytes=VMEM_BYTES),
        name="convolve",
    )(pairs, *tables)


def correlate(pairs, signal, kernel, tables, step=8):
    blocks, half, rows, _ = pairs.shape
    chans = 2 * half
    outer = blocks * rows // 2
    spec_block = pl.BlockSpec((step, outer, 2 * LANES), lambda i: (i, 0, 0))
    return pl.pallas_call(
        correlate_kernel,
        grid=(chans // step,),
        in_specs=[
            pl.BlockSpec((blocks, step // 2, rows, LANES), lambda i: (0, i, 0, 0)),
            spec_block,
            spec_block,
        ]
        + [whole(table) for table in tables],
        out_specs=pl.BlockSpec((blocks, step, rows, LANES), lambda i: (0, i, 0, 0)),
        out_shape=jax.ShapeDtypeStruct((blocks, chans, rows, LANES), jnp.bfloat16),
        scratch_shapes=[
            pltpu.VMEM((step * outer, 2 * LANES), jnp.bfloat16),
            pltpu.VMEM((2, step * outer, 2 * LANES), jnp.float32),
        ],
        compiler_params=pltpu.CompilerParams(vmem_limit_bytes=VMEM_BYTES),
        name="correlate",
    )(pairs, signal, kernel, *tables)


def body(outer_gate, inner_gate, signal, long_filter, grad_output, out_proj):
    seq_count = lax.axis_size("seq")
    chan_rows, block_len = outer_gate.shape
    owned = chan_rows // seq_count
    per = block_len // LANES
    tables = [jnp.asarray(t) for t in dft_tables(block_len * seq_count, seq_count)]

    def exchange(blocks):
        return lax.all_to_all(blocks, "seq", split_axis=0, concat_axis=0, tiled=True)

    def wide(x):
        return x.astype(jnp.float32)

    mixed_in = (wide(inner_gate) * wide(signal)).astype(jnp.bfloat16)
    pair = jnp.concatenate(
        [mixed_in.reshape(chan_rows, per, LANES), long_filter.reshape(chan_rows, per, LANES)], axis=1
    )
    pair = exchange(pair.reshape(seq_count, owned, 2 * per, LANES))
    conv, spec_signal, spec_filter = convolve(pair, tables)
    conv_out = wide(exchange(conv).reshape(chan_rows, block_len))
    mixed = (wide(outer_gate) * conv_out).astype(jnp.bfloat16)

    grad_mix = wide(
        lax.psum_scatter(
            jnp.dot(out_proj, grad_output, preferred_element_type=jnp.float32).astype(jnp.bfloat16),
            "chan",
            scatter_dimension=0,
            tiled=True,
        )
    )
    grad_conv = (grad_mix * wide(outer_gate)).astype(jnp.bfloat16)
    grad_outer = (grad_mix * conv_out).astype(jnp.bfloat16)
    corr = correlate(
        exchange(grad_conv.reshape(seq_count, owned // 2, 2 * per, LANES)),
        spec_signal,
        spec_filter,
        tables,
    )
    corr = exchange(corr).reshape(chan_rows, 2, block_len)
    grad_prod, grad_filter = wide(corr[:, 0]), wide(corr[:, 1])
    grad_inner = (grad_prod * wide(signal)).astype(jnp.bfloat16)
    grad_signal = (grad_prod * wide(inner_gate)).astype(jnp.bfloat16)

    mixed_all = lax.all_gather(mixed, "chan", axis=0, tiled=True)
    grad_proj = wide(
        lax.psum_scatter(
            lax.dot_general(
                mixed_all, grad_output, (((1,), (1,)), ((), ())), preferred_element_type=jnp.float32
            ).astype(jnp.bfloat16),
            "seq",
            scatter_dimension=0,
            tiled=True,
        )
    )
    return (grad_outer, grad_inner, grad_signal, grad_filter, grad_proj)


def solution(mesh):
    tokens = P("chan", "seq")
    in_specs = (tokens, tokens, tokens, tokens, tokens, P(None, "chan"))
    out_specs = (tokens, tokens, tokens, tokens, P("seq", "chan"))
    return jax.shard_map(body, mesh=mesh, in_specs=in_specs, out_specs=out_specs, check_vma=False)
```

time: 652 us -> 191 us (0.29)
  waiting for transfers between devices: 234 us -> 62 us
  matrix products: 178 us -> 18.7 us
  local copies, waits for them, and re-layouts: 92.6 us -> 4.22 us
  blocking collectives: 98.5 us -> 71.8 us
  other arithmetic: 21.5 us -> 7.96 us
  Pallas kernels: 0 us -> 12.3 us
  starting transfers between devices: 8.84 us -> 0.12 us
    dot_general x22 -> x2, matrix products: 178 us -> 18.7 us  [the longest x1 9.38 us: body(): jnp.dot(out_proj, grad_output, preferred_element_type=jnp.float32)]
    all_to_all x2 -> x0, waiting for transfers between devices: 97.7 us -> none  [the longest x1 71.1 us: split_transform(): lax.all_to_all(jnp.stack([part_re, part_im]).astype(jnp.bfloat16), 'seq',...]
    reduce_scatter x2, waiting for transfers between devices: 92.5 us -> 16.6 us  [the longest x1 10.3 us: body(): lax.psum_scatter(lax.dot_general(mixed_all, grad_output, (((1,), (1,)), (...]
    another operation x2 -> x0, local copies, waits for them, and re-layouts: 30.4 us -> none  [the longest x1 26.1 us: split_transform(): jnp.stack([back_re, back_im])]
    all_to_all x4 -> x0, local copies, waits for them, and re-layouts: 27.8 us -> none  [the longest x1 21.4 us: split_transform(): lax.all_to_all(as_sent(jnp.stack([back_re, back_im])), 'seq', split_axis=...]
    all_to_all x2 -> x4, blocking collectives: 98.5 us -> 71.8 us  [exchange(): lax.all_to_all(blocks, 'seq', split_axis=0, concat_axis=0, tiled=True)]
    slice x5 -> x1, local copies, waits for them, and re-layouts: 18.4 us -> 1.5 us  [body(): grad_prod, grad_filter = (wide(corr[:, 0]), wide(corr[:, 1]))]
    pallas_call x0 -> x2, Pallas kernels: none -> 12.3 us  [the longest x1 6.28 us: correlate(): pl.pallas_call(correlate_kernel, grid=(chans // step,), in_specs=[pl.Bloc...]
  transfers between devices with their start and end apart: 5 -> 3, of which waited for: 5 -> 3; matrix products, arithmetic and copies ran while one was open for 1% -> 4% of each run, Pallas kernels for 0% -> 6%
where the time goes in v1:
time: 191 us
  blocking collectives  71.8 us (38%)
  waiting for transfers between devices  62 us (32%)
  matrix products  18.7 us (10%)
  between operations  13.9 us (7%)
  Pallas kernels  12.3 us (6%)
  other arithmetic  7.96 us (4%)
  local copies, waits for them, and re-layouts  4.22 us (2%)
    all_to_all x4, blocking collectives, exchange(): lax.all_to_all(blocks, 'seq', split_axis=0, concat_axis=0, tiled=True)  71.8 us
    all_gather x1, waiting for transfers between devices, body(): mixed_all = lax.all_gather(mixed, 'chan', axis=0, tiled=True)  45.4 us
    reduce_scatter x1, waiting for transfers between devices, body(): lax.psum_scatter(lax.dot_general(mixed_all, grad_output, (((1,), (1,)), (...  10.3 us
    dot_general x1, matrix products, body(): jnp.dot(out_proj, grad_output, preferred_element_type=jnp.float32)  9.38 us
    dot_general x1, matrix products, body(): lax.dot_general(mixed_all, grad_output, (((1,), (1,)), ((), ())), preferr...  9.32 us
    pallas_call x1, Pallas kernels, correlate(): pl.pallas_call(correlate_kernel, grid=(chans // step,), in_specs=[pl.Bloc...  6.28 us
    reduce_scatter x1, waiting for transfers between devices, body(): lax.psum_scatter(jnp.dot(out_proj, grad_output, preferred_element_type=jn...  6.25 us
    pallas_call x1, Pallas kernels, convolve(): pl.pallas_call(convolve_kernel, grid=(chans // step,), in_specs=[pl.Block...  6.06 us
  transfers between devices with their start and end apart: 3, of which 3 were waited for; matrix products, arithmetic and copies ran while one was open for 4% of the time, Pallas kernels for 6%

profile of v1, /device:TPU:0, one launch (start us, length us, event | category | flops | bytes accessed | tf_op | source)
XLA Modules:
  0.0 191.0 jit_solution(9760546696445439115)
XLA Ops:
  7.2 0.0 reduce-scatter.3.cloned.1.call-start
  7.2 9.4 %convolution_convert_fusion.1 = bf16[1024,1024]{1,0:T(8,128)(2,1)} fusion(bf16[1024,2048]{1,0:T(8,128)(2,1)} %param.16, bf16[2048,1024]{1,0:T(8,128)(2,1)} %param.15), kind=kOutput, calls=%fused_computation.1 | convolution fusion | flops 4296015872 | bytes 10485760 | tf_op jit(solution)/shard_map/dot_general | solution.py:206
  16.6 0.0 reduce-scatter.3.cloned.1.call-update
  16.7 0.0 copy-start
  16.7 0.0 copy-start.1
  16.7 0.0 copy-start.2
  16.7 0.0 all-gather.2.cloned.1.call-start
  16.8 0.1 copy.21
  16.9 0.2 fusion.6
  17.1 0.1 copy.20
  17.2 0.2 pad_maximum_fusion
  17.4 20.3 %all_to_all.20.pairs_ref = bf16[8,32,16,128]{3,2,1,0:T(8,128)(2,1)S(1)} all-to-all(bf16[8,32,16,128]{3,2,1,0:T(8,128)(2,1)S(1)} %pad_maximum_fusion), channel_id=1, replica_groups=mesh['seq'=8,'chan'=4] {'seq'}, dimensions={0} | all-to-all | bytes 2097152 | tf_op jit(solution)/shard_map/all_to_all | solution.py:190
  37.7 6.1 %convolve.1 = (bf16[8,16,16,128]{3,2,1,0:T(8,128)(2,1)S(1)}, f32[32,64,256]{2,1,0:T(8,128)S(1)}, f32[32,64,256]{2,1,0:T(8,128)}) custom-call(bf16[8,32,16,128]{3,2,1,0:T(8,128)(2,1)S(1)} %all_to_all.20.pairs_ref, bf16[256,256]{1,0:T(8,128)(2,1)S(1)} %copy-done.3, bf16[512,256]{1,0:T(8,128)(2,1)S(1)} %copy-done.1, bf16[512,256]{1,0:T(8,128)(2,1)S(1)} %copy-done, ...), custom_call_target="tpu_custom_call" | custom-call | tf_op jit(solution)/shard_map/convolve/pallas_call | solution.py:137
  43.8 12.1 %all_to_all.21 = bf16[8,16,16,128]{3,2,1,0:T(8,128)(2,1)S(1)} all-to-all(bf16[8,16,16,128]{3,2,1,0:T(8,128)(2,1)S(1)} %get-tuple-element.8), channel_id=1, replica_groups=mesh['seq'=8,'chan'=4] {'seq'}, dimensions={0} | all-to-all | bytes 1048576 | tf_op jit(solution)/shard_map/all_to_all | solution.py:190
  55.9 1.2 reshape.32
  57.1 6.2 %reduce-scatter.3.cloned.1.call-done = bf16[256,1024]{1,0:T(8,128)(2,1)} async-done(((bf16[1024,1024]{1,0:T(8,128)(2,1)}), bf16[256,1024]{1,0:T(8,128)(2,1)}) %reduce-scatter.3.cloned.1.call-update) | async-done | bytes 524304 | tf_op jit(solution)/shard_map/reduce_scatter | solution.py:205
  63.4 2.9 %fusion.3 = (bf16[256,1024]{1,0:T(8,128)(2,1)}, bf16[256,1024]{1,0:T(8,128)(2,1)}, bf16[256,1024]{1,0:T(8,128)(2,1)S(1)}) fusion(f32[256,1024]{1,0:T(8,128)} %reshape.32, bf16[256,1024]{1,0:T(8,128)(2,1)} %param.11, bf16[256,1024]{1,0:T(8,128)(2,1)} %reduce-scatter.3.cloned.1.call-done), kind=kLoop, calls=%fused_computation.11 | loop fusion | flops 2097152 | bytes 3670016 | tf_op jit(solution)/shard_map/convert_element_type | solution.py:202
  66.2 0.0 all-gather.2.cloned.1.call-update
  66.3 0.0 reduce-scatter.5.cloned.1.call-start
  66.3 45.4 %all-gather.2.cloned.1.call-done = bf16[1024,1024]{1,0:T(8,128)(2,1)} async-done(((bf16[256,1024]{1,0:T(8,128)(2,1)}), bf16[1024,1024]{1,0:T(8,128)(2,1)}) %all-gather.2.cloned.1.call-update) | async-done | bytes 2097168 | tf_op jit(solution)/shard_map/all_gather | solution.py:225
  111.7 9.3 %convolution_convert_fusion = bf16[1024,2048]{1,0:T(8,128)(2,1)} fusion(bf16[1024,1024]{1,0:T(8,128)(2,1)} %all-gather.2.cloned.1.call-done, bf16[2048,1024]{1,0:T(8,128)(2,1)} %param.15), kind=kOutput, calls=%fused_computation | convolution fusion | flops 4297064448 | bytes 10485760 | tf_op jit(solution)/shard_map/dot_general | solution.py:228
  121.0 0.0 reduce-scatter.5.cloned.1.call-update
  121.0 1.0 reshape.30
  122.0 13.4 %all_to_all.22.pairs_ref = bf16[8,16,16,128]{3,2,1,0:T(8,128)(2,1)S(1)} all-to-all(bf16[8,16,16,128]{3,2,1,0:T(8,128)(2,1)} %reshape.30), channel_id=1, replica_groups=mesh['seq'=8,'chan'=4] {'seq'}, dimensions={0} | all-to-all | bytes 1048576 | tf_op jit(solution)/shard_map/all_to_all | solution.py:190
  135.4 6.3 %correlate.1 = bf16[8,32,16,128]{3,2,1,0:T(8,128)(2,1)S(1)} custom-call(bf16[8,16,16,128]{3,2,1,0:T(8,128)(2,1)S(1)} %all_to_all.22.pairs_ref, f32[32,64,256]{2,1,0:T(8,128)S(1)} %get-tuple-element.9.signal_ref, f32[32,64,256]{2,1,0:T(8,128)} %get-tuple-element.10.filter_ref, bf16[256,256]{1,0:T(8,128)(2,1)S(1)} %copy-done.3, ...), custom_call_target="tpu_custom_call" | custom-call | tf_op jit(solution)/shard_map/correlate/pallas_call | solution.py:162
  141.7 25.9 %all_to_all.23 = bf16[8,32,16,128]{3,2,1,0:T(8,128)(2,1)S(1)} all-to-all(bf16[8,32,16,128]{3,2,1,0:T(8,128)(2,1)S(1)} %correlate.1), channel_id=1, replica_groups=mesh['seq'=8,'chan'=4] {'seq'}, dimensions={0} | all-to-all | bytes 2097152 | tf_op jit(solution)/shard_map/all_to_all | solution.py:190
  167.6 0.3 reshape.31
  167.9 1.5 fusion.8
  169.4 1.2 fusion.7
  170.6 1.4 fusion.5
  172.0 10.3 %reduce-scatter.5.cloned.1.call-done = bf16[128,2048]{1,0:T(8,128)(2,1)} async-done(((bf16[1024,2048]{1,0:T(8,128)(2,1)}), bf16[128,2048]{1,0:T(8,128)(2,1)}) %reduce-scatter.5.cloned.1.call-update) | async-done | bytes 524304 | tf_op jit(solution)/shard_map/reduce_scatter | solution.py:227
  182.3 2.1 %convert_element_type.78 = f32[128,2048]{1,0:T(8,128)} convert(bf16[128,2048]{1,0:T(8,128)(2,1)} %reduce-scatter.5.cloned.1.call-done) | non-fusion elementwise | flops 262144 | bytes 1572864 | tf_op jit(solution)/shard_map/convert_element_type | solution.py:193
  (17 shorter events, 0.0 us)
Async XLA Ops:
  7.2 9.6 %copy-start.9 = (bf16[256,1024]{1,0:T(8,128)(2,1)S(1)}, bf16[256,1024]{1,0:T(8,128)(2,1)}, u32[]{:S(2)}) copy-start(bf16[256,1024]{1,0:T(8,128)(2,1)} %param.14) | copy-start | bytes 1572868
  7.2 9.7 %copy-start.5 = (bf16[256,1024]{1,0:T(8,128)(2,1)S(1)}, bf16[256,1024]{1,0:T(8,128)(2,1)}, u32[]{:S(2)}) copy-start(bf16[256,1024]{1,0:T(8,128)(2,1)} %param.13) | copy-start | bytes 1572868
  7.2 9.7 %copy-start.7 = (bf16[256,1024]{1,0:T(8,128)(2,1)S(1)}, bf16[256,1024]{1,0:T(8,128)(2,1)}, u32[]{:S(2)}) copy-start(bf16[256,1024]{1,0:T(8,128)(2,1)} %param.12) | copy-start | bytes 1572868
  7.2 56.2 %reduce-scatter.3.cloned.1.call-start = ((), (), s32[]{:S(2)}) async-start(), calls=%async_computation.6 | async-start | bytes 2621440 | tf_op jit(solution)/shard_map/reduce_scatter | solution.py:205
  16.7 21.1 %copy-start = (bf16[512,256]{1,0:T(8,128)(2,1)S(1)}, bf16[512,256]{1,0:T(8,128)(2,1)}, u32[]{:S(2)}) copy-start(bf16[512,256]{1,0:T(8,128)(2,1)} %constant.12.clone.inverse_ref) | copy-start | bytes 786436
  16.7 21.1 %copy-start.1 = (bf16[512,256]{1,0:T(8,128)(2,1)S(1)}, bf16[512,256]{1,0:T(8,128)(2,1)}, u32[]{:S(2)}) copy-start(bf16[512,256]{1,0:T(8,128)(2,1)} %constant.11.clone.forward_ref) | copy-start | bytes 786436
  16.7 21.0 %copy-start.2 = (bf16[128,512]{1,0:T(8,128)(2,1)S(1)}, bf16[128,512]{1,0:T(8,128)(2,1)}, u32[]{:S(2)}) copy-start(bf16[128,512]{1,0:T(8,128)(2,1)} %constant.13.clone.last_ref) | copy-start | bytes 393220
  16.7 21.0 %copy-start.3 = (bf16[256,256]{1,0:T(8,128)(2,1)S(1)}, bf16[256,256]{1,0:T(8,128)(2,1)}, u32[]{:S(2)}) copy-start(bf16[256,256]{1,0:T(8,128)(2,1)} %constant.10.clone.first_ref) | copy-start | bytes 393220
  16.7 21.0 %copy-start.4 = (f32[2,64,128]{2,1,0:T(8,128)S(1)}, f32[2,64,128]{2,1,0:T(8,128)}, u32[]{:S(2)}) copy-start(f32[2,64,128]{2,1,0:T(8,128)} %constant.14.clone.twiddle_ref) | copy-start | bytes 196612
  16.7 95.0 %all-gather.2.cloned.1.call-start = ((), (), s32[]{:S(2)}) async-start(), calls=%async_computation.7 | async-start | bytes 2621440 | tf_op jit(solution)/shard_map/all_gather | solution.py:225
  66.3 116.1 %reduce-scatter.5.cloned.1.call-start = ((), (), s32[]{:S(2)}) async-start(), calls=%async_computation.8 | async-start | bytes 4718592 | tf_op jit(solution)/shard_map/reduce_scatter | solution.py:227
  167.6 3.0 %copy-start.6 = (bf16[256,1024]{1,0:T(8,128)(2,1)S(1)}, bf16[256,1024]{1,0:T(8,128)(2,1)}, u32[]{:S(2)}) copy-start(bf16[256,1024]{1,0:T(8,128)(2,1)} %param.13) | copy-start | bytes 1572868
  167.6 3.0 %copy-start.8 = (bf16[256,1024]{1,0:T(8,128)(2,1)S(1)}, bf16[256,1024]{1,0:T(8,128)(2,1)}, u32[]{:S(2)}) copy-start(bf16[256,1024]{1,0:T(8,128)(2,1)} %param.12) | copy-start | bytes 1572868
Sparse Core Ops, SparseCore 0:
  16.8 46.5 reduce-scatter.2
  66.4 45.2 all-gather.1
  121.1 61.1 reduce-scatter.4

commit v2 on v1

--- a/solution.py
+++ b/solution.py
@@ -10,7 +10,16 @@
 from jax.sharding import PartitionSpec as P
 
 LANES = 128
+CHUNKS = 2
 VMEM_BYTES = 48 * 1024 * 1024
+
+
+def wide(x):
+    return x.astype(jnp.float32)
+
+
+def short(x):
+    return x.astype(jnp.bfloat16)
 
 
 def high_low(table, axis):
@@ -129,8 +138,9 @@
     return pl.BlockSpec(table.shape, lambda i: zeros)
 
 
-def convolve(pairs, tables, step=8):
+def convolve(pairs, tables):
     blocks, chans, rows, _ = pairs.shape
+    step = min(8, chans)
     outer = blocks * rows // 2
     spec = jax.ShapeDtypeStruct((chans, outer, 2 * LANES), jnp.float32)
     spec_block = pl.BlockSpec((step, outer, 2 * LANES), lambda i: (i, 0, 0))
@@ -154,9 +164,10 @@
     )(pairs, *tables)
 
 
-def correlate(pairs, signal, kernel, tables, step=8):
-    blocks, half, rows, _ = pairs.shape
-    chans = 2 * half
+def correlate(pairs, signal, kernel, tables):
+    blocks, _, rows, _ = pairs.shape
+    chans = signal.shape[0]
+    step = min(8, chans)
     outer = blocks * rows // 2
     spec_block = pl.BlockSpec((step, outer, 2 * LANES), lambda i: (i, 0, 0))
     return pl.pallas_call(
@@ -179,60 +190,315 @@
     )(pairs, signal, kernel, *tables)
 
 
+def params():
+    return pltpu.CompilerParams(vmem_limit_bytes=VMEM_BYTES)
+
+
+def spread_lanes(target, rows, first, stride):
+    count = rows.shape[0]
+    for lane in range(rows.shape[1] // LANES):
+        target[pl.ds(first + lane, count, stride=stride), :] = rows[:, lane * LANES : (lane + 1) * LANES]
+
+
+def prepare_kernel(gate_ref, signal_ref, filter_ref, pair_ref, lines):
+    per = gate_ref.shape[1] // LANES
+    spread_lanes(lines, short(wide(gate_ref[...]) * wide(signal_ref[...])).astype(jnp.float32), 0, 2 * per)
+    spread_lanes(lines, wide(filter_ref[...]), per, 2 * per)
+    pair_ref[...] = short(lines[...]).reshape(pair_ref.shape)
+
+
+def prepare(inner_gate, signal, long_filter):
+    rows, length = signal.shape
+    per = length // LANES
+    step = rows // 4
+    block = pl.BlockSpec((step, length), lambda i: (i, 0))
+    return pl.pallas_call(
+        prepare_kernel,
+        grid=(4,),
+        in_specs=[block] * 3,
+        out_specs=pl.BlockSpec((step, 2 * per, LANES), lambda i: (i, 0, 0)),
+        out_shape=jax.ShapeDtypeStruct((rows, 2 * per, LANES), jnp.bfloat16),
+        scratch_shapes=[pltpu.VMEM((step * 2 * per, LANES), jnp.float32)],
+        compiler_params=params(),
+        name="prepare",
+    )(inner_gate, signal, long_filter)
+
+
+def mix_kernel(conv_ref, gate_ref, *refs):
+    mixed_refs, out_ref, lines = refs[:CHUNKS], refs[CHUNKS], refs[CHUNKS + 1]
+    rows, length = gate_ref.shape
+    per = length // LANES
+    lines[...] = wide(conv_ref[...].reshape(rows * per, LANES))
+    small = rows // CHUNKS
+    for lane in range(per):
+        cols = slice(lane * LANES, (lane + 1) * LANES)
+        conv = lines[pl.ds(lane, rows, stride=per), :]
+        out_ref[:, cols] = short(conv)
+        mixed = short(conv * wide(gate_ref[:, cols]))
+        for cut in range(CHUNKS):
+            mixed_refs[cut][:, cols] = mixed[cut * small : (cut + 1) * small]
+
+
+def mix(conv, outer_gate):
+    rows, length = outer_gate.shape
+    per = length // LANES
+    conv = conv.reshape(rows * per // 16, 16, LANES)
+    step = rows // 2
+    token_rows = pl.BlockSpec((step, length), lambda i: (i, 0))
+    cut_rows = pl.BlockSpec((step // CHUNKS, length), lambda i: (i, 0))
+    return pl.pallas_call(
+        mix_kernel,
+        grid=(2,),
+        in_specs=[pl.BlockSpec((step * per // 16, 16, LANES), lambda i: (i, 0, 0)), token_rows],
+        out_specs=[cut_rows] * CHUNKS + [token_rows],
+        out_shape=[jax.ShapeDtypeStruct((rows // CHUNKS, length), jnp.bfloat16)] * CHUNKS
+        + [jax.ShapeDtypeStruct((rows, length), jnp.bfloat16)],
+        scratch_shapes=[pltpu.VMEM((step * per, LANES), jnp.float32)],
+        compiler_params=params(),
+        name="mix",
+    )(conv, outer_gate)
+
+
+def regard_kernel(*refs):
+    *share_refs, gate_ref, conv_ref, outer_ref, grad_ref, lines = refs
+    per = gate_ref.shape[1] // LANES
+    grad_mix = wide(share_refs[0][...])
+    for ref in share_refs[1:]:
+        grad_mix = grad_mix + wide(ref[...])
+    outer_ref[...] = short(grad_mix * wide(conv_ref[...]))
+    spread_lanes(lines, grad_mix * wide(gate_ref[...]), 0, per)
+    grad_ref[...] = short(lines[...]).reshape(grad_ref.shape)
+
+
+def regard(shares, outer_gate, conv_out):
+    rows, length = outer_gate.shape
+    per = length // LANES
+    step = rows // 2
+    block = pl.BlockSpec((step, length), lambda i: (i, 0))
+    return pl.pallas_call(
+        regard_kernel,
+        grid=(2,),
+        in_specs=[block] * (len(shares) + 2),
+        out_specs=[block, pl.BlockSpec((step * per // 16, 16, LANES), lambda i: (i, 0, 0))],
+        out_shape=[
+            jax.ShapeDtypeStruct((rows, length), jnp.bfloat16),
+            jax.ShapeDtypeStruct((rows * per // 16, 16, LANES), jnp.bfloat16),
+        ],
+        scratch_shapes=[pltpu.VMEM((step * per, LANES), jnp.float32)],
+        compiler_params=params(),
+        name="regard",
+    )(*shares, outer_gate, conv_out)
+
+
+def finish_kernel(corr_ref, signal_ref, gate_ref, inner_ref, signal_out_ref, filter_ref, lines):
+    rows, length = signal_ref.shape
+    per = length // LANES
+    lines[...] = wide(corr_ref[...].reshape(rows * 2 * per, LANES))
+    for lane in range(per):
+        cols = slice(lane * LANES, (lane + 1) * LANES)
+        grad_prod = lines[pl.ds(lane, rows, stride=2 * per), :]
+        filter_ref[:, cols] = lines[pl.ds(per + lane, rows, stride=2 * per), :]
+        inner_ref[:, cols] = short(grad_prod * wide(signal_ref[:, cols]))
+        signal_out_ref[:, cols] = short(grad_prod * wide(gate_ref[:, cols]))
+
+
+def finish(corr, signal, inner_gate):
+    rows, length = signal.shape
+    per = length // LANES
+    step = rows // 2
+    block = pl.BlockSpec((step, length), lambda i: (i, 0))
+    return pl.pallas_call(
+        finish_kernel,
+        grid=(2,),
+        in_specs=[pl.BlockSpec((step, 2 * per, LANES), lambda i: (i, 0, 0)), block, block],
+        out_specs=[block] * 3,
+        out_shape=[jax.ShapeDtypeStruct((rows, length), jnp.bfloat16)] * 2
+        + [jax.ShapeDtypeStruct((rows, length), jnp.float32)],
+        scratch_shapes=[pltpu.VMEM((step * 2 * per, LANES), jnp.float32)],
+        compiler_params=params(),
+        name="finish",
+    )(corr.reshape(rows, 2 * per, LANES), signal, inner_gate)
+
+
+def unproject_kernel(count, place_ref, *refs):
+    grad_ref = refs[count]
+    for row in range(count):
+        refs[count + 1 + row][...] = short(mxu(refs[row][...], grad_ref[...]))
+
+
+def unproject(out_proj, grad_output, offsets, place, count):
+    width, length = grad_output.shape
+    rows = out_proj.shape[0] // count
+    step = 256
+    in_specs = [
+        pl.BlockSpec((rows, width), lambda i, at, by=by: (lax.rem(at[0] + by, count), 0))
+        for by in offsets
+    ]
+    return pl.pallas_call(
+        functools.partial(unproject_kernel, len(offsets)),
+        grid_spec=pltpu.PrefetchScalarGridSpec(
+            num_scalar_prefetch=1,
+            grid=(length // step,),
+            in_specs=in_specs + [pl.BlockSpec((width, step), lambda i, at: (0, i))],
+            out_specs=[pl.BlockSpec((rows, step), lambda i, at: (0, i))] * len(offsets),
+        ),
+        out_shape=[jax.ShapeDtypeStruct((rows, length), jnp.bfloat16)] * len(offsets),
+        compiler_params=params(),
+        name="unproject",
+    )(place.reshape(1), *[out_proj] * len(offsets), grad_output)
+
+
+def project_kernel(core_ref, *refs):
+    *piece_refs, grad_ref, other_ref, mine_ref = refs
+    small = mine_ref.shape[1]
+    for ref, which in ((other_ref, 1 - core_ref[0]), (mine_ref, core_ref[0])):
+        first = pl.multiple_of(which * small, small)
+        rows = jnp.concatenate([piece[pl.ds(first, small), :] for piece in piece_refs], axis=0)
+        out = lax.dot_general(
+            rows, grad_ref[...], (((1,), (1,)), ((), ())), preferred_element_type=jnp.float32
+        )
+        ref[...] = short(out).reshape(ref.shape)
+
+
+def project(pieces, grad_output, core):
+    width, length = grad_output.shape
+    small = pieces[0].shape[0] // 2
+    step = 512
+    out_block = pl.BlockSpec((len(pieces), small, step), lambda i, at: (0, 0, i))
+    out = jax.ShapeDtypeStruct((len(pieces), small, width), jnp.bfloat16)
+    return pl.pallas_call(
+        project_kernel,
+        grid_spec=pltpu.PrefetchScalarGridSpec(
+            num_scalar_prefetch=1,
+            grid=(width // step,),
+            in_specs=[pl.BlockSpec(pieces[0].shape, lambda i, at: (0, 0))] * len(pieces)
+            + [pl.BlockSpec((step, length), lambda i, at: (i, 0))],
+            out_specs=[out_block, out_block],
+        ),
+        out_shape=[out, out],
+        compiler_params=params(),
+        name="project",
+    )(core.reshape(1), *pieces, grad_output)
+
+
+def pick_kernel(order_ref, mine_ref, got_ref, *out_refs):
+    for slot, ref in enumerate(out_refs):
+        at = order_ref[slot]
+        ref[...] = short(wide(mine_ref[at]) + wide(got_ref[at]))
+
+
+def pick(mine, got, order):
+    count, small, width = mine.shape
+    step = width // 2
+    block = pl.BlockSpec((count, small, step), lambda i, at: (0, 0, i))
+    return pl.pallas_call(
+        pick_kernel,
+        grid_spec=pltpu.PrefetchScalarGridSpec(
+            num_scalar_prefetch=1,
+            grid=(2,),
+            in_specs=[block, block],
+            out_specs=[pl.BlockSpec((small, step), lambda i, at: (0, i))] * count,
+        ),
+        out_shape=[jax.ShapeDtypeStruct((small, width), jnp.bfloat16)] * count,
+        compiler_params=params(),
+        name="pick",
+    )(order, mine, got)
+
+
+def swaps(count, bit):
+    return [(place, place ^ bit) for place in range(count)]
+
+
+def exchange(blocks):
+    return lax.all_to_all(blocks, "seq", split_axis=0, concat_axis=0, tiled=True)
+
+
+def tie(first, *others):
+    return lax.optimization_barrier((first,) + others)[0]
+
+
+def shift(block, by):
+    count = lax.axis_size("chan")
+    return lax.ppermute(block, "chan", [(i, (i + by) % count) for i in range(count)])
+
+
+def gather_first(shard):
+    count, place = lax.axis_size("chan"), lax.axis_index("chan")
+    if count != 4:
+        return [shard] + [shift(shard, by) for by in range(1, count)]
+    low, high = shift(shard, 1), shift(shard, 3)
+    return [lax.select_n(place, shard, high, low, shard), shard, low, high]
+
+
+def gather_second(held):
+    if lax.axis_size("chan") == 4:
+        passed, shard, low, high = held
+        return [shard, low, lax.ppermute(passed, "chan", [(0, 2), (3, 1), (2, 3), (1, 0)]), high]
+    return held
+
+
+def scatter_seq(other, mine):
+    count, chips = lax.axis_size("seq"), lax.axis_size("chan")
+    line, chip = lax.axis_index("chan"), lax.axis_index("seq") // 2
+    got = lax.ppermute(other, "seq", swaps(count, 1))
+    bits = sorted(range(1, chips), key=lambda bit: (-bin(bit).count("1"), bit)) + [0]
+    order = jnp.stack([lax.rem(line - (chip ^ bit) + chips, chips) for bit in bits])
+    blocks = pick(mine, got, order.astype(jnp.int32))
+    return [
+        lax.ppermute(block, "seq", swaps(count, 2 * bit)) for block, bit in zip(blocks, bits[:-1])
+    ] + [blocks[-1]]
+
+
+def sum_of(parts):
+    total = wide(parts[0])
+    for part in parts[1:]:
+        total = total + wide(part)
+    return total
+
+
 def body(outer_gate, inner_gate, signal, long_filter, grad_output, out_proj):
-    seq_count = lax.axis_size("seq")
+    seq_count, chan_count = lax.axis_size("seq"), lax.axis_size("chan")
     chan_rows, block_len = outer_gate.shape
     owned = chan_rows // seq_count
     per = block_len // LANES
+    line = lax.axis_index("chan")
+    core = lax.axis_index("seq") % 2
     tables = [jnp.asarray(t) for t in dft_tables(block_len * seq_count, seq_count)]
 
-    def exchange(blocks):
-        return lax.all_to_all(blocks, "seq", split_axis=0, concat_axis=0, tiled=True)
-
-    def wide(x):
-        return x.astype(jnp.float32)
-
-    mixed_in = (wide(inner_gate) * wide(signal)).astype(jnp.bfloat16)
-    pair = jnp.concatenate(
-        [mixed_in.reshape(chan_rows, per, LANES), long_filter.reshape(chan_rows, per, LANES)], axis=1
-    )
-    pair = exchange(pair.reshape(seq_count, owned, 2 * per, LANES))
-    conv, spec_signal, spec_filter = convolve(pair, tables)
-    conv_out = wide(exchange(conv).reshape(chan_rows, block_len))
-    mixed = (wide(outer_gate) * conv_out).astype(jnp.bfloat16)
-
-    grad_mix = wide(
-        lax.psum_scatter(
-            jnp.dot(out_proj, grad_output, preferred_element_type=jnp.float32).astype(jnp.bfloat16),
-            "chan",
-            scatter_dimension=0,
-            tiled=True,
-        )
-    )
-    grad_conv = (grad_mix * wide(outer_gate)).astype(jnp.bfloat16)
-    grad_outer = (grad_mix * conv_out).astype(jnp.bfloat16)
-    corr = correlate(
-        exchange(grad_conv.reshape(seq_count, owned // 2, 2 * per, LANES)),
-        spec_signal,
-        spec_filter,
-        tables,
-    )
-    corr = exchange(corr).reshape(chan_rows, 2, block_len)
-    grad_prod, grad_filter = wide(corr[:, 0]), wide(corr[:, 1])
-    grad_inner = (grad_prod * wide(signal)).astype(jnp.bfloat16)
-    grad_signal = (grad_prod * wide(inner_gate)).astype(jnp.bfloat16)
-
-    mixed_all = lax.all_gather(mixed, "chan", axis=0, tiled=True)
-    grad_proj = wide(
-        lax.psum_scatter(
-            lax.dot_general(
-                mixed_all, grad_output, (((1,), (1,)), ((), ())), preferred_element_type=jnp.float32
-            ).astype(jnp.bfloat16),
-            "seq",
-            scatter_dimension=0,
-            tiled=True,
-        )
-    )
+    pair = prepare(inner_gate, signal, long_filter).reshape(seq_count, owned, 2 * per, LANES)
+    sent = exchange(pair)
+
+    weights = tie(out_proj, pair)
+    if chan_count == 4:
+        far = unproject(weights, grad_output, [2], line, chan_count)[0]
+        near = unproject(tie(weights, far), grad_output, [0, 1, 3], line, chan_count)
+        far = lax.ppermute(far, "chan", [(2, 0), (1, 3), (3, 2), (0, 1)])
+        sent = tie(sent, *near)
+        none = jnp.zeros_like(far)
+        up = shift(short(wide(near[1]) + wide(jnp.where(line == 1, far, none))), 1)
+        down = shift(short(wide(near[2]) + wide(jnp.where(line == 2, far, none))), 3)
+        ends = jnp.where((line == 0) | (line == 3), far, none)
+        shares = [near[0], up, down, ends]
+    else:
+        blocks = unproject(weights, grad_output, list(range(chan_count)), line, chan_count)
+        shares = [blocks[0]] + [shift(block, by) for by, block in enumerate(blocks) if by > 0]
+
+    conv, spec_signal, spec_filter = convolve(sent, tables)
+    *mixed, conv_out = mix(exchange(conv), outer_gate)
+    held = [gather_first(part) for part in mixed]
+    held, shares = lax.optimization_barrier((held, shares))
+
+    grad_outer, grad_conv = regard(shares, outer_gate, conv_out)
+    grad_conv = grad_conv.reshape(seq_count, owned // 2, 2 * per, LANES)
+    pieces = [gather_second(part) for part in held]
+    pieces[0] = tie(pieces[0], grad_conv)
+    projs = [scatter_seq(*project(pieces[0], grad_output, core))]
+    corr = correlate(exchange(grad_conv), spec_signal, spec_filter, tables)
+    pieces[1] = tie(pieces[1], corr)
+    projs.append(scatter_seq(*project(pieces[1], grad_output, core)))
+
+    grad_inner, grad_signal, grad_filter = finish(exchange(corr), signal, inner_gate)
+    grad_proj = jnp.concatenate([sum_of(parts) for parts in projs], axis=0)
     return (grad_outer, grad_inner, grad_signal, grad_filter, grad_proj)
 
 

time: 191 us -> 178 us (0.932)
  blocking collectives: 71.8 us -> 0 us
  starting transfers between devices: 0.12 us -> 51.3 us
  Pallas kernels: 12.3 us -> 44.7 us
  matrix products: 18.7 us -> 0 us
  local copies, waits for them, and re-layouts: 4.22 us -> 19.9 us
  between operations: 13.9 us -> 0.85 us
  waiting for transfers between devices: 62 us -> 53.1 us
    all_to_all x4 -> x0, blocking collectives: 71.8 us -> none  [exchange(): lax.all_to_all(blocks, 'seq', split_axis=0, concat_axis=0, tiled=True)]
    all_gather x1 -> x0, waiting for transfers between devices: 45.4 us -> none  [body(): mixed_all = lax.all_gather(mixed, 'chan', axis=0, tiled=True)]
    ppermute x0 -> x17, waiting for transfers between devices: none -> 34.8 us  [the longest x6 22.7 us: shift(): lax.ppermute(block, 'chan', [(i, (i + by) % count) for i in range(count)])]
    ppermute x0 -> x17, starting transfers between devices: none -> 33 us  [the longest x6 20.6 us: shift(): lax.ppermute(block, 'chan', [(i, (i + by) % count) for i in range(count)])]
    pallas_call x0 -> x10, Pallas kernels: none -> 31.7 us  [the longest x2 10.8 us: project(): pl.pallas_call(project_kernel, grid_spec=pltpu.PrefetchScalarGridSpec(num...]
    unnamed x22 -> x70, local copies, waits for them, and re-layouts: 0.25 us -> 19.9 us
    dot_general x2 -> x0, matrix products: 18.7 us -> none  [the longest x1 9.38 us: body(): jnp.dot(out_proj, grad_output, preferred_element_type=jnp.float32)]
    all_to_all x0 -> x4, waiting for transfers between devices: none -> 18.3 us  [exchange(): lax.all_to_all(blocks, 'seq', split_axis=0, concat_axis=0, tiled=True)]
  transfers between devices with their start and end apart: 3 -> 21, of which waited for: 3 -> 8; matrix products, arithmetic and copies ran while one was open for 4% -> 3% of each run, Pallas kernels for 6% -> 24%
where the time goes in v2:
time: 178 us; the launch traced here: 177 us
  waiting for transfers between devices  53.1 us (30%)
  starting transfers between devices  51.3 us (29%)
  Pallas kernels  44.7 us (25%)
  local copies, waits for them, and re-layouts  19.9 us (11%)
  other arithmetic  6.83 us (4%)
    ppermute x6, waiting for transfers between devices, shift(): lax.ppermute(block, 'chan', [(i, (i + by) % count) for i in range(count)])  22.7 us
    ppermute x6, starting transfers between devices, shift(): lax.ppermute(block, 'chan', [(i, (i + by) % count) for i in range(count)])  20.6 us
    unnamed x70, local copies, waits for them, and re-layouts  19.9 us
    all_to_all x4, waiting for transfers between devices, exchange(): lax.all_to_all(blocks, 'seq', split_axis=0, concat_axis=0, tiled=True)  18.3 us
    all_to_all x4, starting transfers between devices, exchange(): lax.all_to_all(blocks, 'seq', split_axis=0, concat_axis=0, tiled=True)  18.2 us
    ppermute x6, waiting for transfers between devices, scatter_seq(): lax.ppermute(block, 'seq', swaps(count, 2 * bit))  12.2 us
    pallas_call x2, Pallas kernels, project(): pl.pallas_call(project_kernel, grid_spec=pltpu.PrefetchScalarGridSpec(num...  10.8 us
    pallas_call x2, Pallas kernels, unproject(): pl.pallas_call(functools.partial(unproject_kernel, len(offsets)), grid_sp...  10.3 us
  transfers between devices with their start and end apart: 21, of which 8 were waited for; matrix products, arithmetic and copies ran while one was open for 3% of the time, Pallas kernels for 24%

profile of v2, /device:TPU:0, one launch (start us, length us, event | category | flops | bytes accessed | tf_op | source)
XLA Modules:
  0.0 176.7 jit_solution(15644763134789228446)
XLA Ops:
  3.8 2.0 %prepare.1 = bf16[256,16,128]{2,1,0:T(8,128)(2,1)} custom-call(bf16[256,1024]{1,0:T(8,128)(2,1)S(1)} %copy-done.1, bf16[256,1024]{1,0:T(8,128)(2,1)S(1)} %copy-done.3, bf16[256,1024]{1,0:T(8,128)(2,1)S(1)} %copy-done.23), custom_call_target="tpu_custom_call" | custom-call | tf_op jit(solution)/shard_map/prepare/pallas_call | solution.py:215
  5.8 5.2 %all-to-all-start = ((bf16[8,32,16,128]{3,2,1,0:T(8,128)(2,1)}), bf16[8,32,16,128]{3,2,1,0:T(8,128)(2,1)S(1)}, u32[]{:S(2)}, u32[]{:S(2)}) async-start(bf16[8,32,16,128]{3,2,1,0:T(8,128)(2,1)} %bitcast), calls=%async_computation | async-start | bytes 2097152 | tf_op jit(solution)/shard_map/all_to_all | solution.py:413
  11.0 2.2 %copy-done = bf16[1024,2048]{1,0:T(8,128)(2,1)S(1)} copy-done((bf16[1024,2048]{1,0:T(8,128)(2,1)S(1)}, bf16[1024,2048]{1,0:T(8,128)(2,1)}, u32[]{:S(2)}) %copy-start) | copy-done | bytes 4194328
  13.1 4.7 %unproject.2 = bf16[256,1024]{1,0:T(8,128)(2,1)} custom-call(s32[1]{0:T(128)} %bitcast.1.place_ref, bf16[1024,2048]{1,0:T(8,128)(2,1)S(1)} %copy-done, bf16[2048,1024]{1,0:T(8,128)(2,1)} %refs_4_.5), custom_call_target="tpu_custom_call" | custom-call | tf_op jit(solution)/shard_map/unproject/pallas_call | solution.py:337
  17.9 1.6 collective-permute-start.4
  19.4 5.6 %unproject.3 = (bf16[256,1024]{1,0:T(8,128)(2,1)S(1)}, bf16[256,1024]{1,0:T(8,128)(2,1)S(1)}, bf16[256,1024]{1,0:T(8,128)(2,1)S(1)}) custom-call(s32[1]{0:T(128)} %bitcast.1.place_ref, bf16[1024,2048]{1,0:T(8,128)(2,1)S(1)} %copy-done, bf16[1024,2048]{1,0:T(8,128)(2,1)S(1)} %copy-done, bf16[1024,2048]{1,0:T(8,128)(2,1)S(1)} %copy-done, ...), custom_call_target="tpu_custom_call" | custom-call | tf_op jit(solution)/shard_map/unproject/pallas_call | solution.py:337
  30.1 6.0 %convolve.1 = (bf16[8,16,16,128]{3,2,1,0:T(8,128)(2,1)S(1)}, f32[32,64,256]{2,1,0:T(8,128)S(1)}, f32[32,64,256]{2,1,0:T(8,128)}) custom-call(bf16[8,32,16,128]{3,2,1,0:T(8,128)(2,1)S(1)} %all-to-all-done.pairs_ref, bf16[256,256]{1,0:T(8,128)(2,1)S(1)} %copy-done.31, bf16[512,256]{1,0:T(8,128)(2,1)S(1)} %copy-done.9, bf16[512,256]{1,0:T(8,128)(2,1)S(1)} %copy-done.8, ...), custom_call_target="tpu_custom_call" | custom-call | tf_op jit(solution)/shard_map/convolve/pallas_call | solution.py:147
  37.0 4.3 %all-to-all-start.1 = ((bf16[8,16,16,128]{3,2,1,0:T(8,128)(2,1)}), bf16[8,16,16,128]{3,2,1,0:T(8,128)(2,1)S(1)}, u32[]{:S(2)}, u32[]{:S(2)}) async-start(bf16[8,16,16,128]{3,2,1,0:T(8,128)(2,1)} %copy-done.27), calls=%async_computation.1 | async-start | bytes 1048576 | tf_op jit(solution)/shard_map/all_to_all | solution.py:413
  41.3 9.7 %all-to-all-done.1 = bf16[8,16,16,128]{3,2,1,0:T(8,128)(2,1)S(1)} async-done(((bf16[8,16,16,128]{3,2,1,0:T(8,128)(2,1)}), bf16[8,16,16,128]{3,2,1,0:T(8,128)(2,1)S(1)}, u32[]{:S(2)}, u32[]{:S(2)}) %all-to-all-start.1) | async-done | bytes 524320 | tf_op jit(solution)/shard_map/all_to_all | solution.py:413
  52.5 2.6 %collective-permute-start.1 = (bf16[128,1024]{1,0:T(8,128)(2,1)S(1)}, bf16[128,1024]{1,0:T(8,128)(2,1)S(1)}, u32[]{:S(2)}, u32[]{:S(2)}) collective-permute-start(bf16[128,1024]{1,0:T(8,128)(2,1)S(1)} %get-tuple-element.79.refs_0_), channel_id=1, source_target_pairs={{0,1},{1,2},{2,3},{3,0},{4,5},{5,6},{6,7},{7,4},{8,9},{9,10},{10,1... | collective-permute-start | bytes 786440 | tf_op jit(solution)/shard_map/ppermute | solution.py:422
  56.4 1.7 add_convert_fusion
  61.0 2.6 %collective-permute-done.1.refs_1_ = bf16[128,1024]{1,0:T(8,128)(2,1)S(1)} collective-permute-done((bf16[128,1024]{1,0:T(8,128)(2,1)S(1)}, bf16[128,1024]{1,0:T(8,128)(2,1)S(1)}, u32[]{:S(2)}, u32[]{:S(2)}) %collective-permute-start.1) | collective-permute-done | bytes 262176 | tf_op jit(solution)/shard_map/ppermute | solution.py:422
  63.6 13.9 %collective-permute-start.2 = (bf16[128,1024]{1,0:T(8,128)(2,1)S(1)}, bf16[128,1024]{1,0:T(8,128)(2,1)S(1)}, u32[]{:S(2)}, u32[]{:S(2)}) collective-permute-start(bf16[128,1024]{1,0:T(8,128)(2,1)S(1)} %get-tuple-element.93.refs_0_), channel_id=1, source_target_pairs={{0,3},{1,0},{2,1},{3,2},{4,7},{5,4},{6,5},{7,6},{8,11},{9,8},{10,9... | collective-permute-start | bytes 786440 | tf_op jit(solution)/shard_map/ppermute | solution.py:422
  79.4 17.3 %collective-permute-done.3.refs_1_ = bf16[128,1024]{1,0:T(8,128)(2,1)S(1)} collective-permute-done((bf16[128,1024]{1,0:T(8,128)(2,1)S(1)}, bf16[128,1024]{1,0:T(8,128)(2,1)S(1)}, u32[]{:S(2)}, u32[]{:S(2)}) %collective-permute-start.3) | collective-permute-done | bytes 262176 | tf_op jit(solution)/shard_map/ppermute | solution.py:422
  96.7 2.7 %collective-permute-done.2.refs_3_ = bf16[128,1024]{1,0:T(8,128)(2,1)S(1)} collective-permute-done((bf16[128,1024]{1,0:T(8,128)(2,1)S(1)}, bf16[128,1024]{1,0:T(8,128)(2,1)S(1)}, u32[]{:S(2)}, u32[]{:S(2)}) %collective-permute-start.2) | collective-permute-done | bytes 262176 | tf_op jit(solution)/shard_map/ppermute | solution.py:422
  100.9 1.4 regard.1
  103.1 4.5 %all-to-all-start.2 = ((bf16[8,16,16,128]{3,2,1,0:T(8,128)(2,1)}), bf16[8,16,16,128]{3,2,1,0:T(8,128)(2,1)S(1)}, u32[]{:S(2)}, u32[]{:S(2)}) async-start(bf16[8,16,16,128]{3,2,1,0:T(8,128)(2,1)} %bitcast.12), calls=%async_computation.2 | async-start | bytes 1048576 | tf_op jit(solution)/shard_map/all_to_all | solution.py:413
  107.7 2.5 %collective-permute-start.12 = (bf16[128,1024]{1,0:T(8,128)(2,1)}, bf16[128,1024]{1,0:T(8,128)(2,1)}, u32[]{:S(2)}, u32[]{:S(2)}) collective-permute-start(bf16[128,1024]{1,0:T(8,128)(2,1)} %select_select_fusion), channel_id=1, source_target_pairs={{0,2},{3,1},{2,3},{1,0},{4,6},{7,5},{6,7},{5,4},{8,10},{11,9},{10,... | collective-permute-start | bytes 786440 | tf_op jit(solution)/shard_map/ppermute | solution.py:436
  113.1 5.3 %project.2 = (bf16[4,64,2048]{2,1,0:T(8,128)(2,1)}, bf16[4,64,2048]{2,1,0:T(8,128)(2,1)S(1)}) custom-call(s32[1]{0:T(128)} %bitcast.9.core_ref, bf16[128,1024]{1,0:T(8,128)(2,1)S(1)} %copy-done.14, bf16[128,1024]{1,0:T(8,128)(2,1)S(1)} %copy-done.18, bf16[128,1024]{1,0:T(8,128)(2,1)} %collective-permute-done.7.refs_2_, bf16[128,1024]{1,0:T(8,128)(2,1)S(1)} %copy-done.20, ...), custom_call_target="tpu_custom_call" | custom-call | tf_op jit(solution)/shard_map/project/pallas_call | solution.py:369
  121.5 6.9 %correlate.1 = bf16[8,32,16,128]{3,2,1,0:T(8,128)(2,1)} custom-call(bf16[8,16,16,128]{3,2,1,0:T(8,128)(2,1)S(1)} %all-to-all-done.2.pairs_ref, f32[32,64,256]{2,1,0:T(8,128)S(1)} %get-tuple-element.70.signal_ref, f32[32,64,256]{2,1,0:T(8,128)} %get-tuple-element.71.filter_ref, bf16[256,256]{1,0:T(8,128)(2,1)S(1)} %copy-done.32, ...), custom_call_target="tpu_custom_call" | custom-call | tf_op jit(solution)/shard_map/correlate/pallas_call | solution.py:173
  128.4 5.5 %project.3 = (bf16[4,64,2048]{2,1,0:T(8,128)(2,1)}, bf16[4,64,2048]{2,1,0:T(8,128)(2,1)S(1)}) custom-call(s32[1]{0:T(128)} %bitcast.9.core_ref, bf16[128,1024]{1,0:T(8,128)(2,1)S(1)} %copy-done.12, bf16[128,1024]{1,0:T(8,128)(2,1)S(1)} %copy-done.16, bf16[128,1024]{1,0:T(8,128)(2,1)} %collective-permute-done.12.refs_2_, bf16[128,1024]{1,0:T(8,128)(2,1)S(1)} %copy-done.22, ...), custom_call_target="tpu_custom_call" | custom-call | tf_op jit(solution)/shard_map/project/pallas_call | solution.py:369
  134.2 4.2 %all-to-all-start.3 = ((bf16[8,32,16,128]{3,2,1,0:T(8,128)(2,1)}), bf16[8,32,16,128]{3,2,1,0:T(8,128)(2,1)S(1)}, u32[]{:S(2)}, u32[]{:S(2)}) async-start(bf16[8,32,16,128]{3,2,1,0:T(8,128)(2,1)} %correlate.1), calls=%async_computation.3 | async-start | bytes 2097152 | tf_op jit(solution)/shard_map/all_to_all | solution.py:413
  139.7 2.6 %pick.2 = (bf16[64,2048]{1,0:T(8,128)(2,1)}, bf16[64,2048]{1,0:T(8,128)(2,1)}, bf16[64,2048]{1,0:T(8,128)(2,1)}, bf16[64,2048]{1,0:T(8,128)(2,1)S(1)}) custom-call(s32[4]{0:T(128)S(1)} %pad_add_fusion.order_ref, bf16[4,64,2048]{2,1,0:T(8,128)(2,1)S(1)} %copy-done.7, bf16[4,64,2048]{2,1,0:T(8,128)(2,1)} %collective-permute-done.8.got_ref), custom_call_target="tpu_custom_call" | custom-call | tf_op jit(solution)/shard_map/pick/pallas_call | solution.py:394
  142.3 2.9 %collective-permute-start.9 = (bf16[64,2048]{1,0:T(8,128)(2,1)}, bf16[64,2048]{1,0:T(8,128)(2,1)}, u32[]{:S(2)}, u32[]{:S(2)}) collective-permute-start(bf16[64,2048]{1,0:T(8,128)(2,1)} %get-tuple-element.85), channel_id=1, source_target_pairs={{0,24},{4,28},{8,16},{12,20},{16,8},{20,12},{24,0},{28,4},{1,25},{... | collective-permute-start | bytes 786440 | tf_op jit(solution)/shard_map/ppermute | solution.py:448
  145.8 8.6 %all-to-all-done.3 = bf16[8,32,16,128]{3,2,1,0:T(8,128)(2,1)S(1)} async-done(((bf16[8,32,16,128]{3,2,1,0:T(8,128)(2,1)}), bf16[8,32,16,128]{3,2,1,0:T(8,128)(2,1)S(1)}, u32[]{:S(2)}, u32[]{:S(2)}) %all-to-all-start.3) | async-done | bytes 1048608 | tf_op jit(solution)/shard_map/all_to_all | solution.py:413
  154.4 2.1 %finish.1 = (bf16[256,1024]{1,0:T(8,128)(2,1)}, bf16[256,1024]{1,0:T(8,128)(2,1)}, f32[256,1024]{1,0:T(8,128)}) custom-call(bf16[256,16,128]{2,1,0:T(8,128)(2,1)S(1)} %bitcast.10, bf16[256,1024]{1,0:T(8,128)(2,1)S(1)} %copy-done.4, bf16[256,1024]{1,0:T(8,128)(2,1)S(1)} %copy-done.2), custom_call_target="tpu_custom_call" | custom-call | tf_op jit(solution)/shard_map/finish/pallas_call | solution.py:310
  156.5 2.0 %pick.3 = (bf16[64,2048]{1,0:T(8,128)(2,1)S(1)}, bf16[64,2048]{1,0:T(8,128)(2,1)S(1)}, bf16[64,2048]{1,0:T(8,128)(2,1)S(1)}, bf16[64,2048]{1,0:T(8,128)(2,1)S(1)}) custom-call(s32[4]{0:T(128)S(1)} %pad_add_fusion.order_ref, bf16[4,64,2048]{2,1,0:T(8,128)(2,1)S(1)} %get-tuple-element.97.mine_ref, bf16[4,64,2048]{2,1,0:T(8,128)(2,1)} %collective-permute-done.13.got_ref), custom_call_target="tpu_custom_call" | custom-call | tf_op jit(solution)/shard_map/pick/pallas_call | solution.py:394
  159.1 1.5 collective-permute-start.15
  160.6 1.5 collective-permute-start.16
  162.1 2.7 %collective-permute-done.10 = bf16[64,2048]{1,0:T(8,128)(2,1)} collective-permute-done((bf16[64,2048]{1,0:T(8,128)(2,1)}, bf16[64,2048]{1,0:T(8,128)(2,1)}, u32[]{:S(2)}, u32[]{:S(2)}) %collective-permute-start.10) | collective-permute-done | bytes 262176 | tf_op jit(solution)/shard_map/ppermute | solution.py:448
  166.0 5.2 %collective-permute-done.14 = bf16[64,2048]{1,0:T(8,128)(2,1)S(1)} collective-permute-done((bf16[64,2048]{1,0:T(8,128)(2,1)S(1)}, bf16[64,2048]{1,0:T(8,128)(2,1)S(1)}, u32[]{:S(2)}, u32[]{:S(2)}) %collective-permute-start.14) | collective-permute-done | bytes 262176 | tf_op jit(solution)/shard_map/ppermute | solution.py:448
  171.2 4.2 %collective-permute-done.15 = bf16[64,2048]{1,0:T(8,128)(2,1)S(1)} collective-permute-done((bf16[64,2048]{1,0:T(8,128)(2,1)S(1)}, bf16[64,2048]{1,0:T(8,128)(2,1)S(1)}, u32[]{:S(2)}, u32[]{:S(2)}) %collective-permute-start.15) | collective-permute-done | bytes 262176 | tf_op jit(solution)/shard_map/ppermute | solution.py:448
  (100 shorter events, 29.7 us)
Async XLA Ops:
  5.8 21.6 %all-to-all-start = ((bf16[8,32,16,128]{3,2,1,0:T(8,128)(2,1)}), bf16[8,32,16,128]{3,2,1,0:T(8,128)(2,1)S(1)}, u32[]{:S(2)}, u32[]{:S(2)}) async-start(bf16[8,32,16,128]{3,2,1,0:T(8,128)(2,1)} %bitcast), calls=%async_computation | async-start | bytes 2097152 | tf_op jit(solution)/shard_map/all_to_all | solution.py:413
  17.9 9.6 %copy-start.8 = (bf16[512,256]{1,0:T(8,128)(2,1)S(1)}, bf16[512,256]{1,0:T(8,128)(2,1)}, u32[]{:S(2)}) copy-start(bf16[512,256]{1,0:T(8,128)(2,1)} %constant.63.clone.inverse_ref) | copy-start | bytes 786436
  17.9 9.6 %copy-start.30 = (bf16[128,512]{1,0:T(8,128)(2,1)S(1)}, bf16[128,512]{1,0:T(8,128)(2,1)}, u32[]{:S(2)}) copy-start(bf16[128,512]{1,0:T(8,128)(2,1)} %constant.64.clone.last_ref) | copy-start | bytes 393220
  17.9 38.5 %collective-permute-start.4 = (bf16[256,1024]{1,0:T(8,128)(2,1)}, bf16[256,1024]{1,0:T(8,128)(2,1)}, u32[]{:S(2)}, u32[]{:S(2)}) collective-permute-start(bf16[256,1024]{1,0:T(8,128)(2,1)} %unproject.2), channel_id=1, source_target_pairs={{2,0},{1,3},{3,2},{0,1},{6,4},{5,7},{7,6},{4,5},{10,8},{9,11},{11,... | collective-permute-start | bytes 1572872 | tf_op jit(solution)/shard_map/ppermute | solution.py:475
  36.9 64.0 %copy-start.29 = (bf16[256,1024]{1,0:T(8,128)(2,1)S(1)}, bf16[256,1024]{1,0:T(8,128)(2,1)}, u32[]{:S(2)}) copy-start(bf16[256,1024]{1,0:T(8,128)(2,1)} %copy-done.28) | copy-start | bytes 1572868
  37.0 14.1 %all-to-all-start.1 = ((bf16[8,16,16,128]{3,2,1,0:T(8,128)(2,1)}), bf16[8,16,16,128]{3,2,1,0:T(8,128)(2,1)S(1)}, u32[]{:S(2)}, u32[]{:S(2)}) async-start(bf16[8,16,16,128]{3,2,1,0:T(8,128)(2,1)} %copy-done.27), calls=%async_computation.1 | async-start | bytes 1048576 | tf_op jit(solution)/shard_map/all_to_all | solution.py:413
  52.5 46.9 %copy-start.11 = (bf16[128,1024]{1,0:T(8,128)(2,1)}, bf16[128,1024]{1,0:T(8,128)(2,1)S(1)}, u32[]{:S(2)}) copy-start(bf16[128,1024]{1,0:T(8,128)(2,1)S(1)} %get-tuple-element.93.refs_0_) | copy-start | bytes 786436
  52.5 47.7 %copy-start.13 = (bf16[128,1024]{1,0:T(8,128)(2,1)}, bf16[128,1024]{1,0:T(8,128)(2,1)S(1)}, u32[]{:S(2)}) copy-start(bf16[128,1024]{1,0:T(8,128)(2,1)S(1)} %get-tuple-element.79.refs_0_) | copy-start | bytes 786436
  52.5 11.1 %collective-permute-start.1 = (bf16[128,1024]{1,0:T(8,128)(2,1)S(1)}, bf16[128,1024]{1,0:T(8,128)(2,1)S(1)}, u32[]{:S(2)}, u32[]{:S(2)}) collective-permute-start(bf16[128,1024]{1,0:T(8,128)(2,1)S(1)} %get-tuple-element.79.refs_0_), channel_id=1, source_target_pairs={{0,1},{1,2},{2,3},{3,0},{4,5},{5,6},{6,7},{7,4},{8,9},{9,10},{10,1... | collective-permute-start | bytes 786440 | tf_op jit(solution)/shard_map/ppermute | solution.py:422
  55.2 23.4 %collective-permute-start = (bf16[128,1024]{1,0:T(8,128)(2,1)S(1)}, bf16[128,1024]{1,0:T(8,128)(2,1)S(1)}, u32[]{:S(2)}, u32[]{:S(2)}) collective-permute-start(bf16[128,1024]{1,0:T(8,128)(2,1)S(1)} %get-tuple-element.79.refs_0_), channel_id=1, source_target_pairs={{0,3},{1,0},{2,1},{3,2},{4,7},{5,4},{6,5},{7,6},{8,11},{9,8},{10,9... | collective-permute-start | bytes 786440 | tf_op jit(solution)/shard_map/ppermute | solution.py:422
  58.1 42.1 %collective-permute-start.6 = (bf16[256,1024]{1,0:T(8,128)(2,1)S(1)}, bf16[256,1024]{1,0:T(8,128)(2,1)S(1)}, u32[]{:S(2)}, u32[]{:S(2)}) collective-permute-start(bf16[256,1024]{1,0:T(8,128)(2,1)S(1)} %get-tuple-element.103), channel_id=1, source_target_pairs={{0,3},{1,0},{2,1},{3,2},{4,7},{5,4},{6,5},{7,6},{8,11},{9,8},{10,9... | collective-permute-start | bytes 1572872 | tf_op jit(solution)/shard_map/ppermute | solution.py:422
  58.8 41.4 %collective-permute-start.5 = (bf16[256,1024]{1,0:T(8,128)(2,1)S(1)}, bf16[256,1024]{1,0:T(8,128)(2,1)S(1)}, u32[]{:S(2)}, u32[]{:S(2)}) collective-permute-start(bf16[256,1024]{1,0:T(8,128)(2,1)S(1)} %get-tuple-element.104), channel_id=1, source_target_pairs={{0,1},{1,2},{2,3},{3,0},{4,5},{5,6},{6,7},{7,4},{8,9},{9,10},{10,1... | collective-permute-start | bytes 1572872 | tf_op jit(solution)/shard_map/ppermute | solution.py:422
  60.2 36.6 %collective-permute-start.3 = (bf16[128,1024]{1,0:T(8,128)(2,1)S(1)}, bf16[128,1024]{1,0:T(8,128)(2,1)S(1)}, u32[]{:S(2)}, u32[]{:S(2)}) collective-permute-start(bf16[128,1024]{1,0:T(8,128)(2,1)S(1)} %get-tuple-element.93.refs_0_), channel_id=1, source_target_pairs={{0,1},{1,2},{2,3},{3,0},{4,5},{5,6},{6,7},{7,4},{8,9},{9,10},{10,1... | collective-permute-start | bytes 786440 | tf_op jit(solution)/shard_map/ppermute | solution.py:422
  63.6 36.6 %copy-start.17 = (bf16[128,1024]{1,0:T(8,128)(2,1)}, bf16[128,1024]{1,0:T(8,128)(2,1)S(1)}, u32[]{:S(2)}) copy-start(bf16[128,1024]{1,0:T(8,128)(2,1)S(1)} %collective-permute-done.1.refs_1_) | copy-start | bytes 786436
  63.6 35.8 %collective-permute-start.2 = (bf16[128,1024]{1,0:T(8,128)(2,1)S(1)}, bf16[128,1024]{1,0:T(8,128)(2,1)S(1)}, u32[]{:S(2)}, u32[]{:S(2)}) collective-permute-start(bf16[128,1024]{1,0:T(8,128)(2,1)S(1)} %get-tuple-element.93.refs_0_), channel_id=1, source_target_pairs={{0,3},{1,0},{2,1},{3,2},{4,7},{5,4},{6,5},{7,6},{8,11},{9,8},{10,9... | collective-permute-start | bytes 786440 | tf_op jit(solution)/shard_map/ppermute | solution.py:422
  78.6 22.3 %copy-start.19 = (bf16[128,1024]{1,0:T(8,128)(2,1)}, bf16[128,1024]{1,0:T(8,128)(2,1)S(1)}, u32[]{:S(2)}) copy-start(bf16[128,1024]{1,0:T(8,128)(2,1)S(1)} %collective-permute-done.refs_3_) | copy-start | bytes 786436
  100.2 10.0 %collective-permute-start.7 = (bf16[128,1024]{1,0:T(8,128)(2,1)}, bf16[128,1024]{1,0:T(8,128)(2,1)}, u32[]{:S(2)}, u32[]{:S(2)}) collective-permute-start(bf16[128,1024]{1,0:T(8,128)(2,1)} %select_select_fusion.1), channel_id=1, source_target_pairs={{0,2},{3,1},{2,3},{1,0},{4,6},{7,5},{6,7},{5,4},{8,10},{11,9},{10,... | collective-permute-start | bytes 786440 | tf_op jit(solution)/shard_map/ppermute | solution.py:436
  103.1 16.5 %copy-start.10 = (bf16[512,256]{1,0:T(8,128)(2,1)S(1)}, bf16[512,256]{1,0:T(8,128)(2,1)}, u32[]{:S(2)}) copy-start(bf16[512,256]{1,0:T(8,128)(2,1)} %constant.62.clone.forward_ref) | copy-start | bytes 786436
  103.1 16.5 %all-to-all-start.2 = ((bf16[8,16,16,128]{3,2,1,0:T(8,128)(2,1)}), bf16[8,16,16,128]{3,2,1,0:T(8,128)(2,1)S(1)}, u32[]{:S(2)}, u32[]{:S(2)}) async-start(bf16[8,16,16,128]{3,2,1,0:T(8,128)(2,1)} %bitcast.12), calls=%async_computation.2 | async-start | bytes 1048576 | tf_op jit(solution)/shard_map/all_to_all | solution.py:413
  107.7 20.7 %collective-permute-start.12 = (bf16[128,1024]{1,0:T(8,128)(2,1)}, bf16[128,1024]{1,0:T(8,128)(2,1)}, u32[]{:S(2)}, u32[]{:S(2)}) collective-permute-start(bf16[128,1024]{1,0:T(8,128)(2,1)} %select_select_fusion), channel_id=1, source_target_pairs={{0,2},{3,1},{2,3},{1,0},{4,6},{7,5},{6,7},{5,4},{8,10},{11,9},{10,... | collective-permute-start | bytes 786440 | tf_op jit(solution)/shard_map/ppermute | solution.py:436
  119.4 9.0 %copy-start.12 = (bf16[128,1024]{1,0:T(8,128)(2,1)S(1)}, bf16[128,1024]{1,0:T(8,128)(2,1)}, u32[]{:S(2)}) copy-start(bf16[128,1024]{1,0:T(8,128)(2,1)} %copy-done.11) | copy-start | bytes 786436
  119.4 19.1 %collective-permute-start.8 = (bf16[4,64,2048]{2,1,0:T(8,128)(2,1)}, bf16[4,64,2048]{2,1,0:T(8,128)(2,1)}, u32[]{:S(2)}, u32[]{:S(2)}) collective-permute-start(bf16[4,64,2048]{2,1,0:T(8,128)(2,1)} %get-tuple-element.84), channel_id=1, source_target_pairs={{0,4},{4,0},{8,12},{12,8},{16,20},{20,16},{24,28},{28,24},{1,5},{5... | collective-permute-start | bytes 3145736 | tf_op jit(solution)/shard_map/ppermute | solution.py:443
  128.4 26.0 %copy-start.2 = (bf16[256,1024]{1,0:T(8,128)(2,1)S(1)}, bf16[256,1024]{1,0:T(8,128)(2,1)}, u32[]{:S(2)}) copy-start(bf16[256,1024]{1,0:T(8,128)(2,1)} %gate_ref.5) | copy-start | bytes 1572868
  128.4 26.0 %copy-start.4 = (bf16[256,1024]{1,0:T(8,128)(2,1)S(1)}, bf16[256,1024]{1,0:T(8,128)(2,1)}, u32[]{:S(2)}) copy-start(bf16[256,1024]{1,0:T(8,128)(2,1)} %signal_ref.3) | copy-start | bytes 1572868
  133.9 22.6 %collective-permute-start.13 = (bf16[4,64,2048]{2,1,0:T(8,128)(2,1)}, bf16[4,64,2048]{2,1,0:T(8,128)(2,1)}, u32[]{:S(2)}, u32[]{:S(2)}) collective-permute-start(bf16[4,64,2048]{2,1,0:T(8,128)(2,1)} %get-tuple-element.98), channel_id=1, source_target_pairs={{0,4},{4,0},{8,12},{12,8},{16,20},{20,16},{24,28},{28,24},{1,5},{5... | collective-permute-start | bytes 3145736 | tf_op jit(solution)/shard_map/ppermute | solution.py:443
  134.2 20.2 %all-to-all-start.3 = ((bf16[8,32,16,128]{3,2,1,0:T(8,128)(2,1)}), bf16[8,32,16,128]{3,2,1,0:T(8,128)(2,1)S(1)}, u32[]{:S(2)}, u32[]{:S(2)}) async-start(bf16[8,32,16,128]{3,2,1,0:T(8,128)(2,1)} %correlate.1), calls=%async_computation.3 | async-start | bytes 2097152 | tf_op jit(solution)/shard_map/all_to_all | solution.py:413
  142.3 18.3 %collective-permute-start.9 = (bf16[64,2048]{1,0:T(8,128)(2,1)}, bf16[64,2048]{1,0:T(8,128)(2,1)}, u32[]{:S(2)}, u32[]{:S(2)}) collective-permute-start(bf16[64,2048]{1,0:T(8,128)(2,1)} %get-tuple-element.85), channel_id=1, source_target_pairs={{0,24},{4,28},{8,16},{12,20},{16,8},{20,12},{24,0},{28,4},{1,25},{... | collective-permute-start | bytes 786440 | tf_op jit(solution)/shard_map/ppermute | solution.py:448
  145.3 19.5 %collective-permute-start.10 = (bf16[64,2048]{1,0:T(8,128)(2,1)}, bf16[64,2048]{1,0:T(8,128)(2,1)}, u32[]{:S(2)}, u32[]{:S(2)}) collective-permute-start(bf16[64,2048]{1,0:T(8,128)(2,1)} %get-tuple-element.86), channel_id=1, source_target_pairs={{0,8},{4,12},{8,0},{12,4},{16,24},{20,28},{24,16},{28,20},{1,9},{5... | collective-permute-start | bytes 786440 | tf_op jit(solution)/shard_map/ppermute | solution.py:448
  145.8 19.0 %collective-permute-start.11 = (bf16[64,2048]{1,0:T(8,128)(2,1)}, bf16[64,2048]{1,0:T(8,128)(2,1)}, u32[]{:S(2)}, u32[]{:S(2)}) collective-permute-start(bf16[64,2048]{1,0:T(8,128)(2,1)} %get-tuple-element.87), channel_id=1, source_target_pairs={{0,16},{4,20},{8,24},{12,28},{16,0},{20,4},{24,8},{28,12},{1,17},{... | collective-permute-start | bytes 786440 | tf_op jit(solution)/shard_map/ppermute | solution.py:448
  158.5 12.7 %collective-permute-start.14 = (bf16[64,2048]{1,0:T(8,128)(2,1)S(1)}, bf16[64,2048]{1,0:T(8,128)(2,1)S(1)}, u32[]{:S(2)}, u32[]{:S(2)}) collective-permute-start(bf16[64,2048]{1,0:T(8,128)(2,1)S(1)} %get-tuple-element.99), channel_id=1, source_target_pairs={{0,24},{4,28},{8,16},{12,20},{16,8},{20,12},{24,0},{28,4},{1,25},{... | collective-permute-start | bytes 786440 | tf_op jit(solution)/shard_map/ppermute | solution.py:448
  159.1 16.4 %collective-permute-start.15 = (bf16[64,2048]{1,0:T(8,128)(2,1)S(1)}, bf16[64,2048]{1,0:T(8,128)(2,1)S(1)}, u32[]{:S(2)}, u32[]{:S(2)}) collective-permute-start(bf16[64,2048]{1,0:T(8,128)(2,1)S(1)} %get-tuple-element.100), channel_id=1, source_target_pairs={{0,8},{4,12},{8,0},{12,4},{16,24},{20,28},{24,16},{28,20},{1,9},{5... | collective-permute-start | bytes 786440 | tf_op jit(solution)/shard_map/ppermute | solution.py:448
  160.6 14.9 %collective-permute-start.16 = (bf16[64,2048]{1,0:T(8,128)(2,1)S(1)}, bf16[64,2048]{1,0:T(8,128)(2,1)S(1)}, u32[]{:S(2)}, u32[]{:S(2)}) collective-permute-start(bf16[64,2048]{1,0:T(8,128)(2,1)S(1)} %get-tuple-element.101), channel_id=1, source_target_pairs={{0,16},{4,20},{8,24},{12,28},{16,0},{20,4},{24,8},{28,12},{1,17},{... | collective-permute-start | bytes 786440 | tf_op jit(solution)/shard_map/ppermute | solution.py:448
  (24 other events, 42.4 us)

commit v3 on v2

--- a/solution.py
+++ b/solution.py
@@ -20,6 +20,14 @@
 
 def short(x):
     return x.astype(jnp.bfloat16)
+
+
+def held_in_hbm(*arrays):
+    return [pltpu.with_memory_space_constraint(array, pltpu.HBM) for array in arrays]
+
+
+def in_hbm(shape, dtype=jnp.bfloat16):
+    return pltpu.HBM(shape, dtype)
 
 
 def high_low(table, axis):
@@ -142,7 +150,7 @@
     blocks, chans, rows, _ = pairs.shape
     step = min(8, chans)
     outer = blocks * rows // 2
-    spec = jax.ShapeDtypeStruct((chans, outer, 2 * LANES), jnp.float32)
+    spec = in_hbm((chans, outer, 2 * LANES), jnp.float32)
     spec_block = pl.BlockSpec((step, outer, 2 * LANES), lambda i: (i, 0, 0))
     return pl.pallas_call(
         convolve_kernel,
@@ -154,14 +162,14 @@
             spec_block,
             spec_block,
         ],
-        out_shape=[jax.ShapeDtypeStruct((blocks, chans // 2, rows, LANES), jnp.bfloat16), spec, spec],
+        out_shape=[in_hbm((blocks, chans // 2, rows, LANES)), spec, spec],
         scratch_shapes=[
             pltpu.VMEM((2 * step * outer, 2 * LANES), jnp.bfloat16),
             pltpu.VMEM((step * outer, 2 * LANES), jnp.float32),
         ],
         compiler_params=pltpu.CompilerParams(vmem_limit_bytes=VMEM_BYTES),
         name="convolve",
-    )(pairs, *tables)
+    )(*held_in_hbm(pairs, *tables))
 
 
 def correlate(pairs, signal, kernel, tables):
@@ -180,14 +188,14 @@
         ]
         + [whole(table) for table in tables],
         out_specs=pl.BlockSpec((blocks, step, rows, LANES), lambda i: (0, i, 0, 0)),
-        out_shape=jax.ShapeDtypeStruct((blocks, chans, rows, LANES), jnp.bfloat16),
+        out_shape=in_hbm((blocks, chans, rows, LANES)),
         scratch_shapes=[
             pltpu.VMEM((step * outer, 2 * LANES), jnp.bfloat16),
             pltpu.VMEM((2, step * outer, 2 * LANES), jnp.float32),
         ],
         compiler_params=pltpu.CompilerParams(vmem_limit_bytes=VMEM_BYTES),
         name="correlate",
-    )(pairs, signal, kernel, *tables)
+    )(*held_in_hbm(pairs, signal, kernel, *tables))
 
 
 def params():
@@ -217,11 +225,11 @@
         grid=(4,),
         in_specs=[block] * 3,
         out_specs=pl.BlockSpec((step, 2 * per, LANES), lambda i: (i, 0, 0)),
-        out_shape=jax.ShapeDtypeStruct((rows, 2 * per, LANES), jnp.bfloat16),
+        out_shape=in_hbm((rows, 2 * per, LANES)),
         scratch_shapes=[pltpu.VMEM((step * 2 * per, LANES), jnp.float32)],
         compiler_params=params(),
         name="prepare",
-    )(inner_gate, signal, long_filter)
+    )(*held_in_hbm(inner_gate, signal, long_filter))
 
 
 def mix_kernel(conv_ref, gate_ref, *refs):
@@ -251,43 +259,44 @@
         grid=(2,),
         in_specs=[pl.BlockSpec((step * per // 16, 16, LANES), lambda i: (i, 0, 0)), token_rows],
         out_specs=[cut_rows] * CHUNKS + [token_rows],
-        out_shape=[jax.ShapeDtypeStruct((rows // CHUNKS, length), jnp.bfloat16)] * CHUNKS
-        + [jax.ShapeDtypeStruct((rows, length), jnp.bfloat16)],
+        out_shape=[in_hbm((rows // CHUNKS, length))] * CHUNKS + [in_hbm((rows, length))],
         scratch_shapes=[pltpu.VMEM((step * per, LANES), jnp.float32)],
         compiler_params=params(),
         name="mix",
     )(conv, outer_gate)
 
 
-def regard_kernel(*refs):
+def regard_kernel(flag_ref, *refs):
     *share_refs, gate_ref, conv_ref, outer_ref, grad_ref, lines = refs
     per = gate_ref.shape[1] // LANES
     grad_mix = wide(share_refs[0][...])
-    for ref in share_refs[1:]:
+    for ref in share_refs[1:-1]:
         grad_mix = grad_mix + wide(ref[...])
+    last = wide(share_refs[-1][...])
+    grad_mix = grad_mix + jnp.where(flag_ref[0] != 0, last, jnp.zeros_like(last))
     outer_ref[...] = short(grad_mix * wide(conv_ref[...]))
     spread_lanes(lines, grad_mix * wide(gate_ref[...]), 0, per)
     grad_ref[...] = short(lines[...]).reshape(grad_ref.shape)
 
 
-def regard(shares, outer_gate, conv_out):
+def regard(shares, flag, outer_gate, conv_out):
     rows, length = outer_gate.shape
     per = length // LANES
     step = rows // 2
-    block = pl.BlockSpec((step, length), lambda i: (i, 0))
+    block = pl.BlockSpec((step, length), lambda i, at: (i, 0))
     return pl.pallas_call(
         regard_kernel,
-        grid=(2,),
-        in_specs=[block] * (len(shares) + 2),
-        out_specs=[block, pl.BlockSpec((step * per // 16, 16, LANES), lambda i: (i, 0, 0))],
-        out_shape=[
-            jax.ShapeDtypeStruct((rows, length), jnp.bfloat16),
-            jax.ShapeDtypeStruct((rows * per // 16, 16, LANES), jnp.bfloat16),
-        ],
-        scratch_shapes=[pltpu.VMEM((step * per, LANES), jnp.float32)],
+        grid_spec=pltpu.PrefetchScalarGridSpec(
+            num_scalar_prefetch=1,
+            grid=(2,),
+            in_specs=[block] * (len(shares) + 2),
+            out_specs=[block, pl.BlockSpec((step * per // 16, 16, LANES), lambda i, at: (i, 0, 0))],
+            scratch_shapes=[pltpu.VMEM((step * per, LANES), jnp.float32)],
+        ),
+        out_shape=[in_hbm((rows, length)), in_hbm((rows * per // 16, 16, LANES))],
         compiler_params=params(),
         name="regard",
-    )(*shares, outer_gate, conv_out)
+    )(flag.astype(jnp.int32).reshape(1), *held_in_hbm(*shares, outer_gate, conv_out))
 
 
 def finish_kernel(corr_ref, signal_ref, gate_ref, inner_ref, signal_out_ref, filter_ref, lines):
@@ -317,13 +326,21 @@
         scratch_shapes=[pltpu.VMEM((step * 2 * per, LANES), jnp.float32)],
         compiler_params=params(),
         name="finish",
-    )(corr.reshape(rows, 2 * per, LANES), signal, inner_gate)
+    )(*held_in_hbm(corr.reshape(rows, 2 * per, LANES), signal, inner_gate))
 
 
 def unproject_kernel(count, place_ref, *refs):
-    grad_ref = refs[count]
+    rows, width = refs[0].shape
+    grad_ref, weights = refs[count], refs[-1]
+
+    @pl.when(pl.program_id(0) == 0)
+    def _():
+        for row in range(count):
+            weights[pl.ds(row * rows, rows), :] = refs[row][...]
+
+    out = short(mxu(weights[...], grad_ref[...]))
     for row in range(count):
-        refs[count + 1 + row][...] = short(mxu(refs[row][...], grad_ref[...]))
+        refs[count + 1 + row][...] = out[row * rows : (row + 1) * rows]
 
 
 def unproject(out_proj, grad_output, offsets, place, count):
@@ -341,23 +358,31 @@
             grid=(length // step,),
             in_specs=in_specs + [pl.BlockSpec((width, step), lambda i, at: (0, i))],
             out_specs=[pl.BlockSpec((rows, step), lambda i, at: (0, i))] * len(offsets),
+            scratch_shapes=[pltpu.VMEM((len(offsets) * rows, width), jnp.bfloat16)],
         ),
-        out_shape=[jax.ShapeDtypeStruct((rows, length), jnp.bfloat16)] * len(offsets),
+        out_shape=[in_hbm((rows, length))] * len(offsets),
         compiler_params=params(),
         name="unproject",
-    )(place.reshape(1), *[out_proj] * len(offsets), grad_output)
+    )(place.reshape(1), *held_in_hbm(*[out_proj] * len(offsets), grad_output))
 
 
 def project_kernel(core_ref, *refs):
-    *piece_refs, grad_ref, other_ref, mine_ref = refs
-    small = mine_ref.shape[1]
-    for ref, which in ((other_ref, 1 - core_ref[0]), (mine_ref, core_ref[0])):
-        first = pl.multiple_of(which * small, small)
-        rows = jnp.concatenate([piece[pl.ds(first, small), :] for piece in piece_refs], axis=0)
-        out = lax.dot_general(
-            rows, grad_ref[...], (((1,), (1,)), ((), ())), preferred_element_type=jnp.float32
-        )
-        ref[...] = short(out).reshape(ref.shape)
+    *piece_refs, grad_ref, other_ref, mine_ref, rows = refs
+    count, small, _ = mine_ref.shape
+
+    @pl.when(pl.program_id(0) == 0)
+    def _():
+        for place, which in enumerate((1 - core_ref[0], core_ref[0])):
+            first = pl.multiple_of(which * small, small)
+            for slot, piece in enumerate(piece_refs):
+                rows[pl.ds((place * count + slot) * small, small), :] = piece[pl.ds(first, small), :]
+
+    out = lax.dot_general(
+        rows[...], grad_ref[...], (((1,), (1,)), ((), ())), preferred_element_type=jnp.float32
+    )
+    out = short(out).reshape(2, count, small, -1)
+    other_ref[...] = out[0]
+    mine_ref[...] = out[1]
 
 
 def project(pieces, grad_output, core):
@@ -365,7 +390,7 @@
     small = pieces[0].shape[0] // 2
     step = 512
     out_block = pl.BlockSpec((len(pieces), small, step), lambda i, at: (0, 0, i))
-    out = jax.ShapeDtypeStruct((len(pieces), small, width), jnp.bfloat16)
+    out = in_hbm((len(pieces), small, width))
     return pl.pallas_call(
         project_kernel,
         grid_spec=pltpu.PrefetchScalarGridSpec(
@@ -374,11 +399,12 @@
             in_specs=[pl.BlockSpec(pieces[0].shape, lambda i, at: (0, 0))] * len(pieces)
             + [pl.BlockSpec((step, length), lambda i, at: (i, 0))],
             out_specs=[out_block, out_block],
+            scratch_shapes=[pltpu.VMEM((2 * len(pieces) * small, length), jnp.bfloat16)],
         ),
         out_shape=[out, out],
         compiler_params=params(),
         name="project",
-    )(core.reshape(1), *pieces, grad_output)
+    )(core.reshape(1), *held_in_hbm(*pieces, grad_output))
 
 
 def pick_kernel(order_ref, mine_ref, got_ref, *out_refs):
@@ -399,10 +425,10 @@
             in_specs=[block, block],
             out_specs=[pl.BlockSpec((small, step), lambda i, at: (0, i))] * count,
         ),
-        out_shape=[jax.ShapeDtypeStruct((small, width), jnp.bfloat16)] * count,
+        out_shape=[in_hbm((small, width))] * count,
         compiler_params=params(),
         name="pick",
-    )(order, mine, got)
+    )(order, *held_in_hbm(mine, got))
 
 
 def swaps(count, bit):
@@ -437,13 +463,13 @@
     return held
 
 
-def scatter_seq(other, mine):
+def scatter_seq(other, mine, *before):
     count, chips = lax.axis_size("seq"), lax.axis_size("chan")
     line, chip = lax.axis_index("chan"), lax.axis_index("seq") // 2
     got = lax.ppermute(other, "seq", swaps(count, 1))
     bits = sorted(range(1, chips), key=lambda bit: (-bin(bit).count("1"), bit)) + [0]
     order = jnp.stack([lax.rem(line - (chip ^ bit) + chips, chips) for bit in bits])
-    blocks = pick(mine, got, order.astype(jnp.int32))
+    blocks = pick(tie(mine, *before), got, order.astype(jnp.int32))
     return [
         lax.ppermute(block, "seq", swaps(count, 2 * bit)) for block, bit in zip(blocks, bits[:-1])
     ] + [blocks[-1]]
@@ -465,39 +491,40 @@
     core = lax.axis_index("seq") % 2
     tables = [jnp.asarray(t) for t in dft_tables(block_len * seq_count, seq_count)]
 
-    pair = prepare(inner_gate, signal, long_filter).reshape(seq_count, owned, 2 * per, LANES)
-    sent = exchange(pair)
-
-    weights = tie(out_proj, pair)
     if chan_count == 4:
-        far = unproject(weights, grad_output, [2], line, chan_count)[0]
-        near = unproject(tie(weights, far), grad_output, [0, 1, 3], line, chan_count)
+        far = unproject(out_proj, grad_output, [2], line, chan_count)[0]
+        pair = prepare(inner_gate, signal, tie(long_filter, far))
+        pair = pair.reshape(seq_count, owned, 2 * per, LANES)
+        sent = exchange(pair)
+        near = unproject(tie(out_proj, pair), grad_output, [0, 1, 3], line, chan_count)
         far = lax.ppermute(far, "chan", [(2, 0), (1, 3), (3, 2), (0, 1)])
-        sent = tie(sent, *near)
         none = jnp.zeros_like(far)
-        up = shift(short(wide(near[1]) + wide(jnp.where(line == 1, far, none))), 1)
-        down = shift(short(wide(near[2]) + wide(jnp.where(line == 2, far, none))), 3)
-        ends = jnp.where((line == 0) | (line == 3), far, none)
-        shares = [near[0], up, down, ends]
+        rising = short(wide(near[1]) + wide(jnp.where(line == 1, far, none)))
+        falling = short(wide(near[2]) + wide(jnp.where(line == 2, far, none)))
+        sent = tie(sent, rising, falling)
+        up, down = shift(rising, 1), shift(falling, 3)
+        shares, flag = [near[0], up, down, far], (line == 0) | (line == 3)
     else:
-        blocks = unproject(weights, grad_output, list(range(chan_count)), line, chan_count)
+        pair = prepare(inner_gate, signal, long_filter)
+        pair = pair.reshape(seq_count, owned, 2 * per, LANES)
+        sent = exchange(pair)
+        blocks = unproject(out_proj, grad_output, list(range(chan_count)), line, chan_count)
         shares = [blocks[0]] + [shift(block, by) for by, block in enumerate(blocks) if by > 0]
+        flag = line >= 0
 
     conv, spec_signal, spec_filter = convolve(sent, tables)
-    *mixed, conv_out = mix(exchange(conv), outer_gate)
+    *mixed, conv_out = mix(tie(exchange(conv), *shares), outer_gate)
     held = [gather_first(part) for part in mixed]
-    held, shares = lax.optimization_barrier((held, shares))
-
-    grad_outer, grad_conv = regard(shares, outer_gate, conv_out)
+    grad_outer, grad_conv = regard(shares, flag, outer_gate, conv_out)
     grad_conv = grad_conv.reshape(seq_count, owned // 2, 2 * per, LANES)
+    corr = correlate(exchange(grad_conv), spec_signal, spec_filter, tables)
     pieces = [gather_second(part) for part in held]
-    pieces[0] = tie(pieces[0], grad_conv)
-    projs = [scatter_seq(*project(pieces[0], grad_output, core))]
-    corr = correlate(exchange(grad_conv), spec_signal, spec_filter, tables)
-    pieces[1] = tie(pieces[1], corr)
-    projs.append(scatter_seq(*project(pieces[1], grad_output, core)))
-
-    grad_inner, grad_signal, grad_filter = finish(exchange(corr), signal, inner_gate)
+    pieces[0] = tie(pieces[0], corr)
+    partials = [project(part, grad_output, core) for part in pieces]
+    projs = [scatter_seq(*partials[0])]
+    projs.append(scatter_seq(*partials[1], *projs[0][-1:]))
+
+    grad_inner, grad_signal, grad_filter = finish(tie(exchange(corr), projs[1][-1]), signal, inner_gate)
     grad_proj = jnp.concatenate([sum_of(parts) for parts in projs], axis=0)
     return (grad_outer, grad_inner, grad_signal, grad_filter, grad_proj)
 

time: 178 us -> 154 us (0.87)
  local copies, waits for them, and re-layouts: 19.9 us -> 6.11 us
  Pallas kernels: 44.7 us -> 56.8 us
  starting transfers between devices: 51.3 us -> 40.6 us
  waiting for transfers between devices: 53.1 us -> 44.1 us
  other arithmetic: 6.83 us -> 4.12 us
    unnamed x70 -> x36, local copies, waits for them, and re-layouts: 19.9 us -> 6.11 us
    all_to_all x4, waiting for transfers between devices: 18.3 us -> 4.84 us  [exchange(): lax.all_to_all(blocks, 'seq', split_axis=0, concat_axis=0, tiled=True)]
    ppermute x6, starting transfers between devices: 20.6 us -> 11.6 us  [shift(): lax.ppermute(block, 'chan', [(i, (i + by) % count) for i in range(count)])]
    ppermute x1, waiting for transfers between devices: 0.01 us -> 6.16 us  [body(): far = lax.ppermute(far, 'chan', [(2, 0), (1, 3), (3, 2), (0, 1)])]
    ppermute x6, waiting for transfers between devices: 22.7 us -> 19.9 us  [shift(): lax.ppermute(block, 'chan', [(i, (i + by) % count) for i in range(count)])]
    pallas_call x2, Pallas kernels: 10.3 us -> 12.6 us  [unproject(): pl.pallas_call(functools.partial(unproject_kernel, len(offsets)), grid_sp...]
    all_to_all x4, starting transfers between devices: 18.2 us -> 16.1 us  [exchange(): lax.all_to_all(blocks, 'seq', split_axis=0, concat_axis=0, tiled=True)]
    pallas_call x1, Pallas kernels: 2.02 us -> 3.95 us  [prepare(): pl.pallas_call(prepare_kernel, grid=(4,), in_specs=[block] * 3, out_specs...]
  transfers between devices with their start and end apart: 21 -> 21, of which waited for: 8 -> 12; matrix products, arithmetic and copies ran while one was open for 3% -> 2% of each run, Pallas kernels for 24% -> 31%
where the time goes in v3:
time: 154 us; the launch traced here: 153 us
  Pallas kernels  56.8 us (37%)
  waiting for transfers between devices  44.1 us (29%)
  starting transfers between devices  40.6 us (26%)
  local copies, waits for them, and re-layouts  6.11 us (4%)
  other arithmetic  4.12 us (3%)
    ppermute x6, waiting for transfers between devices, shift(): lax.ppermute(block, 'chan', [(i, (i + by) % count) for i in range(count)])  19.9 us
    all_to_all x4, starting transfers between devices, exchange(): lax.all_to_all(blocks, 'seq', split_axis=0, concat_axis=0, tiled=True)  16.1 us
    ppermute x6, waiting for transfers between devices, scatter_seq(): lax.ppermute(block, 'seq', swaps(count, 2 * bit))  13.2 us
    pallas_call x2, Pallas kernels, unproject(): pl.pallas_call(functools.partial(unproject_kernel, len(offsets)), grid_sp...  12.6 us
    pallas_call x2, Pallas kernels, project(): pl.pallas_call(project_kernel, grid_spec=pltpu.PrefetchScalarGridSpec(num...  12.1 us
    ppermute x6, starting transfers between devices, shift(): lax.ppermute(block, 'chan', [(i, (i + by) % count) for i in range(count)])  11.6 us
    pallas_call x1, Pallas kernels, correlate(): pl.pallas_call(correlate_kernel, grid=(chans // step,), in_specs=[pl.Bloc...  7.46 us
    pallas_call x1, Pallas kernels, convolve(): pl.pallas_call(convolve_kernel, grid=(chans // step,), in_specs=[pl.Block...  7.44 us
  transfers between devices with their start and end apart: 21, of which 12 were waited for; matrix products, arithmetic and copies ran while one was open for 2% of the time, Pallas kernels for 31%

profile of v3, /device:TPU:0, one launch (start us, length us, event | category | flops | bytes accessed | tf_op | source)
XLA Modules:
  0.0 152.6 jit_solution(7642074560167659524)
XLA Ops:
  0.6 5.1 %unproject.2 = bf16[256,1024]{1,0:T(8,128)(2,1)} custom-call(s32[1]{0:T(128)} %bitcast.1.place_ref, bf16[1024,2048]{1,0:T(8,128)(2,1)} %refs_2_, bf16[2048,1024]{1,0:T(8,128)(2,1)} %refs_4_.5), custom_call_target="tpu_custom_call" | custom-call | tf_op jit(solution)/shard_map/unproject/pallas_call | solution.py:354
  5.8 4.0 %prepare.1 = bf16[256,16,128]{2,1,0:T(8,128)(2,1)} custom-call(bf16[256,1024]{1,0:T(8,128)(2,1)} %gate_ref.5, bf16[256,1024]{1,0:T(8,128)(2,1)} %signal_ref.3, bf16[256,1024]{1,0:T(8,128)(2,1)} %filter_ref), custom_call_target="tpu_custom_call" | custom-call | tf_op jit(solution)/shard_map/prepare/pallas_call | solution.py:223
  9.7 5.2 %all-to-all-start = ((bf16[8,32,16,128]{3,2,1,0:T(8,128)(2,1)}), bf16[8,32,16,128]{3,2,1,0:T(8,128)(2,1)S(1)}, u32[]{:S(2)}, u32[]{:S(2)}) async-start(bf16[8,32,16,128]{3,2,1,0:T(8,128)(2,1)} %bitcast.13), calls=%async_computation | async-start | bytes 2097152 | tf_op jit(solution)/shard_map/all_to_all | solution.py:439
  14.9 1.6 %collective-permute-start = (bf16[256,1024]{1,0:T(8,128)(2,1)S(1)}, bf16[256,1024]{1,0:T(8,128)(2,1)S(1)}, u32[]{:S(2)}, u32[]{:S(2)}) collective-permute-start(bf16[256,1024]{1,0:T(8,128)(2,1)S(1)} %copy-done.13), channel_id=1, source_target_pairs={{2,0},{1,3},{3,2},{0,1},{6,4},{5,7},{7,6},{4,5},{10,8},{9,11},{11,... | collective-permute-start | bytes 1572872 | tf_op jit(solution)/shard_map/ppermute | solution.py:500
  16.5 7.4 %unproject.3 = (bf16[256,1024]{1,0:T(8,128)(2,1)}, bf16[256,1024]{1,0:T(8,128)(2,1)}, bf16[256,1024]{1,0:T(8,128)(2,1)}) custom-call(s32[1]{0:T(128)} %bitcast.1.place_ref, bf16[1024,2048]{1,0:T(8,128)(2,1)} %refs_2_, bf16[1024,2048]{1,0:T(8,128)(2,1)} %refs_2_, bf16[1024,2048]{1,0:T(8,128)(2,1)} %refs_2_, bf16[2048,1024]{1,0:T(8,128)(2,1)} %refs_4_.5), custom_call_target="tpu_custom_call" | custom-call | tf_op jit(solution)/shard_map/unproject/pallas_call | solution.py:354
  24.0 6.2 %collective-permute-done.refs_3_ = bf16[256,1024]{1,0:T(8,128)(2,1)S(1)} collective-permute-done((bf16[256,1024]{1,0:T(8,128)(2,1)S(1)}, bf16[256,1024]{1,0:T(8,128)(2,1)S(1)}, u32[]{:S(2)}, u32[]{:S(2)}) %collective-permute-start) | collective-permute-done | bytes 524320 | tf_op jit(solution)/shard_map/ppermute | solution.py:500
  30.1 1.7 %add_convert_fusion = (bf16[256,1024]{1,0:T(8,128)(2,1)S(1)}, bf16[256,1024]{1,0:T(8,128)(2,1)S(1)}) fusion(bf16[256,1024]{1,0:T(8,128)(2,1)} %get-tuple-element.45, bf16[256,1024]{1,0:T(8,128)(2,1)S(1)} %collective-permute-done.refs_3_, pred[]{:T(512)S(6)} %eq.17, pred[]{:T(512)S(6)} %eq.16, bf16[256,1024]{1,0:T(8,128)(2,1)} %get-tuple-element.44), kind=kLoop, calls=%fused_computation.1 | loop fusion | flops 2621440 | bytes 2621442 | tf_op jit(solution)/shard_map/convert_element_type | solution.py:22
  32.7 3.0 %collective-permute-start.2 = (bf16[256,1024]{1,0:T(8,128)(2,1)S(1)}, bf16[256,1024]{1,0:T(8,128)(2,1)}, u32[]{:S(2)}, u32[]{:S(2)}) collective-permute-start(bf16[256,1024]{1,0:T(8,128)(2,1)S(1)} %get-tuple-element.77), channel_id=1, source_target_pairs={{0,3},{1,0},{2,1},{3,2},{4,7},{5,4},{6,5},{7,6},{8,11},{9,8},{10,9... | collective-permute-start | bytes 1572872 | tf_op jit(solution)/shard_map/ppermute | solution.py:448
  36.7 7.4 %convolve.1 = (bf16[8,16,16,128]{3,2,1,0:T(8,128)(2,1)}, f32[32,64,256]{2,1,0:T(8,128)}, f32[32,64,256]{2,1,0:T(8,128)}) custom-call(bf16[8,32,16,128]{3,2,1,0:T(8,128)(2,1)} %copy-done.2, bf16[256,256]{1,0:T(8,128)(2,1)} %constant.61.clone.first_ref, bf16[512,256]{1,0:T(8,128)(2,1)} %constant.62.clone.forward_ref, ...), custom_call_target="tpu_custom_call" | custom-call | tf_op jit(solution)/shard_map/convolve/pallas_call | solution.py:155
  44.2 3.8 %all-to-all-start.1 = ((bf16[8,16,16,128]{3,2,1,0:T(8,128)(2,1)}), bf16[8,16,16,128]{3,2,1,0:T(8,128)(2,1)S(1)}, u32[]{:S(2)}, u32[]{:S(2)}) async-start(bf16[8,16,16,128]{3,2,1,0:T(8,128)(2,1)} %get-tuple-element.47), calls=%async_computation.1 | async-start | bytes 1048576 | tf_op jit(solution)/shard_map/all_to_all | solution.py:439
  48.7 8.6 %collective-permute-done.2.refs_2_ = bf16[256,1024]{1,0:T(8,128)(2,1)} collective-permute-done((bf16[256,1024]{1,0:T(8,128)(2,1)S(1)}, bf16[256,1024]{1,0:T(8,128)(2,1)}, u32[]{:S(2)}, u32[]{:S(2)}) %collective-permute-start.2) | collective-permute-done | bytes 524320 | tf_op jit(solution)/shard_map/ppermute | solution.py:448
  60.4 2.4 %collective-permute-start.7 = (bf16[128,1024]{1,0:T(8,128)(2,1)}, bf16[128,1024]{1,0:T(8,128)(2,1)S(1)}, u32[]{:S(2)}, u32[]{:S(2)}) collective-permute-start(bf16[128,1024]{1,0:T(8,128)(2,1)} %get-tuple-element.57.refs_0_), channel_id=1, source_target_pairs={{0,3},{1,0},{2,1},{3,2},{4,7},{5,4},{6,5},{7,6},{8,11},{9,8},{10,9... | collective-permute-start | bytes 786440 | tf_op jit(solution)/shard_map/ppermute | solution.py:448
  62.8 3.8 %collective-permute-start.4 = (bf16[128,1024]{1,0:T(8,128)(2,1)}, bf16[128,1024]{1,0:T(8,128)(2,1)S(1)}, u32[]{:S(2)}, u32[]{:S(2)}) collective-permute-start(bf16[128,1024]{1,0:T(8,128)(2,1)} %get-tuple-element.54.refs_0_), channel_id=1, source_target_pairs={{0,3},{1,0},{2,1},{3,2},{4,7},{5,4},{6,5},{7,6},{8,11},{9,8},{10,9... | collective-permute-start | bytes 786440 | tf_op jit(solution)/shard_map/ppermute | solution.py:448
  66.6 3.0 %regard.1 = (bf16[256,1024]{1,0:T(8,128)(2,1)}, bf16[128,16,128]{2,1,0:T(8,128)(2,1)}) custom-call(s32[1]{0:T(128)} %bitcast.flag_ref, bf16[256,1024]{1,0:T(8,128)(2,1)} %get-tuple-element.43.refs_0_, bf16[256,1024]{1,0:T(8,128)(2,1)} %collective-permute-done.1.refs_1_, bf16[256,1024]{1,0:T(8,128)(2,1)} %collective-permute-done.2.refs_2_, ...), custom_call_target="tpu_custom_call" | custom-call | tf_op jit(solution)/shard_map/regard/pallas_call | solution.py:287
  69.6 3.5 %all-to-all-start.2 = ((bf16[8,16,16,128]{3,2,1,0:T(8,128)(2,1)}), bf16[8,16,16,128]{3,2,1,0:T(8,128)(2,1)S(1)}, u32[]{:S(2)}, u32[]{:S(2)}) async-start(bf16[8,16,16,128]{3,2,1,0:T(8,128)(2,1)} %bitcast.14), calls=%async_computation.2 | async-start | bytes 1048576 | tf_op jit(solution)/shard_map/all_to_all | solution.py:439
  73.1 2.8 %collective-permute-done.7.refs_3_ = bf16[128,1024]{1,0:T(8,128)(2,1)S(1)} collective-permute-done((bf16[128,1024]{1,0:T(8,128)(2,1)}, bf16[128,1024]{1,0:T(8,128)(2,1)S(1)}, u32[]{:S(2)}, u32[]{:S(2)}) %collective-permute-start.7) | collective-permute-done | bytes 262176 | tf_op jit(solution)/shard_map/ppermute | solution.py:448
  76.5 5.0 %collective-permute-done.3.refs_1_ = bf16[128,1024]{1,0:T(8,128)(2,1)S(1)} collective-permute-done((bf16[128,1024]{1,0:T(8,128)(2,1)}, bf16[128,1024]{1,0:T(8,128)(2,1)S(1)}, u32[]{:S(2)}, u32[]{:S(2)}) %collective-permute-start.3) | collective-permute-done | bytes 262176 | tf_op jit(solution)/shard_map/ppermute | solution.py:448
  81.4 2.9 %collective-permute-done.4.refs_3_ = bf16[128,1024]{1,0:T(8,128)(2,1)S(1)} collective-permute-done((bf16[128,1024]{1,0:T(8,128)(2,1)}, bf16[128,1024]{1,0:T(8,128)(2,1)S(1)}, u32[]{:S(2)}, u32[]{:S(2)}) %collective-permute-start.4) | collective-permute-done | bytes 262176 | tf_op jit(solution)/shard_map/ppermute | solution.py:448
  84.4 3.3 %collective-permute-start.5 = (bf16[128,1024]{1,0:T(8,128)(2,1)S(1)}, bf16[128,1024]{1,0:T(8,128)(2,1)S(1)}, u32[]{:S(2)}, u32[]{:S(2)}) collective-permute-start(bf16[128,1024]{1,0:T(8,128)(2,1)S(1)} %select_select_fusion.1), channel_id=1, source_target_pairs={{0,2},{3,1},{2,3},{1,0},{4,6},{7,5},{6,7},{5,4},{8,10},{11,9},{10,... | collective-permute-start | bytes 786440 | tf_op jit(solution)/shard_map/ppermute | solution.py:462
  88.4 7.5 %correlate.1 = bf16[8,32,16,128]{3,2,1,0:T(8,128)(2,1)} custom-call(bf16[8,16,16,128]{3,2,1,0:T(8,128)(2,1)} %copy-done.3, f32[32,64,256]{2,1,0:T(8,128)} %get-tuple-element.52.signal_ref, f32[32,64,256]{2,1,0:T(8,128)} %get-tuple-element.53.filter_ref, bf16[256,256]{1,0:T(8,128)(2,1)} %constant.61.clone.first_ref, ...), custom_call_target="tpu_custom_call" | custom-call | tf_op jit(solution)/shard_map/correlate/pallas_call | solution.py:181
  96.6 6.0 %project.3 = (bf16[4,64,2048]{2,1,0:T(8,128)(2,1)}, bf16[4,64,2048]{2,1,0:T(8,128)(2,1)}) custom-call(s32[1]{0:T(128)} %bitcast.9.core_ref, bf16[128,1024]{1,0:T(8,128)(2,1)} %get-tuple-element.57.refs_0_, bf16[128,1024]{1,0:T(8,128)(2,1)} %copy-done.11, bf16[128,1024]{1,0:T(8,128)(2,1)} %copy-done.16, bf16[128,1024]{1,0:T(8,128)(2,1)} %copy-done.12, ...), custom_call_target="tpu_custom_call" | custom-call | tf_op jit(solution)/shard_map/project/pallas_call | solution.py:394
  103.5 6.0 %project.2 = (bf16[4,64,2048]{2,1,0:T(8,128)(2,1)}, bf16[4,64,2048]{2,1,0:T(8,128)(2,1)}) custom-call(s32[1]{0:T(128)} %bitcast.9.core_ref, bf16[128,1024]{1,0:T(8,128)(2,1)} %get-tuple-element.54.refs_0_, bf16[128,1024]{1,0:T(8,128)(2,1)} %copy-done.8, bf16[128,1024]{1,0:T(8,128)(2,1)} %copy-done.15, bf16[128,1024]{1,0:T(8,128)(2,1)} %copy-done.10, ...), custom_call_target="tpu_custom_call" | custom-call | tf_op jit(solution)/shard_map/project/pallas_call | solution.py:394
  110.0 3.6 %all-to-all-start.3 = ((bf16[8,32,16,128]{3,2,1,0:T(8,128)(2,1)}), bf16[8,32,16,128]{3,2,1,0:T(8,128)(2,1)S(1)}, u32[]{:S(2)}, u32[]{:S(2)}) async-start(bf16[8,32,16,128]{3,2,1,0:T(8,128)(2,1)} %correlate.1), calls=%async_computation.3 | async-start | bytes 2097152 | tf_op jit(solution)/shard_map/all_to_all | solution.py:439
  114.7 3.0 %pick.2 = (bf16[64,2048]{1,0:T(8,128)(2,1)}, bf16[64,2048]{1,0:T(8,128)(2,1)}, bf16[64,2048]{1,0:T(8,128)(2,1)}, bf16[64,2048]{1,0:T(8,128)(2,1)}) custom-call(s32[4]{0:T(128)S(1)} %pad_add_fusion.order_ref, bf16[4,64,2048]{2,1,0:T(8,128)(2,1)} %get-tuple-element.61.mine_ref, bf16[4,64,2048]{2,1,0:T(8,128)(2,1)} %copy-done.5), custom_call_target="tpu_custom_call" | custom-call | tf_op jit(solution)/shard_map/pick/pallas_call | solution.py:420
  118.6 2.9 %pick.3 = (bf16[64,2048]{1,0:T(8,128)(2,1)}, bf16[64,2048]{1,0:T(8,128)(2,1)}, bf16[64,2048]{1,0:T(8,128)(2,1)}, bf16[64,2048]{1,0:T(8,128)(2,1)}) custom-call(s32[4]{0:T(128)S(1)} %pad_add_fusion.order_ref, bf16[4,64,2048]{2,1,0:T(8,128)(2,1)} %get-tuple-element.64.mine_ref, bf16[4,64,2048]{2,1,0:T(8,128)(2,1)} %copy-done.6), custom_call_target="tpu_custom_call" | custom-call | tf_op jit(solution)/shard_map/pick/pallas_call | solution.py:420
  121.6 1.9 %collective-permute-start.16 = (bf16[64,2048]{1,0:T(8,128)(2,1)}, bf16[64,2048]{1,0:T(8,128)(2,1)S(1)}, u32[]{:S(2)}, u32[]{:S(2)}) collective-permute-start(bf16[64,2048]{1,0:T(8,128)(2,1)} %get-tuple-element.76), channel_id=1, source_target_pairs={{0,16},{4,20},{8,24},{12,28},{16,0},{20,4},{24,8},{28,12},{1,17},{... | collective-permute-start | bytes 786440 | tf_op jit(solution)/shard_map/ppermute | solution.py:474
  125.1 4.4 %all-to-all-done.3 = bf16[8,32,16,128]{3,2,1,0:T(8,128)(2,1)S(1)} async-done(((bf16[8,32,16,128]{3,2,1,0:T(8,128)(2,1)}), bf16[8,32,16,128]{3,2,1,0:T(8,128)(2,1)S(1)}, u32[]{:S(2)}, u32[]{:S(2)}) %all-to-all-start.3) | async-done | bytes 1048608 | tf_op jit(solution)/shard_map/all_to_all | solution.py:439
  130.4 3.3 %finish.1 = (bf16[256,1024]{1,0:T(8,128)(2,1)}, bf16[256,1024]{1,0:T(8,128)(2,1)}, f32[256,1024]{1,0:T(8,128)}) custom-call(bf16[256,16,128]{2,1,0:T(8,128)(2,1)} %bitcast.12, bf16[256,1024]{1,0:T(8,128)(2,1)} %signal_ref.3, bf16[256,1024]{1,0:T(8,128)(2,1)} %gate_ref.5), custom_call_target="tpu_custom_call" | custom-call | tf_op jit(solution)/shard_map/finish/pallas_call | solution.py:319
  134.8 2.4 %collective-permute-start.11 = (bf16[64,2048]{1,0:T(8,128)(2,1)S(1)}, bf16[64,2048]{1,0:T(8,128)(2,1)S(1)}, u32[]{:S(2)}, u32[]{:S(2)}) collective-permute-start(bf16[64,2048]{1,0:T(8,128)(2,1)S(1)} %copy-done.17), channel_id=1, source_target_pairs={{0,24},{4,28},{8,16},{12,20},{16,8},{20,12},{24,0},{28,4},{1,25},{... | collective-permute-start | bytes 786440 | tf_op jit(solution)/shard_map/ppermute | solution.py:474
  137.2 3.5 %collective-permute-done.14 = bf16[64,2048]{1,0:T(8,128)(2,1)S(1)} collective-permute-done((bf16[64,2048]{1,0:T(8,128)(2,1)}, bf16[64,2048]{1,0:T(8,128)(2,1)S(1)}, u32[]{:S(2)}, u32[]{:S(2)}) %collective-permute-start.14) | collective-permute-done | bytes 262176 | tf_op jit(solution)/shard_map/ppermute | solution.py:474
  141.8 3.0 %collective-permute-done.13 = bf16[64,2048]{1,0:T(8,128)(2,1)S(1)} collective-permute-done((bf16[64,2048]{1,0:T(8,128)(2,1)}, bf16[64,2048]{1,0:T(8,128)(2,1)S(1)}, u32[]{:S(2)}, u32[]{:S(2)}) %collective-permute-start.13) | collective-permute-done | bytes 262176 | tf_op jit(solution)/shard_map/ppermute | solution.py:474
  145.4 6.1 %collective-permute-done.11 = bf16[64,2048]{1,0:T(8,128)(2,1)S(1)} collective-permute-done((bf16[64,2048]{1,0:T(8,128)(2,1)S(1)}, bf16[64,2048]{1,0:T(8,128)(2,1)S(1)}, u32[]{:S(2)}, u32[]{:S(2)}) %collective-permute-start.11) | collective-permute-done | bytes 262176 | tf_op jit(solution)/shard_map/ppermute | solution.py:474
  (65 shorter events, 17.6 us)
Async XLA Ops:
  5.8 9.1 %copy-start.13 = (bf16[256,1024]{1,0:T(8,128)(2,1)S(1)}, bf16[256,1024]{1,0:T(8,128)(2,1)}, u32[]{:S(2)}) copy-start(bf16[256,1024]{1,0:T(8,128)(2,1)} %unproject.2) | copy-start | bytes 1572868
  9.7 26.0 %all-to-all-start = ((bf16[8,32,16,128]{3,2,1,0:T(8,128)(2,1)}), bf16[8,32,16,128]{3,2,1,0:T(8,128)(2,1)S(1)}, u32[]{:S(2)}, u32[]{:S(2)}) async-start(bf16[8,32,16,128]{3,2,1,0:T(8,128)(2,1)} %bitcast.13), calls=%async_computation | async-start | bytes 2097152 | tf_op jit(solution)/shard_map/all_to_all | solution.py:439
  14.9 15.2 %collective-permute-start = (bf16[256,1024]{1,0:T(8,128)(2,1)S(1)}, bf16[256,1024]{1,0:T(8,128)(2,1)S(1)}, u32[]{:S(2)}, u32[]{:S(2)}) collective-permute-start(bf16[256,1024]{1,0:T(8,128)(2,1)S(1)} %copy-done.13), channel_id=1, source_target_pairs={{2,0},{1,3},{3,2},{0,1},{6,4},{5,7},{7,6},{4,5},{10,8},{9,11},{11,... | collective-permute-start | bytes 1572872 | tf_op jit(solution)/shard_map/ppermute | solution.py:500
  24.0 33.8 %copy-start = (bf16[256,1024]{1,0:T(8,128)(2,1)S(1)}, bf16[256,1024]{1,0:T(8,128)(2,1)}, u32[]{:S(2)}) copy-start(bf16[256,1024]{1,0:T(8,128)(2,1)} %refs_4_.3) | copy-start | bytes 1572868
  30.1 36.5 %copy-start.4 = (bf16[256,1024]{1,0:T(8,128)(2,1)}, bf16[256,1024]{1,0:T(8,128)(2,1)S(1)}, u32[]{:S(2)}) copy-start(bf16[256,1024]{1,0:T(8,128)(2,1)S(1)} %collective-permute-done.refs_3_) | copy-start | bytes 1572868
  31.9 16.8 %collective-permute-start.1 = (bf16[256,1024]{1,0:T(8,128)(2,1)S(1)}, bf16[256,1024]{1,0:T(8,128)(2,1)}, u32[]{:S(2)}, u32[]{:S(2)}) collective-permute-start(bf16[256,1024]{1,0:T(8,128)(2,1)S(1)} %get-tuple-element.78), channel_id=1, source_target_pairs={{0,1},{1,2},{2,3},{3,0},{4,5},{5,6},{6,7},{7,4},{8,9},{9,10},{10,1... | collective-permute-start | bytes 1572872 | tf_op jit(solution)/shard_map/ppermute | solution.py:448
  32.7 24.6 %collective-permute-start.2 = (bf16[256,1024]{1,0:T(8,128)(2,1)S(1)}, bf16[256,1024]{1,0:T(8,128)(2,1)}, u32[]{:S(2)}, u32[]{:S(2)}) collective-permute-start(bf16[256,1024]{1,0:T(8,128)(2,1)S(1)} %get-tuple-element.77), channel_id=1, source_target_pairs={{0,3},{1,0},{2,1},{3,2},{4,7},{5,4},{6,5},{7,6},{8,11},{9,8},{10,9... | collective-permute-start | bytes 1572872 | tf_op jit(solution)/shard_map/ppermute | solution.py:448
  44.2 13.6 %all-to-all-start.1 = ((bf16[8,16,16,128]{3,2,1,0:T(8,128)(2,1)}), bf16[8,16,16,128]{3,2,1,0:T(8,128)(2,1)S(1)}, u32[]{:S(2)}, u32[]{:S(2)}) async-start(bf16[8,16,16,128]{3,2,1,0:T(8,128)(2,1)} %get-tuple-element.47), calls=%async_computation.1 | async-start | bytes 1048576 | tf_op jit(solution)/shard_map/all_to_all | solution.py:439
  58.9 17.0 %copy-start.9 = (bf16[128,1024]{1,0:T(8,128)(2,1)S(1)}, bf16[128,1024]{1,0:T(8,128)(2,1)}, u32[]{:S(2)}) copy-start(bf16[128,1024]{1,0:T(8,128)(2,1)} %get-tuple-element.57.refs_0_) | copy-start | bytes 786436
  58.9 25.4 %copy-start.7 = (bf16[128,1024]{1,0:T(8,128)(2,1)S(1)}, bf16[128,1024]{1,0:T(8,128)(2,1)}, u32[]{:S(2)}) copy-start(bf16[128,1024]{1,0:T(8,128)(2,1)} %get-tuple-element.54.refs_0_) | copy-start | bytes 786436
  58.9 14.2 %collective-permute-start.6 = (bf16[128,1024]{1,0:T(8,128)(2,1)}, bf16[128,1024]{1,0:T(8,128)(2,1)S(1)}, u32[]{:S(2)}, u32[]{:S(2)}) collective-permute-start(bf16[128,1024]{1,0:T(8,128)(2,1)} %get-tuple-element.57.refs_0_), channel_id=1, source_target_pairs={{0,1},{1,2},{2,3},{3,0},{4,5},{5,6},{6,7},{7,4},{8,9},{9,10},{10,1... | collective-permute-start | bytes 786440 | tf_op jit(solution)/shard_map/ppermute | solution.py:448
  60.4 15.5 %collective-permute-start.7 = (bf16[128,1024]{1,0:T(8,128)(2,1)}, bf16[128,1024]{1,0:T(8,128)(2,1)S(1)}, u32[]{:S(2)}, u32[]{:S(2)}) collective-permute-start(bf16[128,1024]{1,0:T(8,128)(2,1)} %get-tuple-element.57.refs_0_), channel_id=1, source_target_pairs={{0,3},{1,0},{2,1},{3,2},{4,7},{5,4},{6,5},{7,6},{8,11},{9,8},{10,9... | collective-permute-start | bytes 786440 | tf_op jit(solution)/shard_map/ppermute | solution.py:448
  62.8 18.7 %collective-permute-start.3 = (bf16[128,1024]{1,0:T(8,128)(2,1)}, bf16[128,1024]{1,0:T(8,128)(2,1)S(1)}, u32[]{:S(2)}, u32[]{:S(2)}) collective-permute-start(bf16[128,1024]{1,0:T(8,128)(2,1)} %get-tuple-element.54.refs_0_), channel_id=1, source_target_pairs={{0,1},{1,2},{2,3},{3,0},{4,5},{5,6},{6,7},{7,4},{8,9},{9,10},{10,1... | collective-permute-start | bytes 786440 | tf_op jit(solution)/shard_map/ppermute | solution.py:448
  62.8 21.5 %collective-permute-start.4 = (bf16[128,1024]{1,0:T(8,128)(2,1)}, bf16[128,1024]{1,0:T(8,128)(2,1)S(1)}, u32[]{:S(2)}, u32[]{:S(2)}) collective-permute-start(bf16[128,1024]{1,0:T(8,128)(2,1)} %get-tuple-element.54.refs_0_), channel_id=1, source_target_pairs={{0,3},{1,0},{2,1},{3,2},{4,7},{5,4},{6,5},{7,6},{8,11},{9,8},{10,9... | collective-permute-start | bytes 786440 | tf_op jit(solution)/shard_map/ppermute | solution.py:448
  69.6 18.1 %all-to-all-start.2 = ((bf16[8,16,16,128]{3,2,1,0:T(8,128)(2,1)}), bf16[8,16,16,128]{3,2,1,0:T(8,128)(2,1)S(1)}, u32[]{:S(2)}, u32[]{:S(2)}) async-start(bf16[8,16,16,128]{3,2,1,0:T(8,128)(2,1)} %bitcast.14), calls=%async_computation.2 | async-start | bytes 1048576 | tf_op jit(solution)/shard_map/all_to_all | solution.py:439
  73.1 22.8 %copy-start.11 = (bf16[128,1024]{1,0:T(8,128)(2,1)}, bf16[128,1024]{1,0:T(8,128)(2,1)S(1)}, u32[]{:S(2)}) copy-start(bf16[128,1024]{1,0:T(8,128)(2,1)S(1)} %collective-permute-done.6.refs_1_) | copy-start | bytes 786436
  75.9 20.0 %copy-start.12 = (bf16[128,1024]{1,0:T(8,128)(2,1)}, bf16[128,1024]{1,0:T(8,128)(2,1)S(1)}, u32[]{:S(2)}) copy-start(bf16[128,1024]{1,0:T(8,128)(2,1)S(1)} %collective-permute-done.7.refs_3_) | copy-start | bytes 786436
  76.0 20.0 %collective-permute-start.8 = (bf16[128,1024]{1,0:T(8,128)(2,1)S(1)}, bf16[128,1024]{1,0:T(8,128)(2,1)S(1)}, u32[]{:S(2)}, u32[]{:S(2)}) collective-permute-start(bf16[128,1024]{1,0:T(8,128)(2,1)S(1)} %select_select_fusion), channel_id=1, source_target_pairs={{0,2},{3,1},{2,3},{1,0},{4,6},{7,5},{6,7},{5,4},{8,10},{11,9},{10,... | collective-permute-start | bytes 786440 | tf_op jit(solution)/shard_map/ppermute | solution.py:462
  81.4 21.2 %copy-start.8 = (bf16[128,1024]{1,0:T(8,128)(2,1)}, bf16[128,1024]{1,0:T(8,128)(2,1)S(1)}, u32[]{:S(2)}) copy-start(bf16[128,1024]{1,0:T(8,128)(2,1)S(1)} %collective-permute-done.3.refs_1_) | copy-start | bytes 786436
  84.3 18.4 %copy-start.10 = (bf16[128,1024]{1,0:T(8,128)(2,1)}, bf16[128,1024]{1,0:T(8,128)(2,1)S(1)}, u32[]{:S(2)}) copy-start(bf16[128,1024]{1,0:T(8,128)(2,1)S(1)} %collective-permute-done.4.refs_3_) | copy-start | bytes 786436
  84.4 18.4 %collective-permute-start.5 = (bf16[128,1024]{1,0:T(8,128)(2,1)S(1)}, bf16[128,1024]{1,0:T(8,128)(2,1)S(1)}, u32[]{:S(2)}, u32[]{:S(2)}) collective-permute-start(bf16[128,1024]{1,0:T(8,128)(2,1)S(1)} %select_select_fusion.1), channel_id=1, source_target_pairs={{0,2},{3,1},{2,3},{1,0},{4,6},{7,5},{6,7},{5,4},{8,10},{11,9},{10,... | collective-permute-start | bytes 786440 | tf_op jit(solution)/shard_map/ppermute | solution.py:462
  102.7 11.0 %collective-permute-start.9 = (bf16[4,64,2048]{2,1,0:T(8,128)(2,1)}, bf16[4,64,2048]{2,1,0:T(8,128)(2,1)S(1)}, u32[]{:S(2)}, u32[]{:S(2)}) collective-permute-start(bf16[4,64,2048]{2,1,0:T(8,128)(2,1)} %get-tuple-element.62), channel_id=1, source_target_pairs={{0,4},{4,0},{8,12},{12,8},{16,20},{20,16},{24,28},{28,24},{1,5},{5... | collective-permute-start | bytes 3145736 | tf_op jit(solution)/shard_map/ppermute | solution.py:469
  109.5 8.1 %collective-permute-start.10 = (bf16[4,64,2048]{2,1,0:T(8,128)(2,1)}, bf16[4,64,2048]{2,1,0:T(8,128)(2,1)S(1)}, u32[]{:S(2)}, u32[]{:S(2)}) collective-permute-start(bf16[4,64,2048]{2,1,0:T(8,128)(2,1)} %get-tuple-element.65), channel_id=1, source_target_pairs={{0,4},{4,0},{8,12},{12,8},{16,20},{20,16},{24,28},{28,24},{1,5},{5... | collective-permute-start | bytes 3145736 | tf_op jit(solution)/shard_map/ppermute | solution.py:469
  110.0 19.4 %all-to-all-start.3 = ((bf16[8,32,16,128]{3,2,1,0:T(8,128)(2,1)}), bf16[8,32,16,128]{3,2,1,0:T(8,128)(2,1)S(1)}, u32[]{:S(2)}, u32[]{:S(2)}) async-start(bf16[8,32,16,128]{3,2,1,0:T(8,128)(2,1)} %correlate.1), calls=%async_computation.3 | async-start | bytes 2097152 | tf_op jit(solution)/shard_map/all_to_all | solution.py:439
  117.6 17.2 %copy-start.17 = (bf16[64,2048]{1,0:T(8,128)(2,1)S(1)}, bf16[64,2048]{1,0:T(8,128)(2,1)}, u32[]{:S(2)}) copy-start(bf16[64,2048]{1,0:T(8,128)(2,1)} %get-tuple-element.71) | copy-start | bytes 786436
  117.6 33.8 %copy-start.14 = (bf16[64,2048]{1,0:T(8,128)(2,1)S(1)}, bf16[64,2048]{1,0:T(8,128)(2,1)}, u32[]{:S(2)}) copy-start(bf16[64,2048]{1,0:T(8,128)(2,1)} %get-tuple-element.63) | copy-start | bytes 786436
  121.6 13.2 %collective-permute-start.16 = (bf16[64,2048]{1,0:T(8,128)(2,1)}, bf16[64,2048]{1,0:T(8,128)(2,1)S(1)}, u32[]{:S(2)}, u32[]{:S(2)}) collective-permute-start(bf16[64,2048]{1,0:T(8,128)(2,1)} %get-tuple-element.76), channel_id=1, source_target_pairs={{0,16},{4,20},{8,24},{12,28},{16,0},{20,4},{24,8},{28,12},{1,17},{... | collective-permute-start | bytes 786440 | tf_op jit(solution)/shard_map/ppermute | solution.py:474
  123.5 13.7 %collective-permute-start.15 = (bf16[64,2048]{1,0:T(8,128)(2,1)}, bf16[64,2048]{1,0:T(8,128)(2,1)S(1)}, u32[]{:S(2)}, u32[]{:S(2)}) collective-permute-start(bf16[64,2048]{1,0:T(8,128)(2,1)} %get-tuple-element.75), channel_id=1, source_target_pairs={{0,8},{4,12},{8,0},{12,4},{16,24},{20,28},{24,16},{28,20},{1,9},{5... | collective-permute-start | bytes 786440 | tf_op jit(solution)/shard_map/ppermute | solution.py:474
  124.9 15.8 %collective-permute-start.14 = (bf16[64,2048]{1,0:T(8,128)(2,1)}, bf16[64,2048]{1,0:T(8,128)(2,1)S(1)}, u32[]{:S(2)}, u32[]{:S(2)}) collective-permute-start(bf16[64,2048]{1,0:T(8,128)(2,1)} %get-tuple-element.74), channel_id=1, source_target_pairs={{0,24},{4,28},{8,16},{12,20},{16,8},{20,12},{24,0},{28,4},{1,25},{... | collective-permute-start | bytes 786440 | tf_op jit(solution)/shard_map/ppermute | solution.py:474
  133.7 11.1 %collective-permute-start.13 = (bf16[64,2048]{1,0:T(8,128)(2,1)}, bf16[64,2048]{1,0:T(8,128)(2,1)S(1)}, u32[]{:S(2)}, u32[]{:S(2)}) collective-permute-start(bf16[64,2048]{1,0:T(8,128)(2,1)} %get-tuple-element.73), channel_id=1, source_target_pairs={{0,16},{4,20},{8,24},{12,28},{16,0},{20,4},{24,8},{28,12},{1,17},{... | collective-permute-start | bytes 786440 | tf_op jit(solution)/shard_map/ppermute | solution.py:474
  134.2 11.2 %collective-permute-start.12 = (bf16[64,2048]{1,0:T(8,128)(2,1)}, bf16[64,2048]{1,0:T(8,128)(2,1)S(1)}, u32[]{:S(2)}, u32[]{:S(2)}) collective-permute-start(bf16[64,2048]{1,0:T(8,128)(2,1)} %get-tuple-element.72), channel_id=1, source_target_pairs={{0,8},{4,12},{8,0},{12,4},{16,24},{20,28},{24,16},{28,20},{1,9},{5... | collective-permute-start | bytes 786440 | tf_op jit(solution)/shard_map/ppermute | solution.py:474
  134.8 16.6 %collective-permute-start.11 = (bf16[64,2048]{1,0:T(8,128)(2,1)S(1)}, bf16[64,2048]{1,0:T(8,128)(2,1)S(1)}, u32[]{:S(2)}, u32[]{:S(2)}) collective-permute-start(bf16[64,2048]{1,0:T(8,128)(2,1)S(1)} %copy-done.17), channel_id=1, source_target_pairs={{0,24},{4,28},{8,16},{12,20},{16,8},{20,12},{24,0},{28,4},{1,25},{... | collective-permute-start | bytes 786440 | tf_op jit(solution)/shard_map/ppermute | solution.py:474
  (7 other events, 6.1 us)

commit v4 on v3

--- a/solution.py
+++ b/solution.py
@@ -169,7 +169,7 @@
         ],
         compiler_params=pltpu.CompilerParams(vmem_limit_bytes=VMEM_BYTES),
         name="convolve",
-    )(*held_in_hbm(pairs, *tables))
+    )(pairs, *held_in_hbm(*tables))
 
 
 def correlate(pairs, signal, kernel, tables):
@@ -195,7 +195,7 @@
         ],
         compiler_params=pltpu.CompilerParams(vmem_limit_bytes=VMEM_BYTES),
         name="correlate",
-    )(*held_in_hbm(pairs, signal, kernel, *tables))
+    )(pairs, *held_in_hbm(signal, kernel, *tables))
 
 
 def params():
@@ -218,11 +218,11 @@
 def prepare(inner_gate, signal, long_filter):
     rows, length = signal.shape
     per = length // LANES
-    step = rows // 4
+    step = rows // 2
     block = pl.BlockSpec((step, length), lambda i: (i, 0))
     return pl.pallas_call(
         prepare_kernel,
-        grid=(4,),
+        grid=(2,),
         in_specs=[block] * 3,
         out_specs=pl.BlockSpec((step, 2 * per, LANES), lambda i: (i, 0, 0)),
         out_shape=in_hbm((rows, 2 * per, LANES)),
@@ -233,7 +233,7 @@
 
 
 def mix_kernel(conv_ref, gate_ref, *refs):
-    mixed_refs, out_ref, lines = refs[:CHUNKS], refs[CHUNKS], refs[CHUNKS + 1]
+    mixed_ref, out_ref, lines = refs
     rows, length = gate_ref.shape
     per = length // LANES
     lines[...] = wide(conv_ref[...].reshape(rows * per, LANES))
@@ -244,7 +244,7 @@
         out_ref[:, cols] = short(conv)
         mixed = short(conv * wide(gate_ref[:, cols]))
         for cut in range(CHUNKS):
-            mixed_refs[cut][:, cols] = mixed[cut * small : (cut + 1) * small]
+            mixed_ref[cut, :, cols] = mixed[cut * small : (cut + 1) * small]
 
 
 def mix(conv, outer_gate):
@@ -253,13 +253,13 @@
     conv = conv.reshape(rows * per // 16, 16, LANES)
     step = rows // 2
     token_rows = pl.BlockSpec((step, length), lambda i: (i, 0))
-    cut_rows = pl.BlockSpec((step // CHUNKS, length), lambda i: (i, 0))
+    cut_rows = pl.BlockSpec((CHUNKS, step // CHUNKS, length), lambda i: (0, i, 0))
     return pl.pallas_call(
         mix_kernel,
         grid=(2,),
         in_specs=[pl.BlockSpec((step * per // 16, 16, LANES), lambda i: (i, 0, 0)), token_rows],
-        out_specs=[cut_rows] * CHUNKS + [token_rows],
-        out_shape=[in_hbm((rows // CHUNKS, length))] * CHUNKS + [in_hbm((rows, length))],
+        out_specs=[cut_rows, token_rows],
+        out_shape=[in_hbm((CHUNKS, rows // CHUNKS, length)), in_hbm((rows, length))],
         scratch_shapes=[pltpu.VMEM((step * per, LANES), jnp.float32)],
         compiler_params=params(),
         name="mix",
@@ -296,7 +296,7 @@
         out_shape=[in_hbm((rows, length)), in_hbm((rows * per // 16, 16, LANES))],
         compiler_params=params(),
         name="regard",
-    )(flag.astype(jnp.int32).reshape(1), *held_in_hbm(*shares, outer_gate, conv_out))
+    )(flag.astype(jnp.int32).reshape(1), *shares, *held_in_hbm(outer_gate, conv_out))
 
 
 def finish_kernel(corr_ref, signal_ref, gate_ref, inner_ref, signal_out_ref, filter_ref, lines):
@@ -326,7 +326,7 @@
         scratch_shapes=[pltpu.VMEM((step * 2 * per, LANES), jnp.float32)],
         compiler_params=params(),
         name="finish",
-    )(*held_in_hbm(corr.reshape(rows, 2 * per, LANES), signal, inner_gate))
+    )(corr.reshape(rows, 2 * per, LANES), *held_in_hbm(signal, inner_gate))
 
 
 def unproject_kernel(count, place_ref, *refs):
@@ -346,7 +346,7 @@
 def unproject(out_proj, grad_output, offsets, place, count):
     width, length = grad_output.shape
     rows = out_proj.shape[0] // count
-    step = 256
+    step = 512
     in_specs = [
         pl.BlockSpec((rows, width), lambda i, at, by=by: (lax.rem(at[0] + by, count), 0))
         for by in offsets
@@ -366,71 +366,6 @@
     )(place.reshape(1), *held_in_hbm(*[out_proj] * len(offsets), grad_output))
 
 
-def project_kernel(core_ref, *refs):
-    *piece_refs, grad_ref, other_ref, mine_ref, rows = refs
-    count, small, _ = mine_ref.shape
-
-    @pl.when(pl.program_id(0) == 0)
-    def _():
-        for place, which in enumerate((1 - core_ref[0], core_ref[0])):
-            first = pl.multiple_of(which * small, small)
-            for slot, piece in enumerate(piece_refs):
-                rows[pl.ds((place * count + slot) * small, small), :] = piece[pl.ds(first, small), :]
-
-    out = lax.dot_general(
-        rows[...], grad_ref[...], (((1,), (1,)), ((), ())), preferred_element_type=jnp.float32
-    )
-    out = short(out).reshape(2, count, small, -1)
-    other_ref[...] = out[0]
-    mine_ref[...] = out[1]
-
-
-def project(pieces, grad_output, core):
-    width, length = grad_output.shape
-    small = pieces[0].shape[0] // 2
-    step = 512
-    out_block = pl.BlockSpec((len(pieces), small, step), lambda i, at: (0, 0, i))
-    out = in_hbm((len(pieces), small, width))
-    return pl.pallas_call(
-        project_kernel,
-        grid_spec=pltpu.PrefetchScalarGridSpec(
-            num_scalar_prefetch=1,
-            grid=(width // step,),
-            in_specs=[pl.BlockSpec(pieces[0].shape, lambda i, at: (0, 0))] * len(pieces)
-            + [pl.BlockSpec((step, length), lambda i, at: (i, 0))],
-            out_specs=[out_block, out_block],
-            scratch_shapes=[pltpu.VMEM((2 * len(pieces) * small, length), jnp.bfloat16)],
-        ),
-        out_shape=[out, out],
-        compiler_params=params(),
-        name="project",
-    )(core.reshape(1), *held_in_hbm(*pieces, grad_output))
-
-
-def pick_kernel(order_ref, mine_ref, got_ref, *out_refs):
-    for slot, ref in enumerate(out_refs):
-        at = order_ref[slot]
-        ref[...] = short(wide(mine_ref[at]) + wide(got_ref[at]))
-
-
-def pick(mine, got, order):
-    count, small, width = mine.shape
-    step = width // 2
-    block = pl.BlockSpec((count, small, step), lambda i, at: (0, 0, i))
-    return pl.pallas_call(
-        pick_kernel,
-        grid_spec=pltpu.PrefetchScalarGridSpec(
-            num_scalar_prefetch=1,
-            grid=(2,),
-            in_specs=[block, block],
-            out_specs=[pl.BlockSpec((small, step), lambda i, at: (0, i))] * count,
-        ),
-        out_shape=[in_hbm((small, width))] * count,
-        compiler_params=params(),
-        name="pick",
-    )(order, *held_in_hbm(mine, got))
-
-
 def swaps(count, bit):
     return [(place, place ^ bit) for place in range(count)]
 
@@ -452,27 +387,44 @@
     count, place = lax.axis_size("chan"), lax.axis_index("chan")
     if count != 4:
         return [shard] + [shift(shard, by) for by in range(1, count)]
-    low, high = shift(shard, 1), shift(shard, 3)
-    return [lax.select_n(place, shard, high, low, shard), shard, low, high]
-
-
-def gather_second(held):
-    if lax.axis_size("chan") == 4:
-        passed, shard, low, high = held
-        return [shard, low, lax.ppermute(passed, "chan", [(0, 2), (3, 1), (2, 3), (1, 0)]), high]
-    return held
-
-
-def scatter_seq(other, mine, *before):
+    return [shard, shift(shard, 1), shift(shard, 3)]
+
+
+def gather_between(held):
+    shard, low, high = held
+    return [
+        lax.select_n(lax.axis_index("chan"), shard[cut], high[cut], low[cut], shard[cut])
+        for cut in range(CHUNKS)
+    ]
+
+
+def gather_second(held, passed, cut):
+    if lax.axis_size("chan") != 4:
+        return held
+    shard, low, high = held
+    passed = lax.ppermute(passed[cut], "chan", [(0, 2), (3, 1), (2, 3), (1, 0)])
+    return [shard, low, passed[None], high]
+
+
+def project(pieces, cut, grad_output):
     count, chips = lax.axis_size("seq"), lax.axis_size("chan")
-    line, chip = lax.axis_index("chan"), lax.axis_index("seq") // 2
-    got = lax.ppermute(other, "seq", swaps(count, 1))
-    bits = sorted(range(1, chips), key=lambda bit: (-bin(bit).count("1"), bit)) + [0]
-    order = jnp.stack([lax.rem(line - (chip ^ bit) + chips, chips) for bit in bits])
-    blocks = pick(tie(mine, *before), got, order.astype(jnp.int32))
-    return [
-        lax.ppermute(block, "seq", swaps(count, 2 * bit)) for block, bit in zip(blocks, bits[:-1])
-    ] + [blocks[-1]]
+    line, place = lax.axis_index("chan"), lax.axis_index("seq")
+    core, chip = place % 2, place // 2
+    rows = jnp.stack([piece[min(cut, len(piece) - 1)] for piece in pieces])
+    rows = rows.reshape(chips, 2, -1, rows.shape[-1])
+
+    def rows_of(which):
+        chosen = lax.dynamic_index_in_dim(rows, which, 1, False)
+        return jnp.einsum("zct,dt->zcd", chosen, grad_output, preferred_element_type=jnp.float32)
+
+    got = lax.ppermute(short(rows_of(1 - core)), "seq", swaps(count, 1))
+    total = short(rows_of(core) + wide(got))
+
+    def block(bit):
+        return lax.dynamic_index_in_dim(total, (line - (chip ^ bit)) % chips, 0, False)
+
+    bits = sorted(range(1, chips), key=lambda bit: (-bin(bit).count("1"), bit))
+    return [lax.ppermute(block(bit), "seq", swaps(count, 2 * bit)) for bit in bits] + [block(0)]
 
 
 def sum_of(parts):
@@ -488,15 +440,14 @@
     owned = chan_rows // seq_count
     per = block_len // LANES
     line = lax.axis_index("chan")
-    core = lax.axis_index("seq") % 2
     tables = [jnp.asarray(t) for t in dft_tables(block_len * seq_count, seq_count)]
 
+    pair = prepare(inner_gate, signal, long_filter).reshape(seq_count, owned, 2 * per, LANES)
+    sent = exchange(pair)
+    weights = tie(out_proj, pair)
     if chan_count == 4:
-        far = unproject(out_proj, grad_output, [2], line, chan_count)[0]
-        pair = prepare(inner_gate, signal, tie(long_filter, far))
-        pair = pair.reshape(seq_count, owned, 2 * per, LANES)
-        sent = exchange(pair)
-        near = unproject(tie(out_proj, pair), grad_output, [0, 1, 3], line, chan_count)
+        far = unproject(weights, grad_output, [2], line, chan_count)[0]
+        near = unproject(tie(weights, far), grad_output, [0, 1, 3], line, chan_count)
         far = lax.ppermute(far, "chan", [(2, 0), (1, 3), (3, 2), (0, 1)])
         none = jnp.zeros_like(far)
         rising = short(wide(near[1]) + wide(jnp.where(line == 1, far, none)))
@@ -505,28 +456,26 @@
         up, down = shift(rising, 1), shift(falling, 3)
         shares, flag = [near[0], up, down, far], (line == 0) | (line == 3)
     else:
-        pair = prepare(inner_gate, signal, long_filter)
-        pair = pair.reshape(seq_count, owned, 2 * per, LANES)
-        sent = exchange(pair)
-        blocks = unproject(out_proj, grad_output, list(range(chan_count)), line, chan_count)
+        blocks = unproject(weights, grad_output, list(range(chan_count)), line, chan_count)
         shares = [blocks[0]] + [shift(block, by) for by, block in enumerate(blocks) if by > 0]
         flag = line >= 0
 
     conv, spec_signal, spec_filter = convolve(sent, tables)
-    *mixed, conv_out = mix(tie(exchange(conv), *shares), outer_gate)
-    held = [gather_first(part) for part in mixed]
+    mixed, conv_out = mix(tie(exchange(conv), *shares), outer_gate)
+    held = gather_first(mixed)
     grad_outer, grad_conv = regard(shares, flag, outer_gate, conv_out)
     grad_conv = grad_conv.reshape(seq_count, owned // 2, 2 * per, LANES)
     corr = correlate(exchange(grad_conv), spec_signal, spec_filter, tables)
-    pieces = [gather_second(part) for part in held]
-    pieces[0] = tie(pieces[0], corr)
-    partials = [project(part, grad_output, core) for part in pieces]
-    projs = [scatter_seq(*partials[0])]
-    projs.append(scatter_seq(*partials[1], *projs[0][-1:]))
-
-    grad_inner, grad_signal, grad_filter = finish(tie(exchange(corr), projs[1][-1]), signal, inner_gate)
-    grad_proj = jnp.concatenate([sum_of(parts) for parts in projs], axis=0)
-    return (grad_outer, grad_inner, grad_signal, grad_filter, grad_proj)
+    held = tie(held, corr)
+    passed = gather_between(held) if chan_count == 4 else held
+    pieces = [gather_second(held, passed, cut) for cut in range(CHUNKS)]
+    corr = exchange(tie(corr, passed))
+    pieces = tie(pieces, corr)
+    first = project(pieces[0], 0, grad_output)
+    second = project(pieces[1], 1, grad_output)
+    grads = finish(tie(corr, first[-1]), signal, inner_gate)
+    grad_proj = jnp.concatenate([sum_of(first), sum_of(second)], axis=0)
+    return (grad_outer, *grads, grad_proj)
 
 
 def solution(mesh):

time: 154 us -> 145 us (0.942)
  Pallas kernels: 56.8 us -> 35.9 us
  matrix products: 0 us -> 11.1 us
  waiting for transfers between devices: 44.1 us -> 54.3 us
  starting transfers between devices: 40.6 us -> 34.8 us
  local copies, waits for them, and re-layouts: 6.11 us -> 2.4 us
    pallas_call x5 -> x1, Pallas kernels: 21.9 us -> 2.81 us  [prepare(): pl.pallas_call(prepare_kernel, grid=(2,), in_specs=[block] * 3, out_specs...]
    ppermute x10, waiting for transfers between devices: 13.2 us -> 26.4 us  [the longest x6 14 us: project(): lax.ppermute(block(bit), 'seq', swaps(count, 2 * bit))]
    dot_general x0 -> x4, matrix products: none -> 11.1 us  [rows_of(): jnp.einsum('zct,dt->zcd', chosen, grad_output, preferred_element_type=jnp...]
    ppermute x6 -> x4, waiting for transfers between devices: 19.9 us -> 10.6 us  [shift(): lax.ppermute(block, 'chan', [(i, (i + by) % count) for i in range(count)])]
    all_to_all x4, waiting for transfers between devices: 4.84 us -> 10.6 us  [exchange(): lax.all_to_all(blocks, 'seq', split_axis=0, concat_axis=0, tiled=True)]
    unnamed x36 -> x12, local copies, waits for them, and re-layouts: 6.11 us -> 2.15 us
    ppermute x6 -> x4, starting transfers between devices: 11.6 us -> 7.65 us  [shift(): lax.ppermute(block, 'chan', [(i, (i + by) % count) for i in range(count)])]
    ppermute x10, starting transfers between devices: 11.3 us -> 9.43 us  [the longest x6 6.67 us: project(): lax.ppermute(block(bit), 'seq', swaps(count, 2 * bit))]
  transfers between devices with their start and end apart: 21 -> 19, of which waited for: 12 -> 12; matrix products, arithmetic and copies ran while one was open for 2% -> 8% of each run, Pallas kernels for 31% -> 22%
where the time goes in v4:
time: 145 us; the launch traced here: 144 us
  waiting for transfers between devices  54.3 us (37%)
  Pallas kernels  35.9 us (25%)
  starting transfers between devices  34.8 us (24%)
  matrix products  11.1 us (8%)
  other arithmetic  4.84 us (3%)
  local copies, waits for them, and re-layouts  2.4 us (2%)
    all_to_all x4, starting transfers between devices, exchange(): lax.all_to_all(blocks, 'seq', split_axis=0, concat_axis=0, tiled=True)  16.2 us
    ppermute x6, waiting for transfers between devices, project(): lax.ppermute(block(bit), 'seq', swaps(count, 2 * bit))  14 us
    ppermute x2, waiting for transfers between devices, gather_second(): passed = lax.ppermute(passed[cut], 'chan', [(0, 2), (3, 1), (2, 3), (1, 0)])  12.2 us
    pallas_call x2, Pallas kernels, unproject(): pl.pallas_call(functools.partial(unproject_kernel, len(offsets)), grid_sp...  11.2 us
    dot_general x4, matrix products, rows_of(): jnp.einsum('zct,dt->zcd', chosen, grad_output, preferred_element_type=jnp...  11.1 us
    ppermute x4, waiting for transfers between devices, shift(): lax.ppermute(block, 'chan', [(i, (i + by) % count) for i in range(count)])  10.6 us
    all_to_all x4, waiting for transfers between devices, exchange(): lax.all_to_all(blocks, 'seq', split_axis=0, concat_axis=0, tiled=True)  10.6 us
    ppermute x4, starting transfers between devices, shift(): lax.ppermute(block, 'chan', [(i, (i + by) % count) for i in range(count)])  7.65 us
  transfers between devices with their start and end apart: 19, of which 12 were waited for; matrix products, arithmetic and copies ran while one was open for 8% of the time, Pallas kernels for 22%

profile of v4, /device:TPU:0, one launch (start us, length us, event | category | flops | bytes accessed | tf_op | source)
XLA Modules:
  0.0 144.3 jit_solution(12895694991327270605)
XLA Ops:
  0.6 2.8 %prepare.1 = bf16[256,16,128]{2,1,0:T(8,128)(2,1)} custom-call(bf16[256,1024]{1,0:T(8,128)(2,1)} %gate_ref.5, bf16[256,1024]{1,0:T(8,128)(2,1)} %signal_ref.3, bf16[256,1024]{1,0:T(8,128)(2,1)} %filter_ref.1), custom_call_target="tpu_custom_call" | custom-call | tf_op jit(solution)/shard_map/prepare/pallas_call | solution.py:223
  3.4 5.2 %all-to-all-start = ((bf16[8,32,16,128]{3,2,1,0:T(8,128)(2,1)}), bf16[8,32,16,128]{3,2,1,0:T(8,128)(2,1)S(1)}, u32[]{:S(2)}, u32[]{:S(2)}) async-start(bf16[8,32,16,128]{3,2,1,0:T(8,128)(2,1)} %bitcast.67), calls=%async_computation | async-start | bytes 2097152 | tf_op jit(solution)/shard_map/all_to_all | solution.py:374
  8.6 4.1 %unproject.2 = bf16[256,1024]{1,0:T(8,128)(2,1)} custom-call(s32[1]{0:T(128)} %bitcast.1.place_ref, bf16[1024,2048]{1,0:T(8,128)(2,1)} %refs_2_, bf16[2048,1024]{1,0:T(8,128)(2,1)} %refs_3_.1), custom_call_target="tpu_custom_call" | custom-call | tf_op jit(solution)/shard_map/unproject/pallas_call | solution.py:354
  12.7 1.6 %collective-permute-start = (bf16[256,1024]{1,0:T(8,128)(2,1)}, bf16[256,1024]{1,0:T(8,128)(2,1)S(1)}, u32[]{:S(2)}, u32[]{:S(2)}) collective-permute-start(bf16[256,1024]{1,0:T(8,128)(2,1)} %unproject.2), channel_id=1, source_target_pairs={{2,0},{1,3},{3,2},{0,1},{6,4},{5,7},{7,6},{4,5},{10,8},{9,11},{11,... | collective-permute-start | bytes 1572872 | tf_op jit(solution)/shard_map/ppermute | solution.py:451
  14.3 7.1 %unproject.3 = (bf16[256,1024]{1,0:T(8,128)(2,1)}, bf16[256,1024]{1,0:T(8,128)(2,1)}, bf16[256,1024]{1,0:T(8,128)(2,1)}) custom-call(s32[1]{0:T(128)} %bitcast.1.place_ref, bf16[1024,2048]{1,0:T(8,128)(2,1)} %refs_2_, bf16[1024,2048]{1,0:T(8,128)(2,1)} %refs_2_, bf16[1024,2048]{1,0:T(8,128)(2,1)} %refs_2_, bf16[2048,1024]{1,0:T(8,128)(2,1)} %refs_3_.1), custom_call_target="tpu_custom_call" | custom-call | tf_op jit(solution)/shard_map/unproject/pallas_call | solution.py:354
  21.4 6.7 %collective-permute-done.refs_3_ = bf16[256,1024]{1,0:T(8,128)(2,1)S(1)} collective-permute-done((bf16[256,1024]{1,0:T(8,128)(2,1)}, bf16[256,1024]{1,0:T(8,128)(2,1)S(1)}, u32[]{:S(2)}, u32[]{:S(2)}) %collective-permute-start) | collective-permute-done | bytes 524320 | tf_op jit(solution)/shard_map/ppermute | solution.py:451
  28.1 2.5 %add_convert_fusion.2 = (bf16[256,1024]{1,0:T(8,128)(2,1)}, bf16[256,1024]{1,0:T(8,128)(2,1)}) fusion(bf16[256,1024]{1,0:T(8,128)(2,1)} %get-tuple-element.39, bf16[256,1024]{1,0:T(8,128)(2,1)S(1)} %collective-permute-done.refs_3_, pred[]{:T(512)S(6)} %eq.26, pred[]{:T(512)S(6)} %eq.25, bf16[256,1024]{1,0:T(8,128)(2,1)} %get-tuple-element.38), kind=kLoop, calls=%fused_computation.15 | loop fusion | flops 2621440 | bytes 2621442 | tf_op jit(solution)/shard_map/convert_element_type | solution.py:22
  31.5 2.9 %collective-permute-start.2 = (bf16[256,1024]{1,0:T(8,128)(2,1)}, bf16[256,1024]{1,0:T(8,128)(2,1)}, u32[]{:S(2)}, u32[]{:S(2)}) collective-permute-start(bf16[256,1024]{1,0:T(8,128)(2,1)} %get-tuple-element.75), channel_id=1, source_target_pairs={{0,3},{1,0},{2,1},{3,2},{4,7},{5,4},{6,5},{7,6},{8,11},{9,8},{10,9... | collective-permute-start | bytes 1572872 | tf_op jit(solution)/shard_map/ppermute | solution.py:383
  34.5 7.5 %convolve.1 = (bf16[8,16,16,128]{3,2,1,0:T(8,128)(2,1)}, f32[32,64,256]{2,1,0:T(8,128)}, f32[32,64,256]{2,1,0:T(8,128)}) custom-call(bf16[8,32,16,128]{3,2,1,0:T(8,128)(2,1)S(1)} %all-to-all-done.pairs_ref, bf16[256,256]{1,0:T(8,128)(2,1)} %constant.111.clone.first_ref, bf16[512,256]{1,0:T(8,128)(2,1)} %constant.112.clone.forward_ref, ...), custom_call_target="tpu_custom_call" | custom-call | tf_op jit(solution)/shard_map/convolve/pallas_call | solution.py:155
  41.9 3.8 %all-to-all-start.1 = ((bf16[8,16,16,128]{3,2,1,0:T(8,128)(2,1)}), bf16[8,16,16,128]{3,2,1,0:T(8,128)(2,1)S(1)}, u32[]{:S(2)}, u32[]{:S(2)}) async-start(bf16[8,16,16,128]{3,2,1,0:T(8,128)(2,1)} %get-tuple-element.41), calls=%async_computation.1 | async-start | bytes 1048576 | tf_op jit(solution)/shard_map/all_to_all | solution.py:374
  45.7 1.8 %collective-permute-done.1.refs_1_ = bf16[256,1024]{1,0:T(8,128)(2,1)S(1)} collective-permute-done((bf16[256,1024]{1,0:T(8,128)(2,1)}, bf16[256,1024]{1,0:T(8,128)(2,1)S(1)}, u32[]{:S(2)}, u32[]{:S(2)}) %collective-permute-start.1) | collective-permute-done | bytes 524320 | tf_op jit(solution)/shard_map/ppermute | solution.py:383
  47.5 8.8 %collective-permute-done.2.refs_2_ = bf16[256,1024]{1,0:T(8,128)(2,1)} collective-permute-done((bf16[256,1024]{1,0:T(8,128)(2,1)}, bf16[256,1024]{1,0:T(8,128)(2,1)}, u32[]{:S(2)}, u32[]{:S(2)}) %collective-permute-start.2) | collective-permute-done | bytes 524320 | tf_op jit(solution)/shard_map/ppermute | solution.py:383
  57.6 1.8 %collective-permute-start.3 = (bf16[2,128,1024]{2,1,0:T(8,128)(2,1)}, bf16[2,128,1024]{2,1,0:T(8,128)(2,1)S(1)}, u32[]{:S(2)}, u32[]{:S(2)}) collective-permute-start(bf16[2,128,1024]{2,1,0:T(8,128)(2,1)} %get-tuple-element.61), channel_id=1, source_target_pairs={{0,1},{1,2},{2,3},{3,0},{4,5},{5,6},{6,7},{7,4},{8,9},{9,10},{10,1... | collective-permute-start | bytes 1572872 | tf_op jit(solution)/shard_map/ppermute | solution.py:383
  59.4 2.0 %collective-permute-start.4 = (bf16[2,128,1024]{2,1,0:T(8,128)(2,1)}, bf16[2,128,1024]{2,1,0:T(8,128)(2,1)S(1)}, u32[]{:S(2)}, u32[]{:S(2)}) collective-permute-start(bf16[2,128,1024]{2,1,0:T(8,128)(2,1)} %get-tuple-element.61), channel_id=1, source_target_pairs={{0,3},{1,0},{2,1},{3,2},{4,7},{5,4},{6,5},{7,6},{8,11},{9,8},{10,9... | collective-permute-start | bytes 1572872 | tf_op jit(solution)/shard_map/ppermute | solution.py:383
  61.4 2.7 %regard.1 = (bf16[256,1024]{1,0:T(8,128)(2,1)}, bf16[128,16,128]{2,1,0:T(8,128)(2,1)}) custom-call(s32[1]{0:T(128)} %bitcast.flag_ref, bf16[256,1024]{1,0:T(8,128)(2,1)S(1)} %copy-done.1, bf16[256,1024]{1,0:T(8,128)(2,1)S(1)} %collective-permute-done.1.refs_1_, bf16[256,1024]{1,0:T(8,128)(2,1)} %collective-permute-done.2.refs_2_, ...), custom_call_target="tpu_custom_call" | custom-call | tf_op jit(solution)/shard_map/regard/pallas_call | solution.py:287
  64.1 3.6 %all-to-all-start.2 = ((bf16[8,16,16,128]{3,2,1,0:T(8,128)(2,1)}), bf16[8,16,16,128]{3,2,1,0:T(8,128)(2,1)S(1)}, u32[]{:S(2)}, u32[]{:S(2)}) async-start(bf16[8,16,16,128]{3,2,1,0:T(8,128)(2,1)} %bitcast.72), calls=%async_computation.2 | async-start | bytes 1048576 | tf_op jit(solution)/shard_map/all_to_all | solution.py:374
  67.7 9.7 %all-to-all-done.2.pairs_ref = bf16[8,16,16,128]{3,2,1,0:T(8,128)(2,1)S(1)} async-done(((bf16[8,16,16,128]{3,2,1,0:T(8,128)(2,1)}), bf16[8,16,16,128]{3,2,1,0:T(8,128)(2,1)S(1)}, u32[]{:S(2)}, u32[]{:S(2)}) %all-to-all-start.2) | async-done | bytes 524320 | tf_op jit(solution)/shard_map/all_to_all | solution.py:374
  77.4 7.4 %correlate.1 = bf16[8,32,16,128]{3,2,1,0:T(8,128)(2,1)} custom-call(bf16[8,16,16,128]{3,2,1,0:T(8,128)(2,1)S(1)} %all-to-all-done.2.pairs_ref, f32[32,64,256]{2,1,0:T(8,128)} %get-tuple-element.46.signal_ref, f32[32,64,256]{2,1,0:T(8,128)} %get-tuple-element.47.filter_ref, bf16[256,256]{1,0:T(8,128)(2,1)} %constant.111.clone.first_ref, ...), custom_call_target="tpu_custom_call" | custom-call | tf_op jit(solution)/shard_map/correlate/pallas_call | solution.py:181
  85.6 3.6 %all-to-all-start.3 = ((bf16[8,32,16,128]{3,2,1,0:T(8,128)(2,1)}), bf16[8,32,16,128]{3,2,1,0:T(8,128)(2,1)S(1)}, u32[]{:S(2)}, u32[]{:S(2)}) async-start(bf16[8,32,16,128]{3,2,1,0:T(8,128)(2,1)} %correlate.1), calls=%async_computation.3 | async-start | bytes 2097152 | tf_op jit(solution)/shard_map/all_to_all | solution.py:374
  89.3 2.1 %collective-permute-start.6 = (bf16[128,1024]{1,0:T(8,128)(2,1)S(1)}, bf16[128,1024]{1,0:T(8,128)(2,1)S(1)}, u32[]{:S(2)}, u32[]{:S(2)}) collective-permute-start(bf16[128,1024]{1,0:T(8,128)(2,1)S(1)} %get-tuple-element.67), channel_id=1, source_target_pairs={{0,2},{3,1},{2,3},{1,0},{4,6},{7,5},{6,7},{5,4},{8,10},{11,9},{10,... | collective-permute-start | bytes 786440 | tf_op jit(solution)/shard_map/ppermute | solution.py:405
  91.4 7.2 %collective-permute-done.5 = bf16[128,1024]{1,0:T(8,128)(2,1)S(1)} collective-permute-done((bf16[128,1024]{1,0:T(8,128)(2,1)}, bf16[128,1024]{1,0:T(8,128)(2,1)S(1)}, u32[]{:S(2)}, u32[]{:S(2)}) %collective-permute-start.5) | collective-permute-done | bytes 262176 | tf_op jit(solution)/shard_map/ppermute | solution.py:405
  98.6 5.0 %collective-permute-done.6 = bf16[128,1024]{1,0:T(8,128)(2,1)S(1)} collective-permute-done((bf16[128,1024]{1,0:T(8,128)(2,1)S(1)}, bf16[128,1024]{1,0:T(8,128)(2,1)S(1)}, u32[]{:S(2)}, u32[]{:S(2)}) %collective-permute-start.6) | collective-permute-done | bytes 262176 | tf_op jit(solution)/shard_map/ppermute | solution.py:405
  105.0 2.1 %copy-done.2 = bf16[2048,1024]{1,0:T(8,128)(2,1)S(1)} copy-done((bf16[2048,1024]{1,0:T(8,128)(2,1)S(1)}, bf16[2048,1024]{1,0:T(8,128)(2,1)}, u32[]{:S(2)}) %copy-start.2) | copy-done | bytes 4194328
  107.1 2.3 %fusion.8 = bf16[4,64,2048]{2,1,0:T(8,128)(2,1)} fusion(bf16[2048,1024]{1,0:T(8,128)(2,1)S(1)} %copy-done.2, bf16[4,2,64,1024]{3,2,1,0:T(8,128)(2,1)S(1)} %bitcast.70, s32[]{:T(128)S(6)} %select_n.150), kind=kOutput, calls=%fused_computation.8 | convolution fusion | flops 1074266112 | bytes 5767172 | tf_op jit(solution)/shard_map/zct,dt->zcd/dot_general | solution.py:418
  109.3 2.3 %fusion.11 = bf16[4,64,2048]{2,1,0:T(8,128)(2,1)} fusion(bf16[2048,1024]{1,0:T(8,128)(2,1)S(1)} %copy-done.2, bf16[4,2,64,1024]{3,2,1,0:T(8,128)(2,1)S(1)} %bitcast.68, s32[]{:T(128)S(6)} %select_n.150), kind=kOutput, calls=%fused_computation.9 | convolution fusion | flops 1074266112 | bytes 5767172 | tf_op jit(solution)/shard_map/zct,dt->zcd/dot_general | solution.py:418
  112.3 4.1 %add_convert_fusion.1 = bf16[4,64,2048]{2,1,0:T(8,128)(2,1)S(1)} fusion(bf16[4,64,2048]{2,1,0:T(8,128)(2,1)} %collective-permute-done.7, bf16[2048,1024]{1,0:T(8,128)(2,1)} %refs_3_.1, bf16[4,2,64,1024]{3,2,1,0:T(8,128)(2,1)} %bitcast.71, s32[]{:T(128)S(6)} %select_n.149), kind=kOutput, calls=%fused_computation.11 | convolution fusion | flops 1075314688 | bytes 6815748 | tf_op jit(solution)/shard_map/zct,dt->zcd/dot_general | solution.py:418
  120.1 2.5 %add_convert_fusion = bf16[4,64,2048]{2,1,0:T(8,128)(2,1)S(1)} fusion(bf16[4,64,2048]{2,1,0:T(8,128)(2,1)} %collective-permute-done.11, bf16[2048,1024]{1,0:T(8,128)(2,1)S(1)} %copy-done.3, bf16[4,2,64,1024]{3,2,1,0:T(8,128)(2,1)S(1)} %bitcast.69, s32[]{:T(128)S(6)} %select_n.149), kind=kOutput, calls=%fused_computation.10 | convolution fusion | flops 1075314688 | bytes 6815748 | tf_op jit(solution)/shard_map/zct,dt->zcd/dot_general | solution.py:418
  122.7 1.8 %collective-permute-start.12 = (bf16[64,2048]{1,0:T(8,128)(2,1)S(1)}, bf16[64,2048]{1,0:T(8,128)(2,1)S(1)}, u32[]{:S(2)}, u32[]{:S(2)}) collective-permute-start(bf16[64,2048]{1,0:T(8,128)(2,1)S(1)} %get-tuple-element.69), channel_id=1, source_target_pairs={{0,24},{4,28},{8,16},{12,20},{16,8},{20,12},{24,0},{28,4},{1,25},{... | collective-permute-start | bytes 786440 | tf_op jit(solution)/shard_map/ppermute | solution.py:427
  125.0 5.6 %collective-permute-done.10 = bf16[64,2048]{1,0:T(8,128)(2,1)S(1)} collective-permute-done((bf16[64,2048]{1,0:T(8,128)(2,1)S(1)}, bf16[64,2048]{1,0:T(8,128)(2,1)S(1)}, u32[]{:S(2)}, u32[]{:S(2)}) %collective-permute-start.10) | collective-permute-done | bytes 262176 | tf_op jit(solution)/shard_map/ppermute | solution.py:427
  133.0 3.2 %finish.1 = (bf16[256,1024]{1,0:T(8,128)(2,1)}, bf16[256,1024]{1,0:T(8,128)(2,1)}, f32[256,1024]{1,0:T(8,128)}) custom-call(bf16[256,16,128]{2,1,0:T(8,128)(2,1)S(1)} %bitcast.65, bf16[256,1024]{1,0:T(8,128)(2,1)} %signal_ref.3, bf16[256,1024]{1,0:T(8,128)(2,1)} %gate_ref.5), custom_call_target="tpu_custom_call" | custom-call | tf_op jit(solution)/shard_map/finish/pallas_call | solution.py:319
  136.1 2.6 %collective-permute-done.12 = bf16[64,2048]{1,0:T(8,128)(2,1)S(1)} collective-permute-done((bf16[64,2048]{1,0:T(8,128)(2,1)S(1)}, bf16[64,2048]{1,0:T(8,128)(2,1)S(1)}, u32[]{:S(2)}, u32[]{:S(2)}) %collective-permute-start.12) | collective-permute-done | bytes 262176 | tf_op jit(solution)/shard_map/ppermute | solution.py:427
  138.7 4.3 %collective-permute-done.13 = bf16[64,2048]{1,0:T(8,128)(2,1)S(1)} collective-permute-done((bf16[64,2048]{1,0:T(8,128)(2,1)S(1)}, bf16[64,2048]{1,0:T(8,128)(2,1)S(1)}, u32[]{:S(2)}, u32[]{:S(2)}) %collective-permute-start.13) | collective-permute-done | bytes 262176 | tf_op jit(solution)/shard_map/ppermute | solution.py:427
  (44 shorter events, 12.9 us)
Async XLA Ops:
  3.4 31.0 %all-to-all-start = ((bf16[8,32,16,128]{3,2,1,0:T(8,128)(2,1)}), bf16[8,32,16,128]{3,2,1,0:T(8,128)(2,1)S(1)}, u32[]{:S(2)}, u32[]{:S(2)}) async-start(bf16[8,32,16,128]{3,2,1,0:T(8,128)(2,1)} %bitcast.67), calls=%async_computation | async-start | bytes 2097152 | tf_op jit(solution)/shard_map/all_to_all | solution.py:374
  12.7 15.4 %collective-permute-start = (bf16[256,1024]{1,0:T(8,128)(2,1)}, bf16[256,1024]{1,0:T(8,128)(2,1)S(1)}, u32[]{:S(2)}, u32[]{:S(2)}) collective-permute-start(bf16[256,1024]{1,0:T(8,128)(2,1)} %unproject.2), channel_id=1, source_target_pairs={{2,0},{1,3},{3,2},{0,1},{6,4},{5,7},{7,6},{4,5},{10,8},{9,11},{11,... | collective-permute-start | bytes 1572872 | tf_op jit(solution)/shard_map/ppermute | solution.py:451
  21.4 35.0 %copy-start = (bf16[256,1024]{1,0:T(8,128)(2,1)S(1)}, bf16[256,1024]{1,0:T(8,128)(2,1)}, u32[]{:S(2)}) copy-start(bf16[256,1024]{1,0:T(8,128)(2,1)} %refs_4_.1) | copy-start | bytes 1572868
  21.4 40.0 %copy-start.1 = (bf16[256,1024]{1,0:T(8,128)(2,1)S(1)}, bf16[256,1024]{1,0:T(8,128)(2,1)}, u32[]{:S(2)}) copy-start(bf16[256,1024]{1,0:T(8,128)(2,1)} %get-tuple-element.37.refs_0_) | copy-start | bytes 1572868
  30.6 16.9 %collective-permute-start.1 = (bf16[256,1024]{1,0:T(8,128)(2,1)}, bf16[256,1024]{1,0:T(8,128)(2,1)S(1)}, u32[]{:S(2)}, u32[]{:S(2)}) collective-permute-start(bf16[256,1024]{1,0:T(8,128)(2,1)} %get-tuple-element.76), channel_id=1, source_target_pairs={{0,1},{1,2},{2,3},{3,0},{4,5},{5,6},{6,7},{7,4},{8,9},{9,10},{10,1... | collective-permute-start | bytes 1572872 | tf_op jit(solution)/shard_map/ppermute | solution.py:383
  31.5 24.8 %collective-permute-start.2 = (bf16[256,1024]{1,0:T(8,128)(2,1)}, bf16[256,1024]{1,0:T(8,128)(2,1)}, u32[]{:S(2)}, u32[]{:S(2)}) collective-permute-start(bf16[256,1024]{1,0:T(8,128)(2,1)} %get-tuple-element.75), channel_id=1, source_target_pairs={{0,3},{1,0},{2,1},{3,2},{4,7},{5,4},{6,5},{7,6},{8,11},{9,8},{10,9... | collective-permute-start | bytes 1572872 | tf_op jit(solution)/shard_map/ppermute | solution.py:383
  41.9 14.4 %all-to-all-start.1 = ((bf16[8,16,16,128]{3,2,1,0:T(8,128)(2,1)}), bf16[8,16,16,128]{3,2,1,0:T(8,128)(2,1)S(1)}, u32[]{:S(2)}, u32[]{:S(2)}) async-start(bf16[8,16,16,128]{3,2,1,0:T(8,128)(2,1)} %get-tuple-element.41), calls=%async_computation.1 | async-start | bytes 1048576 | tf_op jit(solution)/shard_map/all_to_all | solution.py:374
  57.6 27.2 %collective-permute-start.3 = (bf16[2,128,1024]{2,1,0:T(8,128)(2,1)}, bf16[2,128,1024]{2,1,0:T(8,128)(2,1)S(1)}, u32[]{:S(2)}, u32[]{:S(2)}) collective-permute-start(bf16[2,128,1024]{2,1,0:T(8,128)(2,1)} %get-tuple-element.61), channel_id=1, source_target_pairs={{0,1},{1,2},{2,3},{3,0},{4,5},{5,6},{6,7},{7,4},{8,9},{9,10},{10,1... | collective-permute-start | bytes 1572872 | tf_op jit(solution)/shard_map/ppermute | solution.py:383
  59.4 25.4 %collective-permute-start.4 = (bf16[2,128,1024]{2,1,0:T(8,128)(2,1)}, bf16[2,128,1024]{2,1,0:T(8,128)(2,1)S(1)}, u32[]{:S(2)}, u32[]{:S(2)}) collective-permute-start(bf16[2,128,1024]{2,1,0:T(8,128)(2,1)} %get-tuple-element.61), channel_id=1, source_target_pairs={{0,3},{1,0},{2,1},{3,2},{4,7},{5,4},{6,5},{7,6},{8,11},{9,8},{10,9... | collective-permute-start | bytes 1572872 | tf_op jit(solution)/shard_map/ppermute | solution.py:383
  64.1 20.7 %copy-start.4 = (bf16[2,128,1024]{2,1,0:T(8,128)(2,1)S(1)}, bf16[2,128,1024]{2,1,0:T(8,128)(2,1)}, u32[]{:S(2)}) copy-start(bf16[2,128,1024]{2,1,0:T(8,128)(2,1)} %get-tuple-element.61) | copy-start | bytes 1572868
  64.1 13.3 %all-to-all-start.2 = ((bf16[8,16,16,128]{3,2,1,0:T(8,128)(2,1)}), bf16[8,16,16,128]{3,2,1,0:T(8,128)(2,1)S(1)}, u32[]{:S(2)}, u32[]{:S(2)}) async-start(bf16[8,16,16,128]{3,2,1,0:T(8,128)(2,1)} %bitcast.72), calls=%async_computation.2 | async-start | bytes 1048576 | tf_op jit(solution)/shard_map/all_to_all | solution.py:374
  85.6 18.9 %all-to-all-start.3 = ((bf16[8,32,16,128]{3,2,1,0:T(8,128)(2,1)}), bf16[8,32,16,128]{3,2,1,0:T(8,128)(2,1)S(1)}, u32[]{:S(2)}, u32[]{:S(2)}) async-start(bf16[8,32,16,128]{3,2,1,0:T(8,128)(2,1)} %correlate.1), calls=%async_computation.3 | async-start | bytes 2097152 | tf_op jit(solution)/shard_map/all_to_all | solution.py:374
  89.2 9.4 %collective-permute-start.5 = (bf16[128,1024]{1,0:T(8,128)(2,1)}, bf16[128,1024]{1,0:T(8,128)(2,1)S(1)}, u32[]{:S(2)}, u32[]{:S(2)}) collective-permute-start(bf16[128,1024]{1,0:T(8,128)(2,1)} %get-tuple-element.68), channel_id=1, source_target_pairs={{0,2},{3,1},{2,3},{1,0},{4,6},{7,5},{6,7},{5,4},{8,10},{11,9},{10,... | collective-permute-start | bytes 786440 | tf_op jit(solution)/shard_map/ppermute | solution.py:405
  89.3 14.3 %collective-permute-start.6 = (bf16[128,1024]{1,0:T(8,128)(2,1)S(1)}, bf16[128,1024]{1,0:T(8,128)(2,1)S(1)}, u32[]{:S(2)}, u32[]{:S(2)}) collective-permute-start(bf16[128,1024]{1,0:T(8,128)(2,1)S(1)} %get-tuple-element.67), channel_id=1, source_target_pairs={{0,2},{3,1},{2,3},{1,0},{4,6},{7,5},{6,7},{5,4},{8,10},{11,9},{10,... | collective-permute-start | bytes 786440 | tf_op jit(solution)/shard_map/ppermute | solution.py:405
  104.5 2.6 %copy-start.2 = (bf16[2048,1024]{1,0:T(8,128)(2,1)S(1)}, bf16[2048,1024]{1,0:T(8,128)(2,1)}, u32[]{:S(2)}) copy-start(bf16[2048,1024]{1,0:T(8,128)(2,1)} %refs_3_.1) | copy-start | bytes 12582916
  104.9 6.7 %copy-start.5 = (bf16[4,128,1024]{2,1,0:T(8,128)(2,1)}, bf16[4,128,1024]{2,1,0:T(8,128)(2,1)S(1)}, u32[]{:S(2)}) copy-start(bf16[4,128,1024]{2,1,0:T(8,128)(2,1)S(1)} %get-tuple-element.77) | copy-start | bytes 3145732
  109.3 3.0 %collective-permute-start.7 = (bf16[4,64,2048]{2,1,0:T(8,128)(2,1)}, bf16[4,64,2048]{2,1,0:T(8,128)(2,1)}, u32[]{:S(2)}, u32[]{:S(2)}) collective-permute-start(bf16[4,64,2048]{2,1,0:T(8,128)(2,1)} %fusion.8), channel_id=1, source_target_pairs={{0,4},{4,0},{8,12},{12,8},{16,20},{20,16},{24,28},{28,24},{1,5},{5... | collective-permute-start | bytes 3145736 | tf_op jit(solution)/shard_map/ppermute | solution.py:420
  111.6 8.5 %collective-permute-start.11 = (bf16[4,64,2048]{2,1,0:T(8,128)(2,1)}, bf16[4,64,2048]{2,1,0:T(8,128)(2,1)}, u32[]{:S(2)}, u32[]{:S(2)}) collective-permute-start(bf16[4,64,2048]{2,1,0:T(8,128)(2,1)} %fusion.11), channel_id=1, source_target_pairs={{0,4},{4,0},{8,12},{12,8},{16,20},{20,16},{24,28},{28,24},{1,5},{5... | collective-permute-start | bytes 3145736 | tf_op jit(solution)/shard_map/ppermute | solution.py:420
  112.1 8.0 %copy-start.3 = (bf16[2048,1024]{1,0:T(8,128)(2,1)S(1)}, bf16[2048,1024]{1,0:T(8,128)(2,1)}, u32[]{:S(2)}) copy-start(bf16[2048,1024]{1,0:T(8,128)(2,1)} %refs_3_.1) | copy-start | bytes 12582916
  116.5 14.1 %collective-permute-start.10 = (bf16[64,2048]{1,0:T(8,128)(2,1)S(1)}, bf16[64,2048]{1,0:T(8,128)(2,1)S(1)}, u32[]{:S(2)}, u32[]{:S(2)}) collective-permute-start(bf16[64,2048]{1,0:T(8,128)(2,1)S(1)} %get-tuple-element.73), channel_id=1, source_target_pairs={{0,16},{4,20},{8,24},{12,28},{16,0},{20,4},{24,8},{28,12},{1,17},{... | collective-permute-start | bytes 786440 | tf_op jit(solution)/shard_map/ppermute | solution.py:427
  117.4 14.0 %collective-permute-start.8 = (bf16[64,2048]{1,0:T(8,128)(2,1)S(1)}, bf16[64,2048]{1,0:T(8,128)(2,1)S(1)}, u32[]{:S(2)}, u32[]{:S(2)}) collective-permute-start(bf16[64,2048]{1,0:T(8,128)(2,1)S(1)} %get-tuple-element.72), channel_id=1, source_target_pairs={{0,24},{4,28},{8,16},{12,20},{16,8},{20,12},{24,0},{28,4},{1,25},{... | collective-permute-start | bytes 786440 | tf_op jit(solution)/shard_map/ppermute | solution.py:427
  118.8 14.0 %collective-permute-start.9 = (bf16[64,2048]{1,0:T(8,128)(2,1)S(1)}, bf16[64,2048]{1,0:T(8,128)(2,1)S(1)}, u32[]{:S(2)}, u32[]{:S(2)}) collective-permute-start(bf16[64,2048]{1,0:T(8,128)(2,1)S(1)} %get-tuple-element.74), channel_id=1, source_target_pairs={{0,8},{4,12},{8,0},{12,4},{16,24},{20,28},{24,16},{28,20},{1,9},{5... | collective-permute-start | bytes 786440 | tf_op jit(solution)/shard_map/ppermute | solution.py:427
  122.7 16.1 %collective-permute-start.12 = (bf16[64,2048]{1,0:T(8,128)(2,1)S(1)}, bf16[64,2048]{1,0:T(8,128)(2,1)S(1)}, u32[]{:S(2)}, u32[]{:S(2)}) collective-permute-start(bf16[64,2048]{1,0:T(8,128)(2,1)S(1)} %get-tuple-element.69), channel_id=1, source_target_pairs={{0,24},{4,28},{8,16},{12,20},{16,8},{20,12},{24,0},{28,4},{1,25},{... | collective-permute-start | bytes 786440 | tf_op jit(solution)/shard_map/ppermute | solution.py:427
  124.4 18.6 %collective-permute-start.13 = (bf16[64,2048]{1,0:T(8,128)(2,1)S(1)}, bf16[64,2048]{1,0:T(8,128)(2,1)S(1)}, u32[]{:S(2)}, u32[]{:S(2)}) collective-permute-start(bf16[64,2048]{1,0:T(8,128)(2,1)S(1)} %get-tuple-element.71), channel_id=1, source_target_pairs={{0,8},{4,12},{8,0},{12,4},{16,24},{20,28},{24,16},{28,20},{1,9},{5... | collective-permute-start | bytes 786440 | tf_op jit(solution)/shard_map/ppermute | solution.py:427
  130.6 12.5 %collective-permute-start.14 = (bf16[64,2048]{1,0:T(8,128)(2,1)S(1)}, bf16[64,2048]{1,0:T(8,128)(2,1)S(1)}, u32[]{:S(2)}, u32[]{:S(2)}) collective-permute-start(bf16[64,2048]{1,0:T(8,128)(2,1)S(1)} %get-tuple-element.70), channel_id=1, source_target_pairs={{0,16},{4,20},{8,24},{12,28},{16,0},{20,4},{24,8},{28,12},{1,17},{... | collective-permute-start | bytes 786440 | tf_op jit(solution)/shard_map/ppermute | solution.py:427

commit v5 on v4

--- a/solution.py
+++ b/solution.py
@@ -10,7 +10,7 @@
 from jax.sharding import PartitionSpec as P
 
 LANES = 128
-CHUNKS = 2
+CHUNKS = 1
 VMEM_BYTES = 48 * 1024 * 1024
 
 
@@ -148,7 +148,7 @@
 
 def convolve(pairs, tables):
     blocks, chans, rows, _ = pairs.shape
-    step = min(8, chans)
+    step = min(32, chans)
     outer = blocks * rows // 2
     spec = in_hbm((chans, outer, 2 * LANES), jnp.float32)
     spec_block = pl.BlockSpec((step, outer, 2 * LANES), lambda i: (i, 0, 0))
@@ -175,7 +175,7 @@
 def correlate(pairs, signal, kernel, tables):
     blocks, _, rows, _ = pairs.shape
     chans = signal.shape[0]
-    step = min(8, chans)
+    step = min(16, chans)
     outer = blocks * rows // 2
     spec_block = pl.BlockSpec((step, outer, 2 * LANES), lambda i: (i, 0, 0))
     return pl.pallas_call(
@@ -366,6 +366,47 @@
     )(place.reshape(1), *held_in_hbm(*[out_proj] * len(offsets), grad_output))
 
 
+def project_kernel(core_ref, *refs):
+    *piece_refs, grad_ref, other_ref, mine_ref, rows = refs
+    count, small, _ = mine_ref.shape
+
+    @pl.when(pl.program_id(0) == 0)
+    def _():
+        for place, which in enumerate((1 - core_ref[0], core_ref[0])):
+            first = pl.multiple_of(which * small, small)
+            for slot, piece in enumerate(piece_refs):
+                rows[pl.ds((place * count + slot) * small, small), :] = piece[pl.ds(first, small), :]
+
+    out = lax.dot_general(
+        rows[...], grad_ref[...], (((1,), (1,)), ((), ())), preferred_element_type=jnp.float32
+    )
+    out = short(out).reshape(2, count, small, -1)
+    other_ref[...] = out[0]
+    mine_ref[...] = out[1]
+
+
+def project(pieces, grad_output, core):
+    width, length = grad_output.shape
+    small = pieces[0].shape[0] // 2
+    step = min(1024, width)
+    out_block = pl.BlockSpec((len(pieces), small, step), lambda i, at: (0, 0, i))
+    out = in_hbm((len(pieces), small, width))
+    return pl.pallas_call(
+        project_kernel,
+        grid_spec=pltpu.PrefetchScalarGridSpec(
+            num_scalar_prefetch=1,
+            grid=(width // step,),
+            in_specs=[pl.BlockSpec(pieces[0].shape, lambda i, at: (0, 0))] * len(pieces)
+            + [pl.BlockSpec((step, length), lambda i, at: (i, 0))],
+            out_specs=[out_block, out_block],
+            scratch_shapes=[pltpu.VMEM((2 * len(pieces) * small, length), jnp.bfloat16)],
+        ),
+        out_shape=[out, out],
+        compiler_params=params(),
+        name="project",
+    )(core.reshape(1), *held_in_hbm(*pieces, grad_output))
+
+
 def swaps(count, bit):
     return [(place, place ^ bit) for place in range(count)]
 
@@ -390,35 +431,19 @@
     return [shard, shift(shard, 1), shift(shard, 3)]
 
 
-def gather_between(held):
-    shard, low, high = held
-    return [
-        lax.select_n(lax.axis_index("chan"), shard[cut], high[cut], low[cut], shard[cut])
-        for cut in range(CHUNKS)
-    ]
-
-
-def gather_second(held, passed, cut):
-    if lax.axis_size("chan") != 4:
-        return held
-    shard, low, high = held
-    passed = lax.ppermute(passed[cut], "chan", [(0, 2), (3, 1), (2, 3), (1, 0)])
-    return [shard, low, passed[None], high]
-
-
-def project(pieces, cut, grad_output):
+def both_cores(pieces, grad_output):
+    count, core = lax.axis_size("seq"), lax.axis_index("seq") % 2
+    rows = jnp.stack(pieces)
+    sums = short(
+        jnp.einsum("zct,dt->zcd", rows, grad_output, preferred_element_type=jnp.float32)
+    ).reshape(len(pieces), 2, -1, grad_output.shape[0])
+    got = lax.ppermute(lax.dynamic_index_in_dim(sums, 1 - core, 1, False), "seq", swaps(count, 1))
+    return short(wide(lax.dynamic_index_in_dim(sums, core, 1, False)) + wide(got))
+
+
+def scatter_chips(total):
     count, chips = lax.axis_size("seq"), lax.axis_size("chan")
-    line, place = lax.axis_index("chan"), lax.axis_index("seq")
-    core, chip = place % 2, place // 2
-    rows = jnp.stack([piece[min(cut, len(piece) - 1)] for piece in pieces])
-    rows = rows.reshape(chips, 2, -1, rows.shape[-1])
-
-    def rows_of(which):
-        chosen = lax.dynamic_index_in_dim(rows, which, 1, False)
-        return jnp.einsum("zct,dt->zcd", chosen, grad_output, preferred_element_type=jnp.float32)
-
-    got = lax.ppermute(short(rows_of(1 - core)), "seq", swaps(count, 1))
-    total = short(rows_of(core) + wide(got))
+    line, chip = lax.axis_index("chan"), lax.axis_index("seq") // 2
 
     def block(bit):
         return lax.dynamic_index_in_dim(total, (line - (chip ^ bit)) % chips, 0, False)
@@ -466,16 +491,25 @@
     grad_outer, grad_conv = regard(shares, flag, outer_gate, conv_out)
     grad_conv = grad_conv.reshape(seq_count, owned // 2, 2 * per, LANES)
     corr = correlate(exchange(grad_conv), spec_signal, spec_filter, tables)
-    held = tie(held, corr)
-    passed = gather_between(held) if chan_count == 4 else held
-    pieces = [gather_second(held, passed, cut) for cut in range(CHUNKS)]
-    corr = exchange(tie(corr, passed))
-    pieces = tie(pieces, corr)
-    first = project(pieces[0], 0, grad_output)
-    second = project(pieces[1], 1, grad_output)
-    grads = finish(tie(corr, first[-1]), signal, inner_gate)
-    grad_proj = jnp.concatenate([sum_of(first), sum_of(second)], axis=0)
-    return (grad_outer, *grads, grad_proj)
+    held = [part[0] for part in tie(held, corr)]
+    if chan_count == 4:
+        passed = lax.select_n(line, held[0], held[2], held[1], held[0])
+        middle = lax.ppermute(passed, "chan", [(0, 2), (3, 1), (2, 3), (1, 0)])
+        corr = exchange(tie(corr, passed))
+        held = tie(held, passed)
+        core = lax.axis_index("seq") % 2
+        other, mine = project([held[0], held[1], held[0], held[2]], grad_output, core)
+        middle, other = lax.optimization_barrier((middle, other, corr))[:2]
+        got = lax.ppermute(other, "seq", swaps(seq_count, 1))
+        middle = both_cores([middle], grad_output)
+        total = short(wide(mine) + wide(got))
+        total = lax.dynamic_update_slice(total, middle, (2, 0, 0))
+    else:
+        corr = exchange(corr)
+        total = both_cores(held, grad_output)
+    parts = scatter_chips(total)
+    grads = finish(tie(corr, parts[-1]), signal, inner_gate)
+    return (grad_outer, *grads, sum_of(tie(parts, grads)))
 
 
 def solution(mesh):

time: 145 us -> 139 us (0.959)
  matrix products: 11.1 us -> 3.78 us
  Pallas kernels: 35.9 us -> 43.2 us
  starting transfers between devices: 34.8 us -> 29.7 us
    pallas_call x0 -> x1, Pallas kernels: none -> 8.95 us  [project(): pl.pallas_call(project_kernel, grid_spec=pltpu.PrefetchScalarGridSpec(num...]
    dot_general x4 -> x1, matrix products: 11.1 us -> 3.78 us  [both_cores(): jnp.einsum('zct,dt->zcd', rows, grad_output, preferred_element_type=jnp.f...]
    ppermute x10 -> x6, starting transfers between devices: 9.43 us -> 4.43 us  [the longest x3 3.57 us: scatter_chips(): lax.ppermute(block(bit), 'seq', swaps(count, 2 * bit))]
    ppermute x10 -> x6, waiting for transfers between devices: 26.4 us -> 25.4 us  [the longest x3 19.7 us: scatter_chips(): lax.ppermute(block(bit), 'seq', swaps(count, 2 * bit))]
    convert_element_type x1 -> x2, other arithmetic: 2.5 us -> 3.31 us  [short(): return x.astype(jnp.bfloat16)]
  transfers between devices with their start and end apart: 19 -> 15, of which waited for: 12 -> 10; matrix products, arithmetic and copies ran while one was open for 8% -> 5% of each run, Pallas kernels for 22% -> 28%
where the time goes in v5:
time: 139 us; the launch traced here: 138 us
  waiting for transfers between devices  54.9 us (39%)
  Pallas kernels  43.2 us (31%)
  starting transfers between devices  29.7 us (21%)
  other arithmetic  4.8 us (3%)
  matrix products  3.78 us (3%)
    ppermute x3, waiting for transfers between devices, scatter_chips(): lax.ppermute(block(bit), 'seq', swaps(count, 2 * bit))  19.7 us
    all_to_all x4, starting transfers between devices, exchange(): lax.all_to_all(blocks, 'seq', split_axis=0, concat_axis=0, tiled=True)  16.1 us
    ppermute x4, waiting for transfers between devices, shift(): lax.ppermute(block, 'chan', [(i, (i + by) % count) for i in range(count)])  12 us
    pallas_call x2, Pallas kernels, unproject(): pl.pallas_call(functools.partial(unproject_kernel, len(offsets)), grid_sp...  11.2 us
    all_to_all x4, waiting for transfers between devices, exchange(): lax.all_to_all(blocks, 'seq', split_axis=0, concat_axis=0, tiled=True)  10.8 us
    pallas_call x1, Pallas kernels, project(): pl.pallas_call(project_kernel, grid_spec=pltpu.PrefetchScalarGridSpec(num...  8.95 us
    ppermute x4, starting transfers between devices, shift(): lax.ppermute(block, 'chan', [(i, (i + by) % count) for i in range(count)])  7.65 us
    pallas_call x1, Pallas kernels, correlate(): pl.pallas_call(correlate_kernel, grid=(chans // step,), in_specs=[pl.Bloc...  7.07 us
  transfers between devices with their start and end apart: 15, of which 10 were waited for; matrix products, arithmetic and copies ran while one was open for 5% of the time, Pallas kernels for 28%

profile of v5, /device:TPU:0, one launch (start us, length us, event | category | flops | bytes accessed | tf_op | source)
XLA Modules:
  0.0 138.3 jit_solution(15065618292237595136)
XLA Ops:
  0.6 2.8 %prepare.1 = bf16[256,16,128]{2,1,0:T(8,128)(2,1)} custom-call(bf16[256,1024]{1,0:T(8,128)(2,1)} %gate_ref.5, bf16[256,1024]{1,0:T(8,128)(2,1)} %signal_ref.3, bf16[256,1024]{1,0:T(8,128)(2,1)} %filter_ref.1), custom_call_target="tpu_custom_call" | custom-call | tf_op jit(solution)/shard_map/prepare/pallas_call | solution.py:223
  3.4 5.2 %all-to-all-start = ((bf16[8,32,16,128]{3,2,1,0:T(8,128)(2,1)}), bf16[8,32,16,128]{3,2,1,0:T(8,128)(2,1)S(1)}, u32[]{:S(2)}, u32[]{:S(2)}) async-start(bf16[8,32,16,128]{3,2,1,0:T(8,128)(2,1)} %bitcast.33), calls=%async_computation | async-start | bytes 2097152 | tf_op jit(solution)/shard_map/all_to_all | solution.py:415
  8.6 4.1 %unproject.2 = bf16[256,1024]{1,0:T(8,128)(2,1)} custom-call(s32[1]{0:T(128)} %bitcast.1.place_ref, bf16[1024,2048]{1,0:T(8,128)(2,1)} %refs_2_, bf16[2048,1024]{1,0:T(8,128)(2,1)} %refs_4_.3), custom_call_target="tpu_custom_call" | custom-call | tf_op jit(solution)/shard_map/unproject/pallas_call | solution.py:354
  12.7 1.6 %collective-permute-start = (bf16[256,1024]{1,0:T(8,128)(2,1)}, bf16[256,1024]{1,0:T(8,128)(2,1)S(1)}, u32[]{:S(2)}, u32[]{:S(2)}) collective-permute-start(bf16[256,1024]{1,0:T(8,128)(2,1)} %unproject.2), channel_id=1, source_target_pairs={{2,0},{1,3},{3,2},{0,1},{6,4},{5,7},{7,6},{4,5},{10,8},{9,11},{11,... | collective-permute-start | bytes 1572872 | tf_op jit(solution)/shard_map/ppermute | solution.py:476
  14.3 7.1 %unproject.3 = (bf16[256,1024]{1,0:T(8,128)(2,1)}, bf16[256,1024]{1,0:T(8,128)(2,1)}, bf16[256,1024]{1,0:T(8,128)(2,1)}) custom-call(s32[1]{0:T(128)} %bitcast.1.place_ref, bf16[1024,2048]{1,0:T(8,128)(2,1)} %refs_2_, bf16[1024,2048]{1,0:T(8,128)(2,1)} %refs_2_, bf16[1024,2048]{1,0:T(8,128)(2,1)} %refs_2_, bf16[2048,1024]{1,0:T(8,128)(2,1)} %refs_4_.3), custom_call_target="tpu_custom_call" | custom-call | tf_op jit(solution)/shard_map/unproject/pallas_call | solution.py:354
  21.4 6.7 %collective-permute-done.refs_3_ = bf16[256,1024]{1,0:T(8,128)(2,1)S(1)} collective-permute-done((bf16[256,1024]{1,0:T(8,128)(2,1)}, bf16[256,1024]{1,0:T(8,128)(2,1)S(1)}, u32[]{:S(2)}, u32[]{:S(2)}) %collective-permute-start) | collective-permute-done | bytes 524320 | tf_op jit(solution)/shard_map/ppermute | solution.py:476
  28.1 2.5 %add_convert_fusion.1 = (bf16[256,1024]{1,0:T(8,128)(2,1)}, bf16[256,1024]{1,0:T(8,128)(2,1)}) fusion(bf16[256,1024]{1,0:T(8,128)(2,1)} %get-tuple-element.42, bf16[256,1024]{1,0:T(8,128)(2,1)S(1)} %collective-permute-done.refs_3_, pred[]{:T(512)S(6)} %eq.22, pred[]{:T(512)S(6)} %eq.21, bf16[256,1024]{1,0:T(8,128)(2,1)} %get-tuple-element.41), kind=kLoop, calls=%fused_computation.5 | loop fusion | flops 2621440 | bytes 2621442 | tf_op jit(solution)/shard_map/convert_element_type | solution.py:22
  30.6 0.9 collective-permute-start.1
  31.5 2.9 %collective-permute-start.2 = (bf16[256,1024]{1,0:T(8,128)(2,1)}, bf16[256,1024]{1,0:T(8,128)(2,1)}, u32[]{:S(2)}, u32[]{:S(2)}) collective-permute-start(bf16[256,1024]{1,0:T(8,128)(2,1)} %get-tuple-element.75), channel_id=1, source_target_pairs={{0,3},{1,0},{2,1},{3,2},{4,7},{5,4},{6,5},{7,6},{8,11},{9,8},{10,9... | collective-permute-start | bytes 1572872 | tf_op jit(solution)/shard_map/ppermute | solution.py:424
  34.5 6.1 %convolve.1 = (bf16[8,16,16,128]{3,2,1,0:T(8,128)(2,1)}, f32[32,64,256]{2,1,0:T(8,128)}, f32[32,64,256]{2,1,0:T(8,128)}) custom-call(bf16[8,32,16,128]{3,2,1,0:T(8,128)(2,1)S(1)} %all-to-all-done.pairs_ref, bf16[256,256]{1,0:T(8,128)(2,1)} %constant.89.clone.first_ref, bf16[512,256]{1,0:T(8,128)(2,1)} %constant.90.clone.forward_ref, ...), custom_call_target="tpu_custom_call" | custom-call | tf_op jit(solution)/shard_map/convolve/pallas_call | solution.py:155
  40.5 3.8 %all-to-all-start.1 = ((bf16[8,16,16,128]{3,2,1,0:T(8,128)(2,1)}), bf16[8,16,16,128]{3,2,1,0:T(8,128)(2,1)S(1)}, u32[]{:S(2)}, u32[]{:S(2)}) async-start(bf16[8,16,16,128]{3,2,1,0:T(8,128)(2,1)} %get-tuple-element.44), calls=%async_computation.1 | async-start | bytes 1048576 | tf_op jit(solution)/shard_map/all_to_all | solution.py:415
  44.4 3.1 %collective-permute-done.1.refs_1_ = bf16[256,1024]{1,0:T(8,128)(2,1)S(1)} collective-permute-done((bf16[256,1024]{1,0:T(8,128)(2,1)}, bf16[256,1024]{1,0:T(8,128)(2,1)S(1)}, u32[]{:S(2)}, u32[]{:S(2)}) %collective-permute-start.1) | collective-permute-done | bytes 524320 | tf_op jit(solution)/shard_map/ppermute | solution.py:424
  47.5 8.8 %collective-permute-done.2.refs_2_ = bf16[256,1024]{1,0:T(8,128)(2,1)} collective-permute-done((bf16[256,1024]{1,0:T(8,128)(2,1)}, bf16[256,1024]{1,0:T(8,128)(2,1)}, u32[]{:S(2)}, u32[]{:S(2)}) %collective-permute-start.2) | collective-permute-done | bytes 524320 | tf_op jit(solution)/shard_map/ppermute | solution.py:424
  56.3 1.2 mix.1
  57.6 1.8 %collective-permute-start.3 = (bf16[1,256,1024]{2,1,0:T(8,128)(2,1)}, bf16[1,256,1024]{2,1,0:T(8,128)(2,1)S(1)}, u32[]{:S(2)}, u32[]{:S(2)}) collective-permute-start(bf16[1,256,1024]{2,1,0:T(8,128)(2,1)} %get-tuple-element.52), channel_id=1, source_target_pairs={{0,1},{1,2},{2,3},{3,0},{4,5},{5,6},{6,7},{7,4},{8,9},{9,10},{10,1... | collective-permute-start | bytes 1572872 | tf_op jit(solution)/shard_map/ppermute | solution.py:424
  59.4 2.0 %collective-permute-start.4 = (bf16[1,256,1024]{2,1,0:T(8,128)(2,1)}, bf16[1,256,1024]{2,1,0:T(8,128)(2,1)S(1)}, u32[]{:S(2)}, u32[]{:S(2)}) collective-permute-start(bf16[1,256,1024]{2,1,0:T(8,128)(2,1)} %get-tuple-element.52), channel_id=1, source_target_pairs={{0,3},{1,0},{2,1},{3,2},{4,7},{5,4},{6,5},{7,6},{8,11},{9,8},{10,9... | collective-permute-start | bytes 1572872 | tf_op jit(solution)/shard_map/ppermute | solution.py:424
  61.4 2.7 %regard.1 = (bf16[256,1024]{1,0:T(8,128)(2,1)}, bf16[128,16,128]{2,1,0:T(8,128)(2,1)}) custom-call(s32[1]{0:T(128)} %bitcast.flag_ref, bf16[256,1024]{1,0:T(8,128)(2,1)S(1)} %copy-done.1, bf16[256,1024]{1,0:T(8,128)(2,1)S(1)} %collective-permute-done.1.refs_1_, bf16[256,1024]{1,0:T(8,128)(2,1)} %collective-permute-done.2.refs_2_, ...), custom_call_target="tpu_custom_call" | custom-call | tf_op jit(solution)/shard_map/regard/pallas_call | solution.py:287
  64.1 3.5 %all-to-all-start.2 = ((bf16[8,16,16,128]{3,2,1,0:T(8,128)(2,1)}), bf16[8,16,16,128]{3,2,1,0:T(8,128)(2,1)S(1)}, u32[]{:S(2)}, u32[]{:S(2)}) async-start(bf16[8,16,16,128]{3,2,1,0:T(8,128)(2,1)} %bitcast.38), calls=%async_computation.2 | async-start | bytes 1048576 | tf_op jit(solution)/shard_map/all_to_all | solution.py:415
  67.6 9.7 %all-to-all-done.2.pairs_ref = bf16[8,16,16,128]{3,2,1,0:T(8,128)(2,1)S(1)} async-done(((bf16[8,16,16,128]{3,2,1,0:T(8,128)(2,1)}), bf16[8,16,16,128]{3,2,1,0:T(8,128)(2,1)S(1)}, u32[]{:S(2)}, u32[]{:S(2)}) %all-to-all-start.2) | async-done | bytes 524320 | tf_op jit(solution)/shard_map/all_to_all | solution.py:415
  77.3 7.1 %correlate.1 = bf16[8,32,16,128]{3,2,1,0:T(8,128)(2,1)} custom-call(bf16[8,16,16,128]{3,2,1,0:T(8,128)(2,1)S(1)} %all-to-all-done.2.pairs_ref, f32[32,64,256]{2,1,0:T(8,128)} %get-tuple-element.49.signal_ref, f32[32,64,256]{2,1,0:T(8,128)} %get-tuple-element.50.filter_ref, bf16[256,256]{1,0:T(8,128)(2,1)} %constant.89.clone.first_ref, ...), custom_call_target="tpu_custom_call" | custom-call | tf_op jit(solution)/shard_map/correlate/pallas_call | solution.py:181
  85.3 3.6 %all-to-all-start.3 = ((bf16[8,32,16,128]{3,2,1,0:T(8,128)(2,1)}), bf16[8,32,16,128]{3,2,1,0:T(8,128)(2,1)S(1)}, u32[]{:S(2)}, u32[]{:S(2)}) async-start(bf16[8,32,16,128]{3,2,1,0:T(8,128)(2,1)} %correlate.1), calls=%async_computation.3 | async-start | bytes 2097152 | tf_op jit(solution)/shard_map/all_to_all | solution.py:415
  89.2 9.0 %project.1 = (bf16[4,128,2048]{2,1,0:T(8,128)(2,1)}, bf16[4,128,2048]{2,1,0:T(8,128)(2,1)}) custom-call(s32[1]{0:T(128)} %bitcast.8.core_ref, bf16[256,1024]{1,0:T(8,128)(2,1)} %bitcast.31, bf16[256,1024]{1,0:T(8,128)(2,1)} %bitcast.34, bf16[256,1024]{1,0:T(8,128)(2,1)} %bitcast.32, bf16[256,1024]{1,0:T(8,128)(2,1)} %bitcast.35, bf16[2048,1024]{1,0:T(8,128)(2,1)} %refs_4_.3), custom_call_target="tpu_custom_call" | custom-call | tf_op jit(solution)/shard_map/project/pallas_call | solution.py:394
  98.1 5.0 %collective-permute-done.5 = bf16[256,1024]{1,0:T(8,128)(2,1)S(1)} collective-permute-done((bf16[256,1024]{1,0:T(8,128)(2,1)S(1)}, bf16[256,1024]{1,0:T(8,128)(2,1)S(1)}, u32[]{:S(2)}, u32[]{:S(2)}) %collective-permute-start.5) | collective-permute-done | bytes 524320 | tf_op jit(solution)/shard_map/ppermute | solution.py:497
  103.1 1.1 all-to-all-done.3
  104.2 3.8 %convolution_convert_fusion = bf16[256,2048]{1,0:T(8,128)(2,1)S(1)} fusion(bf16[256,1024]{1,0:T(8,128)(2,1)} %copy-done.6, bf16[2048,1024]{1,0:T(8,128)(2,1)} %refs_4_.3), kind=kOutput, calls=%fused_computation.1 | convolution fusion | flops 1074266112 | bytes 5767168 | tf_op jit(solution)/shard_map/zct,dt->zcd/dot_general | solution.py:438
  108.7 0.8 add_convert_fusion
  109.5 0.7 collective-permute-done.7
  110.6 2.4 %collective-permute-start.8 = (bf16[128,2048]{1,0:T(8,128)(2,1)S(1)}, bf16[128,2048]{1,0:T(8,128)(2,1)S(1)}, u32[]{:S(2)}, u32[]{:S(2)}) collective-permute-start(bf16[128,2048]{1,0:T(8,128)(2,1)S(1)} %get-tuple-element.73), channel_id=1, source_target_pairs={{0,24},{4,28},{8,16},{12,20},{16,8},{20,12},{24,0},{28,4},{1,25},{... | collective-permute-start | bytes 1572872 | tf_op jit(solution)/shard_map/ppermute | solution.py:452
  114.1 3.2 %finish.1 = (bf16[256,1024]{1,0:T(8,128)(2,1)}, bf16[256,1024]{1,0:T(8,128)(2,1)}, f32[256,1024]{1,0:T(8,128)}) custom-call(bf16[256,16,128]{2,1,0:T(8,128)(2,1)S(1)} %bitcast.29, bf16[256,1024]{1,0:T(8,128)(2,1)} %signal_ref.3, bf16[256,1024]{1,0:T(8,128)(2,1)} %gate_ref.5), custom_call_target="tpu_custom_call" | custom-call | tf_op jit(solution)/shard_map/finish/pallas_call | solution.py:319
  117.3 9.0 %collective-permute-done.8 = bf16[128,2048]{1,0:T(8,128)(2,1)S(1)} collective-permute-done((bf16[128,2048]{1,0:T(8,128)(2,1)S(1)}, bf16[128,2048]{1,0:T(8,128)(2,1)S(1)}, u32[]{:S(2)}, u32[]{:S(2)}) %collective-permute-start.8) | collective-permute-done | bytes 524320 | tf_op jit(solution)/shard_map/ppermute | solution.py:452
  126.3 10.6 %collective-permute-done.9 = bf16[128,2048]{1,0:T(8,128)(2,1)S(1)} collective-permute-done((bf16[128,2048]{1,0:T(8,128)(2,1)S(1)}, bf16[128,2048]{1,0:T(8,128)(2,1)S(1)}, u32[]{:S(2)}, u32[]{:S(2)}) %collective-permute-start.9) | collective-permute-done | bytes 524320 | tf_op jit(solution)/shard_map/ppermute | solution.py:452
  137.0 1.3 convert_add_fusion.1
  (29 shorter events, 3.5 us)
Async XLA Ops:
  3.4 31.0 %all-to-all-start = ((bf16[8,32,16,128]{3,2,1,0:T(8,128)(2,1)}), bf16[8,32,16,128]{3,2,1,0:T(8,128)(2,1)S(1)}, u32[]{:S(2)}, u32[]{:S(2)}) async-start(bf16[8,32,16,128]{3,2,1,0:T(8,128)(2,1)} %bitcast.33), calls=%async_computation | async-start | bytes 2097152 | tf_op jit(solution)/shard_map/all_to_all | solution.py:415
  12.7 15.4 %collective-permute-start = (bf16[256,1024]{1,0:T(8,128)(2,1)}, bf16[256,1024]{1,0:T(8,128)(2,1)S(1)}, u32[]{:S(2)}, u32[]{:S(2)}) collective-permute-start(bf16[256,1024]{1,0:T(8,128)(2,1)} %unproject.2), channel_id=1, source_target_pairs={{2,0},{1,3},{3,2},{0,1},{6,4},{5,7},{7,6},{4,5},{10,8},{9,11},{11,... | collective-permute-start | bytes 1572872 | tf_op jit(solution)/shard_map/ppermute | solution.py:476
  30.6 25.7 %copy-start = (bf16[256,1024]{1,0:T(8,128)(2,1)S(1)}, bf16[256,1024]{1,0:T(8,128)(2,1)}, u32[]{:S(2)}) copy-start(bf16[256,1024]{1,0:T(8,128)(2,1)} %refs_4_.2) | copy-start | bytes 1572868
  30.6 30.8 %copy-start.1 = (bf16[256,1024]{1,0:T(8,128)(2,1)S(1)}, bf16[256,1024]{1,0:T(8,128)(2,1)}, u32[]{:S(2)}) copy-start(bf16[256,1024]{1,0:T(8,128)(2,1)} %get-tuple-element.40.refs_0_) | copy-start | bytes 1572868
  30.6 16.9 %collective-permute-start.1 = (bf16[256,1024]{1,0:T(8,128)(2,1)}, bf16[256,1024]{1,0:T(8,128)(2,1)S(1)}, u32[]{:S(2)}, u32[]{:S(2)}) collective-permute-start(bf16[256,1024]{1,0:T(8,128)(2,1)} %get-tuple-element.76), channel_id=1, source_target_pairs={{0,1},{1,2},{2,3},{3,0},{4,5},{5,6},{6,7},{7,4},{8,9},{9,10},{10,1... | collective-permute-start | bytes 1572872 | tf_op jit(solution)/shard_map/ppermute | solution.py:424
  31.5 24.8 %collective-permute-start.2 = (bf16[256,1024]{1,0:T(8,128)(2,1)}, bf16[256,1024]{1,0:T(8,128)(2,1)}, u32[]{:S(2)}, u32[]{:S(2)}) collective-permute-start(bf16[256,1024]{1,0:T(8,128)(2,1)} %get-tuple-element.75), channel_id=1, source_target_pairs={{0,3},{1,0},{2,1},{3,2},{4,7},{5,4},{6,5},{7,6},{8,11},{9,8},{10,9... | collective-permute-start | bytes 1572872 | tf_op jit(solution)/shard_map/ppermute | solution.py:424
  40.5 15.8 %all-to-all-start.1 = ((bf16[8,16,16,128]{3,2,1,0:T(8,128)(2,1)}), bf16[8,16,16,128]{3,2,1,0:T(8,128)(2,1)S(1)}, u32[]{:S(2)}, u32[]{:S(2)}) async-start(bf16[8,16,16,128]{3,2,1,0:T(8,128)(2,1)} %get-tuple-element.44), calls=%async_computation.1 | async-start | bytes 1048576 | tf_op jit(solution)/shard_map/all_to_all | solution.py:415
  57.6 26.8 %collective-permute-start.3 = (bf16[1,256,1024]{2,1,0:T(8,128)(2,1)}, bf16[1,256,1024]{2,1,0:T(8,128)(2,1)S(1)}, u32[]{:S(2)}, u32[]{:S(2)}) collective-permute-start(bf16[1,256,1024]{2,1,0:T(8,128)(2,1)} %get-tuple-element.52), channel_id=1, source_target_pairs={{0,1},{1,2},{2,3},{3,0},{4,5},{5,6},{6,7},{7,4},{8,9},{9,10},{10,1... | collective-permute-start | bytes 1572872 | tf_op jit(solution)/shard_map/ppermute | solution.py:424
  59.4 25.0 %collective-permute-start.4 = (bf16[1,256,1024]{2,1,0:T(8,128)(2,1)}, bf16[1,256,1024]{2,1,0:T(8,128)(2,1)S(1)}, u32[]{:S(2)}, u32[]{:S(2)}) collective-permute-start(bf16[1,256,1024]{2,1,0:T(8,128)(2,1)} %get-tuple-element.52), channel_id=1, source_target_pairs={{0,3},{1,0},{2,1},{3,2},{4,7},{5,4},{6,5},{7,6},{8,11},{9,8},{10,9... | collective-permute-start | bytes 1572872 | tf_op jit(solution)/shard_map/ppermute | solution.py:424
  64.1 13.2 %all-to-all-start.2 = ((bf16[8,16,16,128]{3,2,1,0:T(8,128)(2,1)}), bf16[8,16,16,128]{3,2,1,0:T(8,128)(2,1)S(1)}, u32[]{:S(2)}, u32[]{:S(2)}) async-start(bf16[8,16,16,128]{3,2,1,0:T(8,128)(2,1)} %bitcast.38), calls=%async_computation.2 | async-start | bytes 1048576 | tf_op jit(solution)/shard_map/all_to_all | solution.py:415
  77.3 7.1 %copy-start.2 = (bf16[1,256,1024]{2,1,0:T(8,128)(2,1)S(1)}, bf16[1,256,1024]{2,1,0:T(8,128)(2,1)}, u32[]{:S(2)}) copy-start(bf16[1,256,1024]{2,1,0:T(8,128)(2,1)} %get-tuple-element.52) | copy-start | bytes 1572868
  84.4 0.8 copy-start.4
  84.4 0.9 copy-start.5
  85.3 18.9 %all-to-all-start.3 = ((bf16[8,32,16,128]{3,2,1,0:T(8,128)(2,1)}), bf16[8,32,16,128]{3,2,1,0:T(8,128)(2,1)S(1)}, u32[]{:S(2)}, u32[]{:S(2)}) async-start(bf16[8,32,16,128]{3,2,1,0:T(8,128)(2,1)} %correlate.1), calls=%async_computation.3 | async-start | bytes 2097152 | tf_op jit(solution)/shard_map/all_to_all | solution.py:415
  88.9 14.2 %collective-permute-start.5 = (bf16[256,1024]{1,0:T(8,128)(2,1)S(1)}, bf16[256,1024]{1,0:T(8,128)(2,1)S(1)}, u32[]{:S(2)}, u32[]{:S(2)}) collective-permute-start(bf16[256,1024]{1,0:T(8,128)(2,1)S(1)} %select_select_fusion), channel_id=1, source_target_pairs={{0,2},{3,1},{2,3},{1,0},{4,6},{7,5},{6,7},{5,4},{8,10},{11,9},{10,... | collective-permute-start | bytes 1572872 | tf_op jit(solution)/shard_map/ppermute | solution.py:497
  103.1 1.1 copy-start.6
  104.2 4.4 %collective-permute-start.6 = (bf16[4,128,2048]{2,1,0:T(8,128)(2,1)}, bf16[4,128,2048]{2,1,0:T(8,128)(2,1)S(1)}, u32[]{:S(2)}, u32[]{:S(2)}) collective-permute-start(bf16[4,128,2048]{2,1,0:T(8,128)(2,1)} %get-tuple-element.61), channel_id=1, source_target_pairs={{0,4},{4,0},{8,12},{12,8},{16,20},{20,16},{24,28},{28,24},{1,5},{5... | collective-permute-start | bytes 6291464 | tf_op jit(solution)/shard_map/ppermute | solution.py:503
  104.2 4.4 %copy-start.3 = (bf16[4,128,2048]{2,1,0:T(8,128)(2,1)S(1)}, bf16[4,128,2048]{2,1,0:T(8,128)(2,1)}, u32[]{:S(2)}) copy-start(bf16[4,128,2048]{2,1,0:T(8,128)(2,1)} %get-tuple-element.59) | copy-start | bytes 6291460
  108.1 2.1 %collective-permute-start.7 = (bf16[1,128,2048]{2,1,0:T(8,128)(2,1)S(1)}, bf16[1,128,2048]{2,1,0:T(8,128)(2,1)S(1)}, u32[]{:S(2)}, u32[]{:S(2)}) collective-permute-start(bf16[1,128,2048]{2,1,0:T(8,128)(2,1)S(1)} %dynamic-slice_bitcast_fusion.4), channel_id=1, source_target_pairs={{0,4},{4,0},{8,12},{12,8},{16,20},{20,16},{24,28},{28,24},{1,5},{5... | collective-permute-start | bytes 1572872 | tf_op jit(solution)/shard_map/ppermute | solution.py:440
  110.6 15.8 %collective-permute-start.8 = (bf16[128,2048]{1,0:T(8,128)(2,1)S(1)}, bf16[128,2048]{1,0:T(8,128)(2,1)S(1)}, u32[]{:S(2)}, u32[]{:S(2)}) collective-permute-start(bf16[128,2048]{1,0:T(8,128)(2,1)S(1)} %get-tuple-element.73), channel_id=1, source_target_pairs={{0,24},{4,28},{8,16},{12,20},{16,8},{20,12},{24,0},{28,4},{1,25},{... | collective-permute-start | bytes 1572872 | tf_op jit(solution)/shard_map/ppermute | solution.py:452
  112.9 24.0 %collective-permute-start.9 = (bf16[128,2048]{1,0:T(8,128)(2,1)S(1)}, bf16[128,2048]{1,0:T(8,128)(2,1)S(1)}, u32[]{:S(2)}, u32[]{:S(2)}) collective-permute-start(bf16[128,2048]{1,0:T(8,128)(2,1)S(1)} %get-tuple-element.72), channel_id=1, source_target_pairs={{0,8},{4,12},{8,0},{12,4},{16,24},{20,28},{24,16},{28,20},{1,9},{5... | collective-permute-start | bytes 1572872 | tf_op jit(solution)/shard_map/ppermute | solution.py:452
  113.5 23.5 %collective-permute-start.10 = (bf16[128,2048]{1,0:T(8,128)(2,1)S(1)}, bf16[128,2048]{1,0:T(8,128)(2,1)S(1)}, u32[]{:S(2)}, u32[]{:S(2)}) collective-permute-start(bf16[128,2048]{1,0:T(8,128)(2,1)S(1)} %get-tuple-element.71), channel_id=1, source_target_pairs={{0,16},{4,20},{8,24},{12,28},{16,0},{20,4},{24,8},{28,12},{1,17},{... | collective-permute-start | bytes 1572872 | tf_op jit(solution)/shard_map/ppermute | solution.py:452

commit v6 on v5

--- a/solution.py
+++ b/solution.py
@@ -10,7 +10,6 @@
 from jax.sharding import PartitionSpec as P
 
 LANES = 128
-CHUNKS = 1
 VMEM_BYTES = 48 * 1024 * 1024
 
 
@@ -232,71 +231,46 @@
     )(*held_in_hbm(inner_gate, signal, long_filter))
 
 
-def mix_kernel(conv_ref, gate_ref, *refs):
-    mixed_ref, out_ref, lines = refs
+def mix_kernel(flag_ref, conv_ref, gate_ref, *refs):
+    *share_refs, mixed_ref, outer_ref, grad_ref, lines, grads = refs
     rows, length = gate_ref.shape
     per = length // LANES
     lines[...] = wide(conv_ref[...].reshape(rows * per, LANES))
-    small = rows // CHUNKS
     for lane in range(per):
         cols = slice(lane * LANES, (lane + 1) * LANES)
         conv = lines[pl.ds(lane, rows, stride=per), :]
-        out_ref[:, cols] = short(conv)
-        mixed = short(conv * wide(gate_ref[:, cols]))
-        for cut in range(CHUNKS):
-            mixed_ref[cut, :, cols] = mixed[cut * small : (cut + 1) * small]
-
-
-def mix(conv, outer_gate):
+        gate = wide(gate_ref[:, cols])
+        mixed_ref[:, cols] = short(conv * gate)
+        grad_mix = wide(share_refs[0][:, cols])
+        for ref in share_refs[1:-1]:
+            grad_mix = grad_mix + wide(ref[:, cols])
+        last = wide(share_refs[-1][:, cols])
+        grad_mix = grad_mix + jnp.where(flag_ref[0] != 0, last, jnp.zeros_like(last))
+        outer_ref[:, cols] = short(grad_mix * conv)
+        grads[pl.ds(lane, rows, stride=per), :] = grad_mix * gate
+    grad_ref[...] = short(grads[...]).reshape(grad_ref.shape)
+
+
+def mix(conv, outer_gate, shares, flag):
     rows, length = outer_gate.shape
     per = length // LANES
     conv = conv.reshape(rows * per // 16, 16, LANES)
     step = rows // 2
-    token_rows = pl.BlockSpec((step, length), lambda i: (i, 0))
-    cut_rows = pl.BlockSpec((CHUNKS, step // CHUNKS, length), lambda i: (0, i, 0))
+    token_rows = pl.BlockSpec((step, length), lambda i, at: (i, 0))
+    lane_rows = pl.BlockSpec((step * per // 16, 16, LANES), lambda i, at: (i, 0, 0))
     return pl.pallas_call(
         mix_kernel,
-        grid=(2,),
-        in_specs=[pl.BlockSpec((step * per // 16, 16, LANES), lambda i: (i, 0, 0)), token_rows],
-        out_specs=[cut_rows, token_rows],
-        out_shape=[in_hbm((CHUNKS, rows // CHUNKS, length)), in_hbm((rows, length))],
-        scratch_shapes=[pltpu.VMEM((step * per, LANES), jnp.float32)],
-        compiler_params=params(),
-        name="mix",
-    )(conv, outer_gate)
-
-
-def regard_kernel(flag_ref, *refs):
-    *share_refs, gate_ref, conv_ref, outer_ref, grad_ref, lines = refs
-    per = gate_ref.shape[1] // LANES
-    grad_mix = wide(share_refs[0][...])
-    for ref in share_refs[1:-1]:
-        grad_mix = grad_mix + wide(ref[...])
-    last = wide(share_refs[-1][...])
-    grad_mix = grad_mix + jnp.where(flag_ref[0] != 0, last, jnp.zeros_like(last))
-    outer_ref[...] = short(grad_mix * wide(conv_ref[...]))
-    spread_lanes(lines, grad_mix * wide(gate_ref[...]), 0, per)
-    grad_ref[...] = short(lines[...]).reshape(grad_ref.shape)
-
-
-def regard(shares, flag, outer_gate, conv_out):
-    rows, length = outer_gate.shape
-    per = length // LANES
-    step = rows // 2
-    block = pl.BlockSpec((step, length), lambda i, at: (i, 0))
-    return pl.pallas_call(
-        regard_kernel,
         grid_spec=pltpu.PrefetchScalarGridSpec(
             num_scalar_prefetch=1,
             grid=(2,),
-            in_specs=[block] * (len(shares) + 2),
-            out_specs=[block, pl.BlockSpec((step * per // 16, 16, LANES), lambda i, at: (i, 0, 0))],
-            scratch_shapes=[pltpu.VMEM((step * per, LANES), jnp.float32)],
+            in_specs=[lane_rows, token_rows] + [token_rows] * len(shares),
+            out_specs=[token_rows, token_rows, lane_rows],
+            scratch_shapes=[pltpu.VMEM((step * per, LANES), jnp.float32)] * 2,
         ),
-        out_shape=[in_hbm((rows, length)), in_hbm((rows * per // 16, 16, LANES))],
+        out_shape=[in_hbm((rows, length))] * 2 + [in_hbm((rows * per // 16, 16, LANES))],
         compiler_params=params(),
-        name="regard",
-    )(flag.astype(jnp.int32).reshape(1), *shares, *held_in_hbm(outer_gate, conv_out))
+        name="mix",
+    )(flag.astype(jnp.int32).reshape(1), conv, outer_gate, *shares)
 
 
 def finish_kernel(corr_ref, signal_ref, gate_ref, inner_ref, signal_out_ref, filter_ref, lines):
@@ -329,9 +303,10 @@
     )(corr.reshape(rows, 2 * per, LANES), *held_in_hbm(signal, inner_gate))
 
 
-def unproject_kernel(count, place_ref, *refs):
+def unproject_kernel(count, add_from, place_ref, *refs):
     rows, width = refs[0].shape
     grad_ref, weights = refs[count], refs[-1]
+    out_refs = refs[-1 - count : -1]
 
     @pl.when(pl.program_id(0) == 0)
     def _():
@@ -340,10 +315,14 @@
 
     out = short(mxu(weights[...], grad_ref[...]))
     for row in range(count):
-        refs[count + 1 + row][...] = out[row * rows : (row + 1) * rows]
-
-
-def unproject(out_proj, grad_output, offsets, place, count):
+        part = out[row * rows : (row + 1) * rows]
+        if add_from is not None:
+            more = wide(refs[count + 1][...])
+            part = short(wide(part) + jnp.where(place_ref[0] == add_from[row], more, jnp.zeros_like(more)))
+        out_refs[row][...] = part
+
+
+def unproject(out_proj, grad_output, offsets, place, count, more=None, add_from=None):
     width, length = grad_output.shape
     rows = out_proj.shape[0] // count
     step = 512
@@ -351,19 +330,24 @@
         pl.BlockSpec((rows, width), lambda i, at, by=by: (lax.rem(at[0] + by, count), 0))
         for by in offsets
     ]
-    return pl.pallas_call(
-        functools.partial(unproject_kernel, len(offsets)),
+    out_block = pl.BlockSpec((rows, step), lambda i, at: (0, i))
+    extra = [] if more is None else [more]
+    return pl.pallas_call(
+        functools.partial(unproject_kernel, len(offsets), add_from),
         grid_spec=pltpu.PrefetchScalarGridSpec(
             num_scalar_prefetch=1,
             grid=(length // step,),
-            in_specs=in_specs + [pl.BlockSpec((width, step), lambda i, at: (0, i))],
-            out_specs=[pl.BlockSpec((rows, step), lambda i, at: (0, i))] * len(offsets),
+            in_specs=in_specs
+            + [pl.BlockSpec((width, step), lambda i, at: (0, i))]
+            + [out_block] * len(extra),
+            out_specs=[out_block] * len(offsets),
             scratch_shapes=[pltpu.VMEM((len(offsets) * rows, width), jnp.bfloat16)],
         ),
         out_shape=[in_hbm((rows, length))] * len(offsets),
         compiler_params=params(),
+        cost_estimate=pl.CostEstimate(flops=40 * 10**9, bytes_accessed=10**8, transcendentals=0),
         name="unproject",
-    )(place.reshape(1), *held_in_hbm(*[out_proj] * len(offsets), grad_output))
+    )(place.reshape(1), *held_in_hbm(*[out_proj] * len(offsets), grad_output), *extra)
 
 
 def project_kernel(core_ref, *refs):
@@ -404,7 +388,7 @@
         out_shape=[out, out],
         compiler_params=params(),
         name="project",
-    )(core.reshape(1), *held_in_hbm(*pieces, grad_output))
+    )(core.reshape(1), *pieces, *held_in_hbm(grad_output))
 
 
 def swaps(count, bit):
@@ -467,31 +451,33 @@
     line = lax.axis_index("chan")
     tables = [jnp.asarray(t) for t in dft_tables(block_len * seq_count, seq_count)]
 
-    pair = prepare(inner_gate, signal, long_filter).reshape(seq_count, owned, 2 * per, LANES)
-    sent = exchange(pair)
-    weights = tie(out_proj, pair)
     if chan_count == 4:
-        far = unproject(weights, grad_output, [2], line, chan_count)[0]
-        near = unproject(tie(weights, far), grad_output, [0, 1, 3], line, chan_count)
+        far = unproject(out_proj, grad_output, [2], line, chan_count)[0]
+        pair = prepare(inner_gate, signal, tie(long_filter, far))
+        pair = pair.reshape(seq_count, owned, 2 * per, LANES)
         far = lax.ppermute(far, "chan", [(2, 0), (1, 3), (3, 2), (0, 1)])
-        none = jnp.zeros_like(far)
-        rising = short(wide(near[1]) + wide(jnp.where(line == 1, far, none)))
-        falling = short(wide(near[2]) + wide(jnp.where(line == 2, far, none)))
-        sent = tie(sent, rising, falling)
-        up, down = shift(rising, 1), shift(falling, 3)
-        shares, flag = [near[0], up, down, far], (line == 0) | (line == 3)
+        sent = exchange(pair)
+        near = unproject(tie(out_proj, pair), grad_output, [1, 3], line, chan_count, far, [1, 2])
+        sent = tie(sent, *near)
+        shares = [shift(near[0], 1), shift(near[1], 3), far]
+        flag = (line == 0) | (line == 3)
     else:
-        blocks = unproject(weights, grad_output, list(range(chan_count)), line, chan_count)
-        shares = [blocks[0]] + [shift(block, by) for by, block in enumerate(blocks) if by > 0]
+        pair = prepare(inner_gate, signal, long_filter)
+        pair = pair.reshape(seq_count, owned, 2 * per, LANES)
+        sent = exchange(pair)
+        offsets = list(range(1, chan_count))
+        blocks = unproject(out_proj, grad_output, offsets, line, chan_count)
+        shares = [shift(block, by) for by, block in zip(offsets, blocks)]
         flag = line >= 0
 
     conv, spec_signal, spec_filter = convolve(sent, tables)
-    mixed, conv_out = mix(tie(exchange(conv), *shares), outer_gate)
+    own = unproject(tie(out_proj, conv), grad_output, [0], line, chan_count)
+    shares = [*held_in_hbm(*own), *shares]
+    mixed, grad_outer, grad_conv = mix(exchange(conv), outer_gate, shares, flag)
     held = gather_first(mixed)
-    grad_outer, grad_conv = regard(shares, flag, outer_gate, conv_out)
     grad_conv = grad_conv.reshape(seq_count, owned // 2, 2 * per, LANES)
     corr = correlate(exchange(grad_conv), spec_signal, spec_filter, tables)
-    held = [part[0] for part in tie(held, corr)]
+    held = tie(held, corr)
     if chan_count == 4:
         passed = lax.select_n(line, held[0], held[2], held[1], held[0])
         middle = lax.ppermute(passed, "chan", [(0, 2), (3, 1), (2, 3), (1, 0)])

time: 139 us -> 134 us (0.964)
  waiting for transfers between devices: 54.9 us -> 52.1 us
  other arithmetic: 4.8 us -> 2.29 us
    ppermute x4, waiting for transfers between devices: 12 us -> 8.28 us  [shift(): lax.ppermute(block, 'chan', [(i, (i + by) % count) for i in range(count)])]
    convert_element_type x2 -> x1, other arithmetic: 3.31 us -> 0.8 us  [short(): return x.astype(jnp.bfloat16)]
    pallas_call x4, Pallas kernels: 15.1 us -> 16.8 us  [the longest x3 13.8 us: unproject(): pl.pallas_call(functools.partial(unproject_kernel, len(offsets), add_from...]
    ppermute x1, starting transfers between devices: 1.58 us -> 3.02 us  [body(): far = lax.ppermute(far, 'chan', [(2, 0), (1, 3), (3, 2), (0, 1)])]
  transfers between devices with their start and end apart: 15 -> 15, of which waited for: 10 -> 10; matrix products, arithmetic and copies ran while one was open for 5% -> 3% of each run, Pallas kernels for 28% -> 27%
where the time goes in v6:
time: 134 us; the launch traced here: 133 us
  waiting for transfers between devices  52.1 us (39%)
  Pallas kernels  43.7 us (33%)
  starting transfers between devices  30.6 us (23%)
  matrix products  3.78 us (3%)
  other arithmetic  2.29 us (2%)
    ppermute x3, waiting for transfers between devices, scatter_chips(): lax.ppermute(block(bit), 'seq', swaps(count, 2 * bit))  19.7 us
    all_to_all x4, starting transfers between devices, exchange(): lax.all_to_all(blocks, 'seq', split_axis=0, concat_axis=0, tiled=True)  15.2 us
    pallas_call x3, Pallas kernels, unproject(): pl.pallas_call(functools.partial(unproject_kernel, len(offsets), add_from...  13.8 us
    all_to_all x4, waiting for transfers between devices, exchange(): lax.all_to_all(blocks, 'seq', split_axis=0, concat_axis=0, tiled=True)  10.7 us
    ppermute x4, waiting for transfers between devices, shift(): lax.ppermute(block, 'chan', [(i, (i + by) % count) for i in range(count)])  8.28 us
    pallas_call x1, Pallas kernels, project(): pl.pallas_call(project_kernel, grid_spec=pltpu.PrefetchScalarGridSpec(num...  7.74 us
    ppermute x4, starting transfers between devices, shift(): lax.ppermute(block, 'chan', [(i, (i + by) % count) for i in range(count)])  7.65 us
    pallas_call x1, Pallas kernels, correlate(): pl.pallas_call(correlate_kernel, grid=(chans // step,), in_specs=[pl.Bloc...  7.07 us
  transfers between devices with their start and end apart: 15, of which 10 were waited for; matrix products, arithmetic and copies ran while one was open for 3% of the time, Pallas kernels for 27%

profile of v6, /device:TPU:0, one launch (start us, length us, event | category | flops | bytes accessed | tf_op | source)
XLA Modules:
  0.0 133.4 jit_solution(14764281794691101469)
XLA Ops:
  0.6 4.1 %unproject.3 = bf16[256,1024]{1,0:T(8,128)(2,1)} custom-call(s32[1]{0:T(128)} %bitcast.1.place_ref, bf16[1024,2048]{1,0:T(8,128)(2,1)} %refs_0_.3, bf16[2048,1024]{1,0:T(8,128)(2,1)} %refs_4_.1), custom_call_target="tpu_custom_call" | custom-call | flops 40000000000 | bytes 100000000 | tf_op jit(solution)/shard_map/unproject/pallas_call | solution.py:335
  4.7 3.0 %collective-permute-start = (bf16[256,1024]{1,0:T(8,128)(2,1)}, bf16[256,1024]{1,0:T(8,128)(2,1)S(1)}, u32[]{:S(2)}, u32[]{:S(2)}) collective-permute-start(bf16[256,1024]{1,0:T(8,128)(2,1)} %unproject.3), channel_id=1, source_target_pairs={{2,0},{1,3},{3,2},{0,1},{6,4},{5,7},{7,6},{4,5},{10,8},{9,11},{11,... | collective-permute-start | bytes 1572872 | tf_op jit(solution)/shard_map/ppermute | solution.py:458
  7.7 2.8 %prepare.1 = bf16[256,16,128]{2,1,0:T(8,128)(2,1)} custom-call(bf16[256,1024]{1,0:T(8,128)(2,1)} %gate_ref.5, bf16[256,1024]{1,0:T(8,128)(2,1)} %signal_ref.3, bf16[256,1024]{1,0:T(8,128)(2,1)} %filter_ref), custom_call_target="tpu_custom_call" | custom-call | tf_op jit(solution)/shard_map/prepare/pallas_call | solution.py:222
  10.5 3.7 %all-to-all-start = ((bf16[8,32,16,128]{3,2,1,0:T(8,128)(2,1)}), bf16[8,32,16,128]{3,2,1,0:T(8,128)(2,1)S(1)}, u32[]{:S(2)}, u32[]{:S(2)}) async-start(bf16[8,32,16,128]{3,2,1,0:T(8,128)(2,1)} %bitcast.25), calls=%async_computation | async-start | bytes 2097152 | tf_op jit(solution)/shard_map/all_to_all | solution.py:399
  14.3 6.6 %collective-permute-done.refs_3_ = bf16[256,1024]{1,0:T(8,128)(2,1)S(1)} collective-permute-done((bf16[256,1024]{1,0:T(8,128)(2,1)}, bf16[256,1024]{1,0:T(8,128)(2,1)S(1)}, u32[]{:S(2)}, u32[]{:S(2)}) %collective-permute-start) | collective-permute-done | bytes 524320 | tf_op jit(solution)/shard_map/ppermute | solution.py:458
  20.9 5.6 %unproject.4 = (bf16[256,1024]{1,0:T(8,128)(2,1)}, bf16[256,1024]{1,0:T(8,128)(2,1)}) custom-call(s32[1]{0:T(128)} %bitcast.1.place_ref, bf16[1024,2048]{1,0:T(8,128)(2,1)} %refs_0_.3, bf16[1024,2048]{1,0:T(8,128)(2,1)} %refs_0_.3, bf16[2048,1024]{1,0:T(8,128)(2,1)} %refs_4_.1, bf16[256,1024]{1,0:T(8,128)(2,1)S(1)} %collective-permute-done.refs_3_), custom_call_target="tpu_custom_call" | custom-call | flops 40000000000 | bytes 100000000 | tf_op jit(solution)/shard_map/unproject/pallas_call | solution.py:335
  26.5 0.9 collective-permute-start.1
  27.4 2.9 %collective-permute-start.2 = (bf16[256,1024]{1,0:T(8,128)(2,1)}, bf16[256,1024]{1,0:T(8,128)(2,1)S(1)}, u32[]{:S(2)}, u32[]{:S(2)}) collective-permute-start(bf16[256,1024]{1,0:T(8,128)(2,1)} %get-tuple-element.39), channel_id=1, source_target_pairs={{0,3},{1,0},{2,1},{3,2},{4,7},{5,4},{6,5},{7,6},{8,11},{9,8},{10,9... | collective-permute-start | bytes 1572872 | tf_op jit(solution)/shard_map/ppermute | solution.py:408
  30.3 6.1 %convolve.1 = (bf16[8,16,16,128]{3,2,1,0:T(8,128)(2,1)}, f32[32,64,256]{2,1,0:T(8,128)}, f32[32,64,256]{2,1,0:T(8,128)}) custom-call(bf16[8,32,16,128]{3,2,1,0:T(8,128)(2,1)S(1)} %all-to-all-done.pairs_ref, bf16[256,256]{1,0:T(8,128)(2,1)} %constant.87.clone.first_ref, bf16[512,256]{1,0:T(8,128)(2,1)} %constant.88.clone.forward_ref, ...), custom_call_target="tpu_custom_call" | custom-call | tf_op jit(solution)/shard_map/convolve/pallas_call | solution.py:154
  36.4 3.8 %all-to-all-start.1 = ((bf16[8,16,16,128]{3,2,1,0:T(8,128)(2,1)}), bf16[8,16,16,128]{3,2,1,0:T(8,128)(2,1)S(1)}, u32[]{:S(2)}, u32[]{:S(2)}) async-start(bf16[8,16,16,128]{3,2,1,0:T(8,128)(2,1)} %get-tuple-element.41), calls=%async_computation.1 | async-start | bytes 1048576 | tf_op jit(solution)/shard_map/all_to_all | solution.py:399
  40.2 4.1 %unproject.5.refs_0_ = bf16[256,1024]{1,0:T(8,128)(2,1)} custom-call(s32[1]{0:T(128)} %bitcast.1.place_ref, bf16[1024,2048]{1,0:T(8,128)(2,1)} %refs_0_.3, bf16[2048,1024]{1,0:T(8,128)(2,1)} %refs_4_.1), custom_call_target="tpu_custom_call" | custom-call | flops 40000000000 | bytes 100000000 | tf_op jit(solution)/shard_map/unproject/pallas_call | solution.py:335
  44.3 7.1 %collective-permute-done.2.refs_2_ = bf16[256,1024]{1,0:T(8,128)(2,1)S(1)} collective-permute-done((bf16[256,1024]{1,0:T(8,128)(2,1)}, bf16[256,1024]{1,0:T(8,128)(2,1)S(1)}, u32[]{:S(2)}, u32[]{:S(2)}) %collective-permute-start.2) | collective-permute-done | bytes 524320 | tf_op jit(solution)/shard_map/ppermute | solution.py:408
  51.4 3.0 %mix.1 = (bf16[256,1024]{1,0:T(8,128)(2,1)}, bf16[256,1024]{1,0:T(8,128)(2,1)}, bf16[128,16,128]{2,1,0:T(8,128)(2,1)}) custom-call(s32[1]{0:T(128)} %bitcast.flag_ref, bf16[128,16,128]{2,1,0:T(8,128)(2,1)S(1)} %bitcast.24, bf16[256,1024]{1,0:T(8,128)(2,1)S(1)} %copy-done.1, bf16[256,1024]{1,0:T(8,128)(2,1)} %unproject.5.refs_0_, ...), custom_call_target="tpu_custom_call" | custom-call | tf_op jit(solution)/shard_map/mix/pallas_call | solution.py:261
  54.4 2.0 %collective-permute-start.3 = (bf16[256,1024]{1,0:T(8,128)(2,1)}, bf16[256,1024]{1,0:T(8,128)(2,1)S(1)}, u32[]{:S(2)}, u32[]{:S(2)}) collective-permute-start(bf16[256,1024]{1,0:T(8,128)(2,1)} %get-tuple-element.52.refs_0_.refs_2_), channel_id=1, source_target_pairs={{0,1},{1,2},{2,3},{3,0},{4,5},{5,6},{6,7},{7,4},{8,9},{9,10},{10,1... | collective-permute-start | bytes 1572872 | tf_op jit(solution)/shard_map/ppermute | solution.py:408
  56.4 1.8 %collective-permute-start.4 = (bf16[256,1024]{1,0:T(8,128)(2,1)}, bf16[256,1024]{1,0:T(8,128)(2,1)S(1)}, u32[]{:S(2)}, u32[]{:S(2)}) collective-permute-start(bf16[256,1024]{1,0:T(8,128)(2,1)} %get-tuple-element.52.refs_0_.refs_2_), channel_id=1, source_target_pairs={{0,3},{1,0},{2,1},{3,2},{4,7},{5,4},{6,5},{7,6},{8,11},{9,8},{10,9... | collective-permute-start | bytes 1572872 | tf_op jit(solution)/shard_map/ppermute | solution.py:408
  58.2 3.7 %all-to-all-start.2 = ((bf16[8,16,16,128]{3,2,1,0:T(8,128)(2,1)}), bf16[8,16,16,128]{3,2,1,0:T(8,128)(2,1)S(1)}, u32[]{:S(2)}, u32[]{:S(2)}) async-start(bf16[8,16,16,128]{3,2,1,0:T(8,128)(2,1)} %bitcast.28), calls=%async_computation.2 | async-start | bytes 1048576 | tf_op jit(solution)/shard_map/all_to_all | solution.py:399
  61.9 9.7 %all-to-all-done.2.pairs_ref = bf16[8,16,16,128]{3,2,1,0:T(8,128)(2,1)S(1)} async-done(((bf16[8,16,16,128]{3,2,1,0:T(8,128)(2,1)}), bf16[8,16,16,128]{3,2,1,0:T(8,128)(2,1)S(1)}, u32[]{:S(2)}, u32[]{:S(2)}) %all-to-all-start.2) | async-done | bytes 524320 | tf_op jit(solution)/shard_map/all_to_all | solution.py:399
  71.7 7.1 %correlate.1 = bf16[8,32,16,128]{3,2,1,0:T(8,128)(2,1)} custom-call(bf16[8,16,16,128]{3,2,1,0:T(8,128)(2,1)S(1)} %all-to-all-done.2.pairs_ref, f32[32,64,256]{2,1,0:T(8,128)} %get-tuple-element.45.signal_ref, f32[32,64,256]{2,1,0:T(8,128)} %get-tuple-element.46.filter_ref, bf16[256,256]{1,0:T(8,128)(2,1)} %constant.87.clone.first_ref, ...), custom_call_target="tpu_custom_call" | custom-call | tf_op jit(solution)/shard_map/correlate/pallas_call | solution.py:180
  78.8 1.2 collective-permute-done.4.refs_3_
  80.1 3.9 %all-to-all-start.3 = ((bf16[8,32,16,128]{3,2,1,0:T(8,128)(2,1)}), bf16[8,32,16,128]{3,2,1,0:T(8,128)(2,1)S(1)}, u32[]{:S(2)}, u32[]{:S(2)}) async-start(bf16[8,32,16,128]{3,2,1,0:T(8,128)(2,1)} %correlate.1), calls=%async_computation.3 | async-start | bytes 2097152 | tf_op jit(solution)/shard_map/all_to_all | solution.py:399
  84.6 7.7 %project.1 = (bf16[4,128,2048]{2,1,0:T(8,128)(2,1)}, bf16[4,128,2048]{2,1,0:T(8,128)(2,1)}) custom-call(s32[1]{0:T(128)} %bitcast.5.core_ref, bf16[256,1024]{1,0:T(8,128)(2,1)S(1)} %copy-done, bf16[256,1024]{1,0:T(8,128)(2,1)S(1)} %collective-permute-done.3.refs_1_, bf16[256,1024]{1,0:T(8,128)(2,1)S(1)} %copy-done, ...), custom_call_target="tpu_custom_call" | custom-call | tf_op jit(solution)/shard_map/project/pallas_call | solution.py:378
  92.3 6.1 %collective-permute-done.5 = bf16[256,1024]{1,0:T(8,128)(2,1)} collective-permute-done((bf16[256,1024]{1,0:T(8,128)(2,1)S(1)}, bf16[256,1024]{1,0:T(8,128)(2,1)}, u32[]{:S(2)}, u32[]{:S(2)}) %collective-permute-start.5) | collective-permute-done | bytes 524320 | tf_op jit(solution)/shard_map/ppermute | solution.py:483
  98.4 1.0 all-to-all-done.3
  99.4 3.8 %convolution_convert_fusion = bf16[256,2048]{1,0:T(8,128)(2,1)S(1)} fusion(bf16[256,1024]{1,0:T(8,128)(2,1)} %collective-permute-done.5, bf16[2048,1024]{1,0:T(8,128)(2,1)} %refs_4_.1), kind=kOutput, calls=%fused_computation.1 | convolution fusion | flops 1074266112 | bytes 5767168 | tf_op jit(solution)/shard_map/zct,dt->zcd/dot_general | solution.py:422
  103.8 0.8 add_convert_fusion
  104.6 0.7 collective-permute-done.7
  105.7 1.7 %collective-permute-start.8 = (bf16[128,2048]{1,0:T(8,128)(2,1)S(1)}, bf16[128,2048]{1,0:T(8,128)(2,1)S(1)}, u32[]{:S(2)}, u32[]{:S(2)}) collective-permute-start(bf16[128,2048]{1,0:T(8,128)(2,1)S(1)} %get-tuple-element.69), channel_id=1, source_target_pairs={{0,24},{4,28},{8,16},{12,20},{16,8},{20,12},{24,0},{28,4},{1,25},{... | collective-permute-start | bytes 1572872 | tf_op jit(solution)/shard_map/ppermute | solution.py:436
  108.0 1.3 collective-permute-start.10
  109.3 3.2 %finish.1 = (bf16[256,1024]{1,0:T(8,128)(2,1)}, bf16[256,1024]{1,0:T(8,128)(2,1)}, f32[256,1024]{1,0:T(8,128)}) custom-call(bf16[256,16,128]{2,1,0:T(8,128)(2,1)S(1)} %bitcast.23, bf16[256,1024]{1,0:T(8,128)(2,1)} %signal_ref.3, bf16[256,1024]{1,0:T(8,128)(2,1)} %gate_ref.5), custom_call_target="tpu_custom_call" | custom-call | tf_op jit(solution)/shard_map/finish/pallas_call | solution.py:293
  112.5 9.0 %collective-permute-done.8 = bf16[128,2048]{1,0:T(8,128)(2,1)S(1)} collective-permute-done((bf16[128,2048]{1,0:T(8,128)(2,1)S(1)}, bf16[128,2048]{1,0:T(8,128)(2,1)S(1)}, u32[]{:S(2)}, u32[]{:S(2)}) %collective-permute-start.8) | collective-permute-done | bytes 524320 | tf_op jit(solution)/shard_map/ppermute | solution.py:436
  121.5 9.9 %collective-permute-done.9 = bf16[128,2048]{1,0:T(8,128)(2,1)S(1)} collective-permute-done((bf16[128,2048]{1,0:T(8,128)(2,1)S(1)}, bf16[128,2048]{1,0:T(8,128)(2,1)S(1)}, u32[]{:S(2)}, u32[]{:S(2)}) %collective-permute-start.9) | collective-permute-done | bytes 524320 | tf_op jit(solution)/shard_map/ppermute | solution.py:436
  132.1 1.3 convert_add_fusion.1
  (20 shorter events, 3.0 us)
Async XLA Ops:
  4.7 16.2 %collective-permute-start = (bf16[256,1024]{1,0:T(8,128)(2,1)}, bf16[256,1024]{1,0:T(8,128)(2,1)S(1)}, u32[]{:S(2)}, u32[]{:S(2)}) collective-permute-start(bf16[256,1024]{1,0:T(8,128)(2,1)} %unproject.3), channel_id=1, source_target_pairs={{2,0},{1,3},{3,2},{0,1},{6,4},{5,7},{7,6},{4,5},{10,8},{9,11},{11,... | collective-permute-start | bytes 1572872 | tf_op jit(solution)/shard_map/ppermute | solution.py:458
  10.5 19.8 %all-to-all-start = ((bf16[8,32,16,128]{3,2,1,0:T(8,128)(2,1)}), bf16[8,32,16,128]{3,2,1,0:T(8,128)(2,1)S(1)}, u32[]{:S(2)}, u32[]{:S(2)}) async-start(bf16[8,32,16,128]{3,2,1,0:T(8,128)(2,1)} %bitcast.25), calls=%async_computation | async-start | bytes 2097152 | tf_op jit(solution)/shard_map/all_to_all | solution.py:399
  26.5 17.8 %collective-permute-start.1 = (bf16[256,1024]{1,0:T(8,128)(2,1)}, bf16[256,1024]{1,0:T(8,128)(2,1)S(1)}, u32[]{:S(2)}, u32[]{:S(2)}) collective-permute-start(bf16[256,1024]{1,0:T(8,128)(2,1)} %get-tuple-element.38), channel_id=1, source_target_pairs={{0,1},{1,2},{2,3},{3,0},{4,5},{5,6},{6,7},{7,4},{8,9},{9,10},{10,1... | collective-permute-start | bytes 1572872 | tf_op jit(solution)/shard_map/ppermute | solution.py:408
  27.4 24.0 %collective-permute-start.2 = (bf16[256,1024]{1,0:T(8,128)(2,1)}, bf16[256,1024]{1,0:T(8,128)(2,1)S(1)}, u32[]{:S(2)}, u32[]{:S(2)}) collective-permute-start(bf16[256,1024]{1,0:T(8,128)(2,1)} %get-tuple-element.39), channel_id=1, source_target_pairs={{0,3},{1,0},{2,1},{3,2},{4,7},{5,4},{6,5},{7,6},{8,11},{9,8},{10,9... | collective-permute-start | bytes 1572872 | tf_op jit(solution)/shard_map/ppermute | solution.py:408
  36.4 15.0 %all-to-all-start.1 = ((bf16[8,16,16,128]{3,2,1,0:T(8,128)(2,1)}), bf16[8,16,16,128]{3,2,1,0:T(8,128)(2,1)S(1)}, u32[]{:S(2)}, u32[]{:S(2)}) async-start(bf16[8,16,16,128]{3,2,1,0:T(8,128)(2,1)} %get-tuple-element.41), calls=%async_computation.1 | async-start | bytes 1048576 | tf_op jit(solution)/shard_map/all_to_all | solution.py:399
  40.2 11.2 %copy-start.1 = (bf16[256,1024]{1,0:T(8,128)(2,1)S(1)}, bf16[256,1024]{1,0:T(8,128)(2,1)}, u32[]{:S(2)}) copy-start(bf16[256,1024]{1,0:T(8,128)(2,1)} %gate_ref.4) | copy-start | bytes 1572868
  54.4 24.4 %collective-permute-start.3 = (bf16[256,1024]{1,0:T(8,128)(2,1)}, bf16[256,1024]{1,0:T(8,128)(2,1)S(1)}, u32[]{:S(2)}, u32[]{:S(2)}) collective-permute-start(bf16[256,1024]{1,0:T(8,128)(2,1)} %get-tuple-element.52.refs_0_.refs_2_), channel_id=1, source_target_pairs={{0,1},{1,2},{2,3},{3,0},{4,5},{5,6},{6,7},{7,4},{8,9},{9,10},{10,1... | collective-permute-start | bytes 1572872 | tf_op jit(solution)/shard_map/ppermute | solution.py:408
  56.4 23.6 %collective-permute-start.4 = (bf16[256,1024]{1,0:T(8,128)(2,1)}, bf16[256,1024]{1,0:T(8,128)(2,1)S(1)}, u32[]{:S(2)}, u32[]{:S(2)}) collective-permute-start(bf16[256,1024]{1,0:T(8,128)(2,1)} %get-tuple-element.52.refs_0_.refs_2_), channel_id=1, source_target_pairs={{0,3},{1,0},{2,1},{3,2},{4,7},{5,4},{6,5},{7,6},{8,11},{9,8},{10,9... | collective-permute-start | bytes 1572872 | tf_op jit(solution)/shard_map/ppermute | solution.py:408
  58.2 13.5 %all-to-all-start.2 = ((bf16[8,16,16,128]{3,2,1,0:T(8,128)(2,1)}), bf16[8,16,16,128]{3,2,1,0:T(8,128)(2,1)S(1)}, u32[]{:S(2)}, u32[]{:S(2)}) async-start(bf16[8,16,16,128]{3,2,1,0:T(8,128)(2,1)} %bitcast.28), calls=%async_computation.2 | async-start | bytes 1048576 | tf_op jit(solution)/shard_map/all_to_all | solution.py:399
  71.7 8.3 %copy-start = (bf16[256,1024]{1,0:T(8,128)(2,1)S(1)}, bf16[256,1024]{1,0:T(8,128)(2,1)}, u32[]{:S(2)}) copy-start(bf16[256,1024]{1,0:T(8,128)(2,1)} %get-tuple-element.52.refs_0_.refs_2_) | copy-start | bytes 1572868
  80.1 19.3 %all-to-all-start.3 = ((bf16[8,32,16,128]{3,2,1,0:T(8,128)(2,1)}), bf16[8,32,16,128]{3,2,1,0:T(8,128)(2,1)S(1)}, u32[]{:S(2)}, u32[]{:S(2)}) async-start(bf16[8,32,16,128]{3,2,1,0:T(8,128)(2,1)} %correlate.1), calls=%async_computation.3 | async-start | bytes 2097152 | tf_op jit(solution)/shard_map/all_to_all | solution.py:399
  84.0 14.4 %collective-permute-start.5 = (bf16[256,1024]{1,0:T(8,128)(2,1)S(1)}, bf16[256,1024]{1,0:T(8,128)(2,1)}, u32[]{:S(2)}, u32[]{:S(2)}) collective-permute-start(bf16[256,1024]{1,0:T(8,128)(2,1)S(1)} %select_select_fusion), channel_id=1, source_target_pairs={{0,2},{3,1},{2,3},{1,0},{4,6},{7,5},{6,7},{5,4},{8,10},{11,9},{10,... | collective-permute-start | bytes 1572872 | tf_op jit(solution)/shard_map/ppermute | solution.py:483
  99.4 4.4 %collective-permute-start.6 = (bf16[4,128,2048]{2,1,0:T(8,128)(2,1)}, bf16[4,128,2048]{2,1,0:T(8,128)(2,1)S(1)}, u32[]{:S(2)}, u32[]{:S(2)}) collective-permute-start(bf16[4,128,2048]{2,1,0:T(8,128)(2,1)} %get-tuple-element.57), channel_id=1, source_target_pairs={{0,4},{4,0},{8,12},{12,8},{16,20},{20,16},{24,28},{28,24},{1,5},{5... | collective-permute-start | bytes 6291464 | tf_op jit(solution)/shard_map/ppermute | solution.py:489
  99.4 4.4 %copy-start.2 = (bf16[4,128,2048]{2,1,0:T(8,128)(2,1)S(1)}, bf16[4,128,2048]{2,1,0:T(8,128)(2,1)}, u32[]{:S(2)}) copy-start(bf16[4,128,2048]{2,1,0:T(8,128)(2,1)} %get-tuple-element.55) | copy-start | bytes 6291460
  103.2 2.1 %collective-permute-start.7 = (bf16[1,128,2048]{2,1,0:T(8,128)(2,1)S(1)}, bf16[1,128,2048]{2,1,0:T(8,128)(2,1)S(1)}, u32[]{:S(2)}, u32[]{:S(2)}) collective-permute-start(bf16[1,128,2048]{2,1,0:T(8,128)(2,1)S(1)} %dynamic-slice_bitcast_fusion.4), channel_id=1, source_target_pairs={{0,4},{4,0},{8,12},{12,8},{16,20},{20,16},{24,28},{28,24},{1,5},{5... | collective-permute-start | bytes 1572872 | tf_op jit(solution)/shard_map/ppermute | solution.py:424
  105.7 15.8 %collective-permute-start.8 = (bf16[128,2048]{1,0:T(8,128)(2,1)S(1)}, bf16[128,2048]{1,0:T(8,128)(2,1)S(1)}, u32[]{:S(2)}, u32[]{:S(2)}) collective-permute-start(bf16[128,2048]{1,0:T(8,128)(2,1)S(1)} %get-tuple-element.69), channel_id=1, source_target_pairs={{0,24},{4,28},{8,16},{12,20},{16,8},{20,12},{24,0},{28,4},{1,25},{... | collective-permute-start | bytes 1572872 | tf_op jit(solution)/shard_map/ppermute | solution.py:436
  107.4 24.0 %collective-permute-start.9 = (bf16[128,2048]{1,0:T(8,128)(2,1)S(1)}, bf16[128,2048]{1,0:T(8,128)(2,1)S(1)}, u32[]{:S(2)}, u32[]{:S(2)}) collective-permute-start(bf16[128,2048]{1,0:T(8,128)(2,1)S(1)} %get-tuple-element.68), channel_id=1, source_target_pairs={{0,8},{4,12},{8,0},{12,4},{16,24},{20,28},{24,16},{28,20},{1,9},{5... | collective-permute-start | bytes 1572872 | tf_op jit(solution)/shard_map/ppermute | solution.py:436
  108.0 24.2 %collective-permute-start.10 = (bf16[128,2048]{1,0:T(8,128)(2,1)S(1)}, bf16[128,2048]{1,0:T(8,128)(2,1)S(1)}, u32[]{:S(2)}, u32[]{:S(2)}) collective-permute-start(bf16[128,2048]{1,0:T(8,128)(2,1)S(1)} %get-tuple-element.67), channel_id=1, source_target_pairs={{0,16},{4,20},{8,24},{12,28},{16,0},{20,4},{24,8},{28,12},{1,17},{... | collective-permute-start | bytes 1572872 | tf_op jit(solution)/shard_map/ppermute | solution.py:436

commit v7 on v6

--- a/solution.py
+++ b/solution.py
@@ -53,8 +53,8 @@
     twiddle = np.stack([np.cos(turn), np.sin(turn)]).astype(np.float32)
     lane = 2.0 * math.pi / LANES * np.outer(np.arange(LANES), np.arange(LANES))
     cos, sin = np.cos(lane), np.sin(lane)
-    forward = high_low(np.block([[cos, -sin], [sin, cos]]), 0)
-    inverse = high_low(np.block([[cos, sin], [-sin, cos]]), 0)
+    forward = np.block([[cos, -sin], [sin, cos]]).astype(jnp.bfloat16)
+    inverse = np.block([[cos, sin], [-sin, cos]]).astype(jnp.bfloat16)
     return first, forward, inverse, last, twiddle
 
 
@@ -90,7 +90,7 @@
 
 
 def lanes_dft(rows, table):
-    return mxu(jnp.concatenate([rows, rows], axis=1), table)
+    return mxu(rows, table)
 
 
 def convolve_kernel(pairs_ref, first_ref, forward_ref, inverse_ref, last_ref, twiddle_ref,
@@ -231,21 +231,29 @@
     )(*held_in_hbm(inner_gate, signal, long_filter))
 
 
-def mix_kernel(flag_ref, conv_ref, gate_ref, *refs):
+def mix_kernel(parts, flag_ref, conv_ref, gate_ref, *refs):
     *share_refs, mixed_ref, outer_ref, grad_ref, lines, grads = refs
     rows, length = gate_ref.shape
     per = length // LANES
     lines[...] = wide(conv_ref[...].reshape(rows * per, LANES))
+    groups = []
+    for count in parts:
+        groups.append(share_refs[:count])
+        share_refs = share_refs[count:]
     for lane in range(per):
         cols = slice(lane * LANES, (lane + 1) * LANES)
+        shares = []
+        for group in groups:
+            held = group[lane * len(group) // per]
+            at = lane % (per // len(group)) * LANES
+            shares.append(wide(held[:, at : at + LANES]))
         conv = lines[pl.ds(lane, rows, stride=per), :]
         gate = wide(gate_ref[:, cols])
         mixed_ref[:, cols] = short(conv * gate)
-        grad_mix = wide(share_refs[0][:, cols])
-        for ref in share_refs[1:-1]:
-            grad_mix = grad_mix + wide(ref[:, cols])
-        last = wide(share_refs[-1][:, cols])
-        grad_mix = grad_mix + jnp.where(flag_ref[0] != 0, last, jnp.zeros_like(last))
+        grad_mix = shares[0]
+        for share in shares[1:-1]:
+            grad_mix = grad_mix + share
+        grad_mix = grad_mix + jnp.where(flag_ref[0] != 0, shares[-1], jnp.zeros_like(shares[-1]))
         outer_ref[:, cols] = short(grad_mix * conv)
         grads[pl.ds(lane, rows, stride=per), :] = grad_mix * gate
     grad_ref[...] = short(grads[...]).reshape(grad_ref.shape)
@@ -253,24 +261,27 @@
 
 def mix(conv, outer_gate, shares, flag):
     rows, length = outer_gate.shape
+    parts = [len(share) for share in shares]
+    cuts = [cut for share in shares for cut in share]
     per = length // LANES
     conv = conv.reshape(rows * per // 16, 16, LANES)
     step = rows // 2
     token_rows = pl.BlockSpec((step, length), lambda i, at: (i, 0))
     lane_rows = pl.BlockSpec((step * per // 16, 16, LANES), lambda i, at: (i, 0, 0))
     return pl.pallas_call(
-        mix_kernel,
+        functools.partial(mix_kernel, parts),
         grid_spec=pltpu.PrefetchScalarGridSpec(
             num_scalar_prefetch=1,
             grid=(2,),
-            in_specs=[lane_rows, token_rows] + [token_rows] * len(shares),
+            in_specs=[lane_rows, token_rows]
+            + [pl.BlockSpec((step, cut.shape[1]), lambda i, at: (i, 0)) for cut in cuts],
             out_specs=[token_rows, token_rows, lane_rows],
             scratch_shapes=[pltpu.VMEM((step * per, LANES), jnp.float32)] * 2,
         ),
         out_shape=[in_hbm((rows, length))] * 2 + [in_hbm((rows * per // 16, 16, LANES))],
         compiler_params=params(),
         name="mix",
-    )(flag.astype(jnp.int32).reshape(1), conv, outer_gate, *shares)
+    )(flag.astype(jnp.int32).reshape(1), conv, outer_gate, *cuts)
 
 
 def finish_kernel(corr_ref, signal_ref, gate_ref, inner_ref, signal_out_ref, filter_ref, lines):
@@ -303,10 +314,10 @@
     )(corr.reshape(rows, 2 * per, LANES), *held_in_hbm(signal, inner_gate))
 
 
-def unproject_kernel(count, add_from, place_ref, *refs):
+def unproject_kernel(count, splits, add_from, place_ref, *refs):
     rows, width = refs[0].shape
     grad_ref, weights = refs[count], refs[-1]
-    out_refs = refs[-1 - count : -1]
+    out_refs = refs[-1 - count * splits : -1]
 
     @pl.when(pl.program_id(0) == 0)
     def _():
@@ -319,31 +330,37 @@
         if add_from is not None:
             more = wide(refs[count + 1][...])
             part = short(wide(part) + jnp.where(place_ref[0] == add_from[row], more, jnp.zeros_like(more)))
-        out_refs[row][...] = part
-
-
-def unproject(out_proj, grad_output, offsets, place, count, more=None, add_from=None):
+        for split in range(splits):
+
+            @pl.when(pl.program_id(0) * splits // pl.num_programs(0) == split)
+            def _(part=part, ref=out_refs[row * splits + split]):
+                ref[...] = part
+
+
+def unproject(out_proj, grad_output, offsets, place, count, more=None, add_from=None, half=None, splits=1):
     width, length = grad_output.shape
     rows = out_proj.shape[0] // count
-    step = 512
+    step = 512 if half is None else 256
+    length = length if half is None else length // 2
+    first = 0 if half is None else half * (length // step)
     in_specs = [
         pl.BlockSpec((rows, width), lambda i, at, by=by: (lax.rem(at[0] + by, count), 0))
         for by in offsets
     ]
-    out_block = pl.BlockSpec((rows, step), lambda i, at: (0, i))
+    out_block = pl.BlockSpec((rows, step), lambda i, at: (0, i if splits == 1 else 0))
     extra = [] if more is None else [more]
     return pl.pallas_call(
-        functools.partial(unproject_kernel, len(offsets), add_from),
+        functools.partial(unproject_kernel, len(offsets), splits, add_from),
         grid_spec=pltpu.PrefetchScalarGridSpec(
             num_scalar_prefetch=1,
             grid=(length // step,),
             in_specs=in_specs
-            + [pl.BlockSpec((width, step), lambda i, at: (0, i))]
+            + [pl.BlockSpec((width, step), lambda i, at: (0, first + i))]
             + [out_block] * len(extra),
-            out_specs=[out_block] * len(offsets),
+            out_specs=[out_block] * (len(offsets) * splits),
             scratch_shapes=[pltpu.VMEM((len(offsets) * rows, width), jnp.bfloat16)],
         ),
-        out_shape=[in_hbm((rows, length))] * len(offsets),
+        out_shape=[in_hbm((rows, length // splits))] * (len(offsets) * splits),
         compiler_params=params(),
         cost_estimate=pl.CostEstimate(flops=40 * 10**9, bytes_accessed=10**8, transcendentals=0),
         name="unproject",
@@ -452,14 +469,22 @@
     tables = [jnp.asarray(t) for t in dft_tables(block_len * seq_count, seq_count)]
 
     if chan_count == 4:
-        far = unproject(out_proj, grad_output, [2], line, chan_count)[0]
-        pair = prepare(inner_gate, signal, tie(long_filter, far))
+        fars = unproject(out_proj, grad_output, [2], line, chan_count, splits=2)
+        pair = prepare(inner_gate, signal, tie(long_filter, *fars))
         pair = pair.reshape(seq_count, owned, 2 * per, LANES)
-        far = lax.ppermute(far, "chan", [(2, 0), (1, 3), (3, 2), (0, 1)])
+        fars = [fars[0], tie(fars[1], pair)]
+        fars = [lax.ppermute(far, "chan", [(2, 0), (1, 3), (3, 2), (0, 1)]) for far in fars]
         sent = exchange(pair)
-        near = unproject(tie(out_proj, pair), grad_output, [1, 3], line, chan_count, far, [1, 2])
-        sent = tie(sent, *near)
-        shares = [shift(near[0], 1), shift(near[1], 3), far]
+        after, ups, downs = pair, [], []
+        for half, far in enumerate(fars):
+            near = unproject(
+                tie(out_proj, after), grad_output, [1, 3], line, chan_count, far, [1, 2], half
+            )
+            ups.append(shift(near[0], 1))
+            downs.append(shift(near[1], 3))
+            after = near[1]
+        sent = tie(sent, after)
+        shares = [ups, downs, fars]
         flag = (line == 0) | (line == 3)
     else:
         pair = prepare(inner_gate, signal, long_filter)
@@ -467,12 +492,12 @@
         sent = exchange(pair)
         offsets = list(range(1, chan_count))
         blocks = unproject(out_proj, grad_output, offsets, line, chan_count)
-        shares = [shift(block, by) for by, block in zip(offsets, blocks)]
+        shares = [[shift(block, by)] for by, block in zip(offsets, blocks)]
         flag = line >= 0
 
     conv, spec_signal, spec_filter = convolve(sent, tables)
     own = unproject(tie(out_proj, conv), grad_output, [0], line, chan_count)
-    shares = [*held_in_hbm(*own), *shares]
+    shares = [held_in_hbm(*own), *shares]
     mixed, grad_outer, grad_conv = mix(exchange(conv), outer_gate, shares, flag)
     held = gather_first(mixed)
     grad_conv = grad_conv.reshape(seq_count, owned // 2, 2 * per, LANES)

time: 134 us -> 131 us (0.978)
  waiting for transfers between devices: 52.1 us -> 42.1 us
  starting transfers between devices: 30.6 us -> 37.1 us
    ppermute x4 -> x6, waiting for transfers between devices: 8.28 us -> 1.84 us  [shift(): lax.ppermute(block, 'chan', [(i, (i + by) % count) for i in range(count)])]
    ppermute x1 -> x2, waiting for transfers between devices: 6.63 us -> 0.64 us  [body(): lax.ppermute(far, 'chan', [(2, 0), (1, 3), (3, 2), (0, 1)])]
    all_to_all x4, waiting for transfers between devices: 10.7 us -> 14.7 us  [exchange(): lax.all_to_all(blocks, 'seq', split_axis=0, concat_axis=0, tiled=True)]
    pallas_call x4 -> x5, Pallas kernels: 16.8 us -> 20 us  [the longest x4 17 us: unproject(): pl.pallas_call(functools.partial(unproject_kernel, len(offsets), splits,...]
    ppermute x1 -> x2, starting transfers between devices: 3.02 us -> 5.67 us  [body(): lax.ppermute(far, 'chan', [(2, 0), (1, 3), (3, 2), (0, 1)])]
    ppermute x4 -> x6, starting transfers between devices: 7.65 us -> 9.67 us  [shift(): lax.ppermute(block, 'chan', [(i, (i + by) % count) for i in range(count)])]
    ppermute x1, waiting for transfers between devices: 6.09 us -> 4.57 us  [body(): middle = lax.ppermute(passed, 'chan', [(0, 2), (3, 1), (2, 3), (1, 0)])]
    ppermute x1, starting transfers between devices: 0.61 us -> 2.13 us  [body(): middle = lax.ppermute(passed, 'chan', [(0, 2), (3, 1), (2, 3), (1, 0)])]
  transfers between devices with their start and end apart: 15 -> 18, of which waited for: 10 -> 11; matrix products, arithmetic and copies ran while one was open for 3% -> 4% of each run, Pallas kernels for 27% -> 29%
where the time goes in v7:
time: 131 us
  Pallas kernels  44.5 us (34%)
  waiting for transfers between devices  42.1 us (32%)
  starting transfers between devices  37.1 us (28%)
  matrix products  3.78 us (3%)
  other arithmetic  2.29 us (2%)
    ppermute x3, waiting for transfers between devices, scatter_chips(): lax.ppermute(block(bit), 'seq', swaps(count, 2 * bit))  19.7 us
    pallas_call x4, Pallas kernels, unproject(): pl.pallas_call(functools.partial(unproject_kernel, len(offsets), splits,...  17 us
    all_to_all x4, starting transfers between devices, exchange(): lax.all_to_all(blocks, 'seq', split_axis=0, concat_axis=0, tiled=True)  15.5 us
    all_to_all x4, waiting for transfers between devices, exchange(): lax.all_to_all(blocks, 'seq', split_axis=0, concat_axis=0, tiled=True)  14.7 us
    ppermute x6, starting transfers between devices, shift(): lax.ppermute(block, 'chan', [(i, (i + by) % count) for i in range(count)])  9.67 us
    pallas_call x1, Pallas kernels, project(): pl.pallas_call(project_kernel, grid_spec=pltpu.PrefetchScalarGridSpec(num...  7.74 us
    pallas_call x1, Pallas kernels, correlate(): pl.pallas_call(correlate_kernel, grid=(chans // step,), in_specs=[pl.Bloc...  5.72 us
    ppermute x2, starting transfers between devices, body(): lax.ppermute(far, 'chan', [(2, 0), (1, 3), (3, 2), (0, 1)])  5.67 us
  transfers between devices with their start and end apart: 18, of which 11 were waited for; matrix products, arithmetic and copies ran while one was open for 4% of the time, Pallas kernels for 29%

profile of v7, /device:TPU:0, one launch (start us, length us, event | category | flops | bytes accessed | tf_op | source)
XLA Modules:
  0.0 130.9 jit_solution(509796666342970348)
XLA Ops:
  0.6 4.2 %unproject.4 = (bf16[256,512]{1,0:T(8,128)(2,1)}, bf16[256,512]{1,0:T(8,128)(2,1)}) custom-call(s32[1]{0:T(128)} %bitcast.1.place_ref, bf16[1024,2048]{1,0:T(8,128)(2,1)} %refs_0_.4, bf16[2048,1024]{1,0:T(8,128)(2,1)} %refs_4_.1), custom_call_target="tpu_custom_call" | custom-call | flops 40000000000 | bytes 100000000 | tf_op jit(solution)/shard_map/unproject/pallas_call | solution.py:352
  4.9 3.0 %collective-permute-start = (bf16[256,512]{1,0:T(8,128)(2,1)}, bf16[256,512]{1,0:T(8,128)(2,1)S(1)}, u32[]{:S(2)}, u32[]{:S(2)}) collective-permute-start(bf16[256,512]{1,0:T(8,128)(2,1)} %get-tuple-element.42), channel_id=1, source_target_pairs={{2,0},{1,3},{3,2},{0,1},{6,4},{5,7},{7,6},{4,5},{10,8},{9,11},{11,... | collective-permute-start | bytes 786440 | tf_op jit(solution)/shard_map/ppermute | solution.py:476
  7.9 2.8 %prepare.1 = bf16[256,16,128]{2,1,0:T(8,128)(2,1)} custom-call(bf16[256,1024]{1,0:T(8,128)(2,1)} %gate_ref.5, bf16[256,1024]{1,0:T(8,128)(2,1)} %signal_ref.3, bf16[256,1024]{1,0:T(8,128)(2,1)} %filter_ref), custom_call_target="tpu_custom_call" | custom-call | tf_op jit(solution)/shard_map/prepare/pallas_call | solution.py:222
  10.7 3.7 %all-to-all-start = ((bf16[8,32,16,128]{3,2,1,0:T(8,128)(2,1)}), bf16[8,32,16,128]{3,2,1,0:T(8,128)(2,1)S(1)}, u32[]{:S(2)}, u32[]{:S(2)}) async-start(bf16[8,32,16,128]{3,2,1,0:T(8,128)(2,1)} %bitcast.25), calls=%async_computation | async-start | bytes 2097152 | tf_op jit(solution)/shard_map/all_to_all | solution.py:416
  14.4 2.6 %collective-permute-start.1 = (bf16[256,512]{1,0:T(8,128)(2,1)S(1)}, bf16[256,512]{1,0:T(8,128)(2,1)S(1)}, u32[]{:S(2)}, u32[]{:S(2)}) collective-permute-start(bf16[256,512]{1,0:T(8,128)(2,1)S(1)} %copy-done.3), channel_id=1, source_target_pairs={{2,0},{1,3},{3,2},{0,1},{6,4},{5,7},{7,6},{4,5},{10,8},{9,11},{11,... | collective-permute-start | bytes 786440 | tf_op jit(solution)/shard_map/ppermute | solution.py:476
  17.1 4.3 %unproject.5 = (bf16[256,512]{1,0:T(8,128)(2,1)}, bf16[256,512]{1,0:T(8,128)(2,1)}) custom-call(s32[1]{0:T(128)} %bitcast.1.place_ref, bf16[1024,2048]{1,0:T(8,128)(2,1)} %refs_0_.4, bf16[1024,2048]{1,0:T(8,128)(2,1)} %refs_0_.4, bf16[2048,1024]{1,0:T(8,128)(2,1)} %refs_4_.1, bf16[256,512]{1,0:T(8,128)(2,1)S(1)} %collective-permute-done.refs_3_.refs_5_), custom_call_target="tpu_custom_call" | custom-call | flops 40000000000 | bytes 100000000 | tf_op jit(solution)/shard_map/unproject/pallas_call | solution.py:352
  21.4 2.0 %collective-permute-start.4 = (bf16[256,512]{1,0:T(8,128)(2,1)}, bf16[256,512]{1,0:T(8,128)(2,1)S(1)}, u32[]{:S(2)}, u32[]{:S(2)}) collective-permute-start(bf16[256,512]{1,0:T(8,128)(2,1)} %get-tuple-element.46), channel_id=1, source_target_pairs={{0,3},{1,0},{2,1},{3,2},{4,7},{5,4},{6,5},{7,6},{8,11},{9,8},{10,9... | collective-permute-start | bytes 786440 | tf_op jit(solution)/shard_map/ppermute | solution.py:425
  24.1 4.3 %unproject.6 = (bf16[256,512]{1,0:T(8,128)(2,1)}, bf16[256,512]{1,0:T(8,128)(2,1)}) custom-call(s32[1]{0:T(128)} %bitcast.1.place_ref, bf16[1024,2048]{1,0:T(8,128)(2,1)} %refs_0_.4, bf16[1024,2048]{1,0:T(8,128)(2,1)} %refs_0_.4, bf16[2048,1024]{1,0:T(8,128)(2,1)} %refs_4_.1, bf16[256,512]{1,0:T(8,128)(2,1)S(1)} %collective-permute-done.1.refs_3_.refs_6_), custom_call_target="tpu_custom_call" | custom-call | flops 40000000000 | bytes 100000000 | tf_op jit(solution)/shard_map/unproject/pallas_call | solution.py:352
  28.4 2.1 %collective-permute-start.3 = (bf16[256,512]{1,0:T(8,128)(2,1)}, bf16[256,512]{1,0:T(8,128)(2,1)S(1)}, u32[]{:S(2)}, u32[]{:S(2)}) collective-permute-start(bf16[256,512]{1,0:T(8,128)(2,1)} %get-tuple-element.54), channel_id=1, source_target_pairs={{0,1},{1,2},{2,3},{3,0},{4,5},{5,6},{6,7},{7,4},{8,9},{9,10},{10,1... | collective-permute-start | bytes 786440 | tf_op jit(solution)/shard_map/ppermute | solution.py:425
  30.5 1.7 %collective-permute-start.5 = (bf16[256,512]{1,0:T(8,128)(2,1)}, bf16[256,512]{1,0:T(8,128)(2,1)S(1)}, u32[]{:S(2)}, u32[]{:S(2)}) collective-permute-start(bf16[256,512]{1,0:T(8,128)(2,1)} %get-tuple-element.49), channel_id=1, source_target_pairs={{0,3},{1,0},{2,1},{3,2},{4,7},{5,4},{6,5},{7,6},{8,11},{9,8},{10,9... | collective-permute-start | bytes 786440 | tf_op jit(solution)/shard_map/ppermute | solution.py:425
  32.2 5.1 %convolve.1 = (bf16[8,16,16,128]{3,2,1,0:T(8,128)(2,1)}, f32[32,64,256]{2,1,0:T(8,128)}, f32[32,64,256]{2,1,0:T(8,128)}) custom-call(bf16[8,32,16,128]{3,2,1,0:T(8,128)(2,1)S(1)} %all-to-all-done.pairs_ref, bf16[256,256]{1,0:T(8,128)(2,1)} %constant.87.clone.first_ref, bf16[256,256]{1,0:T(8,128)(2,1)} %constant.88.clone.forward_ref, ...), custom_call_target="tpu_custom_call" | custom-call | tf_op jit(solution)/shard_map/convolve/pallas_call | solution.py:154
  37.3 3.8 %all-to-all-start.1 = ((bf16[8,16,16,128]{3,2,1,0:T(8,128)(2,1)}), bf16[8,16,16,128]{3,2,1,0:T(8,128)(2,1)S(1)}, u32[]{:S(2)}, u32[]{:S(2)}) async-start(bf16[8,16,16,128]{3,2,1,0:T(8,128)(2,1)} %get-tuple-element.51), calls=%async_computation.1 | async-start | bytes 1048576 | tf_op jit(solution)/shard_map/all_to_all | solution.py:416
  41.1 4.2 %unproject.7.refs_0_ = bf16[256,1024]{1,0:T(8,128)(2,1)} custom-call(s32[1]{0:T(128)} %bitcast.1.place_ref, bf16[1024,2048]{1,0:T(8,128)(2,1)} %refs_0_.4, bf16[2048,1024]{1,0:T(8,128)(2,1)} %refs_4_.1), custom_call_target="tpu_custom_call" | custom-call | flops 40000000000 | bytes 100000000 | tf_op jit(solution)/shard_map/unproject/pallas_call | solution.py:352
  45.3 1.5 %collective-permute-done.5.refs_4_ = bf16[256,512]{1,0:T(8,128)(2,1)S(1)} collective-permute-done((bf16[256,512]{1,0:T(8,128)(2,1)}, bf16[256,512]{1,0:T(8,128)(2,1)S(1)}, u32[]{:S(2)}, u32[]{:S(2)}) %collective-permute-start.5) | collective-permute-done | bytes 262176 | tf_op jit(solution)/shard_map/ppermute | solution.py:425
  46.8 4.0 %all-to-all-done.1 = bf16[8,16,16,128]{3,2,1,0:T(8,128)(2,1)S(1)} async-done(((bf16[8,16,16,128]{3,2,1,0:T(8,128)(2,1)}), bf16[8,16,16,128]{3,2,1,0:T(8,128)(2,1)S(1)}, u32[]{:S(2)}, u32[]{:S(2)}) %all-to-all-start.1) | async-done | bytes 524320 | tf_op jit(solution)/shard_map/all_to_all | solution.py:416
  50.9 3.0 %mix.1 = (bf16[256,1024]{1,0:T(8,128)(2,1)}, bf16[256,1024]{1,0:T(8,128)(2,1)}, bf16[128,16,128]{2,1,0:T(8,128)(2,1)}) custom-call(s32[1]{0:T(128)} %bitcast.flag_ref, bf16[128,16,128]{2,1,0:T(8,128)(2,1)S(1)} %bitcast.24, bf16[256,1024]{1,0:T(8,128)(2,1)S(1)} %copy-done.1, bf16[256,1024]{1,0:T(8,128)(2,1)} %unproject.7.refs_0_, ...), custom_call_target="tpu_custom_call" | custom-call | tf_op jit(solution)/shard_map/mix/pallas_call | solution.py:271
  54.4 3.3 %collective-permute-start.7 = (bf16[256,1024]{1,0:T(8,128)(2,1)}, bf16[256,1024]{1,0:T(8,128)(2,1)S(1)}, u32[]{:S(2)}, u32[]{:S(2)}) collective-permute-start(bf16[256,1024]{1,0:T(8,128)(2,1)} %get-tuple-element.64.refs_0_.refs_2_), channel_id=1, source_target_pairs={{0,3},{1,0},{2,1},{3,2},{4,7},{5,4},{6,5},{7,6},{8,11},{9,8},{10,9... | collective-permute-start | bytes 1572872 | tf_op jit(solution)/shard_map/ppermute | solution.py:425
  57.7 3.5 %all-to-all-start.2 = ((bf16[8,16,16,128]{3,2,1,0:T(8,128)(2,1)}), bf16[8,16,16,128]{3,2,1,0:T(8,128)(2,1)S(1)}, u32[]{:S(2)}, u32[]{:S(2)}) async-start(bf16[8,16,16,128]{3,2,1,0:T(8,128)(2,1)} %bitcast.28), calls=%async_computation.2 | async-start | bytes 1048576 | tf_op jit(solution)/shard_map/all_to_all | solution.py:416
  61.2 9.7 %all-to-all-done.2.pairs_ref = bf16[8,16,16,128]{3,2,1,0:T(8,128)(2,1)S(1)} async-done(((bf16[8,16,16,128]{3,2,1,0:T(8,128)(2,1)}), bf16[8,16,16,128]{3,2,1,0:T(8,128)(2,1)S(1)}, u32[]{:S(2)}, u32[]{:S(2)}) %all-to-all-start.2) | async-done | bytes 524320 | tf_op jit(solution)/shard_map/all_to_all | solution.py:416
  70.9 5.7 %correlate.1 = bf16[8,32,16,128]{3,2,1,0:T(8,128)(2,1)} custom-call(bf16[8,16,16,128]{3,2,1,0:T(8,128)(2,1)S(1)} %all-to-all-done.2.pairs_ref, f32[32,64,256]{2,1,0:T(8,128)} %get-tuple-element.57.signal_ref, f32[32,64,256]{2,1,0:T(8,128)} %get-tuple-element.58.filter_ref, bf16[256,256]{1,0:T(8,128)(2,1)} %constant.87.clone.first_ref, ...), custom_call_target="tpu_custom_call" | custom-call | tf_op jit(solution)/shard_map/correlate/pallas_call | solution.py:180
  77.0 4.4 %all-to-all-start.3 = ((bf16[8,32,16,128]{3,2,1,0:T(8,128)(2,1)}), bf16[8,32,16,128]{3,2,1,0:T(8,128)(2,1)S(1)}, u32[]{:S(2)}, u32[]{:S(2)}) async-start(bf16[8,32,16,128]{3,2,1,0:T(8,128)(2,1)} %correlate.1), calls=%async_computation.3 | async-start | bytes 2097152 | tf_op jit(solution)/shard_map/all_to_all | solution.py:416
  81.4 2.1 %collective-permute-start.8 = (bf16[256,1024]{1,0:T(8,128)(2,1)S(1)}, bf16[256,1024]{1,0:T(8,128)(2,1)}, u32[]{:S(2)}, u32[]{:S(2)}) collective-permute-start(bf16[256,1024]{1,0:T(8,128)(2,1)S(1)} %select_select_fusion), channel_id=1, source_target_pairs={{0,2},{3,1},{2,3},{1,0},{4,6},{7,5},{6,7},{5,4},{8,10},{11,9},{10,... | collective-permute-start | bytes 1572872 | tf_op jit(solution)/shard_map/ppermute | solution.py:508
  83.5 7.7 %project.1 = (bf16[4,128,2048]{2,1,0:T(8,128)(2,1)}, bf16[4,128,2048]{2,1,0:T(8,128)(2,1)}) custom-call(s32[1]{0:T(128)} %bitcast.5.core_ref, bf16[256,1024]{1,0:T(8,128)(2,1)S(1)} %copy-done, bf16[256,1024]{1,0:T(8,128)(2,1)S(1)} %collective-permute-done.6.refs_1_, bf16[256,1024]{1,0:T(8,128)(2,1)S(1)} %copy-done, ...), custom_call_target="tpu_custom_call" | custom-call | tf_op jit(solution)/shard_map/project/pallas_call | solution.py:395
  91.3 4.6 %collective-permute-done.8 = bf16[256,1024]{1,0:T(8,128)(2,1)} collective-permute-done((bf16[256,1024]{1,0:T(8,128)(2,1)S(1)}, bf16[256,1024]{1,0:T(8,128)(2,1)}, u32[]{:S(2)}, u32[]{:S(2)}) %collective-permute-start.8) | collective-permute-done | bytes 524320 | tf_op jit(solution)/shard_map/ppermute | solution.py:508
  95.9 1.0 all-to-all-done.3
  96.8 3.8 %convolution_convert_fusion = bf16[256,2048]{1,0:T(8,128)(2,1)S(1)} fusion(bf16[256,1024]{1,0:T(8,128)(2,1)} %collective-permute-done.8, bf16[2048,1024]{1,0:T(8,128)(2,1)} %refs_4_.1), kind=kOutput, calls=%fused_computation.1 | convolution fusion | flops 1074266112 | bytes 5767168 | tf_op jit(solution)/shard_map/zct,dt->zcd/dot_general | solution.py:439
  103.2 1.7 %collective-permute-start.11 = (bf16[128,2048]{1,0:T(8,128)(2,1)S(1)}, bf16[128,2048]{1,0:T(8,128)(2,1)S(1)}, u32[]{:S(2)}, u32[]{:S(2)}) collective-permute-start(bf16[128,2048]{1,0:T(8,128)(2,1)S(1)} %get-tuple-element.81), channel_id=1, source_target_pairs={{0,24},{4,28},{8,16},{12,20},{16,8},{20,12},{24,0},{28,4},{1,25},{... | collective-permute-start | bytes 1572872 | tf_op jit(solution)/shard_map/ppermute | solution.py:453
  105.4 1.3 %collective-permute-start.13 = (bf16[128,2048]{1,0:T(8,128)(2,1)S(1)}, bf16[128,2048]{1,0:T(8,128)(2,1)S(1)}, u32[]{:S(2)}, u32[]{:S(2)}) collective-permute-start(bf16[128,2048]{1,0:T(8,128)(2,1)S(1)} %get-tuple-element.79), channel_id=1, source_target_pairs={{0,16},{4,20},{8,24},{12,28},{16,0},{20,4},{24,8},{28,12},{1,17},{... | collective-permute-start | bytes 1572872 | tf_op jit(solution)/shard_map/ppermute | solution.py:453
  106.7 3.2 %finish.1 = (bf16[256,1024]{1,0:T(8,128)(2,1)}, bf16[256,1024]{1,0:T(8,128)(2,1)}, f32[256,1024]{1,0:T(8,128)}) custom-call(bf16[256,16,128]{2,1,0:T(8,128)(2,1)S(1)} %bitcast.23, bf16[256,1024]{1,0:T(8,128)(2,1)} %signal_ref.3, bf16[256,1024]{1,0:T(8,128)(2,1)} %gate_ref.5), custom_call_target="tpu_custom_call" | custom-call | tf_op jit(solution)/shard_map/finish/pallas_call | solution.py:304
  109.9 9.0 %collective-permute-done.11 = bf16[128,2048]{1,0:T(8,128)(2,1)S(1)} collective-permute-done((bf16[128,2048]{1,0:T(8,128)(2,1)S(1)}, bf16[128,2048]{1,0:T(8,128)(2,1)S(1)}, u32[]{:S(2)}, u32[]{:S(2)}) %collective-permute-start.11) | collective-permute-done | bytes 524320 | tf_op jit(solution)/shard_map/ppermute | solution.py:453
  118.9 9.9 %collective-permute-done.12 = bf16[128,2048]{1,0:T(8,128)(2,1)S(1)} collective-permute-done((bf16[128,2048]{1,0:T(8,128)(2,1)S(1)}, bf16[128,2048]{1,0:T(8,128)(2,1)S(1)}, u32[]{:S(2)}, u32[]{:S(2)}) %collective-permute-start.12) | collective-permute-done | bytes 524320 | tf_op jit(solution)/shard_map/ppermute | solution.py:453
  129.6 1.3 convert_add_fusion.1
  (29 shorter events, 5.5 us)
Async XLA Ops:
  4.9 12.2 %collective-permute-start = (bf16[256,512]{1,0:T(8,128)(2,1)}, bf16[256,512]{1,0:T(8,128)(2,1)S(1)}, u32[]{:S(2)}, u32[]{:S(2)}) collective-permute-start(bf16[256,512]{1,0:T(8,128)(2,1)} %get-tuple-element.42), channel_id=1, source_target_pairs={{2,0},{1,3},{3,2},{0,1},{6,4},{5,7},{7,6},{4,5},{10,8},{9,11},{11,... | collective-permute-start | bytes 786440 | tf_op jit(solution)/shard_map/ppermute | solution.py:476
  7.9 6.6 %copy-start.3 = (bf16[256,512]{1,0:T(8,128)(2,1)S(1)}, bf16[256,512]{1,0:T(8,128)(2,1)}, u32[]{:S(2)}) copy-start(bf16[256,512]{1,0:T(8,128)(2,1)} %get-tuple-element.48) | copy-start | bytes 786436
  10.7 21.5 %all-to-all-start = ((bf16[8,32,16,128]{3,2,1,0:T(8,128)(2,1)}), bf16[8,32,16,128]{3,2,1,0:T(8,128)(2,1)S(1)}, u32[]{:S(2)}, u32[]{:S(2)}) async-start(bf16[8,32,16,128]{3,2,1,0:T(8,128)(2,1)} %bitcast.25), calls=%async_computation | async-start | bytes 2097152 | tf_op jit(solution)/shard_map/all_to_all | solution.py:416
  14.4 9.6 %collective-permute-start.1 = (bf16[256,512]{1,0:T(8,128)(2,1)S(1)}, bf16[256,512]{1,0:T(8,128)(2,1)S(1)}, u32[]{:S(2)}, u32[]{:S(2)}) collective-permute-start(bf16[256,512]{1,0:T(8,128)(2,1)S(1)} %copy-done.3), channel_id=1, source_target_pairs={{2,0},{1,3},{3,2},{0,1},{6,4},{5,7},{7,6},{4,5},{10,8},{9,11},{11,... | collective-permute-start | bytes 786440 | tf_op jit(solution)/shard_map/ppermute | solution.py:476
  21.4 23.9 %collective-permute-start.4 = (bf16[256,512]{1,0:T(8,128)(2,1)}, bf16[256,512]{1,0:T(8,128)(2,1)S(1)}, u32[]{:S(2)}, u32[]{:S(2)}) collective-permute-start(bf16[256,512]{1,0:T(8,128)(2,1)} %get-tuple-element.46), channel_id=1, source_target_pairs={{0,3},{1,0},{2,1},{3,2},{4,7},{5,4},{6,5},{7,6},{8,11},{9,8},{10,9... | collective-permute-start | bytes 786440 | tf_op jit(solution)/shard_map/ppermute | solution.py:425
  23.4 21.9 %collective-permute-start.2 = (bf16[256,512]{1,0:T(8,128)(2,1)}, bf16[256,512]{1,0:T(8,128)(2,1)S(1)}, u32[]{:S(2)}, u32[]{:S(2)}) collective-permute-start(bf16[256,512]{1,0:T(8,128)(2,1)} %get-tuple-element.53), channel_id=1, source_target_pairs={{0,1},{1,2},{2,3},{3,0},{4,5},{5,6},{6,7},{7,4},{8,9},{9,10},{10,1... | collective-permute-start | bytes 786440 | tf_op jit(solution)/shard_map/ppermute | solution.py:425
  28.4 16.9 %collective-permute-start.3 = (bf16[256,512]{1,0:T(8,128)(2,1)}, bf16[256,512]{1,0:T(8,128)(2,1)S(1)}, u32[]{:S(2)}, u32[]{:S(2)}) collective-permute-start(bf16[256,512]{1,0:T(8,128)(2,1)} %get-tuple-element.54), channel_id=1, source_target_pairs={{0,1},{1,2},{2,3},{3,0},{4,5},{5,6},{6,7},{7,4},{8,9},{9,10},{10,1... | collective-permute-start | bytes 786440 | tf_op jit(solution)/shard_map/ppermute | solution.py:425
  30.5 16.3 %collective-permute-start.5 = (bf16[256,512]{1,0:T(8,128)(2,1)}, bf16[256,512]{1,0:T(8,128)(2,1)S(1)}, u32[]{:S(2)}, u32[]{:S(2)}) collective-permute-start(bf16[256,512]{1,0:T(8,128)(2,1)} %get-tuple-element.49), channel_id=1, source_target_pairs={{0,3},{1,0},{2,1},{3,2},{4,7},{5,4},{6,5},{7,6},{8,11},{9,8},{10,9... | collective-permute-start | bytes 786440 | tf_op jit(solution)/shard_map/ppermute | solution.py:425
  37.3 13.6 %all-to-all-start.1 = ((bf16[8,16,16,128]{3,2,1,0:T(8,128)(2,1)}), bf16[8,16,16,128]{3,2,1,0:T(8,128)(2,1)S(1)}, u32[]{:S(2)}, u32[]{:S(2)}) async-start(bf16[8,16,16,128]{3,2,1,0:T(8,128)(2,1)} %get-tuple-element.51), calls=%async_computation.1 | async-start | bytes 1048576 | tf_op jit(solution)/shard_map/all_to_all | solution.py:416
  41.1 9.7 %copy-start.1 = (bf16[256,1024]{1,0:T(8,128)(2,1)S(1)}, bf16[256,1024]{1,0:T(8,128)(2,1)}, u32[]{:S(2)}) copy-start(bf16[256,1024]{1,0:T(8,128)(2,1)} %gate_ref.4) | copy-start | bytes 1572868
  53.9 22.7 %collective-permute-start.6 = (bf16[256,1024]{1,0:T(8,128)(2,1)}, bf16[256,1024]{1,0:T(8,128)(2,1)S(1)}, u32[]{:S(2)}, u32[]{:S(2)}) collective-permute-start(bf16[256,1024]{1,0:T(8,128)(2,1)} %get-tuple-element.64.refs_0_.refs_2_), channel_id=1, source_target_pairs={{0,1},{1,2},{2,3},{3,0},{4,5},{5,6},{6,7},{7,4},{8,9},{9,10},{10,1... | collective-permute-start | bytes 1572872 | tf_op jit(solution)/shard_map/ppermute | solution.py:425
  54.4 22.5 %collective-permute-start.7 = (bf16[256,1024]{1,0:T(8,128)(2,1)}, bf16[256,1024]{1,0:T(8,128)(2,1)S(1)}, u32[]{:S(2)}, u32[]{:S(2)}) collective-permute-start(bf16[256,1024]{1,0:T(8,128)(2,1)} %get-tuple-element.64.refs_0_.refs_2_), channel_id=1, source_target_pairs={{0,3},{1,0},{2,1},{3,2},{4,7},{5,4},{6,5},{7,6},{8,11},{9,8},{10,9... | collective-permute-start | bytes 1572872 | tf_op jit(solution)/shard_map/ppermute | solution.py:425
  57.7 13.2 %all-to-all-start.2 = ((bf16[8,16,16,128]{3,2,1,0:T(8,128)(2,1)}), bf16[8,16,16,128]{3,2,1,0:T(8,128)(2,1)S(1)}, u32[]{:S(2)}, u32[]{:S(2)}) async-start(bf16[8,16,16,128]{3,2,1,0:T(8,128)(2,1)} %bitcast.28), calls=%async_computation.2 | async-start | bytes 1048576 | tf_op jit(solution)/shard_map/all_to_all | solution.py:416
  70.9 6.0 %copy-start = (bf16[256,1024]{1,0:T(8,128)(2,1)S(1)}, bf16[256,1024]{1,0:T(8,128)(2,1)}, u32[]{:S(2)}) copy-start(bf16[256,1024]{1,0:T(8,128)(2,1)} %get-tuple-element.64.refs_0_.refs_2_) | copy-start | bytes 1572868
  77.0 19.8 %all-to-all-start.3 = ((bf16[8,32,16,128]{3,2,1,0:T(8,128)(2,1)}), bf16[8,32,16,128]{3,2,1,0:T(8,128)(2,1)S(1)}, u32[]{:S(2)}, u32[]{:S(2)}) async-start(bf16[8,32,16,128]{3,2,1,0:T(8,128)(2,1)} %correlate.1), calls=%async_computation.3 | async-start | bytes 2097152 | tf_op jit(solution)/shard_map/all_to_all | solution.py:416
  81.4 14.4 %collective-permute-start.8 = (bf16[256,1024]{1,0:T(8,128)(2,1)S(1)}, bf16[256,1024]{1,0:T(8,128)(2,1)}, u32[]{:S(2)}, u32[]{:S(2)}) collective-permute-start(bf16[256,1024]{1,0:T(8,128)(2,1)S(1)} %select_select_fusion), channel_id=1, source_target_pairs={{0,2},{3,1},{2,3},{1,0},{4,6},{7,5},{6,7},{5,4},{8,10},{11,9},{10,... | collective-permute-start | bytes 1572872 | tf_op jit(solution)/shard_map/ppermute | solution.py:508
  96.8 4.4 %collective-permute-start.9 = (bf16[4,128,2048]{2,1,0:T(8,128)(2,1)}, bf16[4,128,2048]{2,1,0:T(8,128)(2,1)S(1)}, u32[]{:S(2)}, u32[]{:S(2)}) collective-permute-start(bf16[4,128,2048]{2,1,0:T(8,128)(2,1)} %get-tuple-element.69), channel_id=1, source_target_pairs={{0,4},{4,0},{8,12},{12,8},{16,20},{20,16},{24,28},{28,24},{1,5},{5... | collective-permute-start | bytes 6291464 | tf_op jit(solution)/shard_map/ppermute | solution.py:514
  96.8 4.4 %copy-start.2 = (bf16[4,128,2048]{2,1,0:T(8,128)(2,1)S(1)}, bf16[4,128,2048]{2,1,0:T(8,128)(2,1)}, u32[]{:S(2)}) copy-start(bf16[4,128,2048]{2,1,0:T(8,128)(2,1)} %get-tuple-element.67) | copy-start | bytes 6291460
  100.7 2.1 %collective-permute-start.10 = (bf16[1,128,2048]{2,1,0:T(8,128)(2,1)S(1)}, bf16[1,128,2048]{2,1,0:T(8,128)(2,1)S(1)}, u32[]{:S(2)}, u32[]{:S(2)}) collective-permute-start(bf16[1,128,2048]{2,1,0:T(8,128)(2,1)S(1)} %dynamic-slice_bitcast_fusion.4), channel_id=1, source_target_pairs={{0,4},{4,0},{8,12},{12,8},{16,20},{20,16},{24,28},{28,24},{1,5},{5... | collective-permute-start | bytes 1572872 | tf_op jit(solution)/shard_map/ppermute | solution.py:441
  103.2 15.8 %collective-permute-start.11 = (bf16[128,2048]{1,0:T(8,128)(2,1)S(1)}, bf16[128,2048]{1,0:T(8,128)(2,1)S(1)}, u32[]{:S(2)}, u32[]{:S(2)}) collective-permute-start(bf16[128,2048]{1,0:T(8,128)(2,1)S(1)} %get-tuple-element.81), channel_id=1, source_target_pairs={{0,24},{4,28},{8,16},{12,20},{16,8},{20,12},{24,0},{28,4},{1,25},{... | collective-permute-start | bytes 1572872 | tf_op jit(solution)/shard_map/ppermute | solution.py:453
  104.8 24.0 %collective-permute-start.12 = (bf16[128,2048]{1,0:T(8,128)(2,1)S(1)}, bf16[128,2048]{1,0:T(8,128)(2,1)S(1)}, u32[]{:S(2)}, u32[]{:S(2)}) collective-permute-start(bf16[128,2048]{1,0:T(8,128)(2,1)S(1)} %get-tuple-element.80), channel_id=1, source_target_pairs={{0,8},{4,12},{8,0},{12,4},{16,24},{20,28},{24,16},{28,20},{1,9},{5... | collective-permute-start | bytes 1572872 | tf_op jit(solution)/shard_map/ppermute | solution.py:453
  105.4 24.2 %collective-permute-start.13 = (bf16[128,2048]{1,0:T(8,128)(2,1)S(1)}, bf16[128,2048]{1,0:T(8,128)(2,1)S(1)}, u32[]{:S(2)}, u32[]{:S(2)}) collective-permute-start(bf16[128,2048]{1,0:T(8,128)(2,1)S(1)} %get-tuple-element.79), channel_id=1, source_target_pairs={{0,16},{4,20},{8,24},{12,28},{16,0},{20,4},{24,8},{28,12},{1,17},{... | collective-permute-start | bytes 1572872 | tf_op jit(solution)/shard_map/ppermute | solution.py:453

commit v8 on v7

--- a/solution.py
+++ b/solution.py
@@ -231,11 +231,10 @@
     )(*held_in_hbm(inner_gate, signal, long_filter))
 
 
-def mix_kernel(parts, flag_ref, conv_ref, gate_ref, *refs):
-    *share_refs, mixed_ref, outer_ref, grad_ref, lines, grads = refs
+def regard_kernel(parts, flag_ref, gate_ref, *refs):
+    *share_refs, sum_ref, grad_ref, grads = refs
     rows, length = gate_ref.shape
     per = length // LANES
-    lines[...] = wide(conv_ref[...].reshape(rows * per, LANES))
     groups = []
     for count in parts:
         groups.append(share_refs[:count])
@@ -247,41 +246,65 @@
             held = group[lane * len(group) // per]
             at = lane % (per // len(group)) * LANES
             shares.append(wide(held[:, at : at + LANES]))
-        conv = lines[pl.ds(lane, rows, stride=per), :]
-        gate = wide(gate_ref[:, cols])
-        mixed_ref[:, cols] = short(conv * gate)
         grad_mix = shares[0]
         for share in shares[1:-1]:
             grad_mix = grad_mix + share
         grad_mix = grad_mix + jnp.where(flag_ref[0] != 0, shares[-1], jnp.zeros_like(shares[-1]))
-        outer_ref[:, cols] = short(grad_mix * conv)
-        grads[pl.ds(lane, rows, stride=per), :] = grad_mix * gate
+        sum_ref[:, cols] = grad_mix
+        grads[pl.ds(lane, rows, stride=per), :] = grad_mix * wide(gate_ref[:, cols])
     grad_ref[...] = short(grads[...]).reshape(grad_ref.shape)
 
 
-def mix(conv, outer_gate, shares, flag):
+def regard(outer_gate, shares, flag):
     rows, length = outer_gate.shape
     parts = [len(share) for share in shares]
     cuts = [cut for share in shares for cut in share]
     per = length // LANES
-    conv = conv.reshape(rows * per // 16, 16, LANES)
     step = rows // 2
     token_rows = pl.BlockSpec((step, length), lambda i, at: (i, 0))
-    lane_rows = pl.BlockSpec((step * per // 16, 16, LANES), lambda i, at: (i, 0, 0))
-    return pl.pallas_call(
-        functools.partial(mix_kernel, parts),
+    return pl.pallas_call(
+        functools.partial(regard_kernel, parts),
         grid_spec=pltpu.PrefetchScalarGridSpec(
             num_scalar_prefetch=1,
             grid=(2,),
-            in_specs=[lane_rows, token_rows]
+            in_specs=[token_rows]
             + [pl.BlockSpec((step, cut.shape[1]), lambda i, at: (i, 0)) for cut in cuts],
-            out_specs=[token_rows, token_rows, lane_rows],
-            scratch_shapes=[pltpu.VMEM((step * per, LANES), jnp.float32)] * 2,
+            out_specs=[token_rows, pl.BlockSpec((step * per // 16, 16, LANES), lambda i, at: (i, 0, 0))],
+            scratch_shapes=[pltpu.VMEM((step * per, LANES), jnp.float32)],
         ),
-        out_shape=[in_hbm((rows, length))] * 2 + [in_hbm((rows * per // 16, 16, LANES))],
+        out_shape=[in_hbm((rows, length), jnp.float32), in_hbm((rows * per // 16, 16, LANES))],
+        compiler_params=params(),
+        name="regard",
+    )(flag.astype(jnp.int32).reshape(1), outer_gate, *cuts)
+
+
+def mix_kernel(conv_ref, gate_ref, mixed_ref, out_ref, lines):
+    rows, length = gate_ref.shape
+    per = length // LANES
+    lines[...] = wide(conv_ref[...].reshape(rows * per, LANES))
+    for lane in range(per):
+        cols = slice(lane * LANES, (lane + 1) * LANES)
+        conv = lines[pl.ds(lane, rows, stride=per), :]
+        out_ref[:, cols] = short(conv)
+        mixed_ref[:, cols] = short(conv * wide(gate_ref[:, cols]))
+
+
+def mix(conv, outer_gate):
+    rows, length = outer_gate.shape
+    per = length // LANES
+    conv = conv.reshape(rows * per // 16, 16, LANES)
+    step = rows // 2
+    token_rows = pl.BlockSpec((step, length), lambda i: (i, 0))
+    return pl.pallas_call(
+        mix_kernel,
+        grid=(2,),
+        in_specs=[pl.BlockSpec((step * per // 16, 16, LANES), lambda i: (i, 0, 0)), token_rows],
+        out_specs=[token_rows, token_rows],
+        out_shape=[in_hbm((rows, length))] * 2,
+        scratch_shapes=[pltpu.VMEM((step * per, LANES), jnp.float32)],
         compiler_params=params(),
         name="mix",
-    )(flag.astype(jnp.int32).reshape(1), conv, outer_gate, *cuts)
+    )(conv, outer_gate)
 
 
 def finish_kernel(corr_ref, signal_ref, gate_ref, inner_ref, signal_out_ref, filter_ref, lines):
@@ -498,15 +521,16 @@
     conv, spec_signal, spec_filter = convolve(sent, tables)
     own = unproject(tie(out_proj, conv), grad_output, [0], line, chan_count)
     shares = [held_in_hbm(*own), *shares]
-    mixed, grad_outer, grad_conv = mix(exchange(conv), outer_gate, shares, flag)
+    grad_mix, grad_conv = regard(outer_gate, shares, flag)
+    mixed, conv_out = mix(tie(exchange(conv), grad_conv), outer_gate)
     held = gather_first(mixed)
-    grad_conv = grad_conv.reshape(seq_count, owned // 2, 2 * per, LANES)
+    grad_conv = tie(grad_conv, mixed).reshape(seq_count, owned // 2, 2 * per, LANES)
     corr = correlate(exchange(grad_conv), spec_signal, spec_filter, tables)
     held = tie(held, corr)
     if chan_count == 4:
         passed = lax.select_n(line, held[0], held[2], held[1], held[0])
         middle = lax.ppermute(passed, "chan", [(0, 2), (3, 1), (2, 3), (1, 0)])
-        corr = exchange(tie(corr, passed))
+        corr = exchange(corr)
         held = tie(held, passed)
         core = lax.axis_index("seq") % 2
         other, mine = project([held[0], held[1], held[0], held[2]], grad_output, core)
@@ -520,6 +544,7 @@
         total = both_cores(held, grad_output)
     parts = scatter_chips(total)
     grads = finish(tie(corr, parts[-1]), signal, inner_gate)
+    grad_outer = short(tie(grad_mix, corr) * wide(conv_out))
     return (grad_outer, *grads, sum_of(tie(parts, grads)))
 
 

time: 131 us -> 130 us (level)
  waiting for transfers between devices: 42.1 us -> 39.1 us
    all_to_all x4, waiting for transfers between devices: 14.7 us -> 7.19 us  [exchange(): lax.all_to_all(blocks, 'seq', split_axis=0, concat_axis=0, tiled=True)]
    ppermute x6, waiting for transfers between devices: 1.84 us -> 8.43 us  [shift(): lax.ppermute(block, 'chan', [(i, (i + by) % count) for i in range(count)])]
    pallas_call x1 -> x2, Pallas kernels: 2.99 us -> 3.83 us  [the longest x1 2.63 us: regard(): pl.pallas_call(functools.partial(regard_kernel, parts), grid_spec=pltpu.P...]
  transfers between devices with their start and end apart: 18 -> 18, of which waited for: 11 -> 9; matrix products, arithmetic and copies ran while one was open for 4% -> 4% of each run, Pallas kernels for 29% -> 31%
where the time goes in v8:
time: 130 us; the launch traced here: 129 us
  Pallas kernels  45.3 us (35%)
  waiting for transfers between devices  39.1 us (30%)
  starting transfers between devices  36.6 us (28%)
  matrix products  3.78 us (3%)
  other arithmetic  3.24 us (2%)
    ppermute x3, waiting for transfers between devices, scatter_chips(): lax.ppermute(block(bit), 'seq', swaps(count, 2 * bit))  18.8 us
    pallas_call x4, Pallas kernels, unproject(): pl.pallas_call(functools.partial(unproject_kernel, len(offsets), splits,...  17 us
    all_to_all x4, starting transfers between devices, exchange(): lax.all_to_all(blocks, 'seq', split_axis=0, concat_axis=0, tiled=True)  14.7 us
    ppermute x6, starting transfers between devices, shift(): lax.ppermute(block, 'chan', [(i, (i + by) % count) for i in range(count)])  9.73 us
    ppermute x6, waiting for transfers between devices, shift(): lax.ppermute(block, 'chan', [(i, (i + by) % count) for i in range(count)])  8.43 us
    pallas_call x1, Pallas kernels, project(): pl.pallas_call(project_kernel, grid_spec=pltpu.PrefetchScalarGridSpec(num...  7.72 us
    all_to_all x4, waiting for transfers between devices, exchange(): lax.all_to_all(blocks, 'seq', split_axis=0, concat_axis=0, tiled=True)  7.19 us
    ppermute x2, starting transfers between devices, body(): lax.ppermute(far, 'chan', [(2, 0), (1, 3), (3, 2), (0, 1)])  5.67 us
  transfers between devices with their start and end apart: 18, of which 9 were waited for; matrix products, arithmetic and copies ran while one was open for 4% of the time, Pallas kernels for 31%

profile of v8, /device:TPU:0, one launch (start us, length us, event | category | flops | bytes accessed | tf_op | source)
XLA Modules:
  0.0 129.1 jit_solution(8920353090426640535)
XLA Ops:
  0.6 4.2 %unproject.4 = (bf16[256,512]{1,0:T(8,128)(2,1)}, bf16[256,512]{1,0:T(8,128)(2,1)}) custom-call(s32[1]{0:T(128)} %bitcast.1.place_ref, bf16[1024,2048]{1,0:T(8,128)(2,1)} %refs_0_.4, bf16[2048,1024]{1,0:T(8,128)(2,1)} %refs_4_.1), custom_call_target="tpu_custom_call" | custom-call | flops 40000000000 | bytes 100000000 | tf_op jit(solution)/shard_map/unproject/pallas_call | solution.py:375
  4.9 3.0 %collective-permute-start = (bf16[256,512]{1,0:T(8,128)(2,1)}, bf16[256,512]{1,0:T(8,128)(2,1)S(1)}, u32[]{:S(2)}, u32[]{:S(2)}) collective-permute-start(bf16[256,512]{1,0:T(8,128)(2,1)} %get-tuple-element.45), channel_id=1, source_target_pairs={{2,0},{1,3},{3,2},{0,1},{6,4},{5,7},{7,6},{4,5},{10,8},{9,11},{11,... | collective-permute-start | bytes 786440 | tf_op jit(solution)/shard_map/ppermute | solution.py:499
  7.9 2.8 %prepare.1 = bf16[256,16,128]{2,1,0:T(8,128)(2,1)} custom-call(bf16[256,1024]{1,0:T(8,128)(2,1)} %gate_ref.7, bf16[256,1024]{1,0:T(8,128)(2,1)} %signal_ref.3, bf16[256,1024]{1,0:T(8,128)(2,1)} %filter_ref), custom_call_target="tpu_custom_call" | custom-call | tf_op jit(solution)/shard_map/prepare/pallas_call | solution.py:222
  10.7 3.7 %all-to-all-start = ((bf16[8,32,16,128]{3,2,1,0:T(8,128)(2,1)}), bf16[8,32,16,128]{3,2,1,0:T(8,128)(2,1)S(1)}, u32[]{:S(2)}, u32[]{:S(2)}) async-start(bf16[8,32,16,128]{3,2,1,0:T(8,128)(2,1)} %bitcast.25), calls=%async_computation | async-start | bytes 2097152 | tf_op jit(solution)/shard_map/all_to_all | solution.py:439
  14.4 2.6 %collective-permute-start.1 = (bf16[256,512]{1,0:T(8,128)(2,1)S(1)}, bf16[256,512]{1,0:T(8,128)(2,1)S(1)}, u32[]{:S(2)}, u32[]{:S(2)}) collective-permute-start(bf16[256,512]{1,0:T(8,128)(2,1)S(1)} %copy-done.5), channel_id=1, source_target_pairs={{2,0},{1,3},{3,2},{0,1},{6,4},{5,7},{7,6},{4,5},{10,8},{9,11},{11,... | collective-permute-start | bytes 786440 | tf_op jit(solution)/shard_map/ppermute | solution.py:499
  17.1 4.3 %unproject.5 = (bf16[256,512]{1,0:T(8,128)(2,1)}, bf16[256,512]{1,0:T(8,128)(2,1)}) custom-call(s32[1]{0:T(128)} %bitcast.1.place_ref, bf16[1024,2048]{1,0:T(8,128)(2,1)} %refs_0_.4, bf16[1024,2048]{1,0:T(8,128)(2,1)} %refs_0_.4, bf16[2048,1024]{1,0:T(8,128)(2,1)} %refs_4_.1, bf16[256,512]{1,0:T(8,128)(2,1)S(1)} %collective-permute-done.refs_3_.refs_5_), custom_call_target="tpu_custom_call" | custom-call | flops 40000000000 | bytes 100000000 | tf_op jit(solution)/shard_map/unproject/pallas_call | solution.py:375
  21.4 2.0 %collective-permute-start.4 = (bf16[256,512]{1,0:T(8,128)(2,1)}, bf16[256,512]{1,0:T(8,128)(2,1)S(1)}, u32[]{:S(2)}, u32[]{:S(2)}) collective-permute-start(bf16[256,512]{1,0:T(8,128)(2,1)} %get-tuple-element.49), channel_id=1, source_target_pairs={{0,3},{1,0},{2,1},{3,2},{4,7},{5,4},{6,5},{7,6},{8,11},{9,8},{10,9... | collective-permute-start | bytes 786440 | tf_op jit(solution)/shard_map/ppermute | solution.py:448
  24.1 4.3 %unproject.6 = (bf16[256,512]{1,0:T(8,128)(2,1)}, bf16[256,512]{1,0:T(8,128)(2,1)}) custom-call(s32[1]{0:T(128)} %bitcast.1.place_ref, bf16[1024,2048]{1,0:T(8,128)(2,1)} %refs_0_.4, bf16[1024,2048]{1,0:T(8,128)(2,1)} %refs_0_.4, bf16[2048,1024]{1,0:T(8,128)(2,1)} %refs_4_.1, bf16[256,512]{1,0:T(8,128)(2,1)S(1)} %collective-permute-done.1.refs_3_.refs_6_), custom_call_target="tpu_custom_call" | custom-call | flops 40000000000 | bytes 100000000 | tf_op jit(solution)/shard_map/unproject/pallas_call | solution.py:375
  28.4 2.1 %collective-permute-start.3 = (bf16[256,512]{1,0:T(8,128)(2,1)}, bf16[256,512]{1,0:T(8,128)(2,1)S(1)}, u32[]{:S(2)}, u32[]{:S(2)}) collective-permute-start(bf16[256,512]{1,0:T(8,128)(2,1)} %get-tuple-element.57), channel_id=1, source_target_pairs={{0,1},{1,2},{2,3},{3,0},{4,5},{5,6},{6,7},{7,4},{8,9},{9,10},{10,1... | collective-permute-start | bytes 786440 | tf_op jit(solution)/shard_map/ppermute | solution.py:448
  30.5 1.7 %collective-permute-start.5 = (bf16[256,512]{1,0:T(8,128)(2,1)}, bf16[256,512]{1,0:T(8,128)(2,1)S(1)}, u32[]{:S(2)}, u32[]{:S(2)}) collective-permute-start(bf16[256,512]{1,0:T(8,128)(2,1)} %get-tuple-element.52), channel_id=1, source_target_pairs={{0,3},{1,0},{2,1},{3,2},{4,7},{5,4},{6,5},{7,6},{8,11},{9,8},{10,9... | collective-permute-start | bytes 786440 | tf_op jit(solution)/shard_map/ppermute | solution.py:448
  32.2 5.1 %convolve.1 = (bf16[8,16,16,128]{3,2,1,0:T(8,128)(2,1)}, f32[32,64,256]{2,1,0:T(8,128)}, f32[32,64,256]{2,1,0:T(8,128)}) custom-call(bf16[8,32,16,128]{3,2,1,0:T(8,128)(2,1)S(1)} %all-to-all-done.pairs_ref, bf16[256,256]{1,0:T(8,128)(2,1)} %constant.87.clone.first_ref, bf16[256,256]{1,0:T(8,128)(2,1)} %constant.88.clone.forward_ref, ...), custom_call_target="tpu_custom_call" | custom-call | tf_op jit(solution)/shard_map/convolve/pallas_call | solution.py:154
  37.3 3.8 %all-to-all-start.1 = ((bf16[8,16,16,128]{3,2,1,0:T(8,128)(2,1)}), bf16[8,16,16,128]{3,2,1,0:T(8,128)(2,1)S(1)}, u32[]{:S(2)}, u32[]{:S(2)}) async-start(bf16[8,16,16,128]{3,2,1,0:T(8,128)(2,1)} %get-tuple-element.54), calls=%async_computation.1 | async-start | bytes 1048576 | tf_op jit(solution)/shard_map/all_to_all | solution.py:439
  41.1 4.2 %unproject.7.refs_0_ = bf16[256,1024]{1,0:T(8,128)(2,1)} custom-call(s32[1]{0:T(128)} %bitcast.1.place_ref, bf16[1024,2048]{1,0:T(8,128)(2,1)} %refs_0_.4, bf16[2048,1024]{1,0:T(8,128)(2,1)} %refs_4_.1), custom_call_target="tpu_custom_call" | custom-call | flops 40000000000 | bytes 100000000 | tf_op jit(solution)/shard_map/unproject/pallas_call | solution.py:375
  45.3 1.5 %collective-permute-done.5.refs_4_ = bf16[256,512]{1,0:T(8,128)(2,1)S(1)} collective-permute-done((bf16[256,512]{1,0:T(8,128)(2,1)}, bf16[256,512]{1,0:T(8,128)(2,1)S(1)}, u32[]{:S(2)}, u32[]{:S(2)}) %collective-permute-start.5) | collective-permute-done | bytes 262176 | tf_op jit(solution)/shard_map/ppermute | solution.py:448
  46.8 2.6 %regard.1 = (f32[256,1024]{1,0:T(8,128)}, bf16[128,16,128]{2,1,0:T(8,128)(2,1)}) custom-call(s32[1]{0:T(128)} %bitcast.flag_ref, bf16[256,1024]{1,0:T(8,128)(2,1)S(1)} %copy-done.1, bf16[256,1024]{1,0:T(8,128)(2,1)} %unproject.7.refs_0_, bf16[256,512]{1,0:T(8,128)(2,1)S(1)} %collective-permute-done.2.refs_1_, ...), custom_call_target="tpu_custom_call" | custom-call | tf_op jit(solution)/shard_map/regard/pallas_call | solution.py:265
  49.5 1.4 %all-to-all-done.1 = bf16[8,16,16,128]{3,2,1,0:T(8,128)(2,1)S(1)} async-done(((bf16[8,16,16,128]{3,2,1,0:T(8,128)(2,1)}), bf16[8,16,16,128]{3,2,1,0:T(8,128)(2,1)S(1)}, u32[]{:S(2)}, u32[]{:S(2)}) %all-to-all-start.1) | async-done | bytes 524320 | tf_op jit(solution)/shard_map/all_to_all | solution.py:439
  50.9 1.2 mix.1
  52.1 3.5 %all-to-all-start.2 = ((bf16[8,16,16,128]{3,2,1,0:T(8,128)(2,1)}), bf16[8,16,16,128]{3,2,1,0:T(8,128)(2,1)S(1)}, u32[]{:S(2)}, u32[]{:S(2)}) async-start(bf16[8,16,16,128]{3,2,1,0:T(8,128)(2,1)} %bitcast.28), calls=%async_computation.2 | async-start | bytes 1048576 | tf_op jit(solution)/shard_map/all_to_all | solution.py:439
  56.2 3.3 %collective-permute-start.7 = (bf16[256,1024]{1,0:T(8,128)(2,1)}, bf16[256,1024]{1,0:T(8,128)(2,1)S(1)}, u32[]{:S(2)}, u32[]{:S(2)}) collective-permute-start(bf16[256,1024]{1,0:T(8,128)(2,1)} %get-tuple-element.70.refs_0_.refs_2_), channel_id=1, source_target_pairs={{0,3},{1,0},{2,1},{3,2},{4,7},{5,4},{6,5},{7,6},{8,11},{9,8},{10,9... | collective-permute-start | bytes 1572872 | tf_op jit(solution)/shard_map/ppermute | solution.py:448
  59.4 5.8 %all-to-all-done.2.pairs_ref = bf16[8,16,16,128]{3,2,1,0:T(8,128)(2,1)S(1)} async-done(((bf16[8,16,16,128]{3,2,1,0:T(8,128)(2,1)}), bf16[8,16,16,128]{3,2,1,0:T(8,128)(2,1)S(1)}, u32[]{:S(2)}, u32[]{:S(2)}) %all-to-all-start.2) | async-done | bytes 524320 | tf_op jit(solution)/shard_map/all_to_all | solution.py:439
  65.2 5.7 %correlate.1 = bf16[8,32,16,128]{3,2,1,0:T(8,128)(2,1)} custom-call(bf16[8,16,16,128]{3,2,1,0:T(8,128)(2,1)S(1)} %all-to-all-done.2.pairs_ref, f32[32,64,256]{2,1,0:T(8,128)} %get-tuple-element.63.signal_ref, f32[32,64,256]{2,1,0:T(8,128)} %get-tuple-element.64.filter_ref, bf16[256,256]{1,0:T(8,128)(2,1)} %constant.87.clone.first_ref, ...), custom_call_target="tpu_custom_call" | custom-call | tf_op jit(solution)/shard_map/correlate/pallas_call | solution.py:180
  70.9 3.7 %all-to-all-start.3 = ((bf16[8,32,16,128]{3,2,1,0:T(8,128)(2,1)}), bf16[8,32,16,128]{3,2,1,0:T(8,128)(2,1)S(1)}, u32[]{:S(2)}, u32[]{:S(2)}) async-start(bf16[8,32,16,128]{3,2,1,0:T(8,128)(2,1)} %correlate.1), calls=%async_computation.3 | async-start | bytes 2097152 | tf_op jit(solution)/shard_map/all_to_all | solution.py:439
  74.6 6.9 %collective-permute-done.7.refs_3_ = bf16[256,1024]{1,0:T(8,128)(2,1)S(1)} collective-permute-done((bf16[256,1024]{1,0:T(8,128)(2,1)}, bf16[256,1024]{1,0:T(8,128)(2,1)S(1)}, u32[]{:S(2)}, u32[]{:S(2)}) %collective-permute-start.7) | collective-permute-done | bytes 524320 | tf_op jit(solution)/shard_map/ppermute | solution.py:448
  81.6 2.4 %collective-permute-start.8 = (bf16[256,1024]{1,0:T(8,128)(2,1)S(1)}, bf16[256,1024]{1,0:T(8,128)(2,1)}, u32[]{:S(2)}, u32[]{:S(2)}) collective-permute-start(bf16[256,1024]{1,0:T(8,128)(2,1)S(1)} %select_select_fusion), channel_id=1, source_target_pairs={{0,2},{3,1},{2,3},{1,0},{4,6},{7,5},{6,7},{5,4},{8,10},{11,9},{10,... | collective-permute-start | bytes 1572872 | tf_op jit(solution)/shard_map/ppermute | solution.py:532
  84.0 7.7 %project.1 = (bf16[4,128,2048]{2,1,0:T(8,128)(2,1)}, bf16[4,128,2048]{2,1,0:T(8,128)(2,1)}) custom-call(s32[1]{0:T(128)} %bitcast.5.core_ref, bf16[256,1024]{1,0:T(8,128)(2,1)S(1)} %copy-done, bf16[256,1024]{1,0:T(8,128)(2,1)S(1)} %collective-permute-done.6.refs_1_, bf16[256,1024]{1,0:T(8,128)(2,1)S(1)} %copy-done, ...), custom_call_target="tpu_custom_call" | custom-call | tf_op jit(solution)/shard_map/project/pallas_call | solution.py:418
  91.7 3.3 %collective-permute-done.8 = bf16[256,1024]{1,0:T(8,128)(2,1)} collective-permute-done((bf16[256,1024]{1,0:T(8,128)(2,1)S(1)}, bf16[256,1024]{1,0:T(8,128)(2,1)}, u32[]{:S(2)}, u32[]{:S(2)}) %collective-permute-start.8) | collective-permute-done | bytes 524320 | tf_op jit(solution)/shard_map/ppermute | solution.py:532
  95.0 3.8 %convolution_convert_fusion = bf16[256,2048]{1,0:T(8,128)(2,1)S(1)} fusion(bf16[256,1024]{1,0:T(8,128)(2,1)} %collective-permute-done.8, bf16[2048,1024]{1,0:T(8,128)(2,1)} %refs_4_.1), kind=kOutput, calls=%fused_computation.1 | convolution fusion | flops 1074266112 | bytes 5767168 | tf_op jit(solution)/shard_map/zct,dt->zcd/dot_general | solution.py:462
  101.4 2.4 %collective-permute-start.11 = (bf16[128,2048]{1,0:T(8,128)(2,1)S(1)}, bf16[128,2048]{1,0:T(8,128)(2,1)S(1)}, u32[]{:S(2)}, u32[]{:S(2)}) collective-permute-start(bf16[128,2048]{1,0:T(8,128)(2,1)S(1)} %get-tuple-element.87), channel_id=1, source_target_pairs={{0,24},{4,28},{8,16},{12,20},{16,8},{20,12},{24,0},{28,4},{1,25},{... | collective-permute-start | bytes 1572872 | tf_op jit(solution)/shard_map/ppermute | solution.py:476
  105.9 3.2 %finish.1 = (bf16[256,1024]{1,0:T(8,128)(2,1)}, bf16[256,1024]{1,0:T(8,128)(2,1)}, f32[256,1024]{1,0:T(8,128)}) custom-call(bf16[256,16,128]{2,1,0:T(8,128)(2,1)S(1)} %bitcast.23, bf16[256,1024]{1,0:T(8,128)(2,1)} %signal_ref.3, bf16[256,1024]{1,0:T(8,128)(2,1)} %gate_ref.7), custom_call_target="tpu_custom_call" | custom-call | tf_op jit(solution)/shard_map/finish/pallas_call | solution.py:327
  109.0 8.1 %collective-permute-done.11 = bf16[128,2048]{1,0:T(8,128)(2,1)S(1)} collective-permute-done((bf16[128,2048]{1,0:T(8,128)(2,1)S(1)}, bf16[128,2048]{1,0:T(8,128)(2,1)S(1)}, u32[]{:S(2)}, u32[]{:S(2)}) %collective-permute-start.11) | collective-permute-done | bytes 524320 | tf_op jit(solution)/shard_map/ppermute | solution.py:476
  117.1 10.7 %collective-permute-done.12 = bf16[128,2048]{1,0:T(8,128)(2,1)S(1)} collective-permute-done((bf16[128,2048]{1,0:T(8,128)(2,1)S(1)}, bf16[128,2048]{1,0:T(8,128)(2,1)S(1)}, u32[]{:S(2)}, u32[]{:S(2)}) %collective-permute-start.12) | collective-permute-done | bytes 524320 | tf_op jit(solution)/shard_map/ppermute | solution.py:476
  127.8 1.3 %convert_add_fusion.1 = f32[128,2048]{1,0:T(8,128)} fusion(bf16[128,2048]{1,0:T(8,128)(2,1)S(1)} %get-tuple-element.84, bf16[128,2048]{1,0:T(8,128)(2,1)S(1)} %collective-permute-done.13, bf16[128,2048]{1,0:T(8,128)(2,1)S(1)} %collective-permute-done.12, bf16[128,2048]{1,0:T(8,128)(2,1)S(1)} %collective-permute-done.11), kind=kLoop, calls=%fused_computation.4 | loop fusion | flops 1835008 | bytes 3145728 | tf_op jit(solution)/shard_map/add | solution.py:482
  (35 shorter events, 6.0 us)
Async XLA Ops:
  4.9 12.2 %collective-permute-start = (bf16[256,512]{1,0:T(8,128)(2,1)}, bf16[256,512]{1,0:T(8,128)(2,1)S(1)}, u32[]{:S(2)}, u32[]{:S(2)}) collective-permute-start(bf16[256,512]{1,0:T(8,128)(2,1)} %get-tuple-element.45), channel_id=1, source_target_pairs={{2,0},{1,3},{3,2},{0,1},{6,4},{5,7},{7,6},{4,5},{10,8},{9,11},{11,... | collective-permute-start | bytes 786440 | tf_op jit(solution)/shard_map/ppermute | solution.py:499
  7.9 6.6 %copy-start.5 = (bf16[256,512]{1,0:T(8,128)(2,1)S(1)}, bf16[256,512]{1,0:T(8,128)(2,1)}, u32[]{:S(2)}) copy-start(bf16[256,512]{1,0:T(8,128)(2,1)} %get-tuple-element.51) | copy-start | bytes 786436
  10.7 21.5 %all-to-all-start = ((bf16[8,32,16,128]{3,2,1,0:T(8,128)(2,1)}), bf16[8,32,16,128]{3,2,1,0:T(8,128)(2,1)S(1)}, u32[]{:S(2)}, u32[]{:S(2)}) async-start(bf16[8,32,16,128]{3,2,1,0:T(8,128)(2,1)} %bitcast.25), calls=%async_computation | async-start | bytes 2097152 | tf_op jit(solution)/shard_map/all_to_all | solution.py:439
  14.4 9.6 %collective-permute-start.1 = (bf16[256,512]{1,0:T(8,128)(2,1)S(1)}, bf16[256,512]{1,0:T(8,128)(2,1)S(1)}, u32[]{:S(2)}, u32[]{:S(2)}) collective-permute-start(bf16[256,512]{1,0:T(8,128)(2,1)S(1)} %copy-done.5), channel_id=1, source_target_pairs={{2,0},{1,3},{3,2},{0,1},{6,4},{5,7},{7,6},{4,5},{10,8},{9,11},{11,... | collective-permute-start | bytes 786440 | tf_op jit(solution)/shard_map/ppermute | solution.py:499
  21.4 23.9 %collective-permute-start.4 = (bf16[256,512]{1,0:T(8,128)(2,1)}, bf16[256,512]{1,0:T(8,128)(2,1)S(1)}, u32[]{:S(2)}, u32[]{:S(2)}) collective-permute-start(bf16[256,512]{1,0:T(8,128)(2,1)} %get-tuple-element.49), channel_id=1, source_target_pairs={{0,3},{1,0},{2,1},{3,2},{4,7},{5,4},{6,5},{7,6},{8,11},{9,8},{10,9... | collective-permute-start | bytes 786440 | tf_op jit(solution)/shard_map/ppermute | solution.py:448
  23.4 21.9 %collective-permute-start.2 = (bf16[256,512]{1,0:T(8,128)(2,1)}, bf16[256,512]{1,0:T(8,128)(2,1)S(1)}, u32[]{:S(2)}, u32[]{:S(2)}) collective-permute-start(bf16[256,512]{1,0:T(8,128)(2,1)} %get-tuple-element.56), channel_id=1, source_target_pairs={{0,1},{1,2},{2,3},{3,0},{4,5},{5,6},{6,7},{7,4},{8,9},{9,10},{10,1... | collective-permute-start | bytes 786440 | tf_op jit(solution)/shard_map/ppermute | solution.py:448
  28.4 16.9 %collective-permute-start.3 = (bf16[256,512]{1,0:T(8,128)(2,1)}, bf16[256,512]{1,0:T(8,128)(2,1)S(1)}, u32[]{:S(2)}, u32[]{:S(2)}) collective-permute-start(bf16[256,512]{1,0:T(8,128)(2,1)} %get-tuple-element.57), channel_id=1, source_target_pairs={{0,1},{1,2},{2,3},{3,0},{4,5},{5,6},{6,7},{7,4},{8,9},{9,10},{10,1... | collective-permute-start | bytes 786440 | tf_op jit(solution)/shard_map/ppermute | solution.py:448
  30.5 16.3 %collective-permute-start.5 = (bf16[256,512]{1,0:T(8,128)(2,1)}, bf16[256,512]{1,0:T(8,128)(2,1)S(1)}, u32[]{:S(2)}, u32[]{:S(2)}) collective-permute-start(bf16[256,512]{1,0:T(8,128)(2,1)} %get-tuple-element.52), channel_id=1, source_target_pairs={{0,3},{1,0},{2,1},{3,2},{4,7},{5,4},{6,5},{7,6},{8,11},{9,8},{10,9... | collective-permute-start | bytes 786440 | tf_op jit(solution)/shard_map/ppermute | solution.py:448
  37.3 13.6 %all-to-all-start.1 = ((bf16[8,16,16,128]{3,2,1,0:T(8,128)(2,1)}), bf16[8,16,16,128]{3,2,1,0:T(8,128)(2,1)S(1)}, u32[]{:S(2)}, u32[]{:S(2)}) async-start(bf16[8,16,16,128]{3,2,1,0:T(8,128)(2,1)} %get-tuple-element.54), calls=%async_computation.1 | async-start | bytes 1048576 | tf_op jit(solution)/shard_map/all_to_all | solution.py:439
  41.1 5.7 %copy-start.1 = (bf16[256,1024]{1,0:T(8,128)(2,1)S(1)}, bf16[256,1024]{1,0:T(8,128)(2,1)}, u32[]{:S(2)}) copy-start(bf16[256,1024]{1,0:T(8,128)(2,1)} %gate_ref.6) | copy-start | bytes 1572868
  52.1 13.2 %all-to-all-start.2 = ((bf16[8,16,16,128]{3,2,1,0:T(8,128)(2,1)}), bf16[8,16,16,128]{3,2,1,0:T(8,128)(2,1)S(1)}, u32[]{:S(2)}, u32[]{:S(2)}) async-start(bf16[8,16,16,128]{3,2,1,0:T(8,128)(2,1)} %bitcast.28), calls=%async_computation.2 | async-start | bytes 1048576 | tf_op jit(solution)/shard_map/all_to_all | solution.py:439
  55.6 19.1 %collective-permute-start.6 = (bf16[256,1024]{1,0:T(8,128)(2,1)}, bf16[256,1024]{1,0:T(8,128)(2,1)S(1)}, u32[]{:S(2)}, u32[]{:S(2)}) collective-permute-start(bf16[256,1024]{1,0:T(8,128)(2,1)} %get-tuple-element.70.refs_0_.refs_2_), channel_id=1, source_target_pairs={{0,1},{1,2},{2,3},{3,0},{4,5},{5,6},{6,7},{7,4},{8,9},{9,10},{10,1... | collective-permute-start | bytes 1572872 | tf_op jit(solution)/shard_map/ppermute | solution.py:448
  56.2 25.3 %collective-permute-start.7 = (bf16[256,1024]{1,0:T(8,128)(2,1)}, bf16[256,1024]{1,0:T(8,128)(2,1)S(1)}, u32[]{:S(2)}, u32[]{:S(2)}) collective-permute-start(bf16[256,1024]{1,0:T(8,128)(2,1)} %get-tuple-element.70.refs_0_.refs_2_), channel_id=1, source_target_pairs={{0,3},{1,0},{2,1},{3,2},{4,7},{5,4},{6,5},{7,6},{8,11},{9,8},{10,9... | collective-permute-start | bytes 1572872 | tf_op jit(solution)/shard_map/ppermute | solution.py:448
  70.9 10.6 %copy-start = (bf16[256,1024]{1,0:T(8,128)(2,1)S(1)}, bf16[256,1024]{1,0:T(8,128)(2,1)}, u32[]{:S(2)}) copy-start(bf16[256,1024]{1,0:T(8,128)(2,1)} %get-tuple-element.70.refs_0_.refs_2_) | copy-start | bytes 1572868
  70.9 24.1 %all-to-all-start.3 = ((bf16[8,32,16,128]{3,2,1,0:T(8,128)(2,1)}), bf16[8,32,16,128]{3,2,1,0:T(8,128)(2,1)S(1)}, u32[]{:S(2)}, u32[]{:S(2)}) async-start(bf16[8,32,16,128]{3,2,1,0:T(8,128)(2,1)} %correlate.1), calls=%async_computation.3 | async-start | bytes 2097152 | tf_op jit(solution)/shard_map/all_to_all | solution.py:439
  81.6 13.4 %collective-permute-start.8 = (bf16[256,1024]{1,0:T(8,128)(2,1)S(1)}, bf16[256,1024]{1,0:T(8,128)(2,1)}, u32[]{:S(2)}, u32[]{:S(2)}) collective-permute-start(bf16[256,1024]{1,0:T(8,128)(2,1)S(1)} %select_select_fusion), channel_id=1, source_target_pairs={{0,2},{3,1},{2,3},{1,0},{4,6},{7,5},{6,7},{5,4},{8,10},{11,9},{10,... | collective-permute-start | bytes 1572872 | tf_op jit(solution)/shard_map/ppermute | solution.py:532
  95.0 4.4 %collective-permute-start.9 = (bf16[4,128,2048]{2,1,0:T(8,128)(2,1)}, bf16[4,128,2048]{2,1,0:T(8,128)(2,1)S(1)}, u32[]{:S(2)}, u32[]{:S(2)}) collective-permute-start(bf16[4,128,2048]{2,1,0:T(8,128)(2,1)} %get-tuple-element.75), channel_id=1, source_target_pairs={{0,4},{4,0},{8,12},{12,8},{16,20},{20,16},{24,28},{28,24},{1,5},{5... | collective-permute-start | bytes 6291464 | tf_op jit(solution)/shard_map/ppermute | solution.py:538
  95.0 4.4 %copy-start.2 = (bf16[4,128,2048]{2,1,0:T(8,128)(2,1)S(1)}, bf16[4,128,2048]{2,1,0:T(8,128)(2,1)}, u32[]{:S(2)}) copy-start(bf16[4,128,2048]{2,1,0:T(8,128)(2,1)} %get-tuple-element.73) | copy-start | bytes 6291460
  98.8 2.1 %collective-permute-start.10 = (bf16[1,128,2048]{2,1,0:T(8,128)(2,1)S(1)}, bf16[1,128,2048]{2,1,0:T(8,128)(2,1)S(1)}, u32[]{:S(2)}, u32[]{:S(2)}) collective-permute-start(bf16[1,128,2048]{2,1,0:T(8,128)(2,1)S(1)} %dynamic-slice_bitcast_fusion.4), channel_id=1, source_target_pairs={{0,4},{4,0},{8,12},{12,8},{16,20},{20,16},{24,28},{28,24},{1,5},{5... | collective-permute-start | bytes 1572872 | tf_op jit(solution)/shard_map/ppermute | solution.py:464
  101.1 3.9 %copy-start.3 = (f32[256,1024]{1,0:T(8,128)S(1)}, f32[256,1024]{1,0:T(8,128)}, u32[]{:S(2)}) copy-start(f32[256,1024]{1,0:T(8,128)} %get-tuple-element.65) | copy-start | bytes 3145732
  101.1 3.8 %copy-start.4 = (bf16[256,1024]{1,0:T(8,128)(2,1)S(1)}, bf16[256,1024]{1,0:T(8,128)(2,1)}, u32[]{:S(2)}) copy-start(bf16[256,1024]{1,0:T(8,128)(2,1)} %get-tuple-element.66) | copy-start | bytes 1572868
  101.4 15.8 %collective-permute-start.11 = (bf16[128,2048]{1,0:T(8,128)(2,1)S(1)}, bf16[128,2048]{1,0:T(8,128)(2,1)S(1)}, u32[]{:S(2)}, u32[]{:S(2)}) collective-permute-start(bf16[128,2048]{1,0:T(8,128)(2,1)S(1)} %get-tuple-element.87), channel_id=1, source_target_pairs={{0,24},{4,28},{8,16},{12,20},{16,8},{20,12},{24,0},{28,4},{1,25},{... | collective-permute-start | bytes 1572872 | tf_op jit(solution)/shard_map/ppermute | solution.py:476
  103.8 24.0 %collective-permute-start.12 = (bf16[128,2048]{1,0:T(8,128)(2,1)S(1)}, bf16[128,2048]{1,0:T(8,128)(2,1)S(1)}, u32[]{:S(2)}, u32[]{:S(2)}) collective-permute-start(bf16[128,2048]{1,0:T(8,128)(2,1)S(1)} %get-tuple-element.86), channel_id=1, source_target_pairs={{0,8},{4,12},{8,0},{12,4},{16,24},{20,28},{24,16},{28,20},{1,9},{5... | collective-permute-start | bytes 1572872 | tf_op jit(solution)/shard_map/ppermute | solution.py:476
  104.4 23.4 %collective-permute-start.13 = (bf16[128,2048]{1,0:T(8,128)(2,1)S(1)}, bf16[128,2048]{1,0:T(8,128)(2,1)S(1)}, u32[]{:S(2)}, u32[]{:S(2)}) collective-permute-start(bf16[128,2048]{1,0:T(8,128)(2,1)S(1)} %get-tuple-element.85), channel_id=1, source_target_pairs={{0,16},{4,20},{8,24},{12,28},{16,0},{20,4},{24,8},{28,12},{1,17},{... | collective-permute-start | bytes 1572872 | tf_op jit(solution)/shard_map/ppermute | solution.py:476

commit v9 on v8

--- a/solution.py
+++ b/solution.py
@@ -211,7 +211,8 @@
     per = gate_ref.shape[1] // LANES
     spread_lanes(lines, short(wide(gate_ref[...]) * wide(signal_ref[...])).astype(jnp.float32), 0, 2 * per)
     spread_lanes(lines, wide(filter_ref[...]), per, 2 * per)
-    pair_ref[...] = short(lines[...]).reshape(pair_ref.shape)
+    held = lines[pl.ds(0, gate_ref.shape[0] * 2 * per), :]
+    pair_ref[...] = short(held).reshape(pair_ref.shape)
 
 
 def prepare(inner_gate, signal, long_filter):
@@ -225,7 +226,7 @@
         in_specs=[block] * 3,
         out_specs=pl.BlockSpec((step, 2 * per, LANES), lambda i: (i, 0, 0)),
         out_shape=in_hbm((rows, 2 * per, LANES)),
-        scratch_shapes=[pltpu.VMEM((step * 2 * per, LANES), jnp.float32)],
+        scratch_shapes=[pltpu.VMEM(((step + 1) * 2 * per, LANES), jnp.float32)],
         compiler_params=params(),
         name="prepare",
     )(*held_in_hbm(inner_gate, signal, long_filter))
@@ -252,7 +253,7 @@
         grad_mix = grad_mix + jnp.where(flag_ref[0] != 0, shares[-1], jnp.zeros_like(shares[-1]))
         sum_ref[:, cols] = grad_mix
         grads[pl.ds(lane, rows, stride=per), :] = grad_mix * wide(gate_ref[:, cols])
-    grad_ref[...] = short(grads[...]).reshape(grad_ref.shape)
+    grad_ref[...] = short(grads[pl.ds(0, rows * per), :]).reshape(grad_ref.shape)
 
 
 def regard(outer_gate, shares, flag):
@@ -270,7 +271,7 @@
             in_specs=[token_rows]
             + [pl.BlockSpec((step, cut.shape[1]), lambda i, at: (i, 0)) for cut in cuts],
             out_specs=[token_rows, pl.BlockSpec((step * per // 16, 16, LANES), lambda i, at: (i, 0, 0))],
-            scratch_shapes=[pltpu.VMEM((step * per, LANES), jnp.float32)],
+            scratch_shapes=[pltpu.VMEM(((step + 1) * per, LANES), jnp.float32)],
         ),
         out_shape=[in_hbm((rows, length), jnp.float32), in_hbm((rows * per // 16, 16, LANES))],
         compiler_params=params(),
@@ -281,7 +282,7 @@
 def mix_kernel(conv_ref, gate_ref, mixed_ref, out_ref, lines):
     rows, length = gate_ref.shape
     per = length // LANES
-    lines[...] = wide(conv_ref[...].reshape(rows * per, LANES))
+    lines[pl.ds(0, rows * per), :] = wide(conv_ref[...].reshape(rows * per, LANES))
     for lane in range(per):
         cols = slice(lane * LANES, (lane + 1) * LANES)
         conv = lines[pl.ds(lane, rows, stride=per), :]
@@ -301,7 +302,7 @@
         in_specs=[pl.BlockSpec((step * per // 16, 16, LANES), lambda i: (i, 0, 0)), token_rows],
         out_specs=[token_rows, token_rows],
         out_shape=[in_hbm((rows, length))] * 2,
-        scratch_shapes=[pltpu.VMEM((step * per, LANES), jnp.float32)],
+        scratch_shapes=[pltpu.VMEM(((step + 1) * per, LANES), jnp.float32)],
         compiler_params=params(),
         name="mix",
     )(conv, outer_gate)
@@ -310,7 +311,7 @@
 def finish_kernel(corr_ref, signal_ref, gate_ref, inner_ref, signal_out_ref, filter_ref, lines):
     rows, length = signal_ref.shape
     per = length // LANES
-    lines[...] = wide(corr_ref[...].reshape(rows * 2 * per, LANES))
+    lines[pl.ds(0, rows * 2 * per), :] = wide(corr_ref[...].reshape(rows * 2 * per, LANES))
     for lane in range(per):
         cols = slice(lane * LANES, (lane + 1) * LANES)
         grad_prod = lines[pl.ds(lane, rows, stride=2 * per), :]
@@ -331,7 +332,7 @@
         out_specs=[block] * 3,
         out_shape=[jax.ShapeDtypeStruct((rows, length), jnp.bfloat16)] * 2
         + [jax.ShapeDtypeStruct((rows, length), jnp.float32)],
-        scratch_shapes=[pltpu.VMEM((step * 2 * per, LANES), jnp.float32)],
+        scratch_shapes=[pltpu.VMEM(((step + 1) * 2 * per, LANES), jnp.float32)],
         compiler_params=params(),
         name="finish",
     )(corr.reshape(rows, 2 * per, LANES), *held_in_hbm(signal, inner_gate))

time: 130 us -> 130 us (level)
  no operation moved by 1% of the time
where the time goes in v9:
time: 130 us; the launch traced here: 129 us
  Pallas kernels  45.3 us (35%)
  waiting for transfers between devices  39.1 us (30%)
  starting transfers between devices  36.6 us (28%)
  matrix products  3.78 us (3%)
  other arithmetic  3.24 us (2%)
    ppermute x3, waiting for transfers between devices, scatter_chips(): lax.ppermute(block(bit), 'seq', swaps(count, 2 * bit))  18.8 us
    pallas_call x4, Pallas kernels, unproject(): pl.pallas_call(functools.partial(unproject_kernel, len(offsets), splits,...  17 us
    all_to_all x4, starting transfers between devices, exchange(): lax.all_to_all(blocks, 'seq', split_axis=0, concat_axis=0, tiled=True)  14.7 us
    ppermute x6, starting transfers between devices, shift(): lax.ppermute(block, 'chan', [(i, (i + by) % count) for i in range(count)])  9.73 us
    ppermute x6, waiting for transfers between devices, shift(): lax.ppermute(block, 'chan', [(i, (i + by) % count) for i in range(count)])  8.43 us
    pallas_call x1, Pallas kernels, project(): pl.pallas_call(project_kernel, grid_spec=pltpu.PrefetchScalarGridSpec(num...  7.72 us
    all_to_all x4, waiting for transfers between devices, exchange(): lax.all_to_all(blocks, 'seq', split_axis=0, concat_axis=0, tiled=True)  7.23 us
    ppermute x2, starting transfers between devices, body(): lax.ppermute(far, 'chan', [(2, 0), (1, 3), (3, 2), (0, 1)])  5.67 us
  transfers between devices with their start and end apart: 18, of which 9 were waited for; matrix products, arithmetic and copies ran while one was open for 4% of the time, Pallas kernels for 31%

profile of v9, /device:TPU:0, one launch (start us, length us, event | category | flops | bytes accessed | tf_op | source)
XLA Modules:
  0.0 129.1 jit_solution(12052325742857327068)
XLA Ops:
  0.6 4.2 %unproject.4 = (bf16[256,512]{1,0:T(8,128)(2,1)}, bf16[256,512]{1,0:T(8,128)(2,1)}) custom-call(s32[1]{0:T(128)} %bitcast.1.place_ref, bf16[1024,2048]{1,0:T(8,128)(2,1)} %refs_0_.4, bf16[2048,1024]{1,0:T(8,128)(2,1)} %refs_4_.1), custom_call_target="tpu_custom_call" | custom-call | flops 40000000000 | bytes 100000000 | tf_op jit(solution)/shard_map/unproject/pallas_call | solution.py:376
  4.9 3.0 %collective-permute-start = (bf16[256,512]{1,0:T(8,128)(2,1)}, bf16[256,512]{1,0:T(8,128)(2,1)S(1)}, u32[]{:S(2)}, u32[]{:S(2)}) collective-permute-start(bf16[256,512]{1,0:T(8,128)(2,1)} %get-tuple-element.45), channel_id=1, source_target_pairs={{2,0},{1,3},{3,2},{0,1},{6,4},{5,7},{7,6},{4,5},{10,8},{9,11},{11,... | collective-permute-start | bytes 786440 | tf_op jit(solution)/shard_map/ppermute | solution.py:500
  7.9 2.8 %prepare.1 = bf16[256,16,128]{2,1,0:T(8,128)(2,1)} custom-call(bf16[256,1024]{1,0:T(8,128)(2,1)} %gate_ref.7, bf16[256,1024]{1,0:T(8,128)(2,1)} %signal_ref.3, bf16[256,1024]{1,0:T(8,128)(2,1)} %filter_ref), custom_call_target="tpu_custom_call" | custom-call | tf_op jit(solution)/shard_map/prepare/pallas_call | solution.py:223
  10.7 3.7 %all-to-all-start = ((bf16[8,32,16,128]{3,2,1,0:T(8,128)(2,1)}), bf16[8,32,16,128]{3,2,1,0:T(8,128)(2,1)S(1)}, u32[]{:S(2)}, u32[]{:S(2)}) async-start(bf16[8,32,16,128]{3,2,1,0:T(8,128)(2,1)} %bitcast.25), calls=%async_computation | async-start | bytes 2097152 | tf_op jit(solution)/shard_map/all_to_all | solution.py:440
  14.4 2.6 %collective-permute-start.1 = (bf16[256,512]{1,0:T(8,128)(2,1)S(1)}, bf16[256,512]{1,0:T(8,128)(2,1)S(1)}, u32[]{:S(2)}, u32[]{:S(2)}) collective-permute-start(bf16[256,512]{1,0:T(8,128)(2,1)S(1)} %copy-done.5), channel_id=1, source_target_pairs={{2,0},{1,3},{3,2},{0,1},{6,4},{5,7},{7,6},{4,5},{10,8},{9,11},{11,... | collective-permute-start | bytes 786440 | tf_op jit(solution)/shard_map/ppermute | solution.py:500
  17.1 4.3 %unproject.5 = (bf16[256,512]{1,0:T(8,128)(2,1)}, bf16[256,512]{1,0:T(8,128)(2,1)}) custom-call(s32[1]{0:T(128)} %bitcast.1.place_ref, bf16[1024,2048]{1,0:T(8,128)(2,1)} %refs_0_.4, bf16[1024,2048]{1,0:T(8,128)(2,1)} %refs_0_.4, bf16[2048,1024]{1,0:T(8,128)(2,1)} %refs_4_.1, bf16[256,512]{1,0:T(8,128)(2,1)S(1)} %collective-permute-done.refs_3_.refs_5_), custom_call_target="tpu_custom_call" | custom-call | flops 40000000000 | bytes 100000000 | tf_op jit(solution)/shard_map/unproject/pallas_call | solution.py:376
  21.4 2.0 %collective-permute-start.4 = (bf16[256,512]{1,0:T(8,128)(2,1)}, bf16[256,512]{1,0:T(8,128)(2,1)S(1)}, u32[]{:S(2)}, u32[]{:S(2)}) collective-permute-start(bf16[256,512]{1,0:T(8,128)(2,1)} %get-tuple-element.49), channel_id=1, source_target_pairs={{0,3},{1,0},{2,1},{3,2},{4,7},{5,4},{6,5},{7,6},{8,11},{9,8},{10,9... | collective-permute-start | bytes 786440 | tf_op jit(solution)/shard_map/ppermute | solution.py:449
  24.1 4.3 %unproject.6 = (bf16[256,512]{1,0:T(8,128)(2,1)}, bf16[256,512]{1,0:T(8,128)(2,1)}) custom-call(s32[1]{0:T(128)} %bitcast.1.place_ref, bf16[1024,2048]{1,0:T(8,128)(2,1)} %refs_0_.4, bf16[1024,2048]{1,0:T(8,128)(2,1)} %refs_0_.4, bf16[2048,1024]{1,0:T(8,128)(2,1)} %refs_4_.1, bf16[256,512]{1,0:T(8,128)(2,1)S(1)} %collective-permute-done.1.refs_3_.refs_6_), custom_call_target="tpu_custom_call" | custom-call | flops 40000000000 | bytes 100000000 | tf_op jit(solution)/shard_map/unproject/pallas_call | solution.py:376
  28.4 2.1 %collective-permute-start.3 = (bf16[256,512]{1,0:T(8,128)(2,1)}, bf16[256,512]{1,0:T(8,128)(2,1)S(1)}, u32[]{:S(2)}, u32[]{:S(2)}) collective-permute-start(bf16[256,512]{1,0:T(8,128)(2,1)} %get-tuple-element.57), channel_id=1, source_target_pairs={{0,1},{1,2},{2,3},{3,0},{4,5},{5,6},{6,7},{7,4},{8,9},{9,10},{10,1... | collective-permute-start | bytes 786440 | tf_op jit(solution)/shard_map/ppermute | solution.py:449
  30.5 1.7 %collective-permute-start.5 = (bf16[256,512]{1,0:T(8,128)(2,1)}, bf16[256,512]{1,0:T(8,128)(2,1)S(1)}, u32[]{:S(2)}, u32[]{:S(2)}) collective-permute-start(bf16[256,512]{1,0:T(8,128)(2,1)} %get-tuple-element.52), channel_id=1, source_target_pairs={{0,3},{1,0},{2,1},{3,2},{4,7},{5,4},{6,5},{7,6},{8,11},{9,8},{10,9... | collective-permute-start | bytes 786440 | tf_op jit(solution)/shard_map/ppermute | solution.py:449
  32.2 5.1 %convolve.1 = (bf16[8,16,16,128]{3,2,1,0:T(8,128)(2,1)}, f32[32,64,256]{2,1,0:T(8,128)}, f32[32,64,256]{2,1,0:T(8,128)}) custom-call(bf16[8,32,16,128]{3,2,1,0:T(8,128)(2,1)S(1)} %all-to-all-done.pairs_ref, bf16[256,256]{1,0:T(8,128)(2,1)} %constant.87.clone.first_ref, bf16[256,256]{1,0:T(8,128)(2,1)} %constant.88.clone.forward_ref, ...), custom_call_target="tpu_custom_call" | custom-call | tf_op jit(solution)/shard_map/convolve/pallas_call | solution.py:154
  37.3 3.8 %all-to-all-start.1 = ((bf16[8,16,16,128]{3,2,1,0:T(8,128)(2,1)}), bf16[8,16,16,128]{3,2,1,0:T(8,128)(2,1)S(1)}, u32[]{:S(2)}, u32[]{:S(2)}) async-start(bf16[8,16,16,128]{3,2,1,0:T(8,128)(2,1)} %get-tuple-element.54), calls=%async_computation.1 | async-start | bytes 1048576 | tf_op jit(solution)/shard_map/all_to_all | solution.py:440
  41.1 4.2 %unproject.7.refs_0_ = bf16[256,1024]{1,0:T(8,128)(2,1)} custom-call(s32[1]{0:T(128)} %bitcast.1.place_ref, bf16[1024,2048]{1,0:T(8,128)(2,1)} %refs_0_.4, bf16[2048,1024]{1,0:T(8,128)(2,1)} %refs_4_.1), custom_call_target="tpu_custom_call" | custom-call | flops 40000000000 | bytes 100000000 | tf_op jit(solution)/shard_map/unproject/pallas_call | solution.py:376
  45.3 1.5 %collective-permute-done.5.refs_4_ = bf16[256,512]{1,0:T(8,128)(2,1)S(1)} collective-permute-done((bf16[256,512]{1,0:T(8,128)(2,1)}, bf16[256,512]{1,0:T(8,128)(2,1)S(1)}, u32[]{:S(2)}, u32[]{:S(2)}) %collective-permute-start.5) | collective-permute-done | bytes 262176 | tf_op jit(solution)/shard_map/ppermute | solution.py:449
  46.8 2.6 %regard.1 = (f32[256,1024]{1,0:T(8,128)}, bf16[128,16,128]{2,1,0:T(8,128)(2,1)}) custom-call(s32[1]{0:T(128)} %bitcast.flag_ref, bf16[256,1024]{1,0:T(8,128)(2,1)S(1)} %copy-done.1, bf16[256,1024]{1,0:T(8,128)(2,1)} %unproject.7.refs_0_, bf16[256,512]{1,0:T(8,128)(2,1)S(1)} %collective-permute-done.2.refs_1_, ...), custom_call_target="tpu_custom_call" | custom-call | tf_op jit(solution)/shard_map/regard/pallas_call | solution.py:266
  49.4 1.4 %all-to-all-done.1 = bf16[8,16,16,128]{3,2,1,0:T(8,128)(2,1)S(1)} async-done(((bf16[8,16,16,128]{3,2,1,0:T(8,128)(2,1)}), bf16[8,16,16,128]{3,2,1,0:T(8,128)(2,1)S(1)}, u32[]{:S(2)}, u32[]{:S(2)}) %all-to-all-start.1) | async-done | bytes 524320 | tf_op jit(solution)/shard_map/all_to_all | solution.py:440
  50.9 1.2 mix.1
  52.1 3.5 %all-to-all-start.2 = ((bf16[8,16,16,128]{3,2,1,0:T(8,128)(2,1)}), bf16[8,16,16,128]{3,2,1,0:T(8,128)(2,1)S(1)}, u32[]{:S(2)}, u32[]{:S(2)}) async-start(bf16[8,16,16,128]{3,2,1,0:T(8,128)(2,1)} %bitcast.28), calls=%async_computation.2 | async-start | bytes 1048576 | tf_op jit(solution)/shard_map/all_to_all | solution.py:440
  56.2 3.3 %collective-permute-start.7 = (bf16[256,1024]{1,0:T(8,128)(2,1)}, bf16[256,1024]{1,0:T(8,128)(2,1)S(1)}, u32[]{:S(2)}, u32[]{:S(2)}) collective-permute-start(bf16[256,1024]{1,0:T(8,128)(2,1)} %get-tuple-element.70.refs_0_.refs_2_), channel_id=1, source_target_pairs={{0,3},{1,0},{2,1},{3,2},{4,7},{5,4},{6,5},{7,6},{8,11},{9,8},{10,9... | collective-permute-start | bytes 1572872 | tf_op jit(solution)/shard_map/ppermute | solution.py:449
  59.4 5.8 %all-to-all-done.2.pairs_ref = bf16[8,16,16,128]{3,2,1,0:T(8,128)(2,1)S(1)} async-done(((bf16[8,16,16,128]{3,2,1,0:T(8,128)(2,1)}), bf16[8,16,16,128]{3,2,1,0:T(8,128)(2,1)S(1)}, u32[]{:S(2)}, u32[]{:S(2)}) %all-to-all-start.2) | async-done | bytes 524320 | tf_op jit(solution)/shard_map/all_to_all | solution.py:440
  65.2 5.7 %correlate.1 = bf16[8,32,16,128]{3,2,1,0:T(8,128)(2,1)} custom-call(bf16[8,16,16,128]{3,2,1,0:T(8,128)(2,1)S(1)} %all-to-all-done.2.pairs_ref, f32[32,64,256]{2,1,0:T(8,128)} %get-tuple-element.63.signal_ref, f32[32,64,256]{2,1,0:T(8,128)} %get-tuple-element.64.filter_ref, bf16[256,256]{1,0:T(8,128)(2,1)} %constant.87.clone.first_ref, ...), custom_call_target="tpu_custom_call" | custom-call | tf_op jit(solution)/shard_map/correlate/pallas_call | solution.py:180
  70.9 3.7 %all-to-all-start.3 = ((bf16[8,32,16,128]{3,2,1,0:T(8,128)(2,1)}), bf16[8,32,16,128]{3,2,1,0:T(8,128)(2,1)S(1)}, u32[]{:S(2)}, u32[]{:S(2)}) async-start(bf16[8,32,16,128]{3,2,1,0:T(8,128)(2,1)} %correlate.1), calls=%async_computation.3 | async-start | bytes 2097152 | tf_op jit(solution)/shard_map/all_to_all | solution.py:440
  74.6 6.9 %collective-permute-done.7.refs_3_ = bf16[256,1024]{1,0:T(8,128)(2,1)S(1)} collective-permute-done((bf16[256,1024]{1,0:T(8,128)(2,1)}, bf16[256,1024]{1,0:T(8,128)(2,1)S(1)}, u32[]{:S(2)}, u32[]{:S(2)}) %collective-permute-start.7) | collective-permute-done | bytes 524320 | tf_op jit(solution)/shard_map/ppermute | solution.py:449
  81.6 2.4 %collective-permute-start.8 = (bf16[256,1024]{1,0:T(8,128)(2,1)S(1)}, bf16[256,1024]{1,0:T(8,128)(2,1)}, u32[]{:S(2)}, u32[]{:S(2)}) collective-permute-start(bf16[256,1024]{1,0:T(8,128)(2,1)S(1)} %select_select_fusion), channel_id=1, source_target_pairs={{0,2},{3,1},{2,3},{1,0},{4,6},{7,5},{6,7},{5,4},{8,10},{11,9},{10,... | collective-permute-start | bytes 1572872 | tf_op jit(solution)/shard_map/ppermute | solution.py:533
  84.0 7.7 %project.1 = (bf16[4,128,2048]{2,1,0:T(8,128)(2,1)}, bf16[4,128,2048]{2,1,0:T(8,128)(2,1)}) custom-call(s32[1]{0:T(128)} %bitcast.5.core_ref, bf16[256,1024]{1,0:T(8,128)(2,1)S(1)} %copy-done, bf16[256,1024]{1,0:T(8,128)(2,1)S(1)} %collective-permute-done.6.refs_1_, bf16[256,1024]{1,0:T(8,128)(2,1)S(1)} %copy-done, ...), custom_call_target="tpu_custom_call" | custom-call | tf_op jit(solution)/shard_map/project/pallas_call | solution.py:419
  91.7 3.3 %collective-permute-done.8 = bf16[256,1024]{1,0:T(8,128)(2,1)} collective-permute-done((bf16[256,1024]{1,0:T(8,128)(2,1)S(1)}, bf16[256,1024]{1,0:T(8,128)(2,1)}, u32[]{:S(2)}, u32[]{:S(2)}) %collective-permute-start.8) | collective-permute-done | bytes 524320 | tf_op jit(solution)/shard_map/ppermute | solution.py:533
  95.0 3.8 %convolution_convert_fusion = bf16[256,2048]{1,0:T(8,128)(2,1)S(1)} fusion(bf16[256,1024]{1,0:T(8,128)(2,1)} %collective-permute-done.8, bf16[2048,1024]{1,0:T(8,128)(2,1)} %refs_4_.1), kind=kOutput, calls=%fused_computation.1 | convolution fusion | flops 1074266112 | bytes 5767168 | tf_op jit(solution)/shard_map/zct,dt->zcd/dot_general | solution.py:463
  101.4 2.4 %collective-permute-start.11 = (bf16[128,2048]{1,0:T(8,128)(2,1)S(1)}, bf16[128,2048]{1,0:T(8,128)(2,1)S(1)}, u32[]{:S(2)}, u32[]{:S(2)}) collective-permute-start(bf16[128,2048]{1,0:T(8,128)(2,1)S(1)} %get-tuple-element.87), channel_id=1, source_target_pairs={{0,24},{4,28},{8,16},{12,20},{16,8},{20,12},{24,0},{28,4},{1,25},{... | collective-permute-start | bytes 1572872 | tf_op jit(solution)/shard_map/ppermute | solution.py:477
  105.9 3.2 %finish.1 = (bf16[256,1024]{1,0:T(8,128)(2,1)}, bf16[256,1024]{1,0:T(8,128)(2,1)}, f32[256,1024]{1,0:T(8,128)}) custom-call(bf16[256,16,128]{2,1,0:T(8,128)(2,1)S(1)} %bitcast.23, bf16[256,1024]{1,0:T(8,128)(2,1)} %signal_ref.3, bf16[256,1024]{1,0:T(8,128)(2,1)} %gate_ref.7), custom_call_target="tpu_custom_call" | custom-call | tf_op jit(solution)/shard_map/finish/pallas_call | solution.py:328
  109.0 8.1 %collective-permute-done.11 = bf16[128,2048]{1,0:T(8,128)(2,1)S(1)} collective-permute-done((bf16[128,2048]{1,0:T(8,128)(2,1)S(1)}, bf16[128,2048]{1,0:T(8,128)(2,1)S(1)}, u32[]{:S(2)}, u32[]{:S(2)}) %collective-permute-start.11) | collective-permute-done | bytes 524320 | tf_op jit(solution)/shard_map/ppermute | solution.py:477
  117.1 10.7 %collective-permute-done.12 = bf16[128,2048]{1,0:T(8,128)(2,1)S(1)} collective-permute-done((bf16[128,2048]{1,0:T(8,128)(2,1)S(1)}, bf16[128,2048]{1,0:T(8,128)(2,1)S(1)}, u32[]{:S(2)}, u32[]{:S(2)}) %collective-permute-start.12) | collective-permute-done | bytes 524320 | tf_op jit(solution)/shard_map/ppermute | solution.py:477
  127.8 1.3 %convert_add_fusion.1 = f32[128,2048]{1,0:T(8,128)} fusion(bf16[128,2048]{1,0:T(8,128)(2,1)S(1)} %get-tuple-element.84, bf16[128,2048]{1,0:T(8,128)(2,1)S(1)} %collective-permute-done.13, bf16[128,2048]{1,0:T(8,128)(2,1)S(1)} %collective-permute-done.12, bf16[128,2048]{1,0:T(8,128)(2,1)S(1)} %collective-permute-done.11), kind=kLoop, calls=%fused_computation.4 | loop fusion | flops 1835008 | bytes 3145728 | tf_op jit(solution)/shard_map/add | solution.py:483
  (35 shorter events, 6.0 us)
Async XLA Ops:
  4.9 12.2 %collective-permute-start = (bf16[256,512]{1,0:T(8,128)(2,1)}, bf16[256,512]{1,0:T(8,128)(2,1)S(1)}, u32[]{:S(2)}, u32[]{:S(2)}) collective-permute-start(bf16[256,512]{1,0:T(8,128)(2,1)} %get-tuple-element.45), channel_id=1, source_target_pairs={{2,0},{1,3},{3,2},{0,1},{6,4},{5,7},{7,6},{4,5},{10,8},{9,11},{11,... | collective-permute-start | bytes 786440 | tf_op jit(solution)/shard_map/ppermute | solution.py:500
  7.9 6.6 %copy-start.5 = (bf16[256,512]{1,0:T(8,128)(2,1)S(1)}, bf16[256,512]{1,0:T(8,128)(2,1)}, u32[]{:S(2)}) copy-start(bf16[256,512]{1,0:T(8,128)(2,1)} %get-tuple-element.51) | copy-start | bytes 786436
  10.7 21.5 %all-to-all-start = ((bf16[8,32,16,128]{3,2,1,0:T(8,128)(2,1)}), bf16[8,32,16,128]{3,2,1,0:T(8,128)(2,1)S(1)}, u32[]{:S(2)}, u32[]{:S(2)}) async-start(bf16[8,32,16,128]{3,2,1,0:T(8,128)(2,1)} %bitcast.25), calls=%async_computation | async-start | bytes 2097152 | tf_op jit(solution)/shard_map/all_to_all | solution.py:440
  14.4 9.6 %collective-permute-start.1 = (bf16[256,512]{1,0:T(8,128)(2,1)S(1)}, bf16[256,512]{1,0:T(8,128)(2,1)S(1)}, u32[]{:S(2)}, u32[]{:S(2)}) collective-permute-start(bf16[256,512]{1,0:T(8,128)(2,1)S(1)} %copy-done.5), channel_id=1, source_target_pairs={{2,0},{1,3},{3,2},{0,1},{6,4},{5,7},{7,6},{4,5},{10,8},{9,11},{11,... | collective-permute-start | bytes 786440 | tf_op jit(solution)/shard_map/ppermute | solution.py:500
  21.4 23.9 %collective-permute-start.4 = (bf16[256,512]{1,0:T(8,128)(2,1)}, bf16[256,512]{1,0:T(8,128)(2,1)S(1)}, u32[]{:S(2)}, u32[]{:S(2)}) collective-permute-start(bf16[256,512]{1,0:T(8,128)(2,1)} %get-tuple-element.49), channel_id=1, source_target_pairs={{0,3},{1,0},{2,1},{3,2},{4,7},{5,4},{6,5},{7,6},{8,11},{9,8},{10,9... | collective-permute-start | bytes 786440 | tf_op jit(solution)/shard_map/ppermute | solution.py:449
  23.4 21.9 %collective-permute-start.2 = (bf16[256,512]{1,0:T(8,128)(2,1)}, bf16[256,512]{1,0:T(8,128)(2,1)S(1)}, u32[]{:S(2)}, u32[]{:S(2)}) collective-permute-start(bf16[256,512]{1,0:T(8,128)(2,1)} %get-tuple-element.56), channel_id=1, source_target_pairs={{0,1},{1,2},{2,3},{3,0},{4,5},{5,6},{6,7},{7,4},{8,9},{9,10},{10,1... | collective-permute-start | bytes 786440 | tf_op jit(solution)/shard_map/ppermute | solution.py:449
  28.4 16.9 %collective-permute-start.3 = (bf16[256,512]{1,0:T(8,128)(2,1)}, bf16[256,512]{1,0:T(8,128)(2,1)S(1)}, u32[]{:S(2)}, u32[]{:S(2)}) collective-permute-start(bf16[256,512]{1,0:T(8,128)(2,1)} %get-tuple-element.57), channel_id=1, source_target_pairs={{0,1},{1,2},{2,3},{3,0},{4,5},{5,6},{6,7},{7,4},{8,9},{9,10},{10,1... | collective-permute-start | bytes 786440 | tf_op jit(solution)/shard_map/ppermute | solution.py:449
  30.5 16.3 %collective-permute-start.5 = (bf16[256,512]{1,0:T(8,128)(2,1)}, bf16[256,512]{1,0:T(8,128)(2,1)S(1)}, u32[]{:S(2)}, u32[]{:S(2)}) collective-permute-start(bf16[256,512]{1,0:T(8,128)(2,1)} %get-tuple-element.52), channel_id=1, source_target_pairs={{0,3},{1,0},{2,1},{3,2},{4,7},{5,4},{6,5},{7,6},{8,11},{9,8},{10,9... | collective-permute-start | bytes 786440 | tf_op jit(solution)/shard_map/ppermute | solution.py:449
  37.3 13.6 %all-to-all-start.1 = ((bf16[8,16,16,128]{3,2,1,0:T(8,128)(2,1)}), bf16[8,16,16,128]{3,2,1,0:T(8,128)(2,1)S(1)}, u32[]{:S(2)}, u32[]{:S(2)}) async-start(bf16[8,16,16,128]{3,2,1,0:T(8,128)(2,1)} %get-tuple-element.54), calls=%async_computation.1 | async-start | bytes 1048576 | tf_op jit(solution)/shard_map/all_to_all | solution.py:440
  41.1 5.7 %copy-start.1 = (bf16[256,1024]{1,0:T(8,128)(2,1)S(1)}, bf16[256,1024]{1,0:T(8,128)(2,1)}, u32[]{:S(2)}) copy-start(bf16[256,1024]{1,0:T(8,128)(2,1)} %gate_ref.6) | copy-start | bytes 1572868
  52.1 13.2 %all-to-all-start.2 = ((bf16[8,16,16,128]{3,2,1,0:T(8,128)(2,1)}), bf16[8,16,16,128]{3,2,1,0:T(8,128)(2,1)S(1)}, u32[]{:S(2)}, u32[]{:S(2)}) async-start(bf16[8,16,16,128]{3,2,1,0:T(8,128)(2,1)} %bitcast.28), calls=%async_computation.2 | async-start | bytes 1048576 | tf_op jit(solution)/shard_map/all_to_all | solution.py:440
  55.6 19.0 %collective-permute-start.6 = (bf16[256,1024]{1,0:T(8,128)(2,1)}, bf16[256,1024]{1,0:T(8,128)(2,1)S(1)}, u32[]{:S(2)}, u32[]{:S(2)}) collective-permute-start(bf16[256,1024]{1,0:T(8,128)(2,1)} %get-tuple-element.70.refs_0_.refs_2_), channel_id=1, source_target_pairs={{0,1},{1,2},{2,3},{3,0},{4,5},{5,6},{6,7},{7,4},{8,9},{9,10},{10,1... | collective-permute-start | bytes 1572872 | tf_op jit(solution)/shard_map/ppermute | solution.py:449
  56.2 25.3 %collective-permute-start.7 = (bf16[256,1024]{1,0:T(8,128)(2,1)}, bf16[256,1024]{1,0:T(8,128)(2,1)S(1)}, u32[]{:S(2)}, u32[]{:S(2)}) collective-permute-start(bf16[256,1024]{1,0:T(8,128)(2,1)} %get-tuple-element.70.refs_0_.refs_2_), channel_id=1, source_target_pairs={{0,3},{1,0},{2,1},{3,2},{4,7},{5,4},{6,5},{7,6},{8,11},{9,8},{10,9... | collective-permute-start | bytes 1572872 | tf_op jit(solution)/shard_map/ppermute | solution.py:449
  70.9 10.6 %copy-start = (bf16[256,1024]{1,0:T(8,128)(2,1)S(1)}, bf16[256,1024]{1,0:T(8,128)(2,1)}, u32[]{:S(2)}) copy-start(bf16[256,1024]{1,0:T(8,128)(2,1)} %get-tuple-element.70.refs_0_.refs_2_) | copy-start | bytes 1572868
  70.9 24.1 %all-to-all-start.3 = ((bf16[8,32,16,128]{3,2,1,0:T(8,128)(2,1)}), bf16[8,32,16,128]{3,2,1,0:T(8,128)(2,1)S(1)}, u32[]{:S(2)}, u32[]{:S(2)}) async-start(bf16[8,32,16,128]{3,2,1,0:T(8,128)(2,1)} %correlate.1), calls=%async_computation.3 | async-start | bytes 2097152 | tf_op jit(solution)/shard_map/all_to_all | solution.py:440
  81.6 13.4 %collective-permute-start.8 = (bf16[256,1024]{1,0:T(8,128)(2,1)S(1)}, bf16[256,1024]{1,0:T(8,128)(2,1)}, u32[]{:S(2)}, u32[]{:S(2)}) collective-permute-start(bf16[256,1024]{1,0:T(8,128)(2,1)S(1)} %select_select_fusion), channel_id=1, source_target_pairs={{0,2},{3,1},{2,3},{1,0},{4,6},{7,5},{6,7},{5,4},{8,10},{11,9},{10,... | collective-permute-start | bytes 1572872 | tf_op jit(solution)/shard_map/ppermute | solution.py:533
  95.0 4.4 %collective-permute-start.9 = (bf16[4,128,2048]{2,1,0:T(8,128)(2,1)}, bf16[4,128,2048]{2,1,0:T(8,128)(2,1)S(1)}, u32[]{:S(2)}, u32[]{:S(2)}) collective-permute-start(bf16[4,128,2048]{2,1,0:T(8,128)(2,1)} %get-tuple-element.75), channel_id=1, source_target_pairs={{0,4},{4,0},{8,12},{12,8},{16,20},{20,16},{24,28},{28,24},{1,5},{5... | collective-permute-start | bytes 6291464 | tf_op jit(solution)/shard_map/ppermute | solution.py:539
  95.0 4.4 %copy-start.2 = (bf16[4,128,2048]{2,1,0:T(8,128)(2,1)S(1)}, bf16[4,128,2048]{2,1,0:T(8,128)(2,1)}, u32[]{:S(2)}) copy-start(bf16[4,128,2048]{2,1,0:T(8,128)(2,1)} %get-tuple-element.73) | copy-start | bytes 6291460
  98.8 2.1 %collective-permute-start.10 = (bf16[1,128,2048]{2,1,0:T(8,128)(2,1)S(1)}, bf16[1,128,2048]{2,1,0:T(8,128)(2,1)S(1)}, u32[]{:S(2)}, u32[]{:S(2)}) collective-permute-start(bf16[1,128,2048]{2,1,0:T(8,128)(2,1)S(1)} %dynamic-slice_bitcast_fusion.4), channel_id=1, source_target_pairs={{0,4},{4,0},{8,12},{12,8},{16,20},{20,16},{24,28},{28,24},{1,5},{5... | collective-permute-start | bytes 1572872 | tf_op jit(solution)/shard_map/ppermute | solution.py:465
  101.1 3.9 %copy-start.3 = (f32[256,1024]{1,0:T(8,128)S(1)}, f32[256,1024]{1,0:T(8,128)}, u32[]{:S(2)}) copy-start(f32[256,1024]{1,0:T(8,128)} %get-tuple-element.65) | copy-start | bytes 3145732
  101.1 3.8 %copy-start.4 = (bf16[256,1024]{1,0:T(8,128)(2,1)S(1)}, bf16[256,1024]{1,0:T(8,128)(2,1)}, u32[]{:S(2)}) copy-start(bf16[256,1024]{1,0:T(8,128)(2,1)} %get-tuple-element.66) | copy-start | bytes 1572868
  101.4 15.8 %collective-permute-start.11 = (bf16[128,2048]{1,0:T(8,128)(2,1)S(1)}, bf16[128,2048]{1,0:T(8,128)(2,1)S(1)}, u32[]{:S(2)}, u32[]{:S(2)}) collective-permute-start(bf16[128,2048]{1,0:T(8,128)(2,1)S(1)} %get-tuple-element.87), channel_id=1, source_target_pairs={{0,24},{4,28},{8,16},{12,20},{16,8},{20,12},{24,0},{28,4},{1,25},{... | collective-permute-start | bytes 1572872 | tf_op jit(solution)/shard_map/ppermute | solution.py:477
  103.8 24.0 %collective-permute-start.12 = (bf16[128,2048]{1,0:T(8,128)(2,1)S(1)}, bf16[128,2048]{1,0:T(8,128)(2,1)S(1)}, u32[]{:S(2)}, u32[]{:S(2)}) collective-permute-start(bf16[128,2048]{1,0:T(8,128)(2,1)S(1)} %get-tuple-element.86), channel_id=1, source_target_pairs={{0,8},{4,12},{8,0},{12,4},{16,24},{20,28},{24,16},{28,20},{1,9},{5... | collective-permute-start | bytes 1572872 | tf_op jit(solution)/shard_map/ppermute | solution.py:477
  104.4 23.4 %collective-permute-start.13 = (bf16[128,2048]{1,0:T(8,128)(2,1)S(1)}, bf16[128,2048]{1,0:T(8,128)(2,1)S(1)}, u32[]{:S(2)}, u32[]{:S(2)}) collective-permute-start(bf16[128,2048]{1,0:T(8,128)(2,1)S(1)} %get-tuple-element.85), channel_id=1, source_target_pairs={{0,16},{4,20},{8,24},{12,28},{16,0},{20,4},{24,8},{28,12},{1,17},{... | collective-permute-start | bytes 1572872 | tf_op jit(solution)/shard_map/ppermute | solution.py:477

commit v10 on v9

--- a/solution.py
+++ b/solution.py
@@ -466,15 +466,35 @@
     return short(wide(lax.dynamic_index_in_dim(sums, core, 1, False)) + wide(got))
 
 
-def scatter_chips(total):
+def scatter_chips(total, meanwhile):
     count, chips = lax.axis_size("seq"), lax.axis_size("chan")
     line, chip = lax.axis_index("chan"), lax.axis_index("seq") // 2
+    rows, width = total.shape[1:]
 
     def block(bit):
         return lax.dynamic_index_in_dim(total, (line - (chip ^ bit)) % chips, 0, False)
 
-    bits = sorted(range(1, chips), key=lambda bit: (-bin(bit).count("1"), bit))
-    return [lax.ppermute(block(bit), "seq", swaps(count, 2 * bit)) for bit in bits] + [block(0)]
+    if chips != 4:
+        bits = sorted(range(1, chips), key=lambda bit: (-bin(bit).count("1"), bit))
+        parts = [lax.ppermute(block(bit), "seq", swaps(count, 2 * bit)) for bit in bits] + [block(0)]
+        grads = meanwhile(parts[-1])
+        return sum_of(parts), grads
+
+    def part(bit, half):
+        at = ((line - (chip ^ bit)) % chips, half * (rows // 2), 0)
+        return lax.dynamic_slice(total, at, (1, rows // 2, width))[0]
+
+    along_x = lax.ppermute(jnp.stack([part(1, 0), part(3, 0)]), "seq", swaps(count, 2))
+    along_y = lax.ppermute(jnp.stack([part(2, 1), part(3, 1)]), "seq", swaps(count, 4))
+    grads = meanwhile(total)
+    along_x, along_y = tie((along_x, along_y), grads)
+    then_y = lax.ppermute(short(wide(part(2, 0)) + wide(along_x[1])), "seq", swaps(count, 4))
+    then_x = lax.ppermute(short(wide(part(1, 1)) + wide(along_y[1])), "seq", swaps(count, 2))
+    halves = [
+        sum_of([part(0, 0), along_x[0], then_y]),
+        sum_of([part(0, 1), along_y[0], then_x]),
+    ]
+    return jnp.concatenate(halves, axis=0), grads
 
 
 def sum_of(parts):
@@ -543,10 +563,11 @@
     else:
         corr = exchange(corr)
         total = both_cores(held, grad_output)
-    parts = scatter_chips(total)
-    grads = finish(tie(corr, parts[-1]), signal, inner_gate)
+    grad_proj, grads = scatter_chips(
+        total, lambda before: finish(tie(corr, before), signal, inner_gate)
+    )
     grad_outer = short(tie(grad_mix, corr) * wide(conv_out))
-    return (grad_outer, *grads, sum_of(tie(parts, grads)))
+    return (grad_outer, *grads, grad_proj)
 
 
 def solution(mesh):

time: 130 us -> 130 us (level)
  waiting for transfers between devices: 39.1 us -> 34.4 us
  starting transfers between devices: 36.6 us -> 39 us
  other arithmetic: 3.24 us -> 5.6 us
    ppermute x3 -> x4, waiting for transfers between devices: 18.8 us -> 14.1 us  [the longest x1 7.92 us: scatter_chips(): lax.ppermute(jnp.stack([part(1, 0), part(3, 0)]), 'seq', swaps(count, 2))]
    ppermute x3 -> x4, starting transfers between devices: 3.57 us -> 5.91 us  [the longest x1 1.55 us: scatter_chips(): lax.ppermute(jnp.stack([part(2, 1), part(3, 1)]), 'seq', swaps(count, 4))]
    convert_element_type x2 -> x3, other arithmetic: 1.75 us -> 3 us  [short(): return x.astype(jnp.bfloat16)]
  transfers between devices with their start and end apart: 18 -> 19, of which waited for: 9 -> 11; matrix products, arithmetic and copies ran while one was open for 4% -> 4% of each run, Pallas kernels for 31% -> 31%
where the time goes in v10:
time: 130 us; the launch traced here: 129 us
  Pallas kernels  45.4 us (35%)
  starting transfers between devices  39 us (30%)
  waiting for transfers between devices  34.4 us (26%)
  other arithmetic  5.6 us (4%)
  matrix products  3.78 us (3%)
    pallas_call x4, Pallas kernels, unproject(): pl.pallas_call(functools.partial(unproject_kernel, len(offsets), splits,...  17 us
    all_to_all x4, starting transfers between devices, exchange(): lax.all_to_all(blocks, 'seq', split_axis=0, concat_axis=0, tiled=True)  14.8 us
    ppermute x6, starting transfers between devices, shift(): lax.ppermute(block, 'chan', [(i, (i + by) % count) for i in range(count)])  9.73 us
    ppermute x6, waiting for transfers between devices, shift(): lax.ppermute(block, 'chan', [(i, (i + by) % count) for i in range(count)])  8.43 us
    ppermute x1, waiting for transfers between devices, scatter_chips(): lax.ppermute(jnp.stack([part(1, 0), part(3, 0)]), 'seq', swaps(count, 2))  7.92 us
    pallas_call x1, Pallas kernels, project(): pl.pallas_call(project_kernel, grid_spec=pltpu.PrefetchScalarGridSpec(num...  7.74 us
    all_to_all x4, waiting for transfers between devices, exchange(): lax.all_to_all(blocks, 'seq', split_axis=0, concat_axis=0, tiled=True)  7.23 us
    ppermute x2, starting transfers between devices, body(): lax.ppermute(far, 'chan', [(2, 0), (1, 3), (3, 2), (0, 1)])  5.67 us
  transfers between devices with their start and end apart: 19, of which 11 were waited for; matrix products, arithmetic and copies ran while one was open for 4% of the time, Pallas kernels for 31%

profile of v10, /device:TPU:0, one launch (start us, length us, event | category | flops | bytes accessed | tf_op | source)
XLA Modules:
  0.0 129.1 jit_solution(4840130553576833138)
XLA Ops:
  0.6 4.2 %unproject.4 = (bf16[256,512]{1,0:T(8,128)(2,1)}, bf16[256,512]{1,0:T(8,128)(2,1)}) custom-call(s32[1]{0:T(128)} %bitcast.1.place_ref, bf16[1024,2048]{1,0:T(8,128)(2,1)} %refs_0_.4, bf16[2048,1024]{1,0:T(8,128)(2,1)} %refs_4_.1), custom_call_target="tpu_custom_call" | custom-call | flops 40000000000 | bytes 100000000 | tf_op jit(solution)/shard_map/unproject/pallas_call | solution.py:376
  4.9 3.0 %collective-permute-start = (bf16[256,512]{1,0:T(8,128)(2,1)}, bf16[256,512]{1,0:T(8,128)(2,1)S(1)}, u32[]{:S(2)}, u32[]{:S(2)}) collective-permute-start(bf16[256,512]{1,0:T(8,128)(2,1)} %get-tuple-element.43), channel_id=1, source_target_pairs={{2,0},{1,3},{3,2},{0,1},{6,4},{5,7},{7,6},{4,5},{10,8},{9,11},{11,... | collective-permute-start | bytes 786440 | tf_op jit(solution)/shard_map/ppermute | solution.py:520
  7.9 2.8 %prepare.1 = bf16[256,16,128]{2,1,0:T(8,128)(2,1)} custom-call(bf16[256,1024]{1,0:T(8,128)(2,1)} %gate_ref.7, bf16[256,1024]{1,0:T(8,128)(2,1)} %signal_ref.3, bf16[256,1024]{1,0:T(8,128)(2,1)} %filter_ref), custom_call_target="tpu_custom_call" | custom-call | tf_op jit(solution)/shard_map/prepare/pallas_call | solution.py:223
  10.7 3.7 %all-to-all-start = ((bf16[8,32,16,128]{3,2,1,0:T(8,128)(2,1)}), bf16[8,32,16,128]{3,2,1,0:T(8,128)(2,1)S(1)}, u32[]{:S(2)}, u32[]{:S(2)}) async-start(bf16[8,32,16,128]{3,2,1,0:T(8,128)(2,1)} %bitcast.25), calls=%async_computation | async-start | bytes 2097152 | tf_op jit(solution)/shard_map/all_to_all | solution.py:440
  14.4 2.6 %collective-permute-start.1 = (bf16[256,512]{1,0:T(8,128)(2,1)S(1)}, bf16[256,512]{1,0:T(8,128)(2,1)S(1)}, u32[]{:S(2)}, u32[]{:S(2)}) collective-permute-start(bf16[256,512]{1,0:T(8,128)(2,1)S(1)} %copy-done.7), channel_id=1, source_target_pairs={{2,0},{1,3},{3,2},{0,1},{6,4},{5,7},{7,6},{4,5},{10,8},{9,11},{11,... | collective-permute-start | bytes 786440 | tf_op jit(solution)/shard_map/ppermute | solution.py:520
  17.1 4.3 %unproject.5 = (bf16[256,512]{1,0:T(8,128)(2,1)}, bf16[256,512]{1,0:T(8,128)(2,1)}) custom-call(s32[1]{0:T(128)} %bitcast.1.place_ref, bf16[1024,2048]{1,0:T(8,128)(2,1)} %refs_0_.4, bf16[1024,2048]{1,0:T(8,128)(2,1)} %refs_0_.4, bf16[2048,1024]{1,0:T(8,128)(2,1)} %refs_4_.1, bf16[256,512]{1,0:T(8,128)(2,1)S(1)} %collective-permute-done.refs_3_.refs_5_), custom_call_target="tpu_custom_call" | custom-call | flops 40000000000 | bytes 100000000 | tf_op jit(solution)/shard_map/unproject/pallas_call | solution.py:376
  21.4 2.0 %collective-permute-start.4 = (bf16[256,512]{1,0:T(8,128)(2,1)}, bf16[256,512]{1,0:T(8,128)(2,1)S(1)}, u32[]{:S(2)}, u32[]{:S(2)}) collective-permute-start(bf16[256,512]{1,0:T(8,128)(2,1)} %get-tuple-element.47), channel_id=1, source_target_pairs={{0,3},{1,0},{2,1},{3,2},{4,7},{5,4},{6,5},{7,6},{8,11},{9,8},{10,9... | collective-permute-start | bytes 786440 | tf_op jit(solution)/shard_map/ppermute | solution.py:449
  24.1 4.3 %unproject.6 = (bf16[256,512]{1,0:T(8,128)(2,1)}, bf16[256,512]{1,0:T(8,128)(2,1)}) custom-call(s32[1]{0:T(128)} %bitcast.1.place_ref, bf16[1024,2048]{1,0:T(8,128)(2,1)} %refs_0_.4, bf16[1024,2048]{1,0:T(8,128)(2,1)} %refs_0_.4, bf16[2048,1024]{1,0:T(8,128)(2,1)} %refs_4_.1, bf16[256,512]{1,0:T(8,128)(2,1)S(1)} %collective-permute-done.1.refs_3_.refs_6_), custom_call_target="tpu_custom_call" | custom-call | flops 40000000000 | bytes 100000000 | tf_op jit(solution)/shard_map/unproject/pallas_call | solution.py:376
  28.4 2.1 %collective-permute-start.3 = (bf16[256,512]{1,0:T(8,128)(2,1)}, bf16[256,512]{1,0:T(8,128)(2,1)S(1)}, u32[]{:S(2)}, u32[]{:S(2)}) collective-permute-start(bf16[256,512]{1,0:T(8,128)(2,1)} %get-tuple-element.55), channel_id=1, source_target_pairs={{0,1},{1,2},{2,3},{3,0},{4,5},{5,6},{6,7},{7,4},{8,9},{9,10},{10,1... | collective-permute-start | bytes 786440 | tf_op jit(solution)/shard_map/ppermute | solution.py:449
  30.5 1.7 %collective-permute-start.5 = (bf16[256,512]{1,0:T(8,128)(2,1)}, bf16[256,512]{1,0:T(8,128)(2,1)S(1)}, u32[]{:S(2)}, u32[]{:S(2)}) collective-permute-start(bf16[256,512]{1,0:T(8,128)(2,1)} %get-tuple-element.50), channel_id=1, source_target_pairs={{0,3},{1,0},{2,1},{3,2},{4,7},{5,4},{6,5},{7,6},{8,11},{9,8},{10,9... | collective-permute-start | bytes 786440 | tf_op jit(solution)/shard_map/ppermute | solution.py:449
  32.2 5.1 %convolve.1 = (bf16[8,16,16,128]{3,2,1,0:T(8,128)(2,1)}, f32[32,64,256]{2,1,0:T(8,128)}, f32[32,64,256]{2,1,0:T(8,128)}) custom-call(bf16[8,32,16,128]{3,2,1,0:T(8,128)(2,1)S(1)} %all-to-all-done.pairs_ref, bf16[256,256]{1,0:T(8,128)(2,1)} %constant.87.clone.first_ref, bf16[256,256]{1,0:T(8,128)(2,1)} %constant.88.clone.forward_ref, ...), custom_call_target="tpu_custom_call" | custom-call | tf_op jit(solution)/shard_map/convolve/pallas_call | solution.py:154
  37.3 3.8 %all-to-all-start.1 = ((bf16[8,16,16,128]{3,2,1,0:T(8,128)(2,1)}), bf16[8,16,16,128]{3,2,1,0:T(8,128)(2,1)S(1)}, u32[]{:S(2)}, u32[]{:S(2)}) async-start(bf16[8,16,16,128]{3,2,1,0:T(8,128)(2,1)} %get-tuple-element.52), calls=%async_computation.1 | async-start | bytes 1048576 | tf_op jit(solution)/shard_map/all_to_all | solution.py:440
  41.1 4.2 %unproject.7.refs_0_ = bf16[256,1024]{1,0:T(8,128)(2,1)} custom-call(s32[1]{0:T(128)} %bitcast.1.place_ref, bf16[1024,2048]{1,0:T(8,128)(2,1)} %refs_0_.4, bf16[2048,1024]{1,0:T(8,128)(2,1)} %refs_4_.1), custom_call_target="tpu_custom_call" | custom-call | flops 40000000000 | bytes 100000000 | tf_op jit(solution)/shard_map/unproject/pallas_call | solution.py:376
  45.3 1.5 %collective-permute-done.5.refs_4_ = bf16[256,512]{1,0:T(8,128)(2,1)S(1)} collective-permute-done((bf16[256,512]{1,0:T(8,128)(2,1)}, bf16[256,512]{1,0:T(8,128)(2,1)S(1)}, u32[]{:S(2)}, u32[]{:S(2)}) %collective-permute-start.5) | collective-permute-done | bytes 262176 | tf_op jit(solution)/shard_map/ppermute | solution.py:449
  46.8 2.6 %regard.1 = (f32[256,1024]{1,0:T(8,128)}, bf16[128,16,128]{2,1,0:T(8,128)(2,1)}) custom-call(s32[1]{0:T(128)} %bitcast.flag_ref, bf16[256,1024]{1,0:T(8,128)(2,1)S(1)} %copy-done.1, bf16[256,1024]{1,0:T(8,128)(2,1)} %unproject.7.refs_0_, bf16[256,512]{1,0:T(8,128)(2,1)S(1)} %collective-permute-done.2.refs_1_, ...), custom_call_target="tpu_custom_call" | custom-call | tf_op jit(solution)/shard_map/regard/pallas_call | solution.py:266
  49.4 1.4 %all-to-all-done.1 = bf16[8,16,16,128]{3,2,1,0:T(8,128)(2,1)S(1)} async-done(((bf16[8,16,16,128]{3,2,1,0:T(8,128)(2,1)}), bf16[8,16,16,128]{3,2,1,0:T(8,128)(2,1)S(1)}, u32[]{:S(2)}, u32[]{:S(2)}) %all-to-all-start.1) | async-done | bytes 524320 | tf_op jit(solution)/shard_map/all_to_all | solution.py:440
  52.1 3.5 %all-to-all-start.2 = ((bf16[8,16,16,128]{3,2,1,0:T(8,128)(2,1)}), bf16[8,16,16,128]{3,2,1,0:T(8,128)(2,1)S(1)}, u32[]{:S(2)}, u32[]{:S(2)}) async-start(bf16[8,16,16,128]{3,2,1,0:T(8,128)(2,1)} %bitcast.28), calls=%async_computation.2 | async-start | bytes 1048576 | tf_op jit(solution)/shard_map/all_to_all | solution.py:440
  56.2 3.3 %collective-permute-start.7 = (bf16[256,1024]{1,0:T(8,128)(2,1)}, bf16[256,1024]{1,0:T(8,128)(2,1)S(1)}, u32[]{:S(2)}, u32[]{:S(2)}) collective-permute-start(bf16[256,1024]{1,0:T(8,128)(2,1)} %get-tuple-element.68.refs_0_.refs_2_), channel_id=1, source_target_pairs={{0,3},{1,0},{2,1},{3,2},{4,7},{5,4},{6,5},{7,6},{8,11},{9,8},{10,9... | collective-permute-start | bytes 1572872 | tf_op jit(solution)/shard_map/ppermute | solution.py:449
  59.4 5.8 %all-to-all-done.2.pairs_ref = bf16[8,16,16,128]{3,2,1,0:T(8,128)(2,1)S(1)} async-done(((bf16[8,16,16,128]{3,2,1,0:T(8,128)(2,1)}), bf16[8,16,16,128]{3,2,1,0:T(8,128)(2,1)S(1)}, u32[]{:S(2)}, u32[]{:S(2)}) %all-to-all-start.2) | async-done | bytes 524320 | tf_op jit(solution)/shard_map/all_to_all | solution.py:440
  65.2 5.7 %correlate.1 = bf16[8,32,16,128]{3,2,1,0:T(8,128)(2,1)} custom-call(bf16[8,16,16,128]{3,2,1,0:T(8,128)(2,1)S(1)} %all-to-all-done.2.pairs_ref, f32[32,64,256]{2,1,0:T(8,128)} %get-tuple-element.61.signal_ref, f32[32,64,256]{2,1,0:T(8,128)} %get-tuple-element.62.filter_ref, bf16[256,256]{1,0:T(8,128)(2,1)} %constant.87.clone.first_ref, ...), custom_call_target="tpu_custom_call" | custom-call | tf_op jit(solution)/shard_map/correlate/pallas_call | solution.py:180
  70.9 3.7 %all-to-all-start.3 = ((bf16[8,32,16,128]{3,2,1,0:T(8,128)(2,1)}), bf16[8,32,16,128]{3,2,1,0:T(8,128)(2,1)S(1)}, u32[]{:S(2)}, u32[]{:S(2)}) async-start(bf16[8,32,16,128]{3,2,1,0:T(8,128)(2,1)} %correlate.1), calls=%async_computation.3 | async-start | bytes 2097152 | tf_op jit(solution)/shard_map/all_to_all | solution.py:440
  74.6 6.9 %collective-permute-done.7.refs_3_ = bf16[256,1024]{1,0:T(8,128)(2,1)S(1)} collective-permute-done((bf16[256,1024]{1,0:T(8,128)(2,1)}, bf16[256,1024]{1,0:T(8,128)(2,1)S(1)}, u32[]{:S(2)}, u32[]{:S(2)}) %collective-permute-start.7) | collective-permute-done | bytes 524320 | tf_op jit(solution)/shard_map/ppermute | solution.py:449
  81.6 2.4 %collective-permute-start.8 = (bf16[256,1024]{1,0:T(8,128)(2,1)S(1)}, bf16[256,1024]{1,0:T(8,128)(2,1)}, u32[]{:S(2)}, u32[]{:S(2)}) collective-permute-start(bf16[256,1024]{1,0:T(8,128)(2,1)S(1)} %select_select_fusion), channel_id=1, source_target_pairs={{0,2},{3,1},{2,3},{1,0},{4,6},{7,5},{6,7},{5,4},{8,10},{11,9},{10,... | collective-permute-start | bytes 1572872 | tf_op jit(solution)/shard_map/ppermute | solution.py:553
  84.0 7.7 %project.1 = (bf16[4,128,2048]{2,1,0:T(8,128)(2,1)}, bf16[4,128,2048]{2,1,0:T(8,128)(2,1)}) custom-call(s32[1]{0:T(128)} %bitcast.5.core_ref, bf16[256,1024]{1,0:T(8,128)(2,1)S(1)} %copy-done, bf16[256,1024]{1,0:T(8,128)(2,1)S(1)} %collective-permute-done.6.refs_1_, bf16[256,1024]{1,0:T(8,128)(2,1)S(1)} %copy-done, ...), custom_call_target="tpu_custom_call" | custom-call | tf_op jit(solution)/shard_map/project/pallas_call | solution.py:419
  91.7 3.3 %collective-permute-done.8 = bf16[256,1024]{1,0:T(8,128)(2,1)} collective-permute-done((bf16[256,1024]{1,0:T(8,128)(2,1)S(1)}, bf16[256,1024]{1,0:T(8,128)(2,1)}, u32[]{:S(2)}, u32[]{:S(2)}) %collective-permute-start.8) | collective-permute-done | bytes 524320 | tf_op jit(solution)/shard_map/ppermute | solution.py:553
  95.0 3.8 %convolution_convert_fusion = bf16[256,2048]{1,0:T(8,128)(2,1)S(1)} fusion(bf16[256,1024]{1,0:T(8,128)(2,1)} %collective-permute-done.8, bf16[2048,1024]{1,0:T(8,128)(2,1)} %refs_4_.1), kind=kOutput, calls=%fused_computation.1 | convolution fusion | flops 1074266112 | bytes 5767168 | tf_op jit(solution)/shard_map/zct,dt->zcd/dot_general | solution.py:463
  101.2 1.5 %collective-permute-start.11 = (bf16[2,64,2048]{2,1,0:T(8,128)(2,1)S(1)}, bf16[2,64,2048]{2,1,0:T(8,128)(2,1)}, u32[]{:S(2)}, u32[]{:S(2)}) collective-permute-start(bf16[2,64,2048]{2,1,0:T(8,128)(2,1)S(1)} %pad_maximum_fusion.1), channel_id=1, source_target_pairs={{0,8},{4,12},{8,0},{12,4},{16,24},{20,28},{24,16},{28,20},{1,9},{5... | collective-permute-start | bytes 1572872 | tf_op jit(solution)/shard_map/ppermute | solution.py:487
  102.8 1.6 %collective-permute-start.12 = (bf16[2,64,2048]{2,1,0:T(8,128)(2,1)S(1)}, bf16[2,64,2048]{2,1,0:T(8,128)(2,1)}, u32[]{:S(2)}, u32[]{:S(2)}) collective-permute-start(bf16[2,64,2048]{2,1,0:T(8,128)(2,1)S(1)} %pad_maximum_fusion.2), channel_id=1, source_target_pairs={{0,16},{4,20},{8,24},{12,28},{16,0},{20,4},{24,8},{28,12},{1,17},{... | collective-permute-start | bytes 1572872 | tf_op jit(solution)/shard_map/ppermute | solution.py:488
  104.4 3.3 %finish.1 = (bf16[256,1024]{1,0:T(8,128)(2,1)}, bf16[256,1024]{1,0:T(8,128)(2,1)}, f32[256,1024]{1,0:T(8,128)}) custom-call(bf16[256,16,128]{2,1,0:T(8,128)(2,1)S(1)} %bitcast.23, bf16[256,1024]{1,0:T(8,128)(2,1)} %signal_ref.3, bf16[256,1024]{1,0:T(8,128)(2,1)} %gate_ref.7), custom_call_target="tpu_custom_call" | custom-call | tf_op jit(solution)/shard_map/finish/pallas_call | solution.py:328
  107.7 7.9 %collective-permute-done.11 = bf16[2,64,2048]{2,1,0:T(8,128)(2,1)} collective-permute-done((bf16[2,64,2048]{2,1,0:T(8,128)(2,1)S(1)}, bf16[2,64,2048]{2,1,0:T(8,128)(2,1)}, u32[]{:S(2)}, u32[]{:S(2)}) %collective-permute-start.11) | collective-permute-done | bytes 524320 | tf_op jit(solution)/shard_map/ppermute | solution.py:487
  118.1 1.6 %collective-permute-start.13 = (bf16[64,2048]{1,0:T(8,128)(2,1)S(1)}, bf16[64,2048]{1,0:T(8,128)(2,1)S(1)}, u32[]{:S(2)}, u32[]{:S(2)}) collective-permute-start(bf16[64,2048]{1,0:T(8,128)(2,1)S(1)} %get-tuple-element.83), channel_id=1, source_target_pairs={{0,16},{4,20},{8,24},{12,28},{16,0},{20,4},{24,8},{28,12},{1,17},{... | collective-permute-start | bytes 786440 | tf_op jit(solution)/shard_map/ppermute | solution.py:491
  121.9 3.7 %collective-permute-done.13 = bf16[64,2048]{1,0:T(8,128)(2,1)S(1)} collective-permute-done((bf16[64,2048]{1,0:T(8,128)(2,1)S(1)}, bf16[64,2048]{1,0:T(8,128)(2,1)S(1)}, u32[]{:S(2)}, u32[]{:S(2)}) %collective-permute-start.13) | collective-permute-done | bytes 262176 | tf_op jit(solution)/shard_map/ppermute | solution.py:491
  (45 shorter events, 13.2 us)
Async XLA Ops:
  4.9 12.2 %collective-permute-start = (bf16[256,512]{1,0:T(8,128)(2,1)}, bf16[256,512]{1,0:T(8,128)(2,1)S(1)}, u32[]{:S(2)}, u32[]{:S(2)}) collective-permute-start(bf16[256,512]{1,0:T(8,128)(2,1)} %get-tuple-element.43), channel_id=1, source_target_pairs={{2,0},{1,3},{3,2},{0,1},{6,4},{5,7},{7,6},{4,5},{10,8},{9,11},{11,... | collective-permute-start | bytes 786440 | tf_op jit(solution)/shard_map/ppermute | solution.py:520
  7.9 6.6 %copy-start.7 = (bf16[256,512]{1,0:T(8,128)(2,1)S(1)}, bf16[256,512]{1,0:T(8,128)(2,1)}, u32[]{:S(2)}) copy-start(bf16[256,512]{1,0:T(8,128)(2,1)} %get-tuple-element.49) | copy-start | bytes 786436
  10.7 21.5 %all-to-all-start = ((bf16[8,32,16,128]{3,2,1,0:T(8,128)(2,1)}), bf16[8,32,16,128]{3,2,1,0:T(8,128)(2,1)S(1)}, u32[]{:S(2)}, u32[]{:S(2)}) async-start(bf16[8,32,16,128]{3,2,1,0:T(8,128)(2,1)} %bitcast.25), calls=%async_computation | async-start | bytes 2097152 | tf_op jit(solution)/shard_map/all_to_all | solution.py:440
  14.4 9.6 %collective-permute-start.1 = (bf16[256,512]{1,0:T(8,128)(2,1)S(1)}, bf16[256,512]{1,0:T(8,128)(2,1)S(1)}, u32[]{:S(2)}, u32[]{:S(2)}) collective-permute-start(bf16[256,512]{1,0:T(8,128)(2,1)S(1)} %copy-done.7), channel_id=1, source_target_pairs={{2,0},{1,3},{3,2},{0,1},{6,4},{5,7},{7,6},{4,5},{10,8},{9,11},{11,... | collective-permute-start | bytes 786440 | tf_op jit(solution)/shard_map/ppermute | solution.py:520
  21.4 23.9 %collective-permute-start.4 = (bf16[256,512]{1,0:T(8,128)(2,1)}, bf16[256,512]{1,0:T(8,128)(2,1)S(1)}, u32[]{:S(2)}, u32[]{:S(2)}) collective-permute-start(bf16[256,512]{1,0:T(8,128)(2,1)} %get-tuple-element.47), channel_id=1, source_target_pairs={{0,3},{1,0},{2,1},{3,2},{4,7},{5,4},{6,5},{7,6},{8,11},{9,8},{10,9... | collective-permute-start | bytes 786440 | tf_op jit(solution)/shard_map/ppermute | solution.py:449
  23.4 21.9 %collective-permute-start.2 = (bf16[256,512]{1,0:T(8,128)(2,1)}, bf16[256,512]{1,0:T(8,128)(2,1)S(1)}, u32[]{:S(2)}, u32[]{:S(2)}) collective-permute-start(bf16[256,512]{1,0:T(8,128)(2,1)} %get-tuple-element.54), channel_id=1, source_target_pairs={{0,1},{1,2},{2,3},{3,0},{4,5},{5,6},{6,7},{7,4},{8,9},{9,10},{10,1... | collective-permute-start | bytes 786440 | tf_op jit(solution)/shard_map/ppermute | solution.py:449
  28.4 16.9 %collective-permute-start.3 = (bf16[256,512]{1,0:T(8,128)(2,1)}, bf16[256,512]{1,0:T(8,128)(2,1)S(1)}, u32[]{:S(2)}, u32[]{:S(2)}) collective-permute-start(bf16[256,512]{1,0:T(8,128)(2,1)} %get-tuple-element.55), channel_id=1, source_target_pairs={{0,1},{1,2},{2,3},{3,0},{4,5},{5,6},{6,7},{7,4},{8,9},{9,10},{10,1... | collective-permute-start | bytes 786440 | tf_op jit(solution)/shard_map/ppermute | solution.py:449
  30.5 16.3 %collective-permute-start.5 = (bf16[256,512]{1,0:T(8,128)(2,1)}, bf16[256,512]{1,0:T(8,128)(2,1)S(1)}, u32[]{:S(2)}, u32[]{:S(2)}) collective-permute-start(bf16[256,512]{1,0:T(8,128)(2,1)} %get-tuple-element.50), channel_id=1, source_target_pairs={{0,3},{1,0},{2,1},{3,2},{4,7},{5,4},{6,5},{7,6},{8,11},{9,8},{10,9... | collective-permute-start | bytes 786440 | tf_op jit(solution)/shard_map/ppermute | solution.py:449
  37.3 13.6 %all-to-all-start.1 = ((bf16[8,16,16,128]{3,2,1,0:T(8,128)(2,1)}), bf16[8,16,16,128]{3,2,1,0:T(8,128)(2,1)S(1)}, u32[]{:S(2)}, u32[]{:S(2)}) async-start(bf16[8,16,16,128]{3,2,1,0:T(8,128)(2,1)} %get-tuple-element.52), calls=%async_computation.1 | async-start | bytes 1048576 | tf_op jit(solution)/shard_map/all_to_all | solution.py:440
  41.1 5.7 %copy-start.1 = (bf16[256,1024]{1,0:T(8,128)(2,1)S(1)}, bf16[256,1024]{1,0:T(8,128)(2,1)}, u32[]{:S(2)}) copy-start(bf16[256,1024]{1,0:T(8,128)(2,1)} %gate_ref.6) | copy-start | bytes 1572868
  52.1 13.2 %all-to-all-start.2 = ((bf16[8,16,16,128]{3,2,1,0:T(8,128)(2,1)}), bf16[8,16,16,128]{3,2,1,0:T(8,128)(2,1)S(1)}, u32[]{:S(2)}, u32[]{:S(2)}) async-start(bf16[8,16,16,128]{3,2,1,0:T(8,128)(2,1)} %bitcast.28), calls=%async_computation.2 | async-start | bytes 1048576 | tf_op jit(solution)/shard_map/all_to_all | solution.py:440
  55.6 19.0 %collective-permute-start.6 = (bf16[256,1024]{1,0:T(8,128)(2,1)}, bf16[256,1024]{1,0:T(8,128)(2,1)S(1)}, u32[]{:S(2)}, u32[]{:S(2)}) collective-permute-start(bf16[256,1024]{1,0:T(8,128)(2,1)} %get-tuple-element.68.refs_0_.refs_2_), channel_id=1, source_target_pairs={{0,1},{1,2},{2,3},{3,0},{4,5},{5,6},{6,7},{7,4},{8,9},{9,10},{10,1... | collective-permute-start | bytes 1572872 | tf_op jit(solution)/shard_map/ppermute | solution.py:449
  56.2 25.3 %collective-permute-start.7 = (bf16[256,1024]{1,0:T(8,128)(2,1)}, bf16[256,1024]{1,0:T(8,128)(2,1)S(1)}, u32[]{:S(2)}, u32[]{:S(2)}) collective-permute-start(bf16[256,1024]{1,0:T(8,128)(2,1)} %get-tuple-element.68.refs_0_.refs_2_), channel_id=1, source_target_pairs={{0,3},{1,0},{2,1},{3,2},{4,7},{5,4},{6,5},{7,6},{8,11},{9,8},{10,9... | collective-permute-start | bytes 1572872 | tf_op jit(solution)/shard_map/ppermute | solution.py:449
  70.9 10.6 %copy-start = (bf16[256,1024]{1,0:T(8,128)(2,1)S(1)}, bf16[256,1024]{1,0:T(8,128)(2,1)}, u32[]{:S(2)}) copy-start(bf16[256,1024]{1,0:T(8,128)(2,1)} %get-tuple-element.68.refs_0_.refs_2_) | copy-start | bytes 1572868
  70.9 24.1 %all-to-all-start.3 = ((bf16[8,32,16,128]{3,2,1,0:T(8,128)(2,1)}), bf16[8,32,16,128]{3,2,1,0:T(8,128)(2,1)S(1)}, u32[]{:S(2)}, u32[]{:S(2)}) async-start(bf16[8,32,16,128]{3,2,1,0:T(8,128)(2,1)} %correlate.1), calls=%async_computation.3 | async-start | bytes 2097152 | tf_op jit(solution)/shard_map/all_to_all | solution.py:440
  81.6 13.4 %collective-permute-start.8 = (bf16[256,1024]{1,0:T(8,128)(2,1)S(1)}, bf16[256,1024]{1,0:T(8,128)(2,1)}, u32[]{:S(2)}, u32[]{:S(2)}) collective-permute-start(bf16[256,1024]{1,0:T(8,128)(2,1)S(1)} %select_select_fusion), channel_id=1, source_target_pairs={{0,2},{3,1},{2,3},{1,0},{4,6},{7,5},{6,7},{5,4},{8,10},{11,9},{10,... | collective-permute-start | bytes 1572872 | tf_op jit(solution)/shard_map/ppermute | solution.py:553
  95.0 4.4 %collective-permute-start.9 = (bf16[4,128,2048]{2,1,0:T(8,128)(2,1)}, bf16[4,128,2048]{2,1,0:T(8,128)(2,1)S(1)}, u32[]{:S(2)}, u32[]{:S(2)}) collective-permute-start(bf16[4,128,2048]{2,1,0:T(8,128)(2,1)} %get-tuple-element.73), channel_id=1, source_target_pairs={{0,4},{4,0},{8,12},{12,8},{16,20},{20,16},{24,28},{28,24},{1,5},{5... | collective-permute-start | bytes 6291464 | tf_op jit(solution)/shard_map/ppermute | solution.py:559
  95.0 4.4 %copy-start.4 = (bf16[4,128,2048]{2,1,0:T(8,128)(2,1)S(1)}, bf16[4,128,2048]{2,1,0:T(8,128)(2,1)}, u32[]{:S(2)}) copy-start(bf16[4,128,2048]{2,1,0:T(8,128)(2,1)} %get-tuple-element.71) | copy-start | bytes 6291460
  98.9 2.1 %collective-permute-start.10 = (bf16[1,128,2048]{2,1,0:T(8,128)(2,1)S(1)}, bf16[1,128,2048]{2,1,0:T(8,128)(2,1)S(1)}, u32[]{:S(2)}, u32[]{:S(2)}) collective-permute-start(bf16[1,128,2048]{2,1,0:T(8,128)(2,1)S(1)} %dynamic-slice_bitcast_fusion), channel_id=1, source_target_pairs={{0,4},{4,0},{8,12},{12,8},{16,20},{20,16},{24,28},{28,24},{1,5},{5... | collective-permute-start | bytes 1572872 | tf_op jit(solution)/shard_map/ppermute | solution.py:465
  101.1 1.7 %copy-start.2 = (bf16[4,128,2048]{2,1,0:T(8,128)(2,1)}, bf16[4,128,2048]{2,1,0:T(8,128)(2,1)S(1)}, u32[]{:S(2)}) copy-start(bf16[4,128,2048]{2,1,0:T(8,128)(2,1)S(1)} %fusion.1) | copy-start | bytes 6291460
  101.2 14.4 %collective-permute-start.11 = (bf16[2,64,2048]{2,1,0:T(8,128)(2,1)S(1)}, bf16[2,64,2048]{2,1,0:T(8,128)(2,1)}, u32[]{:S(2)}, u32[]{:S(2)}) collective-permute-start(bf16[2,64,2048]{2,1,0:T(8,128)(2,1)S(1)} %pad_maximum_fusion.1), channel_id=1, source_target_pairs={{0,8},{4,12},{8,0},{12,4},{16,24},{20,28},{24,16},{28,20},{1,9},{5... | collective-permute-start | bytes 1572872 | tf_op jit(solution)/shard_map/ppermute | solution.py:487
  102.8 18.1 %copy-start.5 = (f32[256,1024]{1,0:T(8,128)S(1)}, f32[256,1024]{1,0:T(8,128)}, u32[]{:S(2)}) copy-start(f32[256,1024]{1,0:T(8,128)} %get-tuple-element.63) | copy-start | bytes 3145732
  102.8 14.1 %collective-permute-start.12 = (bf16[2,64,2048]{2,1,0:T(8,128)(2,1)S(1)}, bf16[2,64,2048]{2,1,0:T(8,128)(2,1)}, u32[]{:S(2)}, u32[]{:S(2)}) collective-permute-start(bf16[2,64,2048]{2,1,0:T(8,128)(2,1)S(1)} %pad_maximum_fusion.2), channel_id=1, source_target_pairs={{0,16},{4,20},{8,24},{12,28},{16,0},{20,4},{24,8},{28,12},{1,17},{... | collective-permute-start | bytes 1572872 | tf_op jit(solution)/shard_map/ppermute | solution.py:488
  104.4 12.5 %copy-start.3 = (bf16[4,128,2048]{2,1,0:T(8,128)(2,1)S(1)}, bf16[4,128,2048]{2,1,0:T(8,128)(2,1)}, u32[]{:S(2)}) copy-start(bf16[4,128,2048]{2,1,0:T(8,128)(2,1)} %copy-done.2) | copy-start | bytes 6291460
  104.4 16.5 %copy-start.6 = (bf16[256,1024]{1,0:T(8,128)(2,1)S(1)}, bf16[256,1024]{1,0:T(8,128)(2,1)}, u32[]{:S(2)}) copy-start(bf16[256,1024]{1,0:T(8,128)(2,1)} %get-tuple-element.64) | copy-start | bytes 1572868
  118.1 7.5 %collective-permute-start.13 = (bf16[64,2048]{1,0:T(8,128)(2,1)S(1)}, bf16[64,2048]{1,0:T(8,128)(2,1)S(1)}, u32[]{:S(2)}, u32[]{:S(2)}) collective-permute-start(bf16[64,2048]{1,0:T(8,128)(2,1)S(1)} %get-tuple-element.83), channel_id=1, source_target_pairs={{0,16},{4,20},{8,24},{12,28},{16,0},{20,4},{24,8},{28,12},{1,17},{... | collective-permute-start | bytes 786440 | tf_op jit(solution)/shard_map/ppermute | solution.py:491
  119.6 7.2 %collective-permute-start.14 = (bf16[64,2048]{1,0:T(8,128)(2,1)S(1)}, bf16[64,2048]{1,0:T(8,128)(2,1)S(1)}, u32[]{:S(2)}, u32[]{:S(2)}) collective-permute-start(bf16[64,2048]{1,0:T(8,128)(2,1)S(1)} %get-tuple-element.84), channel_id=1, source_target_pairs={{0,8},{4,12},{8,0},{12,4},{16,24},{20,28},{24,16},{28,20},{1,9},{5... | collective-permute-start | bytes 786440 | tf_op jit(solution)/shard_map/ppermute | solution.py:492

commit v11 on v10

--- a/solution.py
+++ b/solution.py
@@ -47,7 +47,7 @@
         first[pair, 1, :, :, pair, :] = -np.sin(angle).reshape(outer, blocks, per)
         last[:, pair, :, pair, 0, :] = np.cos(angle.T).reshape(blocks, per, outer) / tokens
         last[:, pair, :, pair, 1, :] = -np.sin(angle.T).reshape(blocks, per, outer) / tokens
-    first = high_low(first.reshape(4 * outer, 2 * outer), 1)
+    first = first.reshape(4 * outer, 2 * outer).astype(jnp.bfloat16)
     last = high_low(last.reshape(2 * outer, 4 * outer), 1)
     turn = 2.0 * math.pi / tokens * np.outer(freq, np.arange(LANES))
     twiddle = np.stack([np.cos(turn), np.sin(turn)]).astype(np.float32)
@@ -65,7 +65,7 @@
 def forward_pair(pair_block, first, twiddle):
     outer = twiddle.shape[1]
     rows = pair_block.reshape(2 * outer, LANES)
-    part = mxu(first, jnp.concatenate([rows, rows], axis=0))
+    part = mxu(first, rows)
     cos, sin = twiddle[0], twiddle[1]
     turned = []
     for pair in range(2):
@@ -543,7 +543,7 @@
     own = unproject(tie(out_proj, conv), grad_output, [0], line, chan_count)
     shares = [held_in_hbm(*own), *shares]
     grad_mix, grad_conv = regard(outer_gate, shares, flag)
-    mixed, conv_out = mix(tie(exchange(conv), grad_conv), outer_gate)
+    mixed, conv_out = mix(exchange(conv), outer_gate)
     held = gather_first(mixed)
     grad_conv = tie(grad_conv, mixed).reshape(seq_count, owned // 2, 2 * per, LANES)
     corr = correlate(exchange(grad_conv), spec_signal, spec_filter, tables)

time: 130 us -> 130 us (level)
  transfers between devices with their start and end apart: 19 -> 19, of which waited for: 11 -> 11; matrix products, arithmetic and copies ran while one was open for 4% -> 4% of each run, Pallas kernels for 31% -> 30%
where the time goes in v11:
time: 130 us; the launch traced here: 129 us
  Pallas kernels  44.6 us (34%)
  starting transfers between devices  39 us (30%)
  waiting for transfers between devices  35.1 us (27%)
  other arithmetic  5.6 us (4%)
  matrix products  3.78 us (3%)
    pallas_call x4, Pallas kernels, unproject(): pl.pallas_call(functools.partial(unproject_kernel, len(offsets), splits,...  17 us
    all_to_all x4, starting transfers between devices, exchange(): lax.all_to_all(blocks, 'seq', split_axis=0, concat_axis=0, tiled=True)  14.7 us
    ppermute x6, starting transfers between devices, shift(): lax.ppermute(block, 'chan', [(i, (i + by) % count) for i in range(count)])  9.73 us
    ppermute x6, waiting for transfers between devices, shift(): lax.ppermute(block, 'chan', [(i, (i + by) % count) for i in range(count)])  9.24 us
    ppermute x1, waiting for transfers between devices, scatter_chips(): lax.ppermute(jnp.stack([part(1, 0), part(3, 0)]), 'seq', swaps(count, 2))  7.87 us
    pallas_call x1, Pallas kernels, project(): pl.pallas_call(project_kernel, grid_spec=pltpu.PrefetchScalarGridSpec(num...  7.74 us
    all_to_all x4, waiting for transfers between devices, exchange(): lax.all_to_all(blocks, 'seq', split_axis=0, concat_axis=0, tiled=True)  6.7 us
    ppermute x2, starting transfers between devices, body(): lax.ppermute(far, 'chan', [(2, 0), (1, 3), (3, 2), (0, 1)])  5.67 us
  transfers between devices with their start and end apart: 19, of which 11 were waited for; matrix products, arithmetic and copies ran while one was open for 4% of the time, Pallas kernels for 30%

profile of v11, /device:TPU:0, one launch (start us, length us, event | category | flops | bytes accessed | tf_op | source)
XLA Modules:
  0.0 129.0 jit_solution(9188087990403586010)
XLA Ops:
  0.6 4.2 %unproject.4 = (bf16[256,512]{1,0:T(8,128)(2,1)}, bf16[256,512]{1,0:T(8,128)(2,1)}) custom-call(s32[1]{0:T(128)} %bitcast.1.place_ref, bf16[1024,2048]{1,0:T(8,128)(2,1)} %refs_0_.4, bf16[2048,1024]{1,0:T(8,128)(2,1)} %refs_4_.1), custom_call_target="tpu_custom_call" | custom-call | flops 40000000000 | bytes 100000000 | tf_op jit(solution)/shard_map/unproject/pallas_call | solution.py:376
  4.9 3.0 %collective-permute-start = (bf16[256,512]{1,0:T(8,128)(2,1)}, bf16[256,512]{1,0:T(8,128)(2,1)S(1)}, u32[]{:S(2)}, u32[]{:S(2)}) collective-permute-start(bf16[256,512]{1,0:T(8,128)(2,1)} %get-tuple-element.42), channel_id=1, source_target_pairs={{2,0},{1,3},{3,2},{0,1},{6,4},{5,7},{7,6},{4,5},{10,8},{9,11},{11,... | collective-permute-start | bytes 786440 | tf_op jit(solution)/shard_map/ppermute | solution.py:520
  7.9 2.8 %prepare.1 = bf16[256,16,128]{2,1,0:T(8,128)(2,1)} custom-call(bf16[256,1024]{1,0:T(8,128)(2,1)} %gate_ref.7, bf16[256,1024]{1,0:T(8,128)(2,1)} %signal_ref.3, bf16[256,1024]{1,0:T(8,128)(2,1)} %filter_ref), custom_call_target="tpu_custom_call" | custom-call | tf_op jit(solution)/shard_map/prepare/pallas_call | solution.py:223
  10.7 3.7 %all-to-all-start = ((bf16[8,32,16,128]{3,2,1,0:T(8,128)(2,1)}), bf16[8,32,16,128]{3,2,1,0:T(8,128)(2,1)S(1)}, u32[]{:S(2)}, u32[]{:S(2)}) async-start(bf16[8,32,16,128]{3,2,1,0:T(8,128)(2,1)} %bitcast.25), calls=%async_computation | async-start | bytes 2097152 | tf_op jit(solution)/shard_map/all_to_all | solution.py:440
  14.4 2.6 %collective-permute-start.1 = (bf16[256,512]{1,0:T(8,128)(2,1)S(1)}, bf16[256,512]{1,0:T(8,128)(2,1)S(1)}, u32[]{:S(2)}, u32[]{:S(2)}) collective-permute-start(bf16[256,512]{1,0:T(8,128)(2,1)S(1)} %copy-done.7), channel_id=1, source_target_pairs={{2,0},{1,3},{3,2},{0,1},{6,4},{5,7},{7,6},{4,5},{10,8},{9,11},{11,... | collective-permute-start | bytes 786440 | tf_op jit(solution)/shard_map/ppermute | solution.py:520
  17.1 4.3 %unproject.5 = (bf16[256,512]{1,0:T(8,128)(2,1)}, bf16[256,512]{1,0:T(8,128)(2,1)}) custom-call(s32[1]{0:T(128)} %bitcast.1.place_ref, bf16[1024,2048]{1,0:T(8,128)(2,1)} %refs_0_.4, bf16[1024,2048]{1,0:T(8,128)(2,1)} %refs_0_.4, bf16[2048,1024]{1,0:T(8,128)(2,1)} %refs_4_.1, bf16[256,512]{1,0:T(8,128)(2,1)S(1)} %collective-permute-done.refs_3_.refs_5_), custom_call_target="tpu_custom_call" | custom-call | flops 40000000000 | bytes 100000000 | tf_op jit(solution)/shard_map/unproject/pallas_call | solution.py:376
  21.4 2.0 %collective-permute-start.4 = (bf16[256,512]{1,0:T(8,128)(2,1)}, bf16[256,512]{1,0:T(8,128)(2,1)S(1)}, u32[]{:S(2)}, u32[]{:S(2)}) collective-permute-start(bf16[256,512]{1,0:T(8,128)(2,1)} %get-tuple-element.46), channel_id=1, source_target_pairs={{0,3},{1,0},{2,1},{3,2},{4,7},{5,4},{6,5},{7,6},{8,11},{9,8},{10,9... | collective-permute-start | bytes 786440 | tf_op jit(solution)/shard_map/ppermute | solution.py:449
  24.1 4.3 %unproject.6 = (bf16[256,512]{1,0:T(8,128)(2,1)}, bf16[256,512]{1,0:T(8,128)(2,1)}) custom-call(s32[1]{0:T(128)} %bitcast.1.place_ref, bf16[1024,2048]{1,0:T(8,128)(2,1)} %refs_0_.4, bf16[1024,2048]{1,0:T(8,128)(2,1)} %refs_0_.4, bf16[2048,1024]{1,0:T(8,128)(2,1)} %refs_4_.1, bf16[256,512]{1,0:T(8,128)(2,1)S(1)} %collective-permute-done.1.refs_3_.refs_6_), custom_call_target="tpu_custom_call" | custom-call | flops 40000000000 | bytes 100000000 | tf_op jit(solution)/shard_map/unproject/pallas_call | solution.py:376
  28.4 2.1 %collective-permute-start.3 = (bf16[256,512]{1,0:T(8,128)(2,1)}, bf16[256,512]{1,0:T(8,128)(2,1)S(1)}, u32[]{:S(2)}, u32[]{:S(2)}) collective-permute-start(bf16[256,512]{1,0:T(8,128)(2,1)} %get-tuple-element.54), channel_id=1, source_target_pairs={{0,1},{1,2},{2,3},{3,0},{4,5},{5,6},{6,7},{7,4},{8,9},{9,10},{10,1... | collective-permute-start | bytes 786440 | tf_op jit(solution)/shard_map/ppermute | solution.py:449
  30.5 1.7 %collective-permute-start.5 = (bf16[256,512]{1,0:T(8,128)(2,1)}, bf16[256,512]{1,0:T(8,128)(2,1)S(1)}, u32[]{:S(2)}, u32[]{:S(2)}) collective-permute-start(bf16[256,512]{1,0:T(8,128)(2,1)} %get-tuple-element.49), channel_id=1, source_target_pairs={{0,3},{1,0},{2,1},{3,2},{4,7},{5,4},{6,5},{7,6},{8,11},{9,8},{10,9... | collective-permute-start | bytes 786440 | tf_op jit(solution)/shard_map/ppermute | solution.py:449
  32.2 4.5 %convolve.1 = (bf16[8,16,16,128]{3,2,1,0:T(8,128)(2,1)}, f32[32,64,256]{2,1,0:T(8,128)}, f32[32,64,256]{2,1,0:T(8,128)}) custom-call(bf16[8,32,16,128]{3,2,1,0:T(8,128)(2,1)S(1)} %all-to-all-done.pairs_ref, bf16[256,128]{1,0:T(8,128)(2,1)} %constant.87.clone.first_ref, bf16[256,256]{1,0:T(8,128)(2,1)} %constant.88.clone.forward_ref, ...), custom_call_target="tpu_custom_call" | custom-call | tf_op jit(solution)/shard_map/convolve/pallas_call | solution.py:154
  36.8 3.8 %all-to-all-start.1 = ((bf16[8,16,16,128]{3,2,1,0:T(8,128)(2,1)}), bf16[8,16,16,128]{3,2,1,0:T(8,128)(2,1)S(1)}, u32[]{:S(2)}, u32[]{:S(2)}) async-start(bf16[8,16,16,128]{3,2,1,0:T(8,128)(2,1)} %get-tuple-element.51), calls=%async_computation.1 | async-start | bytes 1048576 | tf_op jit(solution)/shard_map/all_to_all | solution.py:440
  40.6 4.2 %unproject.7.refs_0_ = bf16[256,1024]{1,0:T(8,128)(2,1)} custom-call(s32[1]{0:T(128)} %bitcast.1.place_ref, bf16[1024,2048]{1,0:T(8,128)(2,1)} %refs_0_.4, bf16[2048,1024]{1,0:T(8,128)(2,1)} %refs_4_.1), custom_call_target="tpu_custom_call" | custom-call | flops 40000000000 | bytes 100000000 | tf_op jit(solution)/shard_map/unproject/pallas_call | solution.py:376
  44.8 2.0 %collective-permute-done.5.refs_4_ = bf16[256,512]{1,0:T(8,128)(2,1)S(1)} collective-permute-done((bf16[256,512]{1,0:T(8,128)(2,1)}, bf16[256,512]{1,0:T(8,128)(2,1)S(1)}, u32[]{:S(2)}, u32[]{:S(2)}) %collective-permute-start.5) | collective-permute-done | bytes 262176 | tf_op jit(solution)/shard_map/ppermute | solution.py:449
  46.8 2.6 %regard.1 = (f32[256,1024]{1,0:T(8,128)}, bf16[128,16,128]{2,1,0:T(8,128)(2,1)}) custom-call(s32[1]{0:T(128)} %bitcast.flag_ref, bf16[256,1024]{1,0:T(8,128)(2,1)S(1)} %copy-done.1, bf16[256,1024]{1,0:T(8,128)(2,1)} %unproject.7.refs_0_, bf16[256,512]{1,0:T(8,128)(2,1)S(1)} %collective-permute-done.2.refs_1_, ...), custom_call_target="tpu_custom_call" | custom-call | tf_op jit(solution)/shard_map/regard/pallas_call | solution.py:266
  51.5 3.5 %all-to-all-start.2 = ((bf16[8,16,16,128]{3,2,1,0:T(8,128)(2,1)}), bf16[8,16,16,128]{3,2,1,0:T(8,128)(2,1)S(1)}, u32[]{:S(2)}, u32[]{:S(2)}) async-start(bf16[8,16,16,128]{3,2,1,0:T(8,128)(2,1)} %bitcast.28), calls=%async_computation.2 | async-start | bytes 1048576 | tf_op jit(solution)/shard_map/all_to_all | solution.py:440
  55.7 3.3 %collective-permute-start.7 = (bf16[256,1024]{1,0:T(8,128)(2,1)}, bf16[256,1024]{1,0:T(8,128)(2,1)S(1)}, u32[]{:S(2)}, u32[]{:S(2)}) collective-permute-start(bf16[256,1024]{1,0:T(8,128)(2,1)} %get-tuple-element.66.refs_0_.refs_2_), channel_id=1, source_target_pairs={{0,3},{1,0},{2,1},{3,2},{4,7},{5,4},{6,5},{7,6},{8,11},{9,8},{10,9... | collective-permute-start | bytes 1572872 | tf_op jit(solution)/shard_map/ppermute | solution.py:449
  58.9 5.8 %all-to-all-done.2.pairs_ref = bf16[8,16,16,128]{3,2,1,0:T(8,128)(2,1)S(1)} async-done(((bf16[8,16,16,128]{3,2,1,0:T(8,128)(2,1)}), bf16[8,16,16,128]{3,2,1,0:T(8,128)(2,1)S(1)}, u32[]{:S(2)}, u32[]{:S(2)}) %all-to-all-start.2) | async-done | bytes 524320 | tf_op jit(solution)/shard_map/all_to_all | solution.py:440
  64.7 5.4 %correlate.1 = bf16[8,32,16,128]{3,2,1,0:T(8,128)(2,1)} custom-call(bf16[8,16,16,128]{3,2,1,0:T(8,128)(2,1)S(1)} %all-to-all-done.2.pairs_ref, f32[32,64,256]{2,1,0:T(8,128)} %get-tuple-element.59.signal_ref, f32[32,64,256]{2,1,0:T(8,128)} %get-tuple-element.60.filter_ref, bf16[256,128]{1,0:T(8,128)(2,1)} %constant.87.clone.first_ref, ...), custom_call_target="tpu_custom_call" | custom-call | tf_op jit(solution)/shard_map/correlate/pallas_call | solution.py:180
  70.1 3.7 %all-to-all-start.3 = ((bf16[8,32,16,128]{3,2,1,0:T(8,128)(2,1)}), bf16[8,32,16,128]{3,2,1,0:T(8,128)(2,1)S(1)}, u32[]{:S(2)}, u32[]{:S(2)}) async-start(bf16[8,32,16,128]{3,2,1,0:T(8,128)(2,1)} %correlate.1), calls=%async_computation.3 | async-start | bytes 2097152 | tf_op jit(solution)/shard_map/all_to_all | solution.py:440
  73.8 7.2 %collective-permute-done.7.refs_3_ = bf16[256,1024]{1,0:T(8,128)(2,1)S(1)} collective-permute-done((bf16[256,1024]{1,0:T(8,128)(2,1)}, bf16[256,1024]{1,0:T(8,128)(2,1)S(1)}, u32[]{:S(2)}, u32[]{:S(2)}) %collective-permute-start.7) | collective-permute-done | bytes 524320 | tf_op jit(solution)/shard_map/ppermute | solution.py:449
  81.1 2.4 %collective-permute-start.8 = (bf16[256,1024]{1,0:T(8,128)(2,1)S(1)}, bf16[256,1024]{1,0:T(8,128)(2,1)}, u32[]{:S(2)}, u32[]{:S(2)}) collective-permute-start(bf16[256,1024]{1,0:T(8,128)(2,1)S(1)} %select_select_fusion), channel_id=1, source_target_pairs={{0,2},{3,1},{2,3},{1,0},{4,6},{7,5},{6,7},{5,4},{8,10},{11,9},{10,... | collective-permute-start | bytes 1572872 | tf_op jit(solution)/shard_map/ppermute | solution.py:553
  83.4 7.7 %project.1 = (bf16[4,128,2048]{2,1,0:T(8,128)(2,1)}, bf16[4,128,2048]{2,1,0:T(8,128)(2,1)}) custom-call(s32[1]{0:T(128)} %bitcast.5.core_ref, bf16[256,1024]{1,0:T(8,128)(2,1)S(1)} %copy-done, bf16[256,1024]{1,0:T(8,128)(2,1)S(1)} %collective-permute-done.6.refs_1_, bf16[256,1024]{1,0:T(8,128)(2,1)S(1)} %copy-done, ...), custom_call_target="tpu_custom_call" | custom-call | tf_op jit(solution)/shard_map/project/pallas_call | solution.py:419
  91.2 3.7 %collective-permute-done.8 = bf16[256,1024]{1,0:T(8,128)(2,1)} collective-permute-done((bf16[256,1024]{1,0:T(8,128)(2,1)S(1)}, bf16[256,1024]{1,0:T(8,128)(2,1)}, u32[]{:S(2)}, u32[]{:S(2)}) %collective-permute-start.8) | collective-permute-done | bytes 524320 | tf_op jit(solution)/shard_map/ppermute | solution.py:553
  94.9 3.8 %convolution_convert_fusion = bf16[256,2048]{1,0:T(8,128)(2,1)S(1)} fusion(bf16[256,1024]{1,0:T(8,128)(2,1)} %collective-permute-done.8, bf16[2048,1024]{1,0:T(8,128)(2,1)} %refs_4_.1), kind=kOutput, calls=%fused_computation.1 | convolution fusion | flops 1074266112 | bytes 5767168 | tf_op jit(solution)/shard_map/zct,dt->zcd/dot_general | solution.py:463
  101.1 1.6 %collective-permute-start.11 = (bf16[2,64,2048]{2,1,0:T(8,128)(2,1)S(1)}, bf16[2,64,2048]{2,1,0:T(8,128)(2,1)}, u32[]{:S(2)}, u32[]{:S(2)}) collective-permute-start(bf16[2,64,2048]{2,1,0:T(8,128)(2,1)S(1)} %pad_maximum_fusion.1), channel_id=1, source_target_pairs={{0,8},{4,12},{8,0},{12,4},{16,24},{20,28},{24,16},{28,20},{1,9},{5... | collective-permute-start | bytes 1572872 | tf_op jit(solution)/shard_map/ppermute | solution.py:487
  102.8 1.5 %collective-permute-start.12 = (bf16[2,64,2048]{2,1,0:T(8,128)(2,1)S(1)}, bf16[2,64,2048]{2,1,0:T(8,128)(2,1)}, u32[]{:S(2)}, u32[]{:S(2)}) collective-permute-start(bf16[2,64,2048]{2,1,0:T(8,128)(2,1)S(1)} %pad_maximum_fusion.2), channel_id=1, source_target_pairs={{0,16},{4,20},{8,24},{12,28},{16,0},{20,4},{24,8},{28,12},{1,17},{... | collective-permute-start | bytes 1572872 | tf_op jit(solution)/shard_map/ppermute | solution.py:488
  104.3 3.3 %finish.1 = (bf16[256,1024]{1,0:T(8,128)(2,1)}, bf16[256,1024]{1,0:T(8,128)(2,1)}, f32[256,1024]{1,0:T(8,128)}) custom-call(bf16[256,16,128]{2,1,0:T(8,128)(2,1)S(1)} %bitcast.23, bf16[256,1024]{1,0:T(8,128)(2,1)} %signal_ref.3, bf16[256,1024]{1,0:T(8,128)(2,1)} %gate_ref.7), custom_call_target="tpu_custom_call" | custom-call | tf_op jit(solution)/shard_map/finish/pallas_call | solution.py:328
  107.6 7.9 %collective-permute-done.11 = bf16[2,64,2048]{2,1,0:T(8,128)(2,1)} collective-permute-done((bf16[2,64,2048]{2,1,0:T(8,128)(2,1)S(1)}, bf16[2,64,2048]{2,1,0:T(8,128)(2,1)}, u32[]{:S(2)}, u32[]{:S(2)}) %collective-permute-start.11) | collective-permute-done | bytes 524320 | tf_op jit(solution)/shard_map/ppermute | solution.py:487
  115.5 1.4 %collective-permute-done.12 = bf16[2,64,2048]{2,1,0:T(8,128)(2,1)} collective-permute-done((bf16[2,64,2048]{2,1,0:T(8,128)(2,1)S(1)}, bf16[2,64,2048]{2,1,0:T(8,128)(2,1)}, u32[]{:S(2)}, u32[]{:S(2)}) %collective-permute-start.12) | collective-permute-done | bytes 524320 | tf_op jit(solution)/shard_map/ppermute | solution.py:488
  118.0 1.5 %collective-permute-start.13 = (bf16[64,2048]{1,0:T(8,128)(2,1)S(1)}, bf16[64,2048]{1,0:T(8,128)(2,1)S(1)}, u32[]{:S(2)}, u32[]{:S(2)}) collective-permute-start(bf16[64,2048]{1,0:T(8,128)(2,1)S(1)} %get-tuple-element.81), channel_id=1, source_target_pairs={{0,16},{4,20},{8,24},{12,28},{16,0},{20,4},{24,8},{28,12},{1,17},{... | collective-permute-start | bytes 786440 | tf_op jit(solution)/shard_map/ppermute | solution.py:491
  121.8 3.8 %collective-permute-done.13 = bf16[64,2048]{1,0:T(8,128)(2,1)S(1)} collective-permute-done((bf16[64,2048]{1,0:T(8,128)(2,1)S(1)}, bf16[64,2048]{1,0:T(8,128)(2,1)S(1)}, u32[]{:S(2)}, u32[]{:S(2)}) %collective-permute-start.13) | collective-permute-done | bytes 262176 | tf_op jit(solution)/shard_map/ppermute | solution.py:491
  (45 shorter events, 12.8 us)
Async XLA Ops:
  4.9 12.2 %collective-permute-start = (bf16[256,512]{1,0:T(8,128)(2,1)}, bf16[256,512]{1,0:T(8,128)(2,1)S(1)}, u32[]{:S(2)}, u32[]{:S(2)}) collective-permute-start(bf16[256,512]{1,0:T(8,128)(2,1)} %get-tuple-element.42), channel_id=1, source_target_pairs={{2,0},{1,3},{3,2},{0,1},{6,4},{5,7},{7,6},{4,5},{10,8},{9,11},{11,... | collective-permute-start | bytes 786440 | tf_op jit(solution)/shard_map/ppermute | solution.py:520
  7.9 6.6 %copy-start.7 = (bf16[256,512]{1,0:T(8,128)(2,1)S(1)}, bf16[256,512]{1,0:T(8,128)(2,1)}, u32[]{:S(2)}) copy-start(bf16[256,512]{1,0:T(8,128)(2,1)} %get-tuple-element.48) | copy-start | bytes 786436
  10.7 21.5 %all-to-all-start = ((bf16[8,32,16,128]{3,2,1,0:T(8,128)(2,1)}), bf16[8,32,16,128]{3,2,1,0:T(8,128)(2,1)S(1)}, u32[]{:S(2)}, u32[]{:S(2)}) async-start(bf16[8,32,16,128]{3,2,1,0:T(8,128)(2,1)} %bitcast.25), calls=%async_computation | async-start | bytes 2097152 | tf_op jit(solution)/shard_map/all_to_all | solution.py:440
  14.4 9.6 %collective-permute-start.1 = (bf16[256,512]{1,0:T(8,128)(2,1)S(1)}, bf16[256,512]{1,0:T(8,128)(2,1)S(1)}, u32[]{:S(2)}, u32[]{:S(2)}) collective-permute-start(bf16[256,512]{1,0:T(8,128)(2,1)S(1)} %copy-done.7), channel_id=1, source_target_pairs={{2,0},{1,3},{3,2},{0,1},{6,4},{5,7},{7,6},{4,5},{10,8},{9,11},{11,... | collective-permute-start | bytes 786440 | tf_op jit(solution)/shard_map/ppermute | solution.py:520
  21.4 23.4 %collective-permute-start.4 = (bf16[256,512]{1,0:T(8,128)(2,1)}, bf16[256,512]{1,0:T(8,128)(2,1)S(1)}, u32[]{:S(2)}, u32[]{:S(2)}) collective-permute-start(bf16[256,512]{1,0:T(8,128)(2,1)} %get-tuple-element.46), channel_id=1, source_target_pairs={{0,3},{1,0},{2,1},{3,2},{4,7},{5,4},{6,5},{7,6},{8,11},{9,8},{10,9... | collective-permute-start | bytes 786440 | tf_op jit(solution)/shard_map/ppermute | solution.py:449
  23.4 21.4 %collective-permute-start.2 = (bf16[256,512]{1,0:T(8,128)(2,1)}, bf16[256,512]{1,0:T(8,128)(2,1)S(1)}, u32[]{:S(2)}, u32[]{:S(2)}) collective-permute-start(bf16[256,512]{1,0:T(8,128)(2,1)} %get-tuple-element.53), channel_id=1, source_target_pairs={{0,1},{1,2},{2,3},{3,0},{4,5},{5,6},{6,7},{7,4},{8,9},{9,10},{10,1... | collective-permute-start | bytes 786440 | tf_op jit(solution)/shard_map/ppermute | solution.py:449
  28.4 16.4 %collective-permute-start.3 = (bf16[256,512]{1,0:T(8,128)(2,1)}, bf16[256,512]{1,0:T(8,128)(2,1)S(1)}, u32[]{:S(2)}, u32[]{:S(2)}) collective-permute-start(bf16[256,512]{1,0:T(8,128)(2,1)} %get-tuple-element.54), channel_id=1, source_target_pairs={{0,1},{1,2},{2,3},{3,0},{4,5},{5,6},{6,7},{7,4},{8,9},{9,10},{10,1... | collective-permute-start | bytes 786440 | tf_op jit(solution)/shard_map/ppermute | solution.py:449
  30.5 16.3 %collective-permute-start.5 = (bf16[256,512]{1,0:T(8,128)(2,1)}, bf16[256,512]{1,0:T(8,128)(2,1)S(1)}, u32[]{:S(2)}, u32[]{:S(2)}) collective-permute-start(bf16[256,512]{1,0:T(8,128)(2,1)} %get-tuple-element.49), channel_id=1, source_target_pairs={{0,3},{1,0},{2,1},{3,2},{4,7},{5,4},{6,5},{7,6},{8,11},{9,8},{10,9... | collective-permute-start | bytes 786440 | tf_op jit(solution)/shard_map/ppermute | solution.py:449
  36.8 13.6 %all-to-all-start.1 = ((bf16[8,16,16,128]{3,2,1,0:T(8,128)(2,1)}), bf16[8,16,16,128]{3,2,1,0:T(8,128)(2,1)S(1)}, u32[]{:S(2)}, u32[]{:S(2)}) async-start(bf16[8,16,16,128]{3,2,1,0:T(8,128)(2,1)} %get-tuple-element.51), calls=%async_computation.1 | async-start | bytes 1048576 | tf_op jit(solution)/shard_map/all_to_all | solution.py:440
  40.6 6.2 %copy-start.1 = (bf16[256,1024]{1,0:T(8,128)(2,1)S(1)}, bf16[256,1024]{1,0:T(8,128)(2,1)}, u32[]{:S(2)}) copy-start(bf16[256,1024]{1,0:T(8,128)(2,1)} %gate_ref.6) | copy-start | bytes 1572868
  51.5 13.2 %all-to-all-start.2 = ((bf16[8,16,16,128]{3,2,1,0:T(8,128)(2,1)}), bf16[8,16,16,128]{3,2,1,0:T(8,128)(2,1)S(1)}, u32[]{:S(2)}, u32[]{:S(2)}) async-start(bf16[8,16,16,128]{3,2,1,0:T(8,128)(2,1)} %bitcast.28), calls=%async_computation.2 | async-start | bytes 1048576 | tf_op jit(solution)/shard_map/all_to_all | solution.py:440
  55.0 18.8 %collective-permute-start.6 = (bf16[256,1024]{1,0:T(8,128)(2,1)}, bf16[256,1024]{1,0:T(8,128)(2,1)S(1)}, u32[]{:S(2)}, u32[]{:S(2)}) collective-permute-start(bf16[256,1024]{1,0:T(8,128)(2,1)} %get-tuple-element.66.refs_0_.refs_2_), channel_id=1, source_target_pairs={{0,1},{1,2},{2,3},{3,0},{4,5},{5,6},{6,7},{7,4},{8,9},{9,10},{10,1... | collective-permute-start | bytes 1572872 | tf_op jit(solution)/shard_map/ppermute | solution.py:449
  55.7 25.3 %collective-permute-start.7 = (bf16[256,1024]{1,0:T(8,128)(2,1)}, bf16[256,1024]{1,0:T(8,128)(2,1)S(1)}, u32[]{:S(2)}, u32[]{:S(2)}) collective-permute-start(bf16[256,1024]{1,0:T(8,128)(2,1)} %get-tuple-element.66.refs_0_.refs_2_), channel_id=1, source_target_pairs={{0,3},{1,0},{2,1},{3,2},{4,7},{5,4},{6,5},{7,6},{8,11},{9,8},{10,9... | collective-permute-start | bytes 1572872 | tf_op jit(solution)/shard_map/ppermute | solution.py:449
  70.1 10.9 %copy-start = (bf16[256,1024]{1,0:T(8,128)(2,1)S(1)}, bf16[256,1024]{1,0:T(8,128)(2,1)}, u32[]{:S(2)}) copy-start(bf16[256,1024]{1,0:T(8,128)(2,1)} %get-tuple-element.66.refs_0_.refs_2_) | copy-start | bytes 1572868
  70.1 24.8 %all-to-all-start.3 = ((bf16[8,32,16,128]{3,2,1,0:T(8,128)(2,1)}), bf16[8,32,16,128]{3,2,1,0:T(8,128)(2,1)S(1)}, u32[]{:S(2)}, u32[]{:S(2)}) async-start(bf16[8,32,16,128]{3,2,1,0:T(8,128)(2,1)} %correlate.1), calls=%async_computation.3 | async-start | bytes 2097152 | tf_op jit(solution)/shard_map/all_to_all | solution.py:440
  81.1 13.8 %collective-permute-start.8 = (bf16[256,1024]{1,0:T(8,128)(2,1)S(1)}, bf16[256,1024]{1,0:T(8,128)(2,1)}, u32[]{:S(2)}, u32[]{:S(2)}) collective-permute-start(bf16[256,1024]{1,0:T(8,128)(2,1)S(1)} %select_select_fusion), channel_id=1, source_target_pairs={{0,2},{3,1},{2,3},{1,0},{4,6},{7,5},{6,7},{5,4},{8,10},{11,9},{10,... | collective-permute-start | bytes 1572872 | tf_op jit(solution)/shard_map/ppermute | solution.py:553
  94.9 4.4 %collective-permute-start.9 = (bf16[4,128,2048]{2,1,0:T(8,128)(2,1)}, bf16[4,128,2048]{2,1,0:T(8,128)(2,1)S(1)}, u32[]{:S(2)}, u32[]{:S(2)}) collective-permute-start(bf16[4,128,2048]{2,1,0:T(8,128)(2,1)} %get-tuple-element.71), channel_id=1, source_target_pairs={{0,4},{4,0},{8,12},{12,8},{16,20},{20,16},{24,28},{28,24},{1,5},{5... | collective-permute-start | bytes 6291464 | tf_op jit(solution)/shard_map/ppermute | solution.py:559
  94.9 4.4 %copy-start.4 = (bf16[4,128,2048]{2,1,0:T(8,128)(2,1)S(1)}, bf16[4,128,2048]{2,1,0:T(8,128)(2,1)}, u32[]{:S(2)}) copy-start(bf16[4,128,2048]{2,1,0:T(8,128)(2,1)} %get-tuple-element.69) | copy-start | bytes 6291460
  98.7 2.1 %collective-permute-start.10 = (bf16[1,128,2048]{2,1,0:T(8,128)(2,1)S(1)}, bf16[1,128,2048]{2,1,0:T(8,128)(2,1)S(1)}, u32[]{:S(2)}, u32[]{:S(2)}) collective-permute-start(bf16[1,128,2048]{2,1,0:T(8,128)(2,1)S(1)} %dynamic-slice_bitcast_fusion), channel_id=1, source_target_pairs={{0,4},{4,0},{8,12},{12,8},{16,20},{20,16},{24,28},{28,24},{1,5},{5... | collective-permute-start | bytes 1572872 | tf_op jit(solution)/shard_map/ppermute | solution.py:465
  101.0 1.8 %copy-start.2 = (bf16[4,128,2048]{2,1,0:T(8,128)(2,1)}, bf16[4,128,2048]{2,1,0:T(8,128)(2,1)S(1)}, u32[]{:S(2)}) copy-start(bf16[4,128,2048]{2,1,0:T(8,128)(2,1)S(1)} %fusion.1) | copy-start | bytes 6291460
  101.1 14.4 %collective-permute-start.11 = (bf16[2,64,2048]{2,1,0:T(8,128)(2,1)S(1)}, bf16[2,64,2048]{2,1,0:T(8,128)(2,1)}, u32[]{:S(2)}, u32[]{:S(2)}) collective-permute-start(bf16[2,64,2048]{2,1,0:T(8,128)(2,1)S(1)} %pad_maximum_fusion.1), channel_id=1, source_target_pairs={{0,8},{4,12},{8,0},{12,4},{16,24},{20,28},{24,16},{28,20},{1,9},{5... | collective-permute-start | bytes 1572872 | tf_op jit(solution)/shard_map/ppermute | solution.py:487
  102.7 18.1 %copy-start.5 = (f32[256,1024]{1,0:T(8,128)S(1)}, f32[256,1024]{1,0:T(8,128)}, u32[]{:S(2)}) copy-start(f32[256,1024]{1,0:T(8,128)} %get-tuple-element.61) | copy-start | bytes 3145732
  102.8 14.1 %collective-permute-start.12 = (bf16[2,64,2048]{2,1,0:T(8,128)(2,1)S(1)}, bf16[2,64,2048]{2,1,0:T(8,128)(2,1)}, u32[]{:S(2)}, u32[]{:S(2)}) collective-permute-start(bf16[2,64,2048]{2,1,0:T(8,128)(2,1)S(1)} %pad_maximum_fusion.2), channel_id=1, source_target_pairs={{0,16},{4,20},{8,24},{12,28},{16,0},{20,4},{24,8},{28,12},{1,17},{... | collective-permute-start | bytes 1572872 | tf_op jit(solution)/shard_map/ppermute | solution.py:488
  104.3 12.6 %copy-start.3 = (bf16[4,128,2048]{2,1,0:T(8,128)(2,1)S(1)}, bf16[4,128,2048]{2,1,0:T(8,128)(2,1)}, u32[]{:S(2)}) copy-start(bf16[4,128,2048]{2,1,0:T(8,128)(2,1)} %copy-done.2) | copy-start | bytes 6291460
  104.3 16.5 %copy-start.6 = (bf16[256,1024]{1,0:T(8,128)(2,1)S(1)}, bf16[256,1024]{1,0:T(8,128)(2,1)}, u32[]{:S(2)}) copy-start(bf16[256,1024]{1,0:T(8,128)(2,1)} %get-tuple-element.62) | copy-start | bytes 1572868
  118.0 7.5 %collective-permute-start.13 = (bf16[64,2048]{1,0:T(8,128)(2,1)S(1)}, bf16[64,2048]{1,0:T(8,128)(2,1)S(1)}, u32[]{:S(2)}, u32[]{:S(2)}) collective-permute-start(bf16[64,2048]{1,0:T(8,128)(2,1)S(1)} %get-tuple-element.81), channel_id=1, source_target_pairs={{0,16},{4,20},{8,24},{12,28},{16,0},{20,4},{24,8},{28,12},{1,17},{... | collective-permute-start | bytes 786440 | tf_op jit(solution)/shard_map/ppermute | solution.py:491
  119.6 7.2 %collective-permute-start.14 = (bf16[64,2048]{1,0:T(8,128)(2,1)S(1)}, bf16[64,2048]{1,0:T(8,128)(2,1)S(1)}, u32[]{:S(2)}, u32[]{:S(2)}) collective-permute-start(bf16[64,2048]{1,0:T(8,128)(2,1)S(1)} %get-tuple-element.82), channel_id=1, source_target_pairs={{0,8},{4,12},{8,0},{12,4},{16,24},{20,28},{24,16},{28,20},{1,9},{5... | collective-permute-start | bytes 786440 | tf_op jit(solution)/shard_map/ppermute | solution.py:492
